TPU v7x, 32 devices: a whole 2x2x4 slice. The times are simulated.
32 devices in a mesh: group: 2 (over y), pos: 8 (over z, x), tile: 2 (over core).
Axes of the slice: x: 2, y: 2, z: 4, core: 2. Of those that a mesh axis runs over, the one named last changes fastest.
Arguments:
- object_field: float32 [2, 2048, 256], P(None, ('group', 'pos')), parts along dimension 1, may hold values from -5 to 5
- probe: float32 [2, 8, 65536], P(None, 'tile'), may hold values from -2.1 to 2.1
- measured: float32 [32, 256, 256], P(('group', 'pos')), parts along dimension 0, may hold values from 0.3 to 12
- offsets: int32 [32, 2], P(('group', 'pos')), parts along dimension 0, may hold values from 0 to 768, as said below
- counts: int32 [16], P(('group', 'pos')), parts along dimension 0, may hold values from 1 to 2, as said below
Outputs:
- object_out: float32 [2, 2048, 256], P(None, ('group', 'pos', 'tile')), parts along dimension 1
- probe_out: float32 [2, 16, 65536], P(None, ('group', 'tile'), 'pos'), parts along dimension 1
There are 2 independent parts, one for each index of `group`. A program takes and returns all parts, laid end to end along the dimension named above; an argument that names none is the same for every part. Nothing has to cross between parts.
Inputs may be any that keep to these rules, and one draw needn't show every extreme that they name: The row offset of slot j lies between (j // 2) * 128 - 256 / 2 and (j // 2) * 128, kept within 0 and 768; the column offset between 0 and 0, so every patch lies inside the object; the first slot has offsets (0, 0) and the last (768, 0). Entry p counts the live slots among slots p * 2 to p * 2 + 1, which are the first ones of that block; entry 0 is 2 and entry 1 is 1.
All inputs are finite; a program needn't handle non-finite values.
Results may differ from a plain program's by a relative error of at most 0.0001.
Values sent between devices are 32-bit elements; how exact they have to be, the bound alone decides.
No kernel may reach another device: no remote copies, remote signals or barrier semaphores. Data moves between devices by JAX's collectives and lax.ppermute only.
A program may use at most 64 MiB of HBM per device.

v0:
```python
import math

import jax
import jax.numpy as jnp
from jax import lax
from jax.sharding import PartitionSpec as P

damping_factor = 0.1
object_step = 0.5
probe_step = 0.05


def padded(block, sides, width):
    for axis, dim in sides:
        count = lax.axis_size(axis)
        forward = [(i, i + 1) for i in range(count - 1)]
        backward = [(target, source) for source, target in forward]
        low = lax.ppermute(
            lax.slice_in_dim(block, block.shape[dim] - width, None, axis=dim), axis, forward
        )
        high = lax.ppermute(lax.slice_in_dim(block, 0, width, axis=dim), axis, backward)
        block = jnp.concatenate([low, block, high], axis=dim)
    return block


def dft_tables(size, sign):
    counter = jnp.arange(size, dtype=jnp.int32)
    products = counter[:, None] * counter[None, :] % size
    angles = 2.0 * math.pi / size * products.astype(jnp.float32)
    scaling = 1.0 / math.sqrt(size)
    cosine = jnp.cos(angles) * scaling
    sine_part = sign * jnp.sin(angles) * scaling
    return (cosine, -sine_part - cosine, cosine - sine_part)


def right_apply(real_part, imag_part, tables):
    cosine, second, third_table = tables
    highest = lax.Precision.HIGHEST
    summed = jnp.einsum("...k,kj->...j", real_part + imag_part, cosine, precision=highest)
    part_two = jnp.einsum("...k,kj->...j", real_part, second, precision=highest)
    part_three = jnp.einsum("...k,kj->...j", imag_part, third_table, precision=highest)
    return (summed - part_three, summed + part_two)


def left_apply(real_part, imag_part, tables):
    cosine, second, third_table = tables
    highest = lax.Precision.HIGHEST
    summed = jnp.einsum("kj,...kl->...jl", cosine, real_part + imag_part, precision=highest)
    part_two = jnp.einsum("kj,...kl->...jl", second, real_part, precision=highest)
    part_three = jnp.einsum("kj,...kl->...jl", third_table, imag_part, precision=highest)
    return (summed - part_three, summed + part_two)


def transform(real_part, imag_part, tables):
    real_part, imag_part = right_apply(real_part, imag_part, tables)
    return left_apply(real_part, imag_part, tables)


def on_device(object_field, probe, measured, offsets, counts):
    strip_rows = object_field.shape[1]
    patch_size = measured.shape[1]
    slot_count = measured.shape[0]
    local_modes = probe.shape[1]
    position_index = lax.axis_index("pos")
    extended = padded(object_field, (("pos", 1),), strip_rows)
    row_starts = offsets[:, 0] - (position_index * strip_rows - strip_rows)
    col_starts = offsets[:, 1]

    def extract(row_begin, column_begin):
        return lax.dynamic_slice(
            extended, (jnp.int32(0), row_begin, column_begin), (2, patch_size, patch_size)
        )

    patches = jax.vmap(extract)(row_starts, col_starts)
    active = (jnp.arange(slot_count, dtype=jnp.int32) < counts[0]).astype(jnp.float32)
    probe_grid = probe.reshape(2, local_modes, patch_size, patch_size)
    probe_real = probe_grid[0][None]
    probe_imag = probe_grid[1][None]
    patch_real = patches[:, 0][:, None]
    patch_imag = patches[:, 1][:, None]
    wave_real = probe_real * patch_real - probe_imag * patch_imag
    wave_imag = probe_real * patch_imag + probe_imag * patch_real
    forward_tables = dft_tables(patch_size, 1.0)
    inverse_tables = dft_tables(patch_size, -1.0)
    far_real, far_imag = transform(wave_real, wave_imag, forward_tables)
    partial_power = jnp.sum(far_real * far_real + far_imag * far_imag, axis=1)
    model_intensity = lax.psum(partial_power, "tile")
    amplitude_ratio = (
        jnp.sqrt(measured + damping_factor) / jnp.sqrt(model_intensity + damping_factor) - 1.0
    ) * active[:, None, None]
    amplitude_ratio = amplitude_ratio[:, None]
    chi_real, chi_imag = transform(
        far_real * amplitude_ratio, far_imag * amplitude_ratio, inverse_tables
    )
    grad_real = jnp.sum(probe_real * chi_real + probe_imag * chi_imag, axis=1)
    grad_imag = jnp.sum(probe_real * chi_imag - probe_imag * chi_real, axis=1)
    term_real = jnp.sum(patch_real * chi_real + patch_imag * chi_imag, axis=0)
    term_imag = jnp.sum(patch_real * chi_imag - patch_imag * chi_real, axis=0)
    gradient = jnp.zeros_like(extended)
    for slot_index in range(slot_count):
        update = jnp.stack([grad_real[slot_index], grad_imag[slot_index]])
        corner = (jnp.int32(0), row_starts[slot_index], col_starts[slot_index])
        current = lax.dynamic_slice(gradient, corner, (2, patch_size, patch_size))
        gradient = lax.dynamic_update_slice(gradient, current + update, corner)
    rim_sums = jnp.concatenate(
        [gradient[:, :strip_rows], gradient[:, strip_rows + strip_rows :]], axis=1
    )
    neighbours = padded(rim_sums, (("pos", 1),), strip_rows)
    incoming = neighbours[:, :strip_rows] + neighbours[:, 3 * strip_rows :]
    strip_grad = gradient[:, strip_rows : strip_rows + strip_rows] + incoming
    half_grad = lax.psum_scatter(strip_grad, "tile", scatter_dimension=1, tiled=True)
    half_rows = strip_rows // lax.axis_size("tile")
    own_rows = lax.dynamic_slice_in_dim(
        object_field, lax.axis_index("tile") * half_rows, half_rows, 1
    )
    object_out = own_rows + object_step * half_grad
    probe_terms = jnp.stack([term_real, term_imag]).reshape(2, local_modes, patch_size * patch_size)
    pixel_share = patch_size * patch_size // lax.axis_size("pos")
    probe_total = lax.psum(probe_terms, "pos")
    probe_mine = lax.dynamic_slice_in_dim(probe_total, position_index * pixel_share, pixel_share, 2)
    probe_own = lax.dynamic_slice_in_dim(probe, position_index * pixel_share, pixel_share, 2)
    return (object_out, probe_own + probe_step * probe_mine)


def solution(mesh):
    in_specs = (
        P(None, ("group", "pos"), None),
        P(None, "tile", None),
        P(("group", "pos"), None, None),
        P(("group", "pos"), None),
        P(("group", "pos")),
    )
    out_specs = (P(None, ("group", "pos", "tile"), None), P(None, ("group", "tile"), "pos"))
    return jax.shard_map(
        on_device, mesh=mesh, in_specs=in_specs, out_specs=out_specs, check_vma=False
    )
```

profile of v0, /device:TPU:0, one launch (start us, length us, event | category | flops | bytes accessed | tf_op | source)
XLA Modules:
  0.0 284.0 jit_solution(8788779700641577605)
XLA Ops:
  8.4 5.6 %collective-permute-start = (f32[2,128,256]{2,0,1:T(2,128)S(1)}, f32[2,128,256]{2,0,1:T(2,128)}, u32[]{:S(2)}, u32[]{:S(2)}) collective-permute-start(f32[2,128,256]{2,0,1:T(2,128)S(1)} %copy.73), channel_id=1, source_target_pairs={{0,2},{2,4},{4,6},{6,8},{8,10},{10,12},{12,14},{1,3},{3,5},{5,7},{... | collective-permute-start | bytes 786440 | tf_op jit(solution)/shard_map/ppermute | solution.py:18
  15.2 2.7 fusion.131
  18.4 1.4 copy.121
  20.4 4.0 %collective-permute-done = f32[2,128,256]{2,0,1:T(2,128)} collective-permute-done((f32[2,128,256]{2,0,1:T(2,128)S(1)}, f32[2,128,256]{2,0,1:T(2,128)}, u32[]{:S(2)}, u32[]{:S(2)}) %collective-permute-start) | collective-permute-done | bytes 262176 | tf_op jit(solution)/shard_map/ppermute | solution.py:18
  25.8 2.6 gather_fusion
  28.3 3.3 %fusion.132 = (f32[2,1,256,256]{3,1,2,0:T(1,128)S(1)}, f32[2,1,256,256]{3,1,2,0:T(1,128)}) fusion(f32[2,2,256,256]{3,1,2,0:T(2,128)} %gather_fusion), kind=kLoop, calls=%fused_computation.173 | loop fusion | bytes 2097152 | tf_op jit(solution)/shard_map/slice | solution.py:79
  32.0 1.6 copy.116
  33.6 4.7 %fusion.16 = f32[2,4,256,256]{3,2,1,0:T(8,128)S(1)} fusion(f32[2,256,256]{1,2,0:T(8,128)S(1)} %bitcast.126, f32[4,256,256]{1,2,0:T(8,128)S(1)} %copy.79, f32[2,256,256]{1,2,0:T(8,128)S(1)} %bitcast.122, f32[4,256,256]{1,2,0:T(8,128)S(1)} %copy.74), kind=kOutput, calls=%fused_computation.30 | convolution fusion | flops 1615265792 | bytes 5242880 | tf_op jit(solution)/shard_map/...k,kj->...j/dot_general | solution.py:39
  38.3 4.7 %fusion.24 = f32[2,4,256,256]{3,2,1,0:T(8,128)S(1)} fusion(f32[2,4,256,256]{3,2,1,0:T(8,128)S(1)} %fusion.16, f32[2,256,256]{1,2,0:T(8,128)S(1)} %bitcast.127, f32[4,256,256]{1,2,0:T(8,128)S(1)} %copy.79, f32[2,256,256]{1,2,0:T(8,128)S(1)} %bitcast.123, f32[4,256,256]{1,2,0:T(8,128)S(1)} %copy.74), kind=kOutput, calls=%fused_computation.44 | convolution fusion | flops 1613889536 | bytes 7340032 | tf_op jit(solution)/shard_map/...k,kj->...j/dot_general | solution.py:40
  43.0 5.0 %fusion.25 = f32[2,4,256,256]{3,2,1,0:T(8,128)S(1)} fusion(f32[2,4,256,256]{3,2,1,0:T(8,128)S(1)} %fusion.16, f32[2,256,256]{1,2,0:T(8,128)S(1)} %bitcast.128, f32[4,256,256]{1,2,0:T(8,128)S(1)} %copy.79, f32[2,256,256]{1,2,0:T(8,128)S(1)} %bitcast.124, f32[4,256,256]{1,2,0:T(8,128)S(1)} %copy.74), kind=kOutput, calls=%fused_computation.45 | convolution fusion | flops 1613824000 | bytes 7340032 | tf_op jit(solution)/shard_map/...k,kj->...j/dot_general | solution.py:41
  48.0 4.5 %fusion.14 = f32[2,4,256,256]{3,2,1,0:T(8,128)S(1)} fusion(f32[2,4,256,256]{3,2,1,0:T(8,128)S(1)} %fusion.25, f32[2,4,256,256]{3,2,1,0:T(8,128)S(1)} %fusion.24), kind=kOutput, calls=%fused_computation.28 | convolution fusion | flops 1612120064 | bytes 6291456 | tf_op jit(solution)/shard_map/kj,...kl->...jl/dot_general | solution.py:48
  52.6 4.6 %convolution_subtract_fusion.1 = f32[2,4,256,256]{3,2,1,0:T(8,128)S(1)} fusion(f32[2,4,256,256]{3,2,1,0:T(8,128)S(1)} %fusion.14, f32[2,4,256,256]{3,2,1,0:T(8,128)S(1)} %fusion.24), kind=kOutput, calls=%fused_computation.43 | convolution fusion | flops 1612251136 | bytes 6291456 | tf_op jit(solution)/shard_map/kj,...kl->...jl/dot_general | solution.py:50
  57.2 7.2 %fusion.9 = (f32[2,256,256]{1,2,0:T(8,128)}, f32[2,4,256,256]{3,2,1,0:T(8,128)}) fusion(f32[2,4,256,256]{3,2,1,0:T(8,128)S(1)} %convolution_subtract_fusion.1, f32[2,4,256,256]{3,2,1,0:T(8,128)S(1)} %fusion.14, f32[2,4,256,256]{3,2,1,0:T(8,128)S(1)} %fusion.25), kind=kOutput, calls=%fused_computation.21 | convolution fusion | flops 1614282752 | bytes 8912896 | tf_op jit(solution)/shard_map/kj,...kl->...jl/dot_general | solution.py:49
  67.7 2.1 copy.86
  71.7 13.8 %all-reduce.5.cloned.1.call-done = f32[2,256,256]{1,2,0:T(8,128)} async-done(((f32[2,256,256]{1,2,0:T(8,128)}), f32[2,256,256]{1,2,0:T(8,128)}) %all-reduce.5.cloned.1.call-update) | async-done | bytes 524304 | tf_op jit(solution)/shard_map/psum | solution.py:87
  87.0 6.1 %fusion.12 = f32[2,4,256,256]{3,2,1,0:T(8,128)S(1)} fusion(f32[2,4,256,256]{3,2,1,0:T(8,128)S(1)} %convolution_subtract_fusion.1, f32[2,4,256,256]{3,2,1,0:T(8,128)} %get-tuple-element.29, f32[2,256,256]{1,2,0:T(8,128)S(1)} %add_multiply_fusion), kind=kOutput, calls=%fused_computation.26 | convolution fusion | flops 1613168640 | bytes 6815744 | tf_op jit(solution)/shard_map/...k,kj->...j/dot_general | solution.py:39
  93.1 4.6 %fusion.23 = f32[2,4,256,256]{3,2,1,0:T(8,128)S(1)} fusion(f32[2,4,256,256]{3,2,1,0:T(8,128)S(1)} %fusion.12, f32[2,4,256,256]{3,2,1,0:T(8,128)S(1)} %convolution_subtract_fusion.1, f32[2,256,256]{1,2,0:T(8,128)S(1)} %add_multiply_fusion), kind=kOutput, calls=%fused_computation.39 | convolution fusion | flops 1612840960 | bytes 6815744 | tf_op jit(solution)/shard_map/...k,kj->...j/dot_general | solution.py:40
  97.8 4.9 %fusion.22 = f32[2,4,256,256]{3,2,1,0:T(8,128)S(1)} fusion(f32[2,4,256,256]{3,2,1,0:T(8,128)S(1)} %fusion.12, f32[2,4,256,256]{3,2,1,0:T(8,128)S(1)} %copy-done.2, f32[2,256,256]{1,2,0:T(8,128)S(1)} %add_multiply_fusion), kind=kOutput, calls=%fused_computation.38 | convolution fusion | flops 1612775424 | bytes 6815744 | tf_op jit(solution)/shard_map/...k,kj->...j/dot_general | solution.py:41
  102.7 4.4 %fusion.10 = f32[2,4,256,256]{3,2,1,0:T(8,128)S(1)} fusion(f32[2,4,256,256]{3,2,1,0:T(8,128)S(1)} %fusion.22, f32[2,4,256,256]{3,2,1,0:T(8,128)S(1)} %fusion.23), kind=kOutput, calls=%fused_computation.24 | convolution fusion | flops 1612120064 | bytes 6291456 | tf_op jit(solution)/shard_map/kj,...kl->...jl/dot_general | solution.py:48
  107.1 4.6 %convolution_subtract_fusion = f32[2,4,256,256]{3,2,1,0:T(8,128)S(1)} fusion(f32[2,4,256,256]{3,2,1,0:T(8,128)S(1)} %fusion.10, f32[2,4,256,256]{3,2,1,0:T(8,128)S(1)} %fusion.23), kind=kOutput, calls=%fused_computation.41 | convolution fusion | flops 1612251136 | bytes 6291456 | tf_op jit(solution)/shard_map/kj,...kl->...jl/dot_general | solution.py:50
  111.8 5.6 %fusion.5 = (f32[4,256,256]{1,2,0:T(8,128)S(1)}, f32[4,256,256]{1,2,0:T(8,128)S(1)}, f32[2,256,256]{1,2,0:T(8,128)S(1)}, f32[2,256,256]{1,2,0:T(8,128)S(1)}) fusion(f32[2,4,256,256]{3,2,1,0:T(8,128)S(1)} %convolution_subtract_fusion, f32[2,256,256]{1,2,0:T(8,128)S(1)} %bitcast.129, f32[2,256,256]{1,2,0:T(8,128)S(1)} %bitcast.125, ...), kind=kOutput, calls=%fused_computation.11 | convolution fusion | flops 1619918848 | bytes 12582912 | tf_op jit(solution)/shard_map/kj,...kl->...jl/dot_general | solution.py:49
  119.0 3.9 %dynamic_update_slice.8 = f32[2,384,256]{1,2,0:T(8,128)S(1)} dynamic-update-slice(f32[2,384,256]{1,2,0:T(8,128)S(1)} %broadcast_in_dim.2, f32[2,256,256]{1,2,0:T(8,128)} %pad_maximum_fusion.2, s32[]{:T(128)} %constant.20.clone.1, s32[]{:T(128)S(6)} %select_n.60, s32[]{:T(128)} %constant.20.clone.1) | dynamic-update-slice | bytes 1048580 | tf_op jit(solution)/shard_map/dynamic_update_slice | solution.py:104
  122.9 1.9 maximum_add_fusion
  124.8 3.8 %dynamic_update_slice.9 = f32[2,384,256]{1,2,0:T(8,128)S(1)} dynamic-update-slice(f32[2,384,256]{1,2,0:T(8,128)S(1)} %dynamic_update_slice.8, f32[2,256,256]{1,2,0:T(8,128)} %maximum_add_fusion, s32[]{:T(128)} %constant.20.clone.1, s32[]{:T(128)S(6)} %select_n.61, s32[]{:T(128)} %constant.20.clone.1) | dynamic-update-slice | bytes 1048580 | tf_op jit(solution)/shard_map/dynamic_update_slice | solution.py:104
  129.5 5.8 %collective-permute-start.2 = (f32[2,128,256]{1,2,0:T(8,128)}, f32[2,128,256]{1,2,0:T(8,128)}, u32[]{:S(2)}, u32[]{:S(2)}) collective-permute-start(f32[2,128,256]{1,2,0:T(8,128)} %get-tuple-element.21), channel_id=1, source_target_pairs={{0,2},{2,4},{4,6},{6,8},{8,10},{10,12},{12,14},{1,3},{3,5},{5,7},{... | collective-permute-start | bytes 786440 | tf_op jit(solution)/shard_map/ppermute | solution.py:18
  137.9 2.7 stack.17
  141.0 1.5 stack.18
  142.6 4.0 %collective-permute-done.2 = f32[2,128,256]{1,2,0:T(8,128)} collective-permute-done((f32[2,128,256]{1,2,0:T(8,128)}, f32[2,128,256]{1,2,0:T(8,128)}, u32[]{:S(2)}, u32[]{:S(2)}) %collective-permute-start.2) | collective-permute-done | bytes 262176 | tf_op jit(solution)/shard_map/ppermute | solution.py:18
  148.5 1.8 pad_maximum_fusion
  152.2 16.6 %all-reduce.9.cloned.1.call-done = f32[2,128,256]{2,0,1:T(2,128)} async-done(((f32[2,128,256]{2,0,1:T(2,128)}), f32[2,128,256]{2,0,1:T(2,128)}) %all-reduce.9.cloned.1.call-update) | async-done | bytes 262160
  170.5 105.0 %all-reduce.7.cloned.1.call-done = f32[2,4,65536]{2,1,0:T(4,128)} async-done(((f32[2,4,65536]{2,1,0:T(4,128)}), f32[2,4,65536]{2,1,0:T(4,128)}) %all-reduce.7.cloned.1.call-update) | async-done | bytes 2097168 | tf_op jit(solution)/shard_map/psum | solution.py:119
  275.5 1.8 multiply_add_fusion.5
  (53 shorter events, 17.7 us)
Async XLA Ops:
  7.2 78.4 %all-reduce.5.cloned.1.call-start = ((), (), s32[]{:S(2)}) async-start(), calls=%async_computation | async-start | bytes 1048576 | tf_op jit(solution)/shard_map/psum | solution.py:87
  8.4 16.0 %collective-permute-start = (f32[2,128,256]{2,0,1:T(2,128)S(1)}, f32[2,128,256]{2,0,1:T(2,128)}, u32[]{:S(2)}, u32[]{:S(2)}) collective-permute-start(f32[2,128,256]{2,0,1:T(2,128)S(1)} %copy.73), channel_id=1, source_target_pairs={{0,2},{2,4},{4,6},{6,8},{8,10},{10,12},{12,14},{1,3},{3,5},{5,7},{... | collective-permute-start | bytes 786440 | tf_op jit(solution)/shard_map/ppermute | solution.py:18
  13.9 10.5 %collective-permute-start.1 = (f32[2,128,256]{2,0,1:T(2,128)S(1)}, f32[2,128,256]{2,0,1:T(2,128)}, u32[]{:S(2)}, u32[]{:S(2)}) collective-permute-start(f32[2,128,256]{2,0,1:T(2,128)S(1)} %copy.73), channel_id=1, source_target_pairs={{2,0},{4,2},{6,4},{8,6},{10,8},{12,10},{14,12},{3,1},{5,3},{7,5},{... | collective-permute-start | bytes 786440 | tf_op jit(solution)/shard_map/ppermute | solution.py:21
  18.4 1.8 copy-start.9
  20.2 22.7 %copy-start = (f32[4,256,256]{1,2,0:T(8,128)}, f32[4,256,256]{1,2,0:T(8,128)S(1)}, u32[]{:S(2)}) copy-start(f32[4,256,256]{1,2,0:T(8,128)S(1)} %copy.79) | copy-start | bytes 3145732
  31.9 11.0 %copy-start.3 = (f32[2,1,256,256]{2,3,0,1:T(8,128)}, f32[2,1,256,256]{2,3,0,1:T(8,128)S(1)}, u32[]{:S(2)}) copy-start(f32[2,1,256,256]{2,3,0,1:T(8,128)S(1)} %copy.115) | copy-start | bytes 1572868
  33.6 9.4 %copy-start.5 = (f32[2,1,256,256]{2,3,0,1:T(8,128)}, f32[2,1,256,256]{2,3,0,1:T(8,128)S(1)}, u32[]{:S(2)}) copy-start(f32[2,1,256,256]{2,3,0,1:T(8,128)S(1)} %copy.116) | copy-start | bytes 1572868
  64.3 104.5 %all-reduce.9.cloned.1.call-start = ((), (), s32[]{:S(2)}) async-start(), calls=%async_computation.2 | async-start | bytes 524288
  93.1 4.6 %copy-start.2 = (f32[2,4,256,256]{3,2,1,0:T(8,128)S(1)}, f32[2,4,256,256]{3,2,1,0:T(8,128)}, u32[]{:S(2)}) copy-start(f32[2,4,256,256]{3,2,1,0:T(8,128)} %get-tuple-element.29) | copy-start | bytes 6291460
  107.1 4.6 %copy-start.1 = (f32[4,256,256]{1,2,0:T(8,128)S(1)}, f32[4,256,256]{1,2,0:T(8,128)}, u32[]{:S(2)}) copy-start(f32[4,256,256]{1,2,0:T(8,128)} %copy-done) | copy-start | bytes 3145732
  107.1 4.6 %copy-start.4 = (f32[2,1,256,256]{2,3,0,1:T(8,128)S(1)}, f32[2,1,256,256]{2,3,0,1:T(8,128)}, u32[]{:S(2)}) copy-start(f32[2,1,256,256]{2,3,0,1:T(8,128)} %copy-done.3) | copy-start | bytes 1572868
  107.1 4.6 %copy-start.6 = (f32[2,1,256,256]{2,3,0,1:T(8,128)S(1)}, f32[2,1,256,256]{2,3,0,1:T(8,128)}, u32[]{:S(2)}) copy-start(f32[2,1,256,256]{2,3,0,1:T(8,128)} %copy-done.5) | copy-start | bytes 1572868
  129.5 17.1 %collective-permute-start.2 = (f32[2,128,256]{1,2,0:T(8,128)}, f32[2,128,256]{1,2,0:T(8,128)}, u32[]{:S(2)}, u32[]{:S(2)}) collective-permute-start(f32[2,128,256]{1,2,0:T(8,128)} %get-tuple-element.21), channel_id=1, source_target_pairs={{0,2},{2,4},{4,6},{6,8},{8,10},{10,12},{12,14},{1,3},{3,5},{5,7},{... | collective-permute-start | bytes 786440 | tf_op jit(solution)/shard_map/ppermute | solution.py:18
  135.3 11.2 %collective-permute-start.3 = (f32[2,128,256]{1,2,0:T(8,128)}, f32[2,128,256]{1,2,0:T(8,128)}, u32[]{:S(2)}, u32[]{:S(2)}) collective-permute-start(f32[2,128,256]{1,2,0:T(8,128)} %get-tuple-element.20), channel_id=1, source_target_pairs={{2,0},{4,2},{6,4},{8,6},{10,8},{12,10},{14,12},{3,1},{5,3},{7,5},{... | collective-permute-start | bytes 786440 | tf_op jit(solution)/shard_map/ppermute | solution.py:21
  141.0 7.5 %copy-start.7 = (f32[1,4,65536]{2,1,0:T(4,128)S(1)}, f32[1,4,65536]{2,1,0:T(4,128)}, u32[]{:S(2)}) copy-start(f32[1,4,65536]{2,1,0:T(4,128)} %stack.17) | copy-start | bytes 3145732
  142.6 6.0 %copy-start.8 = (f32[1,4,65536]{2,1,0:T(4,128)S(1)}, f32[1,4,65536]{2,1,0:T(4,128)}, u32[]{:S(2)}) copy-start(f32[1,4,65536]{2,1,0:T(4,128)} %stack.18) | copy-start | bytes 3145732
  148.5 127.0 %all-reduce.7.cloned.1.call-start = ((), (), s32[]{:S(2)}) async-start(), calls=%async_computation.1 | async-start | bytes 4194304 | tf_op jit(solution)/shard_map/psum | solution.py:119
  150.3 0.7 copy-start.10
Sparse Core Ops, SparseCore 0:
  64.5 21.0 all-reduce.4
  148.6 20.1 all-reduce.8
  172.4 103.0 all-reduce.6
where the time goes:
time: 288 us; the launch traced here: 284 us
  waiting for transfers between devices  143 us (50%)
  matrix products  60.9 us (21%)
  local copies, waits for them, and re-layouts  34.6 us (12%)
  between operations  19.6 us (7%)
  starting transfers between devices  14.1 us (5%)
  other arithmetic  11.4 us (4%)
    psum x1, waiting for transfers between devices, on_device(): probe_total = lax.psum(probe_terms, 'pos')  105 us
    unnamed x4, waiting for transfers between devices  16.6 us
    psum x1, waiting for transfers between devices, on_device(): model_intensity = lax.psum(partial_power, 'tile')  13.8 us
    dot_general x2, matrix products, left_apply(): jnp.einsum('kj,...kl->...jl', second, real_part, precision=highest)  12.7 us
    ppermute x2, starting transfers between devices, padded(): lax.ppermute(lax.slice_in_dim(block, block.shape[dim] - width, None, axis...  11.4 us
    dot_general x2, matrix products, right_apply(): jnp.einsum('...k,kj->...j', real_part + imag_part, cosine, precision=high...  10.8 us
    dot_general x2, matrix products, right_apply(): jnp.einsum('...k,kj->...j', imag_part, third_table, precision=highest)  9.97 us
    dot_general x2, matrix products, right_apply(): part_two = jnp.einsum('...k,kj->...j', real_part, second, precision=highest)  9.28 us
  transfers between devices with their start and end apart: 7, of which 5 were waited for; matrix products, arithmetic and copies ran while one was open for 6% of the time, Pallas kernels for 0%

commit v1 on v0

v1 whole, which is shorter than its diff:
```python
import functools
import math

import jax
import jax.numpy as jnp
import ml_dtypes
import numpy as np
from jax import lax
from jax.experimental import pallas as pl
from jax.experimental.pallas import tpu as pltpu
from jax.sharding import PartitionSpec as P

damping_factor = 0.1
object_step = 0.5
probe_step = 0.05

F32 = jnp.float32
BF16 = jnp.bfloat16
VMEM_LIMIT = 48 * 1024 * 1024


def real_tables(size):
    half = size // 2
    counter = np.arange(half)
    phase = np.outer(counter, counter) % half
    even = np.exp(-2j * np.pi * phase / half) / math.sqrt(size)
    odd = even * np.exp(-2j * np.pi * counter / size)[:, None]
    tables = []
    for matrix in (even, odd):
        real = np.block([[matrix.real, matrix.imag], [-matrix.imag, matrix.real]])
        for form in (real, real.T):
            high = form.astype(ml_dtypes.bfloat16)
            low = (form - high.astype(np.float64)).astype(ml_dtypes.bfloat16)
            tables += [high, low]
    return np.stack(tables).reshape(2, 2, 2, size, size)


def split(value):
    high = value.astype(BF16)
    return high, (value - high.astype(F32)).astype(BF16)


def product(left, right):
    return jnp.dot(left, right, preferred_element_type=F32)


def times_table(value, table):
    high, low = split(value)
    return product(high, table[0]) + product(high, table[1]) + product(low, table[0])


def table_times(table, value):
    high, low = split(value)
    return product(table[0], high) + product(table[1], high) + product(table[0], low)


def forward_wave(real, imag, tables):
    half = real.shape[1] // 2
    row_even, row_odd, col_even, col_odd = tables
    evens = times_table(
        jnp.concatenate([real[:, :half] + real[:, half:], imag[:, :half] + imag[:, half:]], 1),
        row_even,
    )
    odds = times_table(
        jnp.concatenate([real[:, :half] - real[:, half:], imag[:, :half] - imag[:, half:]], 1),
        row_odd,
    )
    real = jnp.concatenate([evens[:, :half], odds[:, :half]], 1)
    imag = jnp.concatenate([evens[:, half:], odds[:, half:]], 1)
    far_even = table_times(
        col_even,
        jnp.concatenate([real[:half] + real[half:], imag[:half] + imag[half:]], 0),
    )
    far_odd = table_times(
        col_odd,
        jnp.concatenate([real[:half] - real[half:], imag[:half] - imag[half:]], 0),
    )
    return far_even, far_odd


def inverse_wave(far_even, far_odd, tables):
    half = far_even.shape[0] // 2
    row_even, row_odd, col_even, col_odd = tables
    evens = table_times(row_even, far_even)
    odds = table_times(row_odd, far_odd)
    real = jnp.concatenate([evens[:half] + odds[:half], evens[:half] - odds[:half]], 0)
    imag = jnp.concatenate([evens[half:] + odds[half:], evens[half:] - odds[half:]], 0)
    evens = times_table(jnp.concatenate([real[:, :half], imag[:, :half]], 1), col_even)
    odds = times_table(jnp.concatenate([real[:, half:], imag[:, half:]], 1), col_odd)
    real = jnp.concatenate(
        [evens[:, :half] + odds[:, :half], evens[:, :half] - odds[:, :half]], 1
    )
    imag = jnp.concatenate(
        [evens[:, half:] + odds[:, half:], evens[:, half:] - odds[:, half:]], 1
    )
    return real, imag


def load_tables(table_ref):
    return tuple(
        (table_ref[parity, form, 0], table_ref[parity, form, 1])
        for form in (0, 1)
        for parity in (0, 1)
    )


def pieces_of(value):
    high, middle = split(value)
    low = (value - high.astype(F32) - middle.astype(F32)).astype(BF16)
    return high, middle, low


def order_kernel(measured_ref, order_ref, out_ref):
    half = order_ref.shape[1] // 2
    columns, rows = order_ref[0], order_ref[1]
    for slot in range(measured_ref.shape[0]):
        value = jnp.sqrt(measured_ref[slot] + damping_factor)
        value = sum(product(piece, columns) for piece in pieces_of(value))
        value = sum(product(rows, piece) for piece in pieces_of(value))
        out_ref[slot, 0] = value[:half]
        out_ref[slot, 1] = value[half:]


def load_rows(ref, index, begin, count):
    offset = lax.rem(begin, 8)
    span = count + 8
    value = ref[(*index, pl.ds(pl.multiple_of(begin - offset, 8), span))]
    return pltpu.roll(value, lax.rem(span - offset, span), 0)[:count]


def forward_kernel(
    place_ref, own_ref, near_ref, other_ref, probe_ref, table_ref,
    far_ref, power_ref, patch_ref, extended,
):
    rows = own_ref.shape[1]
    size = patch_ref.shape[1]
    start = place_ref[0]
    tile = place_ref[1]
    extended[:, rows : 2 * rows] = own_ref[...]
    extended[tile, :rows] = near_ref[0]
    extended[tile, 2 * rows : 3 * rows] = near_ref[1]
    extended[1 - tile, :rows] = other_ref[0]
    extended[1 - tile, 2 * rows : 3 * rows] = other_ref[1]
    patch_real = load_rows(extended, (0,), start, size)
    patch_imag = load_rows(extended, (1,), start, size)
    patch_ref[0] = patch_real
    patch_ref[1] = patch_imag
    tables = load_tables(table_ref)
    half = size // 2
    for mode in range(probe_ref.shape[1]):
        probe_real = probe_ref[0, mode]
        probe_imag = probe_ref[1, mode]
        pieces = forward_wave(
            probe_real * patch_real - probe_imag * patch_imag,
            probe_real * patch_imag + probe_imag * patch_real,
            tables,
        )
        for parity in (0, 1):
            far = pieces[parity]
            far_ref[mode, parity] = far
            power = far[:half] * far[:half] + far[half:] * far[half:]
            if mode == 0:
                power_ref[parity] = power
            else:
                power_ref[parity] += power


def ratio_kernel(active_ref, amplitude_ref, *refs):
    ratio_ref = refs[-1]
    slots = ratio_ref.shape[0]
    for slot in range(slots):
        model = jnp.sqrt(refs[slot][...] + refs[slots + slot][...] + damping_factor)
        ratio_ref[slot] = (amplitude_ref[slot] / model - 1.0) * active_ref[slot].astype(F32)


def inverse_kernel(modes, first, slots, place_ref, table_ref, ratio_ref, probe_ref, *refs):
    far_refs, patch_refs = refs[:slots], refs[slots : 2 * slots]
    refs = refs[2 * slots :]
    if not first:
        refs = refs[1:]
    grad_ref, keep_ref, send_ref = refs
    inner, outer = place_ref[0], place_ref[1]
    size = probe_ref.shape[2]
    outers, rows = keep_ref.shape[1], keep_ref.shape[3]
    half = size // 2
    tables = load_tables(table_ref)
    for index, mode in enumerate(modes):
        probe_real = probe_ref[0, mode]
        probe_imag = probe_ref[1, mode]
        term_real = term_imag = None
        for slot in range(slots):
            pieces = []
            for parity in (0, 1):
                ratio = ratio_ref[slot, parity]
                far = far_refs[slot][mode, parity]
                pieces.append(jnp.concatenate([far[:half] * ratio, far[half:] * ratio], 0))
            real, imag = inverse_wave(*pieces, tables)
            patch_real = patch_refs[slot][0]
            patch_imag = patch_refs[slot][1]
            grad_real = probe_real * real + probe_imag * imag
            grad_imag = probe_real * imag - probe_imag * real
            if first and index == 0:
                grad_ref[slot, 0] = grad_real
                grad_ref[slot, 1] = grad_imag
            else:
                grad_ref[slot, 0] += grad_real
                grad_ref[slot, 1] += grad_imag
            now_real = patch_real * real + patch_imag * imag
            now_imag = patch_real * imag - patch_imag * real
            if slot == 0:
                term_real, term_imag = now_real, now_imag
            else:
                term_real, term_imag = term_real + now_real, term_imag + now_imag
        for block in range(2 * outers):
            target = lax.rem(block // 2 - outer + outers, outers)
            lines = slice(block * rows, (block + 1) * rows)
            mine = inner == block % 2

            @pl.when(mine)
            def _():
                keep_ref[index, target, 0] = term_real[lines]
                keep_ref[index, target, 1] = term_imag[lines]

            @pl.when(jnp.logical_not(mine))
            def _():
                send_ref[index, target, 0] = term_real[lines]
                send_ref[index, target, 1] = term_imag[lines]


def strip_kernel(place_ref, grad_ref, keep_ref, send_ref, spread):
    slots, _, size, _ = grad_ref.shape
    rows = size // 2
    tile = place_ref[slots]
    half = rows // 2
    spread[:, :, :rows] = jnp.zeros(spread.shape[:2] + (rows, size), F32)
    spread[:, :, rows + size :] = jnp.zeros(spread.shape[:2] + (rows + 8, size), F32)
    spread[:, :, rows : rows + size] = grad_ref[...]
    for part in (0, 1):
        for strip in range(3):
            for ref, which in ((keep_ref, tile), (send_ref, 1 - tile)):
                total = None
                for slot in range(slots):
                    begin = rows - place_ref[slot] + strip * rows + which * half
                    value = load_rows(spread, (slot, part), begin, half)
                    total = value if total is None else total + value
                ref[strip, part] = total


def vmem():
    return pl.BlockSpec(memory_space=pltpu.VMEM)


def smem():
    return pl.BlockSpec(memory_space=pltpu.SMEM)


def params():
    return pltpu.CompilerParams(vmem_limit_bytes=VMEM_LIMIT)


def on_device(object_field, probe, measured, offsets, counts):
    _, strip_rows, columns = object_field.shape
    slots, size, _ = measured.shape
    modes = probe.shape[1]
    positions = lax.axis_size("pos")
    tiles = lax.axis_size("tile")
    position = lax.axis_index("pos")
    tile = lax.axis_index("tile")
    up = [(i, i + 1) for i in range(positions - 1)]
    down = [(i + 1, i) for i in range(positions - 1)]
    swap = [(0, 1), (1, 0)]
    tables = jnp.asarray(real_tables(size))

    component = lax.dynamic_index_in_dim(object_field, tile, 0, keepdims=False)
    low = lax.ppermute(component, "pos", up)
    high = lax.ppermute(component, "pos", down)
    near = jnp.stack([low, high])
    other = lax.ppermute(near, "tile", swap)

    probe_grid = probe.reshape(2, modes, size, size)
    order = np.zeros((size, size), ml_dtypes.bfloat16)
    for parity in (0, 1):
        for index in range(size // 2):
            order[2 * index + parity, parity * (size // 2) + index] = 1
    amplitude = pl.pallas_call(
        order_kernel,
        out_shape=jax.ShapeDtypeStruct((slots, 2, size // 2, size), F32),
        in_specs=[vmem(), vmem()],
        out_specs=vmem(),
        compiler_params=params(),
        name="order",
    )(measured, jnp.asarray(np.stack([order, order.T])))

    starts = offsets[:, 0] - (position * strip_rows - strip_rows)
    far, power, patch = [], [], []
    for slot in range(slots):
        place = jnp.stack([starts[slot], tile]).astype(jnp.int32)
        outs = pl.pallas_call(
            forward_kernel,
            out_shape=(
                jax.ShapeDtypeStruct((modes, 2, size, size), F32),
                jax.ShapeDtypeStruct((2, size // 2, size), F32),
                jax.ShapeDtypeStruct((2, size, size), F32),
            ),
            in_specs=[smem()] + [vmem()] * 5,
            out_specs=(vmem(), vmem(), vmem()),
            scratch_shapes=[pltpu.VMEM((2, 3 * strip_rows + 8, columns), F32)],
            compiler_params=params(),
            name="forward",
        )(place, object_field, near, other, probe_grid, tables)
        far.append(outs[0])
        power.append(outs[1])
        patch.append(outs[2])
    others = [lax.ppermute(value, "tile", swap) for value in power]
    active = (jnp.arange(slots, dtype=jnp.int32) < counts[0]).astype(jnp.int32)
    ratio = pl.pallas_call(
        ratio_kernel,
        out_shape=jax.ShapeDtypeStruct((slots, 2, size // 2, size), F32),
        in_specs=[smem()] + [vmem()] * (1 + 2 * slots),
        out_specs=vmem(),
        compiler_params=params(),
        name="ratio",
    )(active, amplitude, *power, *others)

    outers = positions // 2
    direct = outers <= 4
    block_rows = size // positions
    inner, outer = position % 2, position // 2
    where = jnp.stack([inner, outer]) if direct else jnp.zeros((2,), jnp.int32)
    group = 1
    grad = None
    sums = []
    for begin in range(0, modes, group):
        block_shape = jax.ShapeDtypeStruct((group, outers, 2, block_rows, size), F32)
        grad_shape = jax.ShapeDtypeStruct((slots, 2, size, size), F32)
        first = begin == 0
        arguments = [where.astype(jnp.int32), tables, ratio, probe_grid, *far, *patch]
        if not first:
            arguments.append(grad)
        grad, keep, send = pl.pallas_call(
            functools.partial(inverse_kernel, tuple(range(begin, begin + group)), first, slots),
            out_shape=(grad_shape, block_shape, block_shape),
            in_specs=[smem()] + [vmem()] * (len(arguments) - 1),
            out_specs=(vmem(), vmem(), vmem()),
            input_output_aliases={} if first else {len(arguments) - 1: 0},
            compiler_params=params(),
            name="inverse",
        )(*arguments)
        if direct:
            pair = [(i, i ^ 1) for i in range(positions)]
            got = lax.ppermute(send, "pos", pair)
            both = keep + got
            total = both[:, 0]
            for distance in range(1, outers):
                ring = [(i, (i + 2 * distance) % positions) for i in range(positions)]
                total = total + lax.ppermute(both[:, distance], "pos", ring)
        else:
            both = jnp.stack([keep, send], 2).reshape(group, positions, 2, block_rows, size)
            total = lax.psum_scatter(both, "pos", scatter_dimension=1, tiled=True)[:, 0]
        sums.append(total)

    strip_shape = jax.ShapeDtypeStruct((3, 2, strip_rows // tiles, columns), F32)
    kept, sent = pl.pallas_call(
        strip_kernel,
        out_shape=(strip_shape, strip_shape),
        in_specs=[smem(), vmem()],
        out_specs=(vmem(), vmem()),
        scratch_shapes=[pltpu.VMEM((slots, 2, 2 * strip_rows + size + 8, columns), F32)],
        compiler_params=params(),
        name="strips",
    )(jnp.concatenate([starts, tile[None]]).astype(jnp.int32), grad)
    strips = kept + lax.ppermute(sent, "tile", swap)
    from_above = lax.ppermute(strips[0], "pos", down)
    from_below = lax.ppermute(strips[2], "pos", up)
    half_rows = strip_rows // tiles
    own_rows = lax.dynamic_slice_in_dim(object_field, tile * half_rows, half_rows, 1)
    object_out = own_rows + object_step * (strips[1] + from_above + from_below)

    pixel_share = size * size // positions
    probe_own = lax.dynamic_slice_in_dim(probe, position * pixel_share, pixel_share, 2)
    probe_mine = jnp.concatenate(sums, 0).transpose(1, 0, 2, 3).reshape(2, modes, pixel_share)
    return (object_out, probe_own + probe_step * probe_mine)


def solution(mesh):
    in_specs = (
        P(None, ("group", "pos"), None),
        P(None, "tile", None),
        P(("group", "pos"), None, None),
        P(("group", "pos"), None),
        P(("group", "pos")),
    )
    out_specs = (P(None, ("group", "pos", "tile"), None), P(None, ("group", "tile"), "pos"))
    return jax.shard_map(
        on_device, mesh=mesh, in_specs=in_specs, out_specs=out_specs, check_vma=False
    )
```

time: 288 us -> 106 us (0.37); the launches traced: 284 us -> 105 us
  waiting for transfers between devices: 143 us -> 11.2 us
  matrix products: 60.9 us -> 0 us
  Pallas kernels: 0 us -> 32.3 us
  starting transfers between devices: 14.1 us -> 40.3 us
  local copies, waits for them, and re-layouts: 34.6 us -> 12.5 us
  between operations: 19.6 us -> 1.68 us
  other arithmetic: 11.4 us -> 7.01 us
    psum x2 -> x0, waiting for transfers between devices: 119 us -> none  [the longest x1 105 us: on_device(): probe_total = lax.psum(probe_terms, 'pos')]
    dot_general x12 -> x0, matrix products: 60.9 us -> none  [the longest x2 12.7 us: left_apply(): jnp.einsum('kj,...kl->...jl', second, real_part, precision=highest)]
    pallas_call x0 -> x9, Pallas kernels: none -> 32.3 us  [the longest x4 19.4 us: on_device(): pl.pallas_call(functools.partial(inverse_kernel, tuple(range(begin, begin...]
    ppermute x4 -> x24, starting transfers between devices: 13.9 us -> 40.3 us  [the longest x12 23 us: on_device(): total = total + lax.ppermute(both[:, distance], 'pos', ring)]
    unnamed x4 -> x0, waiting for transfers between devices: 16.6 us -> none
    dynamic_update_slice x2 -> x0, local copies, waits for them, and re-layouts: 7.66 us -> none  [on_device(): gradient = lax.dynamic_update_slice(gradient, current + update, corner)]
    slice x5 -> x1, local copies, waits for them, and re-layouts: 8.11 us -> 0.52 us  [on_device(): place = jnp.stack([starts[slot], tile]).astype(jnp.int32)]
    another operation x2 -> x0, local copies, waits for them, and re-layouts: 4.27 us -> none  [on_device(): jnp.stack([term_real, term_imag])]
  transfers between devices with their start and end apart: 7 -> 24, of which waited for: 5 -> 5; matrix products, arithmetic and copies ran while one was open for 6% -> 10% of each run, Pallas kernels for 0% -> 20%
where the time goes in v1:
time: 106 us; the launch traced here: 105 us
  starting transfers between devices  40.3 us (38%)
  Pallas kernels  32.3 us (30%)
  local copies, waits for them, and re-layouts  12.5 us (12%)
  waiting for transfers between devices  11.2 us (11%)
  other arithmetic  7.01 us (7%)
  between operations  1.68 us (2%)
    ppermute x12, starting transfers between devices, on_device(): total = total + lax.ppermute(both[:, distance], 'pos', ring)  23 us
    pallas_call x4, Pallas kernels, on_device(): pl.pallas_call(functools.partial(inverse_kernel, tuple(range(begin, begin...  19.4 us
    pallas_call x2, Pallas kernels, on_device(): pl.pallas_call(forward_kernel, out_shape=(jax.ShapeDtypeStruct((modes, 2,...  9.57 us
    unnamed x30, local copies, waits for them, and re-layouts  6.99 us
    ppermute x1, starting transfers between devices, on_device(): low = lax.ppermute(component, 'pos', up)  4.85 us
    ppermute x4, starting transfers between devices, on_device(): got = lax.ppermute(send, 'pos', pair)  4.62 us
    ppermute x1, starting transfers between devices, on_device(): from_below = lax.ppermute(strips[2], 'pos', up)  4.55 us
    ppermute x1, waiting for transfers between devices, on_device(): high = lax.ppermute(component, 'pos', down)  4.13 us
  transfers between devices with their start and end apart: 24, of which 5 were waited for; matrix products, arithmetic and copies ran while one was open for 10% of the time, Pallas kernels for 20%

profile of v1, /device:TPU:0, one launch (start us, length us, event | category | flops | bytes accessed | tf_op | source)
XLA Modules:
  0.0 105.0 jit_solution(5066630410681893641)
XLA Ops:
  1.6 4.8 %collective-permute-start = (f32[128,256]{1,0:T(8,128)S(1)}, f32[128,256]{1,0:T(8,128)S(1)}, u32[]{:S(2)}, u32[]{:S(2)}) collective-permute-start(f32[128,256]{1,0:T(8,128)S(1)} %dynamic-slice_bitcast_fusion), channel_id=1, source_target_pairs={{0,2},{2,4},{4,6},{6,8},{8,10},{10,12},{12,14},{1,3},{3,5},{5,7},{... | collective-permute-start | bytes 393224 | tf_op jit(solution)/shard_map/ppermute | solution.py:275
  6.4 1.3 %collective-permute-start.1 = (f32[128,256]{1,0:T(8,128)S(1)}, f32[128,256]{1,0:T(8,128)S(1)}, u32[]{:S(2)}, u32[]{:S(2)}) collective-permute-start(f32[128,256]{1,0:T(8,128)S(1)} %dynamic-slice_bitcast_fusion), channel_id=1, source_target_pairs={{2,0},{4,2},{6,4},{8,6},{10,8},{12,10},{14,12},{3,1},{5,3},{7,5},{... | collective-permute-start | bytes 393224 | tf_op jit(solution)/shard_map/ppermute | solution.py:276
  7.7 1.4 %collective-permute-done = f32[128,256]{1,0:T(8,128)S(1)} collective-permute-done((f32[128,256]{1,0:T(8,128)S(1)}, f32[128,256]{1,0:T(8,128)S(1)}, u32[]{:S(2)}, u32[]{:S(2)}) %collective-permute-start) | collective-permute-done | bytes 131104 | tf_op jit(solution)/shard_map/ppermute | solution.py:275
  9.1 4.1 %collective-permute-done.1 = f32[128,256]{1,0:T(8,128)S(1)} collective-permute-done((f32[128,256]{1,0:T(8,128)S(1)}, f32[128,256]{1,0:T(8,128)S(1)}, u32[]{:S(2)}, u32[]{:S(2)}) %collective-permute-start.1) | collective-permute-done | bytes 131104 | tf_op jit(solution)/shard_map/ppermute | solution.py:276
  14.2 3.8 %reshape.14.probe_ref = f32[2,4,256,256]{3,2,1,0:T(8,128)} reshape(f32[2,4,65536]{2,1,0:T(4,128)} %param.8) | data formatting | bytes 4194304 | tf_op jit(solution)/shard_map/reshape | solution.py:280
  18.5 1.3 %pad_add_fusion.2 = (s32[2]{0:T(128)S(1)}, s32[2]{0:T(128)S(1)}) fusion(s32[1]{0:T(128)} %bitcast.4, s32[1]{0:T(128)} %bitcast, s32[1]{0:T(128)} %bitcast.8), kind=kLoop, calls=%fused_computation.44 | loop fusion | flops 4 | bytes 28 | tf_op jit(solution)/shard_map/stack | solution.py:297
  19.8 4.4 %forward.3 = (f32[4,2,256,256]{3,2,1,0:T(8,128)S(1)}, f32[2,128,256]{2,1,0:T(8,128)S(1)}, f32[2,256,256]{2,1,0:T(8,128)S(1)}) custom-call(s32[2]{0:T(128)S(1)} %get-tuple-element.61.place_ref, f32[2,128,256]{2,1,0:T(8,128)S(1)} %copy-done.6, f32[2,128,256]{2,1,0:T(8,128)S(1)} %pad_maximum_fusion.near_ref, ...), custom_call_target="tpu_custom_call" | custom-call | tf_op jit(solution)/shard_map/forward/pallas_call | solution.py:298
  24.2 1.3 %copy-done.1 = f32[4,2,256,256]{3,2,1,0:T(8,128)} copy-done((f32[4,2,256,256]{3,2,1,0:T(8,128)}, f32[4,2,256,256]{3,2,1,0:T(8,128)S(1)}, u32[]{:S(2)}) %copy-start.1) | copy-done | bytes 2097176
  26.0 5.2 %forward.2 = (f32[4,2,256,256]{3,2,1,0:T(8,128)S(1)}, f32[2,128,256]{2,1,0:T(8,128)}, f32[2,256,256]{2,1,0:T(8,128)S(1)}) custom-call(s32[2]{0:T(128)S(1)} %get-tuple-element.60.place_ref, f32[2,128,256]{2,1,0:T(8,128)S(1)} %copy-done.6, f32[2,128,256]{2,1,0:T(8,128)S(1)} %pad_maximum_fusion.near_ref, f32[2,128,256]{2,1,0:T(8,128)S(1)} %collective-permute-done.2.other_ref, ...), custom_call_target="tpu_custom_call" | custom-call | tf_op jit(solution)/shard_map/forward/pallas_call | solution.py:298
  31.2 1.4 %copy-done.2 = f32[4,2,256,256]{3,2,1,0:T(8,128)} copy-done((f32[4,2,256,256]{3,2,1,0:T(8,128)}, f32[4,2,256,256]{3,2,1,0:T(8,128)S(1)}, u32[]{:S(2)}) %copy-start.2) | copy-done | bytes 2097176
  36.2 1.3 %ratio.1.ratio_ref = f32[2,2,128,256]{3,2,1,0:T(8,128)S(1)} custom-call(s32[2]{0:T(128)S(1)} %compare_convert_fusion.active_ref, f32[2,2,128,256]{3,2,1,0:T(8,128)S(1)} %order.1.amplitude_ref, f32[2,128,256]{2,1,0:T(8,128)} %get-tuple-element.22.refs_0_, f32[2,128,256]{2,1,0:T(8,128)S(1)} %copy-done.14, f32[2,128,256]{2,1,0:T(8,128)} %collective-permute-done.3.refs_2_, ...), custom_call_target="tpu_custom_call" | custom-call | tf_op jit(solution)/shard_map/ratio/pallas_call | solution.py:316
  37.6 5.1 %inverse.4 = (f32[2,2,256,256]{3,2,1,0:T(8,128)S(1)}, f32[1,4,2,32,256]{4,3,2,1,0:T(8,128)S(1)}, f32[1,4,2,32,256]{4,3,2,1,0:T(8,128)}) custom-call(s32[2]{0:T(128)S(1)} %pad_add_fusion.1.place_ref, bf16[2,2,2,256,256]{4,3,2,1,0:T(8,128)(2,1)S(1)} %copy-done, f32[2,2,128,256]{3,2,1,0:T(8,128)S(1)} %ratio.1.ratio_ref, f32[2,4,256,256]{3,2,1,0:T(8,128)} %reshape.14.probe_ref, ...), custom_call_target="tpu_custom_call" | custom-call | tf_op jit(solution)/shard_map/inverse/pallas_call | solution.py:340
  43.5 2.5 %collective-permute-start.8 = (f32[1,4,2,32,256]{4,3,2,1,0:T(8,128)}, f32[1,4,2,32,256]{4,3,2,1,0:T(8,128)}, u32[]{:S(2)}, u32[]{:S(2)}) collective-permute-start(f32[1,4,2,32,256]{4,3,2,1,0:T(8,128)} %get-tuple-element.35), channel_id=1, source_target_pairs={{0,2},{2,0},{4,6},{6,4},{8,10},{10,8},{12,14},{14,12},{1,3},{3,1},... | collective-permute-start | bytes 786440 | tf_op jit(solution)/shard_map/ppermute | solution.py:351
  45.9 5.1 %inverse.5 = (f32[2,2,256,256]{3,2,1,0:T(8,128)S(1)}, f32[1,4,2,32,256]{4,3,2,1,0:T(8,128)S(1)}, f32[1,4,2,32,256]{4,3,2,1,0:T(8,128)}) custom-call(s32[2]{0:T(128)S(1)} %pad_add_fusion.1.place_ref, bf16[2,2,2,256,256]{4,3,2,1,0:T(8,128)(2,1)S(1)} %copy-done, f32[2,2,128,256]{3,2,1,0:T(8,128)S(1)} %ratio.1.ratio_ref, ...), custom_call_target="tpu_custom_call", output_to_operand_aliasing={{0}: (8, {})} | custom-call | tf_op jit(solution)/shard_map/inverse/pallas_call | solution.py:340
  52.9 4.4 %inverse.6 = (f32[2,2,256,256]{3,2,1,0:T(8,128)S(1)}, f32[1,4,2,32,256]{4,3,2,1,0:T(8,128)S(1)}, f32[1,4,2,32,256]{4,3,2,1,0:T(8,128)S(1)}) custom-call(s32[2]{0:T(128)S(1)} %pad_add_fusion.1.place_ref, bf16[2,2,2,256,256]{4,3,2,1,0:T(8,128)(2,1)S(1)} %copy-done, f32[2,2,128,256]{3,2,1,0:T(8,128)S(1)} %ratio.1.ratio_ref, ...), custom_call_target="tpu_custom_call", output_to_operand_aliasing={{0}: (8, {})} | custom-call | tf_op jit(solution)/shard_map/inverse/pallas_call | solution.py:340
  57.3 2.1 %collective-permute-start.16 = (f32[1,4,2,32,256]{4,3,2,1,0:T(8,128)S(1)}, f32[1,4,2,32,256]{4,3,2,1,0:T(8,128)S(1)}, u32[]{:S(2)}, u32[]{:S(2)}) collective-permute-start(f32[1,4,2,32,256]{4,3,2,1,0:T(8,128)S(1)} %get-tuple-element.39), channel_id=1, source_target_pairs={{0,2},{2,0},{4,6},{6,4},{8,10},{10,8},{12,14},{14,12},{1,3},{3,1},... | collective-permute-start | bytes 786440 | tf_op jit(solution)/shard_map/ppermute | solution.py:351
  59.4 4.7 %inverse.7 = (f32[2,2,256,256]{3,2,1,0:T(8,128)S(1)}, f32[1,4,2,32,256]{4,3,2,1,0:T(8,128)S(1)}, f32[1,4,2,32,256]{4,3,2,1,0:T(8,128)S(1)}) custom-call(s32[2]{0:T(128)S(1)} %pad_add_fusion.1.place_ref, bf16[2,2,2,256,256]{4,3,2,1,0:T(8,128)(2,1)S(1)} %copy-done, f32[2,2,128,256]{3,2,1,0:T(8,128)S(1)} %ratio.1.ratio_ref, ...), custom_call_target="tpu_custom_call", output_to_operand_aliasing={{0}: (8, {})} | custom-call | tf_op jit(solution)/shard_map/inverse/pallas_call | solution.py:340
  64.2 1.1 %strips.1 = (f32[3,2,64,256]{3,2,1,0:T(8,128)S(1)}, f32[3,2,64,256]{3,2,1,0:T(8,128)S(1)}) custom-call(s32[3]{0:T(128)S(1)} %pad_add_fusion.place_ref, f32[2,2,256,256]{3,2,1,0:T(8,128)S(1)} %get-tuple-element.31.grad_ref), custom_call_target="tpu_custom_call" | custom-call | tf_op jit(solution)/shard_map/strips/pallas_call | solution.py:363
  66.4 2.8 %collective-permute-start.10 = (f32[1,2,32,256]{3,2,1,0:T(8,128)S(1)}, f32[1,2,32,256]{3,2,1,0:T(8,128)S(1)}, u32[]{:S(2)}, u32[]{:S(2)}) collective-permute-start(f32[1,2,32,256]{3,2,1,0:T(8,128)S(1)} %get-tuple-element.48), channel_id=1, source_target_pairs={{0,8},{2,10},{4,12},{6,14},{8,0},{10,2},{12,4},{14,6},{1,9},{3,11}... | collective-permute-start | bytes 196616 | tf_op jit(solution)/shard_map/ppermute | solution.py:356
  69.2 1.3 %collective-permute-start.11 = (f32[1,2,32,256]{3,2,1,0:T(8,128)S(1)}, f32[1,2,32,256]{3,2,1,0:T(8,128)S(1)}, u32[]{:S(2)}, u32[]{:S(2)}) collective-permute-start(f32[1,2,32,256]{3,2,1,0:T(8,128)S(1)} %get-tuple-element.47), channel_id=1, source_target_pairs={{0,12},{2,14},{4,0},{6,2},{8,4},{10,6},{12,8},{14,10},{1,13},{3,15... | collective-permute-start | bytes 196616 | tf_op jit(solution)/shard_map/ppermute | solution.py:356
  72.4 1.6 %collective-permute-start.13 = (f32[1,2,32,256]{3,2,1,0:T(8,128)S(1)}, f32[1,2,32,256]{3,2,1,0:T(8,128)S(1)}, u32[]{:S(2)}, u32[]{:S(2)}) collective-permute-start(f32[1,2,32,256]{3,2,1,0:T(8,128)S(1)} %get-tuple-element.49), channel_id=1, source_target_pairs={{0,4},{2,6},{4,8},{6,10},{8,12},{10,14},{12,0},{14,2},{1,5},{3,7},... | collective-permute-start | bytes 196616 | tf_op jit(solution)/shard_map/ppermute | solution.py:356
  74.1 2.2 %collective-permute-start.14 = (f32[1,2,32,256]{3,2,1,0:T(8,128)S(1)}, f32[1,2,32,256]{3,2,1,0:T(8,128)S(1)}, u32[]{:S(2)}, u32[]{:S(2)}) collective-permute-start(f32[1,2,32,256]{3,2,1,0:T(8,128)S(1)} %get-tuple-element.51), channel_id=1, source_target_pairs={{0,8},{2,10},{4,12},{6,14},{8,0},{10,2},{12,4},{14,6},{1,9},{3,11}... | collective-permute-start | bytes 196616 | tf_op jit(solution)/shard_map/ppermute | solution.py:356
  76.3 2.1 %collective-permute-start.15 = (f32[1,2,32,256]{3,2,1,0:T(8,128)S(1)}, f32[1,2,32,256]{3,2,1,0:T(8,128)S(1)}, u32[]{:S(2)}, u32[]{:S(2)}) collective-permute-start(f32[1,2,32,256]{3,2,1,0:T(8,128)S(1)} %get-tuple-element.50), channel_id=1, source_target_pairs={{0,12},{2,14},{4,0},{6,2},{8,4},{10,6},{12,8},{14,10},{1,13},{3,15... | collective-permute-start | bytes 196616 | tf_op jit(solution)/shard_map/ppermute | solution.py:356
  79.0 2.6 %collective-permute-start.18 = (f32[1,2,32,256]{3,2,1,0:T(8,128)S(1)}, f32[1,2,32,256]{3,2,1,0:T(8,128)S(1)}, u32[]{:S(2)}, u32[]{:S(2)}) collective-permute-start(f32[1,2,32,256]{3,2,1,0:T(8,128)S(1)} %get-tuple-element.54), channel_id=1, source_target_pairs={{0,8},{2,10},{4,12},{6,14},{8,0},{10,2},{12,4},{14,6},{1,9},{3,11}... | collective-permute-start | bytes 196616 | tf_op jit(solution)/shard_map/ppermute | solution.py:356
  81.7 4.0 %collective-permute-start.19 = (f32[1,2,32,256]{3,2,1,0:T(8,128)S(1)}, f32[1,2,32,256]{3,2,1,0:T(8,128)S(1)}, u32[]{:S(2)}, u32[]{:S(2)}) collective-permute-start(f32[1,2,32,256]{3,2,1,0:T(8,128)S(1)} %get-tuple-element.53), channel_id=1, source_target_pairs={{0,12},{2,14},{4,0},{6,2},{8,4},{10,6},{12,8},{14,10},{1,13},{3,15... | collective-permute-start | bytes 196616 | tf_op jit(solution)/shard_map/ppermute | solution.py:356
  87.6 3.0 %collective-permute-start.23 = (f32[1,2,32,256]{3,2,1,0:T(8,128)S(1)}, f32[1,2,32,256]{3,2,1,0:T(8,128)S(1)}, u32[]{:S(2)}, u32[]{:S(2)}) collective-permute-start(f32[1,2,32,256]{3,2,1,0:T(8,128)S(1)} %get-tuple-element.56), channel_id=1, source_target_pairs={{0,12},{2,14},{4,0},{6,2},{8,4},{10,6},{12,8},{14,10},{1,13},{3,15... | collective-permute-start | bytes 196616 | tf_op jit(solution)/shard_map/ppermute | solution.py:356
  90.6 1.7 %collective-permute-done.21 = f32[1,2,32,256]{3,2,1,0:T(8,128)S(1)} collective-permute-done((f32[1,2,32,256]{3,2,1,0:T(8,128)S(1)}, f32[1,2,32,256]{3,2,1,0:T(8,128)S(1)}, u32[]{:S(2)}, u32[]{:S(2)}) %collective-permute-start.21) | collective-permute-done | bytes 65568 | tf_op jit(solution)/shard_map/ppermute | solution.py:356
  92.3 1.4 %collective-permute-done.22 = f32[1,2,32,256]{3,2,1,0:T(8,128)S(1)} collective-permute-done((f32[1,2,32,256]{3,2,1,0:T(8,128)S(1)}, f32[1,2,32,256]{3,2,1,0:T(8,128)S(1)}, u32[]{:S(2)}, u32[]{:S(2)}) %collective-permute-start.22) | collective-permute-done | bytes 65568 | tf_op jit(solution)/shard_map/ppermute | solution.py:356
  94.0 1.3 %collective-permute-start.6 = (f32[2,64,256]{2,1,0:T(8,128)S(1)}, f32[2,64,256]{2,1,0:T(8,128)S(1)}, u32[]{:S(2)}, u32[]{:S(2)}) collective-permute-start(f32[2,64,256]{2,1,0:T(8,128)S(1)} %get-tuple-element.44), channel_id=1, source_target_pairs={{2,0},{4,2},{6,4},{8,6},{10,8},{12,10},{14,12},{3,1},{5,3},{7,5},{... | collective-permute-start | bytes 393224 | tf_op jit(solution)/shard_map/ppermute | solution.py:373
  95.3 4.6 %collective-permute-start.7 = (f32[2,64,256]{2,1,0:T(8,128)S(1)}, f32[2,64,256]{2,1,0:T(8,128)S(1)}, u32[]{:S(2)}, u32[]{:S(2)}) collective-permute-start(f32[2,64,256]{2,1,0:T(8,128)S(1)} %get-tuple-element.45), channel_id=1, source_target_pairs={{0,2},{2,4},{4,6},{6,8},{8,10},{10,12},{12,14},{1,3},{3,5},{5,7},{... | collective-permute-start | bytes 393224 | tf_op jit(solution)/shard_map/ppermute | solution.py:374
  99.9 1.9 %copy_add_fusion = f32[2,4,8192]{2,1,0:T(4,128)} fusion(f32[2,4,8192]{2,0,1:T(2,128)S(1)} %mul.35, f32[2,4,65536]{2,1,0:T(4,128)} %param.8, s32[]{:T(128)S(6)} %select_n.25), kind=kLoop, calls=%fused_computation.3 | loop fusion | flops 65536 | bytes 786436 | tf_op jit(solution)/shard_map/add | solution.py:382
  101.7 2.6 %collective-permute-done.7 = f32[2,64,256]{2,1,0:T(8,128)S(1)} collective-permute-done((f32[2,64,256]{2,1,0:T(8,128)S(1)}, f32[2,64,256]{2,1,0:T(8,128)S(1)}, u32[]{:S(2)}, u32[]{:S(2)}) %collective-permute-start.7) | collective-permute-done | bytes 131104 | tf_op jit(solution)/shard_map/ppermute | solution.py:374
  (82 shorter events, 14.9 us)
Async XLA Ops:
  1.6 7.6 %collective-permute-start = (f32[128,256]{1,0:T(8,128)S(1)}, f32[128,256]{1,0:T(8,128)S(1)}, u32[]{:S(2)}, u32[]{:S(2)}) collective-permute-start(f32[128,256]{1,0:T(8,128)S(1)} %dynamic-slice_bitcast_fusion), channel_id=1, source_target_pairs={{0,2},{2,4},{4,6},{6,8},{8,10},{10,12},{12,14},{1,3},{3,5},{5,7},{... | collective-permute-start | bytes 393224 | tf_op jit(solution)/shard_map/ppermute | solution.py:275
  6.4 6.9 %collective-permute-start.1 = (f32[128,256]{1,0:T(8,128)S(1)}, f32[128,256]{1,0:T(8,128)S(1)}, u32[]{:S(2)}, u32[]{:S(2)}) collective-permute-start(f32[128,256]{1,0:T(8,128)S(1)} %dynamic-slice_bitcast_fusion), channel_id=1, source_target_pairs={{2,0},{4,2},{6,4},{8,6},{10,8},{12,10},{14,12},{3,1},{5,3},{7,5},{... | collective-permute-start | bytes 393224 | tf_op jit(solution)/shard_map/ppermute | solution.py:276
  13.3 6.5 %collective-permute-start.2 = (f32[2,128,256]{2,1,0:T(8,128)S(1)}, f32[2,128,256]{2,1,0:T(8,128)S(1)}, u32[]{:S(2)}, u32[]{:S(2)}) collective-permute-start(f32[2,128,256]{2,1,0:T(8,128)S(1)} %pad_maximum_fusion.near_ref), channel_id=1, source_target_pairs={{0,1},{1,0},{2,3},{3,2},{4,5},{5,4},{6,7},{7,6},{8,9},{9,8},{10,11... | collective-permute-start | bytes 786440 | tf_op jit(solution)/shard_map/ppermute | solution.py:278
  14.2 5.6 %copy-start = (bf16[2,2,2,256,256]{4,3,2,1,0:T(8,128)(2,1)S(1)}, bf16[2,2,2,256,256]{4,3,2,1,0:T(8,128)(2,1)}, u32[]{:S(2)}) copy-start(bf16[2,2,2,256,256]{4,3,2,1,0:T(8,128)(2,1)} %constant.55.clone.table_ref) | copy-start | bytes 3145732
  14.2 5.6 %copy-start.6 = (f32[2,128,256]{2,1,0:T(8,128)S(1)}, f32[2,128,256]{2,1,0:T(8,128)}, u32[]{:S(2)}) copy-start(f32[2,128,256]{2,1,0:T(8,128)} %own_ref.3) | copy-start | bytes 786436
  25.5 9.6 %copy-start.13 = (f32[2,128,256]{2,1,0:T(8,128)}, f32[2,128,256]{2,1,0:T(8,128)S(1)}, u32[]{:S(2)}) copy-start(f32[2,128,256]{2,1,0:T(8,128)S(1)} %get-tuple-element.23.refs_1_) | copy-start | bytes 786436
  25.5 8.6 %copy-start.7 = (f32[2,256,256]{2,1,0:T(8,128)S(1)}, f32[2,256,256]{2,1,0:T(8,128)}, u32[]{:S(2)}) copy-start(f32[2,256,256]{2,1,0:T(8,128)} %measured_ref.1) | copy-start | bytes 1572868
  25.5 8.6 %copy-start.8 = (bf16[2,256,256]{2,1,0:T(8,128)(2,1)S(1)}, bf16[2,256,256]{2,1,0:T(8,128)(2,1)}, u32[]{:S(2)}) copy-start(bf16[2,256,256]{2,1,0:T(8,128)(2,1)} %constant.56.clone.order_ref) | copy-start | bytes 786436
  25.5 9.7 %collective-permute-start.4 = (f32[2,128,256]{2,1,0:T(8,128)S(1)}, f32[2,128,256]{2,1,0:T(8,128)}, u32[]{:S(2)}, u32[]{:S(2)}) collective-permute-start(f32[2,128,256]{2,1,0:T(8,128)S(1)} %get-tuple-element.23.refs_1_), channel_id=1, source_target_pairs={{0,1},{1,0},{2,3},{3,2},{4,5},{5,4},{6,7},{7,6},{8,9},{9,8},{10,11... | collective-permute-start | bytes 786440 | tf_op jit(solution)/shard_map/ppermute | solution.py:314
  33.4 1.9 %collective-permute-start.3 = (f32[2,128,256]{2,1,0:T(8,128)}, f32[2,128,256]{2,1,0:T(8,128)}, u32[]{:S(2)}, u32[]{:S(2)}) collective-permute-start(f32[2,128,256]{2,1,0:T(8,128)} %get-tuple-element.22.refs_0_), channel_id=1, source_target_pairs={{0,1},{1,0},{2,3},{3,2},{4,5},{5,4},{6,7},{7,6},{8,9},{9,8},{10,11... | collective-permute-start | bytes 786440 | tf_op jit(solution)/shard_map/ppermute | solution.py:314
  35.1 2.5 %copy-start.4 = (f32[2,256,256]{2,1,0:T(8,128)S(1)}, f32[2,256,256]{2,1,0:T(8,128)}, u32[]{:S(2)}) copy-start(f32[2,256,256]{2,1,0:T(8,128)} %copy-done.3) | copy-start | bytes 1572868
  43.5 21.9 %collective-permute-start.8 = (f32[1,4,2,32,256]{4,3,2,1,0:T(8,128)}, f32[1,4,2,32,256]{4,3,2,1,0:T(8,128)}, u32[]{:S(2)}, u32[]{:S(2)}) collective-permute-start(f32[1,4,2,32,256]{4,3,2,1,0:T(8,128)} %get-tuple-element.35), channel_id=1, source_target_pairs={{0,2},{2,0},{4,6},{6,4},{8,10},{10,8},{12,14},{14,12},{1,3},{3,1},... | collective-permute-start | bytes 786440 | tf_op jit(solution)/shard_map/ppermute | solution.py:351
  51.8 17.4 %collective-permute-start.12 = (f32[1,4,2,32,256]{4,3,2,1,0:T(8,128)}, f32[1,4,2,32,256]{4,3,2,1,0:T(8,128)}, u32[]{:S(2)}, u32[]{:S(2)}) collective-permute-start(f32[1,4,2,32,256]{4,3,2,1,0:T(8,128)} %get-tuple-element.37), channel_id=1, source_target_pairs={{0,2},{2,0},{4,6},{6,4},{8,10},{10,8},{12,14},{14,12},{1,3},{3,1},... | collective-permute-start | bytes 786440 | tf_op jit(solution)/shard_map/ppermute | solution.py:351
  57.3 14.2 %collective-permute-start.16 = (f32[1,4,2,32,256]{4,3,2,1,0:T(8,128)S(1)}, f32[1,4,2,32,256]{4,3,2,1,0:T(8,128)S(1)}, u32[]{:S(2)}, u32[]{:S(2)}) collective-permute-start(f32[1,4,2,32,256]{4,3,2,1,0:T(8,128)S(1)} %get-tuple-element.39), channel_id=1, source_target_pairs={{0,2},{2,0},{4,6},{6,4},{8,10},{10,8},{12,14},{14,12},{1,3},{3,1},... | collective-permute-start | bytes 786440 | tf_op jit(solution)/shard_map/ppermute | solution.py:351
  59.4 5.9 %copy-start.12 = (f32[1,4,2,32,256]{4,3,2,1,0:T(8,128)S(1)}, f32[1,4,2,32,256]{4,3,2,1,0:T(8,128)}, u32[]{:S(2)}) copy-start(f32[1,4,2,32,256]{4,3,2,1,0:T(8,128)} %copy-done.11) | copy-start | bytes 786436
  64.1 6.5 %copy-start.10 = (f32[1,4,2,32,256]{4,3,2,1,0:T(8,128)S(1)}, f32[1,4,2,32,256]{4,3,2,1,0:T(8,128)}, u32[]{:S(2)}) copy-start(f32[1,4,2,32,256]{4,3,2,1,0:T(8,128)} %copy-done.9) | copy-start | bytes 786436
  64.1 8.3 %collective-permute-start.20 = (f32[1,4,2,32,256]{4,3,2,1,0:T(8,128)S(1)}, f32[1,4,2,32,256]{4,3,2,1,0:T(8,128)S(1)}, u32[]{:S(2)}, u32[]{:S(2)}) collective-permute-start(f32[1,4,2,32,256]{4,3,2,1,0:T(8,128)S(1)} %get-tuple-element.41), channel_id=1, source_target_pairs={{0,2},{2,0},{4,6},{6,4},{8,10},{10,8},{12,14},{14,12},{1,3},{3,1},... | collective-permute-start | bytes 786440 | tf_op jit(solution)/shard_map/ppermute | solution.py:351
  65.3 28.6 %collective-permute-start.5 = (f32[3,2,64,256]{3,2,1,0:T(8,128)S(1)}, f32[3,2,64,256]{3,2,1,0:T(8,128)S(1)}, u32[]{:S(2)}, u32[]{:S(2)}) collective-permute-start(f32[3,2,64,256]{3,2,1,0:T(8,128)S(1)} %get-tuple-element.33), channel_id=1, source_target_pairs={{0,1},{1,0},{2,3},{3,2},{4,5},{5,4},{6,7},{7,6},{8,9},{9,8},{10,11... | collective-permute-start | bytes 1179656 | tf_op jit(solution)/shard_map/ppermute | solution.py:372
  66.4 7.7 %collective-permute-start.10 = (f32[1,2,32,256]{3,2,1,0:T(8,128)S(1)}, f32[1,2,32,256]{3,2,1,0:T(8,128)S(1)}, u32[]{:S(2)}, u32[]{:S(2)}) collective-permute-start(f32[1,2,32,256]{3,2,1,0:T(8,128)S(1)} %get-tuple-element.48), channel_id=1, source_target_pairs={{0,8},{2,10},{4,12},{6,14},{8,0},{10,2},{12,4},{14,6},{1,9},{3,11}... | collective-permute-start | bytes 196616 | tf_op jit(solution)/shard_map/ppermute | solution.py:356
  69.2 7.1 %collective-permute-start.11 = (f32[1,2,32,256]{3,2,1,0:T(8,128)S(1)}, f32[1,2,32,256]{3,2,1,0:T(8,128)S(1)}, u32[]{:S(2)}, u32[]{:S(2)}) collective-permute-start(f32[1,2,32,256]{3,2,1,0:T(8,128)S(1)} %get-tuple-element.47), channel_id=1, source_target_pairs={{0,12},{2,14},{4,0},{6,2},{8,4},{10,6},{12,8},{14,10},{1,13},{3,15... | collective-permute-start | bytes 196616 | tf_op jit(solution)/shard_map/ppermute | solution.py:356
  71.6 6.8 %collective-permute-start.9 = (f32[1,2,32,256]{3,2,1,0:T(8,128)S(1)}, f32[1,2,32,256]{3,2,1,0:T(8,128)S(1)}, u32[]{:S(2)}, u32[]{:S(2)}) collective-permute-start(f32[1,2,32,256]{3,2,1,0:T(8,128)S(1)} %get-tuple-element.46), channel_id=1, source_target_pairs={{0,4},{2,6},{4,8},{6,10},{8,12},{10,14},{12,0},{14,2},{1,5},{3,7},... | collective-permute-start | bytes 196616 | tf_op jit(solution)/shard_map/ppermute | solution.py:356
  72.4 6.7 %collective-permute-start.13 = (f32[1,2,32,256]{3,2,1,0:T(8,128)S(1)}, f32[1,2,32,256]{3,2,1,0:T(8,128)S(1)}, u32[]{:S(2)}, u32[]{:S(2)}) collective-permute-start(f32[1,2,32,256]{3,2,1,0:T(8,128)S(1)} %get-tuple-element.49), channel_id=1, source_target_pairs={{0,4},{2,6},{4,8},{6,10},{8,12},{10,14},{12,0},{14,2},{1,5},{3,7},... | collective-permute-start | bytes 196616 | tf_op jit(solution)/shard_map/ppermute | solution.py:356
  74.1 7.6 %collective-permute-start.14 = (f32[1,2,32,256]{3,2,1,0:T(8,128)S(1)}, f32[1,2,32,256]{3,2,1,0:T(8,128)S(1)}, u32[]{:S(2)}, u32[]{:S(2)}) collective-permute-start(f32[1,2,32,256]{3,2,1,0:T(8,128)S(1)} %get-tuple-element.51), channel_id=1, source_target_pairs={{0,8},{2,10},{4,12},{6,14},{8,0},{10,2},{12,4},{14,6},{1,9},{3,11}... | collective-permute-start | bytes 196616 | tf_op jit(solution)/shard_map/ppermute | solution.py:356
  76.3 9.4 %collective-permute-start.15 = (f32[1,2,32,256]{3,2,1,0:T(8,128)S(1)}, f32[1,2,32,256]{3,2,1,0:T(8,128)S(1)}, u32[]{:S(2)}, u32[]{:S(2)}) collective-permute-start(f32[1,2,32,256]{3,2,1,0:T(8,128)S(1)} %get-tuple-element.50), channel_id=1, source_target_pairs={{0,12},{2,14},{4,0},{6,2},{8,4},{10,6},{12,8},{14,10},{1,13},{3,15... | collective-permute-start | bytes 196616 | tf_op jit(solution)/shard_map/ppermute | solution.py:356
  78.4 8.4 %collective-permute-start.17 = (f32[1,2,32,256]{3,2,1,0:T(8,128)S(1)}, f32[1,2,32,256]{3,2,1,0:T(8,128)S(1)}, u32[]{:S(2)}, u32[]{:S(2)}) collective-permute-start(f32[1,2,32,256]{3,2,1,0:T(8,128)S(1)} %get-tuple-element.52), channel_id=1, source_target_pairs={{0,4},{2,6},{4,8},{6,10},{8,12},{10,14},{12,0},{14,2},{1,5},{3,7},... | collective-permute-start | bytes 196616 | tf_op jit(solution)/shard_map/ppermute | solution.py:356
  79.0 8.6 %collective-permute-start.18 = (f32[1,2,32,256]{3,2,1,0:T(8,128)S(1)}, f32[1,2,32,256]{3,2,1,0:T(8,128)S(1)}, u32[]{:S(2)}, u32[]{:S(2)}) collective-permute-start(f32[1,2,32,256]{3,2,1,0:T(8,128)S(1)} %get-tuple-element.54), channel_id=1, source_target_pairs={{0,8},{2,10},{4,12},{6,14},{8,0},{10,2},{12,4},{14,6},{1,9},{3,11}... | collective-permute-start | bytes 196616 | tf_op jit(solution)/shard_map/ppermute | solution.py:356
  81.7 9.0 %collective-permute-start.19 = (f32[1,2,32,256]{3,2,1,0:T(8,128)S(1)}, f32[1,2,32,256]{3,2,1,0:T(8,128)S(1)}, u32[]{:S(2)}, u32[]{:S(2)}) collective-permute-start(f32[1,2,32,256]{3,2,1,0:T(8,128)S(1)} %get-tuple-element.53), channel_id=1, source_target_pairs={{0,12},{2,14},{4,0},{6,2},{8,4},{10,6},{12,8},{14,10},{1,13},{3,15... | collective-permute-start | bytes 196616 | tf_op jit(solution)/shard_map/ppermute | solution.py:356
  85.7 6.6 %collective-permute-start.21 = (f32[1,2,32,256]{3,2,1,0:T(8,128)S(1)}, f32[1,2,32,256]{3,2,1,0:T(8,128)S(1)}, u32[]{:S(2)}, u32[]{:S(2)}) collective-permute-start(f32[1,2,32,256]{3,2,1,0:T(8,128)S(1)} %get-tuple-element.55), channel_id=1, source_target_pairs={{0,4},{2,6},{4,8},{6,10},{8,12},{10,14},{12,0},{14,2},{1,5},{3,7},... | collective-permute-start | bytes 196616 | tf_op jit(solution)/shard_map/ppermute | solution.py:356
  86.8 6.9 %collective-permute-start.22 = (f32[1,2,32,256]{3,2,1,0:T(8,128)S(1)}, f32[1,2,32,256]{3,2,1,0:T(8,128)S(1)}, u32[]{:S(2)}, u32[]{:S(2)}) collective-permute-start(f32[1,2,32,256]{3,2,1,0:T(8,128)S(1)} %get-tuple-element.57), channel_id=1, source_target_pairs={{0,8},{2,10},{4,12},{6,14},{8,0},{10,2},{12,4},{14,6},{1,9},{3,11}... | collective-permute-start | bytes 196616 | tf_op jit(solution)/shard_map/ppermute | solution.py:356
  87.6 6.0 %collective-permute-start.23 = (f32[1,2,32,256]{3,2,1,0:T(8,128)S(1)}, f32[1,2,32,256]{3,2,1,0:T(8,128)S(1)}, u32[]{:S(2)}, u32[]{:S(2)}) collective-permute-start(f32[1,2,32,256]{3,2,1,0:T(8,128)S(1)} %get-tuple-element.56), channel_id=1, source_target_pairs={{0,12},{2,14},{4,0},{6,2},{8,4},{10,6},{12,8},{14,10},{1,13},{3,15... | collective-permute-start | bytes 196616 | tf_op jit(solution)/shard_map/ppermute | solution.py:356
  94.0 7.7 %collective-permute-start.6 = (f32[2,64,256]{2,1,0:T(8,128)S(1)}, f32[2,64,256]{2,1,0:T(8,128)S(1)}, u32[]{:S(2)}, u32[]{:S(2)}) collective-permute-start(f32[2,64,256]{2,1,0:T(8,128)S(1)} %get-tuple-element.44), channel_id=1, source_target_pairs={{2,0},{4,2},{6,4},{8,6},{10,8},{12,10},{14,12},{3,1},{5,3},{7,5},{... | collective-permute-start | bytes 393224 | tf_op jit(solution)/shard_map/ppermute | solution.py:373
  95.3 9.0 %collective-permute-start.7 = (f32[2,64,256]{2,1,0:T(8,128)S(1)}, f32[2,64,256]{2,1,0:T(8,128)S(1)}, u32[]{:S(2)}, u32[]{:S(2)}) collective-permute-start(f32[2,64,256]{2,1,0:T(8,128)S(1)} %get-tuple-element.45), channel_id=1, source_target_pairs={{0,2},{2,4},{4,6},{6,8},{8,10},{10,12},{12,14},{1,3},{3,5},{5,7},{... | collective-permute-start | bytes 393224 | tf_op jit(solution)/shard_map/ppermute | solution.py:374
  (7 other events, 7.0 us)

commit v2 on v1

--- a/solution.py
+++ b/solution.py
@@ -16,7 +16,7 @@
 
 F32 = jnp.float32
 BF16 = jnp.bfloat16
-VMEM_LIMIT = 48 * 1024 * 1024
+VMEM_LIMIT = 24 * 1024 * 1024
 
 
 def real_tables(size):
@@ -110,7 +110,17 @@
     return high, middle, low
 
 
-def order_kernel(measured_ref, order_ref, out_ref):
+def prepare_kernel(place_ref, probe_ref, measured_ref, order_ref, grid_ref, own_ref, out_ref):
+    parts, modes, size, columns = grid_ref.shape
+    lines = columns // 128
+    for part in range(parts):
+        for mode in range(modes):
+            for line in range(lines):
+                grid_ref[part, mode, :, line * 128 : (line + 1) * 128] = probe_ref[
+                    part, pl.ds(line * modes + mode, size, stride=lines * modes), :
+                ]
+    share = own_ref.shape[1]
+    own_ref[...] = probe_ref[:, pl.ds(pl.multiple_of(place_ref[0] * share, share), share), :]
     half = order_ref.shape[1] // 2
     columns, rows = order_ref[0], order_ref[1]
     for slot in range(measured_ref.shape[0]):
@@ -165,20 +175,18 @@
                 power_ref[parity] += power
 
 
-def ratio_kernel(active_ref, amplitude_ref, *refs):
-    ratio_ref = refs[-1]
-    slots = ratio_ref.shape[0]
-    for slot in range(slots):
-        model = jnp.sqrt(refs[slot][...] + refs[slots + slot][...] + damping_factor)
-        ratio_ref[slot] = (amplitude_ref[slot] / model - 1.0) * active_ref[slot].astype(F32)
-
-
-def inverse_kernel(modes, first, slots, place_ref, table_ref, ratio_ref, probe_ref, *refs):
+def inverse_kernel(modes, first, slots, place_ref, table_ref, probe_ref, *refs):
     far_refs, patch_refs = refs[:slots], refs[slots : 2 * slots]
     refs = refs[2 * slots :]
-    if not first:
-        refs = refs[1:]
-    grad_ref, keep_ref, send_ref = refs
+    if first:
+        amplitude_ref, power_refs, other_refs = refs[0], refs[1 : 1 + slots], refs[1 + slots : 1 + 2 * slots]
+        grad_ref, keep_ref, send_ref, ratio_ref = refs[1 + 2 * slots :]
+        for slot in range(slots):
+            model = jnp.sqrt(power_refs[slot][...] + other_refs[slot][...] + damping_factor)
+            active = (slot < place_ref[2]).astype(F32)
+            ratio_ref[slot] = (amplitude_ref[slot] / model - 1.0) * active
+    else:
+        _, ratio_ref, grad_ref, keep_ref, send_ref = refs
     inner, outer = place_ref[0], place_ref[1]
     size = probe_ref.shape[2]
     outers, rows = keep_ref.shape[1], keep_ref.shape[3]
@@ -246,22 +254,53 @@
                 ref[strip, part] = total
 
 
-def vmem():
-    return pl.BlockSpec(memory_space=pltpu.VMEM)
-
-
-def smem():
-    return pl.BlockSpec(memory_space=pltpu.SMEM)
-
-
-def params():
-    return pltpu.CompilerParams(vmem_limit_bytes=VMEM_LIMIT)
+def finish_kernel(counts, place_ref, probe_ref, strip_ref, mid_ref, above_ref, below_ref, *refs):
+    object_ref, out_ref = refs[-2:]
+    half = object_ref.shape[1]
+    begin = pl.multiple_of(place_ref[0] * half, half)
+    object_ref[...] = strip_ref[:, pl.ds(begin, half), :] + object_step * (
+        mid_ref[...] + above_ref[...] + below_ref[...]
+    )
+    modes = sum(group for group, _ in counts)
+    mode = 0
+    for group, terms in counts:
+        group_refs, refs = refs[:terms], refs[terms:]
+        for index in range(group):
+            for part in range(out_ref.shape[0]):
+                value = sum(ref[index, part] for ref in group_refs)
+                rows, columns = value.shape
+                lines = columns // 128
+                for line in range(lines):
+                    where = pl.ds(line * modes + mode, rows, stride=lines * modes)
+                    out_ref[part, where, :] = probe_ref[part, where, :] + probe_step * (
+                        value[:, line * 128 : (line + 1) * 128]
+                    )
+            mode += 1
+
+
+def call(kernel, out_shape, scalars, arrays, name, **options):
+    several = isinstance(out_shape, (tuple, list))
+    vmem = pl.BlockSpec(memory_space=pltpu.VMEM)
+    return pl.pallas_call(
+        kernel,
+        out_shape=out_shape,
+        in_specs=[pl.BlockSpec(memory_space=pltpu.SMEM)] + [vmem] * len(arrays),
+        out_specs=(vmem,) * len(out_shape) if several else vmem,
+        compiler_params=pltpu.CompilerParams(vmem_limit_bytes=VMEM_LIMIT),
+        name=name,
+        **options,
+    )(jnp.stack(scalars).astype(jnp.int32), *arrays)
+
+
+def shape(*sizes):
+    return jax.ShapeDtypeStruct(sizes, F32)
 
 
 def on_device(object_field, probe, measured, offsets, counts):
-    _, strip_rows, columns = object_field.shape
+    parts, strip_rows, columns = object_field.shape
     slots, size, _ = measured.shape
     modes = probe.shape[1]
+    half = size // 2
     positions = lax.axis_size("pos")
     tiles = lax.axis_size("tile")
     position = lax.axis_index("pos")
@@ -274,112 +313,112 @@
     component = lax.dynamic_index_in_dim(object_field, tile, 0, keepdims=False)
     low = lax.ppermute(component, "pos", up)
     high = lax.ppermute(component, "pos", down)
+
+    pixel_lines = size * size // 128
+    share = pixel_lines // positions * modes
+    order = np.zeros((size, size), ml_dtypes.bfloat16)
+    for parity in (0, 1):
+        for index in range(half):
+            order[2 * index + parity, parity * half + index] = 1
+    probe_lines = probe.reshape(parts, modes, pixel_lines, 128).transpose(0, 2, 1, 3)
+    probe_grid, probe_own, amplitude = call(
+        prepare_kernel,
+        (shape(parts, modes, size, size), shape(parts, share, 128), shape(slots, 2, half, size)),
+        [position],
+        [
+            probe_lines.reshape(parts, pixel_lines * modes, 128),
+            measured,
+            jnp.asarray(np.stack([order, order.T])),
+        ],
+        "prepare",
+    )
+    low, high, probe_grid = lax.optimization_barrier((low, high, probe_grid))
     near = jnp.stack([low, high])
     other = lax.ppermute(near, "tile", swap)
-
-    probe_grid = probe.reshape(2, modes, size, size)
-    order = np.zeros((size, size), ml_dtypes.bfloat16)
-    for parity in (0, 1):
-        for index in range(size // 2):
-            order[2 * index + parity, parity * (size // 2) + index] = 1
-    amplitude = pl.pallas_call(
-        order_kernel,
-        out_shape=jax.ShapeDtypeStruct((slots, 2, size // 2, size), F32),
-        in_specs=[vmem(), vmem()],
-        out_specs=vmem(),
-        compiler_params=params(),
-        name="order",
-    )(measured, jnp.asarray(np.stack([order, order.T])))
 
     starts = offsets[:, 0] - (position * strip_rows - strip_rows)
     far, power, patch = [], [], []
     for slot in range(slots):
-        place = jnp.stack([starts[slot], tile]).astype(jnp.int32)
-        outs = pl.pallas_call(
+        outs = call(
             forward_kernel,
-            out_shape=(
-                jax.ShapeDtypeStruct((modes, 2, size, size), F32),
-                jax.ShapeDtypeStruct((2, size // 2, size), F32),
-                jax.ShapeDtypeStruct((2, size, size), F32),
-            ),
-            in_specs=[smem()] + [vmem()] * 5,
-            out_specs=(vmem(), vmem(), vmem()),
-            scratch_shapes=[pltpu.VMEM((2, 3 * strip_rows + 8, columns), F32)],
-            compiler_params=params(),
-            name="forward",
-        )(place, object_field, near, other, probe_grid, tables)
+            (shape(modes, 2, size, size), shape(2, half, size), shape(parts, size, size)),
+            [starts[slot], tile],
+            [object_field, near, other, probe_grid, tables],
+            "forward",
+            scratch_shapes=[pltpu.VMEM((parts, 3 * strip_rows + 8, columns), F32)],
+        )
         far.append(outs[0])
         power.append(outs[1])
         patch.append(outs[2])
     others = [lax.ppermute(value, "tile", swap) for value in power]
-    active = (jnp.arange(slots, dtype=jnp.int32) < counts[0]).astype(jnp.int32)
-    ratio = pl.pallas_call(
-        ratio_kernel,
-        out_shape=jax.ShapeDtypeStruct((slots, 2, size // 2, size), F32),
-        in_specs=[smem()] + [vmem()] * (1 + 2 * slots),
-        out_specs=vmem(),
-        compiler_params=params(),
-        name="ratio",
-    )(active, amplitude, *power, *others)
 
     outers = positions // 2
     direct = outers <= 4
     block_rows = size // positions
-    inner, outer = position % 2, position // 2
-    where = jnp.stack([inner, outer]) if direct else jnp.zeros((2,), jnp.int32)
+    where = [position % 2, position // 2] if direct else [jnp.int32(0), jnp.int32(0)]
     group = 1
-    grad = None
     sums = []
     for begin in range(0, modes, group):
-        block_shape = jax.ShapeDtypeStruct((group, outers, 2, block_rows, size), F32)
-        grad_shape = jax.ShapeDtypeStruct((slots, 2, size, size), F32)
+        block_shape = shape(group, outers, 2, block_rows, size)
+        grad_shape = shape(slots, 2, size, size)
         first = begin == 0
-        arguments = [where.astype(jnp.int32), tables, ratio, probe_grid, *far, *patch]
-        if not first:
-            arguments.append(grad)
-        grad, keep, send = pl.pallas_call(
-            functools.partial(inverse_kernel, tuple(range(begin, begin + group)), first, slots),
-            out_shape=(grad_shape, block_shape, block_shape),
-            in_specs=[smem()] + [vmem()] * (len(arguments) - 1),
-            out_specs=(vmem(), vmem(), vmem()),
-            input_output_aliases={} if first else {len(arguments) - 1: 0},
-            compiler_params=params(),
-            name="inverse",
-        )(*arguments)
+        kernel = functools.partial(
+            inverse_kernel, tuple(range(begin, begin + group)), first, slots
+        )
+        arrays = [tables, probe_grid, *far, *patch]
+        if first:
+            grad, keep, send, ratio = call(
+                kernel,
+                (grad_shape, block_shape, block_shape, shape(slots, 2, half, size)),
+                [*where, counts[0]],
+                [*arrays, amplitude, *power, *others],
+                "inverse",
+            )
+        else:
+            arrays += [grad, ratio]
+            grad, keep, send = call(
+                kernel,
+                (grad_shape, block_shape, block_shape),
+                where,
+                arrays,
+                "inverse",
+                input_output_aliases={len(arrays) - 1: 0},
+            )
         if direct:
             pair = [(i, i ^ 1) for i in range(positions)]
-            got = lax.ppermute(send, "pos", pair)
-            both = keep + got
-            total = both[:, 0]
+            both = keep + lax.ppermute(send, "pos", pair)
+            terms = [both[:, 0]]
             for distance in range(1, outers):
                 ring = [(i, (i + 2 * distance) % positions) for i in range(positions)]
-                total = total + lax.ppermute(both[:, distance], "pos", ring)
+                terms.append(lax.ppermute(both[:, distance], "pos", ring))
         else:
             both = jnp.stack([keep, send], 2).reshape(group, positions, 2, block_rows, size)
-            total = lax.psum_scatter(both, "pos", scatter_dimension=1, tiled=True)[:, 0]
-        sums.append(total)
-
-    strip_shape = jax.ShapeDtypeStruct((3, 2, strip_rows // tiles, columns), F32)
-    kept, sent = pl.pallas_call(
+            terms = [lax.psum_scatter(both, "pos", scatter_dimension=1, tiled=True)[:, 0]]
+        sums.append(terms)
+
+    half_rows = strip_rows // tiles
+    strip_shape = shape(3, parts, half_rows, columns)
+    kept, sent = call(
         strip_kernel,
-        out_shape=(strip_shape, strip_shape),
-        in_specs=[smem(), vmem()],
-        out_specs=(vmem(), vmem()),
-        scratch_shapes=[pltpu.VMEM((slots, 2, 2 * strip_rows + size + 8, columns), F32)],
-        compiler_params=params(),
-        name="strips",
-    )(jnp.concatenate([starts, tile[None]]).astype(jnp.int32), grad)
+        (strip_shape, strip_shape),
+        [*(starts[slot] for slot in range(slots)), tile],
+        [grad],
+        "strips",
+        scratch_shapes=[pltpu.VMEM((slots, parts, 2 * strip_rows + size + 8, columns), F32)],
+    )
     strips = kept + lax.ppermute(sent, "tile", swap)
-    from_above = lax.ppermute(strips[0], "pos", down)
-    from_below = lax.ppermute(strips[2], "pos", up)
-    half_rows = strip_rows // tiles
-    own_rows = lax.dynamic_slice_in_dim(object_field, tile * half_rows, half_rows, 1)
-    object_out = own_rows + object_step * (strips[1] + from_above + from_below)
-
-    pixel_share = size * size // positions
-    probe_own = lax.dynamic_slice_in_dim(probe, position * pixel_share, pixel_share, 2)
-    probe_mine = jnp.concatenate(sums, 0).transpose(1, 0, 2, 3).reshape(2, modes, pixel_share)
-    return (object_out, probe_own + probe_step * probe_mine)
+    above = lax.ppermute(strips[0], "pos", down)
+    below = lax.ppermute(strips[2], "pos", up)
+
+    object_out, probe_out = call(
+        functools.partial(finish_kernel, [(group, len(terms)) for terms in sums]),
+        (shape(parts, half_rows, columns), shape(parts, share, 128)),
+        [tile],
+        [probe_own, object_field, strips[1], above, below, *sum(sums, [])],
+        "finish",
+    )
+    probe_out = probe_out.reshape(parts, share // modes, modes, 128).transpose(0, 2, 1, 3)
+    return (object_out, probe_out.reshape(parts, modes, share // modes * 128))
 
 
 def solution(mesh):

time: 106 us -> 96.4 us (0.909)
  Pallas kernels: 32.3 us -> 21 us
  waiting for transfers between devices: 11.2 us -> 15.8 us
  local copies, waits for them, and re-layouts: 12.5 us -> 16.6 us
  other arithmetic: 7.01 us -> 3.06 us
  starting transfers between devices: 40.3 us -> 37.7 us
    pallas_call x9, Pallas kernels: 32.3 us -> 21 us  [call(): pl.pallas_call(kernel, out_shape=out_shape, in_specs=[pl.BlockSpec(memory...]
    ppermute x18, waiting for transfers between devices: 5.65 us -> 14.7 us  [the longest x12 8.22 us: on_device(): terms.append(lax.ppermute(both[:, distance], 'pos', ring))]
    unnamed x30 -> x38, local copies, waits for them, and re-layouts: 6.99 us -> 14.9 us
    add x10 -> x4, other arithmetic: 4.68 us -> 0.15 us  [on_device(): both = keep + lax.ppermute(send, 'pos', pair)]
    ppermute x1, waiting for transfers between devices: 4.13 us -> 0.01 us  [on_device(): high = lax.ppermute(component, 'pos', down)]
    ppermute x18, starting transfers between devices: 33.4 us -> 29.7 us  [the longest x12 19.1 us: on_device(): terms.append(lax.ppermute(both[:, distance], 'pos', ring))]
    reshape x1 -> x0, local copies, waits for them, and re-layouts: 3.77 us -> none  [on_device(): probe_grid = probe.reshape(2, modes, size, size)]
    ppermute x1, waiting for transfers between devices: 1.42 us -> 0.01 us  [on_device(): low = lax.ppermute(component, 'pos', up)]
  transfers between devices with their start and end apart: 24 -> 24, of which waited for: 5 -> 7; matrix products, arithmetic and copies ran while one was open for 10% -> 3% of each run, Pallas kernels for 20% -> 14%
where the time goes in v2:
time: 96.4 us; the launch traced here: 95.8 us
  starting transfers between devices  37.7 us (39%)
  Pallas kernels  21 us (22%)
  local copies, waits for them, and re-layouts  16.6 us (17%)
  waiting for transfers between devices  15.8 us (16%)
  other arithmetic  3.06 us (3%)
  between operations  1.6 us (2%)
    pallas_call x9, Pallas kernels, call(): pl.pallas_call(kernel, out_shape=out_shape, in_specs=[pl.BlockSpec(memory...  21 us
    ppermute x12, starting transfers between devices, on_device(): terms.append(lax.ppermute(both[:, distance], 'pos', ring))  19.1 us
    unnamed x38, local copies, waits for them, and re-layouts  14.9 us
    ppermute x12, waiting for transfers between devices, on_device(): terms.append(lax.ppermute(both[:, distance], 'pos', ring))  8.22 us
    ppermute x4, waiting for transfers between devices, on_device(): both = keep + lax.ppermute(send, 'pos', pair)  6.43 us
    ppermute x1, starting transfers between devices, on_device(): low = lax.ppermute(component, 'pos', up)  6.13 us
    ppermute x1, starting transfers between devices, on_device(): below = lax.ppermute(strips[2], 'pos', up)  4.76 us
    ppermute x4, starting transfers between devices, on_device(): both = keep + lax.ppermute(send, 'pos', pair)  4.53 us
  transfers between devices with their start and end apart: 24, of which 7 were waited for; matrix products, arithmetic and copies ran while one was open for 3% of the time, Pallas kernels for 14%

profile of v2, /device:TPU:0, one launch (start us, length us, event | category | flops | bytes accessed | tf_op | source)
XLA Modules:
  0.0 95.8 jit_solution(787810110113872232)
XLA Ops:
  1.7 1.3 %collective-permute-start.1 = (f32[128,256]{1,0:T(8,128)S(1)}, f32[128,256]{1,0:T(8,128)}, u32[]{:S(2)}, u32[]{:S(2)}) collective-permute-start(f32[128,256]{1,0:T(8,128)S(1)} %dynamic-slice_bitcast_fusion), channel_id=1, source_target_pairs={{2,0},{4,2},{6,4},{8,6},{10,8},{12,10},{14,12},{3,1},{5,3},{7,5},{... | collective-permute-start | bytes 393224 | tf_op jit(solution)/shard_map/ppermute | solution.py:315
  3.0 6.1 %collective-permute-start = (f32[128,256]{1,0:T(8,128)S(1)}, f32[128,256]{1,0:T(8,128)}, u32[]{:S(2)}, u32[]{:S(2)}) collective-permute-start(f32[128,256]{1,0:T(8,128)S(1)} %dynamic-slice_bitcast_fusion), channel_id=1, source_target_pairs={{0,2},{2,4},{4,6},{6,8},{8,10},{10,12},{12,14},{1,3},{3,5},{5,7},{... | collective-permute-start | bytes 393224 | tf_op jit(solution)/shard_map/ppermute | solution.py:314
  9.1 1.6 %copy-done.11 = f32[2,4,65536]{2,1,0:T(4,128)S(1)} copy-done((f32[2,4,65536]{2,1,0:T(4,128)S(1)}, f32[2,4,65536]{2,1,0:T(4,128)}, u32[]{:S(2)}) %copy-start.11) | copy-done | bytes 2097176
  12.7 1.4 %prepare.1 = (f32[2,4,256,256]{3,2,1,0:T(8,128)S(1)}, f32[2,256,128]{2,1,0:T(8,128)S(1)}, f32[2,2,128,256]{3,2,1,0:T(8,128)S(1)}) custom-call(s32[1]{0:T(128)} %bitcast.1.place_ref, f32[2,2048,128]{2,1,0:T(8,128)S(1)} %bitcast.58, f32[2,256,256]{2,1,0:T(8,128)S(1)} %copy-done.14, bf16[2,256,256]{2,1,0:T(8,128)(2,1)S(1)} %copy-done.17), custom_call_target="tpu_custom_call" | custom-call | tf_op jit(solution)/shard_map/prepare/pallas_call | solution.py:284
  14.8 1.2 %pad_maximum_fusion.near_ref = f32[2,128,256]{2,1,0:T(8,128)S(1)} fusion(f32[1,128,256]{2,1,0:T(8,128)} %bitcast.10, f32[1,128,256]{2,1,0:T(8,128)} %bitcast.9), kind=kLoop, calls=%fused_computation | loop fusion | flops 65536 | bytes 524288 | tf_op jit(solution)/shard_map/stack | solution.py:336
  16.7 1.3 %pad_add_fusion.2 = (s32[2]{0:T(128)S(1)}, s32[2]{0:T(128)S(1)}) fusion(s32[1]{0:T(128)} %bitcast.8, s32[1]{0:T(128)} %bitcast.place_ref, s32[1]{0:T(128)} %bitcast.11), kind=kLoop, calls=%fused_computation.24 | loop fusion | flops 4 | bytes 28 | tf_op jit(solution)/shard_map/stack | solution.py:292
  18.1 4.0 %forward.3 = (f32[4,2,256,256]{3,2,1,0:T(8,128)S(1)}, f32[2,128,256]{2,1,0:T(8,128)}, f32[2,256,256]{2,1,0:T(8,128)S(1)}) custom-call(s32[2]{0:T(128)S(1)} %get-tuple-element.84.place_ref, f32[2,128,256]{2,1,0:T(8,128)S(1)} %copy-done.10, f32[2,128,256]{2,1,0:T(8,128)S(1)} %pad_maximum_fusion.near_ref, f32[2,128,256]{2,1,0:T(8,128)S(1)} %collective-permute-done.2.other_ref, ...), custom_call_target="tpu_custom_call" | custom-call | tf_op jit(solution)/shard_map/forward/pallas_call | solution.py:284
  22.1 1.4 %copy-done.1 = f32[4,2,256,256]{3,2,1,0:T(8,128)} copy-done((f32[4,2,256,256]{3,2,1,0:T(8,128)}, f32[4,2,256,256]{3,2,1,0:T(8,128)S(1)}, u32[]{:S(2)}) %copy-start.1) | copy-done | bytes 2097176
  24.8 4.1 %forward.2 = (f32[4,2,256,256]{3,2,1,0:T(8,128)S(1)}, f32[2,128,256]{2,1,0:T(8,128)}, f32[2,256,256]{2,1,0:T(8,128)S(1)}) custom-call(s32[2]{0:T(128)S(1)} %get-tuple-element.83.place_ref, f32[2,128,256]{2,1,0:T(8,128)S(1)} %copy-done.10, f32[2,128,256]{2,1,0:T(8,128)S(1)} %pad_maximum_fusion.near_ref, f32[2,128,256]{2,1,0:T(8,128)S(1)} %collective-permute-done.2.other_ref, ...), custom_call_target="tpu_custom_call" | custom-call | tf_op jit(solution)/shard_map/forward/pallas_call | solution.py:284
  28.9 1.3 %copy-done.3 = f32[4,2,256,256]{3,2,1,0:T(8,128)} copy-done((f32[4,2,256,256]{3,2,1,0:T(8,128)}, f32[4,2,256,256]{3,2,1,0:T(8,128)S(1)}, u32[]{:S(2)}) %copy-start.3) | copy-done | bytes 2097176
  31.8 1.1 %collective-permute-done.3.refs_7_ = f32[2,128,256]{2,1,0:T(8,128)} collective-permute-done((f32[2,128,256]{2,1,0:T(8,128)}, f32[2,128,256]{2,1,0:T(8,128)}, u32[]{:S(2)}, u32[]{:S(2)}) %collective-permute-start.3) | collective-permute-done | bytes 262176 | tf_op jit(solution)/shard_map/ppermute | solution.py:353
  32.9 1.6 %copy-done.2 = f32[4,2,256,256]{3,2,1,0:T(8,128)S(1)} copy-done((f32[4,2,256,256]{3,2,1,0:T(8,128)S(1)}, f32[4,2,256,256]{3,2,1,0:T(8,128)}, u32[]{:S(2)}) %copy-start.2) | copy-done | bytes 2097176
  34.5 1.6 %copy-done.4 = f32[4,2,256,256]{3,2,1,0:T(8,128)S(1)} copy-done((f32[4,2,256,256]{3,2,1,0:T(8,128)S(1)}, f32[4,2,256,256]{3,2,1,0:T(8,128)}, u32[]{:S(2)}) %copy-start.4) | copy-done | bytes 2097176
  39.3 3.0 %inverse.4 = (f32[2,2,256,256]{3,2,1,0:T(8,128)S(1)}, f32[1,4,2,32,256]{4,3,2,1,0:T(8,128)S(1)}, f32[1,4,2,32,256]{4,3,2,1,0:T(8,128)S(1)}, f32[2,2,128,256]{3,2,1,0:T(8,128)S(1)}) custom-call(s32[3]{0:T(128)S(1)} %pad_add_fusion.4.place_ref, bf16[2,2,2,256,256]{4,3,2,1,0:T(8,128)(2,1)S(1)} %copy-done, f32[2,4,256,256]{3,2,1,0:T(8,128)S(1)} %get-tuple-element.33.probe_ref, ...), custom_call_target="tpu_custom_call" | custom-call | tf_op jit(solution)/shard_map/inverse/pallas_call | solution.py:284
  42.3 2.3 %collective-permute-start.8 = (f32[1,4,2,32,256]{4,3,2,1,0:T(8,128)S(1)}, f32[1,4,2,32,256]{4,3,2,1,0:T(8,128)S(1)}, u32[]{:S(2)}, u32[]{:S(2)}) collective-permute-start(f32[1,4,2,32,256]{4,3,2,1,0:T(8,128)S(1)} %get-tuple-element.51), channel_id=1, source_target_pairs={{0,2},{2,0},{4,6},{6,4},{8,10},{10,8},{12,14},{14,12},{1,3},{3,1},... | collective-permute-start | bytes 786440 | tf_op jit(solution)/shard_map/ppermute | solution.py:389
  44.7 2.1 %inverse.5 = (f32[2,2,256,256]{3,2,1,0:T(8,128)S(1)}, f32[1,4,2,32,256]{4,3,2,1,0:T(8,128)S(1)}, f32[1,4,2,32,256]{4,3,2,1,0:T(8,128)S(1)}) custom-call(s32[2]{0:T(128)S(1)} %pad_add_fusion.1.place_ref, bf16[2,2,2,256,256]{4,3,2,1,0:T(8,128)(2,1)S(1)} %copy-done, ...), custom_call_target="tpu_custom_call", output_to_operand_aliasing={{0}: (7, {})} | custom-call | tf_op jit(solution)/shard_map/inverse/pallas_call | solution.py:284
  47.0 2.1 %inverse.6 = (f32[2,2,256,256]{3,2,1,0:T(8,128)S(1)}, f32[1,4,2,32,256]{4,3,2,1,0:T(8,128)S(1)}, f32[1,4,2,32,256]{4,3,2,1,0:T(8,128)S(1)}) custom-call(s32[2]{0:T(128)S(1)} %pad_add_fusion.1.place_ref, bf16[2,2,2,256,256]{4,3,2,1,0:T(8,128)(2,1)S(1)} %copy-done, ...), custom_call_target="tpu_custom_call", output_to_operand_aliasing={{0}: (7, {})} | custom-call | tf_op jit(solution)/shard_map/inverse/pallas_call | solution.py:284
  49.1 2.3 %inverse.7 = (f32[2,2,256,256]{3,2,1,0:T(8,128)S(1)}, f32[1,4,2,32,256]{4,3,2,1,0:T(8,128)S(1)}, f32[1,4,2,32,256]{4,3,2,1,0:T(8,128)S(1)}) custom-call(s32[2]{0:T(128)S(1)} %pad_add_fusion.1.place_ref, bf16[2,2,2,256,256]{4,3,2,1,0:T(8,128)(2,1)S(1)} %copy-done, ...), custom_call_target="tpu_custom_call", output_to_operand_aliasing={{0}: (7, {})} | custom-call | tf_op jit(solution)/shard_map/inverse/pallas_call | solution.py:284
  51.4 2.0 %collective-permute-start.20 = (f32[1,4,2,32,256]{4,3,2,1,0:T(8,128)S(1)}, f32[1,4,2,32,256]{4,3,2,1,0:T(8,128)S(1)}, u32[]{:S(2)}, u32[]{:S(2)}) collective-permute-start(f32[1,4,2,32,256]{4,3,2,1,0:T(8,128)S(1)} %get-tuple-element.57), channel_id=1, source_target_pairs={{0,2},{2,0},{4,6},{6,4},{8,10},{10,8},{12,14},{14,12},{1,3},{3,1},... | collective-permute-start | bytes 786440 | tf_op jit(solution)/shard_map/ppermute | solution.py:389
  54.8 3.9 %collective-permute-start.11 = (f32[1,2,32,256]{3,2,1,0:T(8,128)S(1)}, f32[1,2,32,256]{3,2,1,0:T(8,128)S(1)}, u32[]{:S(2)}, u32[]{:S(2)}) collective-permute-start(f32[1,2,32,256]{3,2,1,0:T(8,128)S(1)} %get-tuple-element.77), channel_id=1, source_target_pairs={{0,12},{2,14},{4,0},{6,2},{8,4},{10,6},{12,8},{14,10},{1,13},{3,15... | collective-permute-start | bytes 196616 | tf_op jit(solution)/shard_map/ppermute | solution.py:393
  58.7 1.3 %collective-permute-start.10 = (f32[1,2,32,256]{3,2,1,0:T(8,128)S(1)}, f32[1,2,32,256]{3,2,1,0:T(8,128)S(1)}, u32[]{:S(2)}, u32[]{:S(2)}) collective-permute-start(f32[1,2,32,256]{3,2,1,0:T(8,128)S(1)} %get-tuple-element.78), channel_id=1, source_target_pairs={{0,8},{2,10},{4,12},{6,14},{8,0},{10,2},{12,4},{14,6},{1,9},{3,11}... | collective-permute-start | bytes 196616 | tf_op jit(solution)/shard_map/ppermute | solution.py:393
  60.0 3.0 %collective-permute-done.20 = f32[1,4,2,32,256]{4,3,2,1,0:T(8,128)S(1)} collective-permute-done((f32[1,4,2,32,256]{4,3,2,1,0:T(8,128)S(1)}, f32[1,4,2,32,256]{4,3,2,1,0:T(8,128)S(1)}, u32[]{:S(2)}, u32[]{:S(2)}) %collective-permute-start.20) | collective-permute-done | bytes 262176 | tf_op jit(solution)/shard_map/ppermute | solution.py:389
  63.0 1.6 %collective-permute-start.9 = (f32[1,2,32,256]{3,2,1,0:T(8,128)S(1)}, f32[1,2,32,256]{3,2,1,0:T(8,128)S(1)}, u32[]{:S(2)}, u32[]{:S(2)}) collective-permute-start(f32[1,2,32,256]{3,2,1,0:T(8,128)S(1)} %get-tuple-element.79), channel_id=1, source_target_pairs={{0,4},{2,6},{4,8},{6,10},{8,12},{10,14},{12,0},{14,2},{1,5},{3,7},... | collective-permute-start | bytes 196616 | tf_op jit(solution)/shard_map/ppermute | solution.py:393
  64.6 3.5 %collective-permute-done.16 = f32[1,4,2,32,256]{4,3,2,1,0:T(8,128)S(1)} collective-permute-done((f32[1,4,2,32,256]{4,3,2,1,0:T(8,128)S(1)}, f32[1,4,2,32,256]{4,3,2,1,0:T(8,128)S(1)}, u32[]{:S(2)}, u32[]{:S(2)}) %collective-permute-start.16) | collective-permute-done | bytes 262176 | tf_op jit(solution)/shard_map/ppermute | solution.py:389
  68.1 3.6 %collective-permute-start.15 = (f32[1,2,32,256]{3,2,1,0:T(8,128)S(1)}, f32[1,2,32,256]{3,2,1,0:T(8,128)S(1)}, u32[]{:S(2)}, u32[]{:S(2)}) collective-permute-start(f32[1,2,32,256]{3,2,1,0:T(8,128)S(1)} %get-tuple-element.73), channel_id=1, source_target_pairs={{0,12},{2,14},{4,0},{6,2},{8,4},{10,6},{12,8},{14,10},{1,13},{3,15... | collective-permute-start | bytes 196616 | tf_op jit(solution)/shard_map/ppermute | solution.py:393
  73.0 2.9 %collective-permute-start.23 = (f32[1,2,32,256]{3,2,1,0:T(8,128)S(1)}, f32[1,2,32,256]{3,2,1,0:T(8,128)S(1)}, u32[]{:S(2)}, u32[]{:S(2)}) collective-permute-start(f32[1,2,32,256]{3,2,1,0:T(8,128)S(1)} %get-tuple-element.65), channel_id=1, source_target_pairs={{0,12},{2,14},{4,0},{6,2},{8,4},{10,6},{12,8},{14,10},{1,13},{3,15... | collective-permute-start | bytes 196616 | tf_op jit(solution)/shard_map/ppermute | solution.py:393
  77.0 2.1 %collective-permute-done.14.refs_6_ = f32[1,2,32,256]{3,2,1,0:T(8,128)S(1)} collective-permute-done((f32[1,2,32,256]{3,2,1,0:T(8,128)S(1)}, f32[1,2,32,256]{3,2,1,0:T(8,128)S(1)}, u32[]{:S(2)}, u32[]{:S(2)}) %collective-permute-start.14) | collective-permute-done | bytes 65568 | tf_op jit(solution)/shard_map/ppermute | solution.py:393
  79.1 4.8 %collective-permute-start.7 = (f32[2,64,256]{2,1,0:T(8,128)S(1)}, f32[2,64,256]{2,1,0:T(8,128)S(1)}, u32[]{:S(2)}, u32[]{:S(2)}) collective-permute-start(f32[2,64,256]{2,1,0:T(8,128)S(1)} %get-tuple-element.62), channel_id=1, source_target_pairs={{0,2},{2,4},{4,6},{6,8},{8,10},{10,12},{12,14},{1,3},{3,5},{5,7},{... | collective-permute-start | bytes 393224 | tf_op jit(solution)/shard_map/ppermute | solution.py:411
  83.9 1.3 %collective-permute-start.6 = (f32[2,64,256]{2,1,0:T(8,128)S(1)}, f32[2,64,256]{2,1,0:T(8,128)S(1)}, u32[]{:S(2)}, u32[]{:S(2)}) collective-permute-start(f32[2,64,256]{2,1,0:T(8,128)S(1)} %get-tuple-element.63), channel_id=1, source_target_pairs={{2,0},{4,2},{6,4},{8,6},{10,8},{12,10},{14,12},{3,1},{5,3},{7,5},{... | collective-permute-start | bytes 393224 | tf_op jit(solution)/shard_map/ppermute | solution.py:410
  85.3 2.7 %collective-permute-start.19 = (f32[1,2,32,256]{3,2,1,0:T(8,128)S(1)}, f32[1,2,32,256]{3,2,1,0:T(8,128)S(1)}, u32[]{:S(2)}, u32[]{:S(2)}) collective-permute-start(f32[1,2,32,256]{3,2,1,0:T(8,128)S(1)} %get-tuple-element.69), channel_id=1, source_target_pairs={{0,12},{2,14},{4,0},{6,2},{8,4},{10,6},{12,8},{14,10},{1,13},{3,15... | collective-permute-start | bytes 196616 | tf_op jit(solution)/shard_map/ppermute | solution.py:393
  88.9 3.2 %collective-permute-done.19.refs_11_ = f32[1,2,32,256]{3,2,1,0:T(8,128)S(1)} collective-permute-done((f32[1,2,32,256]{3,2,1,0:T(8,128)S(1)}, f32[1,2,32,256]{3,2,1,0:T(8,128)S(1)}, u32[]{:S(2)}, u32[]{:S(2)}) %collective-permute-start.19) | collective-permute-done | bytes 65568 | tf_op jit(solution)/shard_map/ppermute | solution.py:393
  93.2 1.8 %collective-permute-done.17.refs_9_ = f32[1,2,32,256]{3,2,1,0:T(8,128)S(1)} collective-permute-done((f32[1,2,32,256]{3,2,1,0:T(8,128)S(1)}, f32[1,2,32,256]{3,2,1,0:T(8,128)S(1)}, u32[]{:S(2)}, u32[]{:S(2)}) %collective-permute-start.17) | collective-permute-done | bytes 65568 | tf_op jit(solution)/shard_map/ppermute | solution.py:393
  (81 shorter events, 16.7 us)
Async XLA Ops:
  0.6 17.5 %copy-start = (bf16[2,2,2,256,256]{4,3,2,1,0:T(8,128)(2,1)S(1)}, bf16[2,2,2,256,256]{4,3,2,1,0:T(8,128)(2,1)}, u32[]{:S(2)}) copy-start(bf16[2,2,2,256,256]{4,3,2,1,0:T(8,128)(2,1)} %constant.44.clone.table_ref) | copy-start | bytes 3145732
  0.6 17.5 %copy-start.10 = (f32[2,128,256]{2,1,0:T(8,128)S(1)}, f32[2,128,256]{2,1,0:T(8,128)}, u32[]{:S(2)}) copy-start(f32[2,128,256]{2,1,0:T(8,128)} %strip_ref.1) | copy-start | bytes 786436
  1.7 13.1 %collective-permute-start.1 = (f32[128,256]{1,0:T(8,128)S(1)}, f32[128,256]{1,0:T(8,128)}, u32[]{:S(2)}, u32[]{:S(2)}) collective-permute-start(f32[128,256]{1,0:T(8,128)S(1)} %dynamic-slice_bitcast_fusion), channel_id=1, source_target_pairs={{2,0},{4,2},{6,4},{8,6},{10,8},{12,10},{14,12},{3,1},{5,3},{7,5},{... | collective-permute-start | bytes 393224 | tf_op jit(solution)/shard_map/ppermute | solution.py:315
  3.0 11.8 %collective-permute-start = (f32[128,256]{1,0:T(8,128)S(1)}, f32[128,256]{1,0:T(8,128)}, u32[]{:S(2)}, u32[]{:S(2)}) collective-permute-start(f32[128,256]{1,0:T(8,128)S(1)} %dynamic-slice_bitcast_fusion), channel_id=1, source_target_pairs={{0,2},{2,4},{4,6},{6,8},{8,10},{10,12},{12,14},{1,3},{3,5},{5,7},{... | collective-permute-start | bytes 393224 | tf_op jit(solution)/shard_map/ppermute | solution.py:314
  9.1 1.6 %copy-start.11 = (f32[2,4,65536]{2,1,0:T(4,128)S(1)}, f32[2,4,65536]{2,1,0:T(4,128)}, u32[]{:S(2)}) copy-start(f32[2,4,65536]{2,1,0:T(4,128)} %param.8) | copy-start | bytes 6291460
  12.7 3.3 %copy-start.18 = (s32[2,2]{1,0:T(2,128)S(1)}, s32[2,2]{1,0:T(2,128)}, u32[]{:S(2)}) copy-start(s32[2,2]{1,0:T(2,128)} %param.10) | copy-start | bytes 52
  14.8 3.3 %copy-start.12 = (f32[2,2,128,256]{3,2,1,0:T(8,128)}, f32[2,2,128,256]{3,2,1,0:T(8,128)S(1)}, u32[]{:S(2)}) copy-start(f32[2,2,128,256]{3,2,1,0:T(8,128)S(1)} %get-tuple-element.40.refs_4_) | copy-start | bytes 1572868
  15.9 2.1 %collective-permute-start.2 = (f32[2,128,256]{2,1,0:T(8,128)S(1)}, f32[2,128,256]{2,1,0:T(8,128)S(1)}, u32[]{:S(2)}, u32[]{:S(2)}) collective-permute-start(f32[2,128,256]{2,1,0:T(8,128)S(1)} %pad_maximum_fusion.near_ref), channel_id=1, source_target_pairs={{0,1},{1,0},{2,3},{3,2},{4,5},{5,4},{6,7},{7,6},{8,9},{9,8},{10,11... | collective-permute-start | bytes 786440 | tf_op jit(solution)/shard_map/ppermute | solution.py:337
  24.3 7.5 %collective-permute-start.4 = (f32[2,128,256]{2,1,0:T(8,128)}, f32[2,128,256]{2,1,0:T(8,128)}, u32[]{:S(2)}, u32[]{:S(2)}) collective-permute-start(f32[2,128,256]{2,1,0:T(8,128)} %get-tuple-element.42.refs_6_), channel_id=1, source_target_pairs={{0,1},{1,0},{2,3},{3,2},{4,5},{5,4},{6,7},{7,6},{8,9},{9,8},{10,11... | collective-permute-start | bytes 786440 | tf_op jit(solution)/shard_map/ppermute | solution.py:353
  31.1 1.9 %collective-permute-start.3 = (f32[2,128,256]{2,1,0:T(8,128)}, f32[2,128,256]{2,1,0:T(8,128)}, u32[]{:S(2)}, u32[]{:S(2)}) collective-permute-start(f32[2,128,256]{2,1,0:T(8,128)} %get-tuple-element.41.refs_5_), channel_id=1, source_target_pairs={{0,1},{1,0},{2,3},{3,2},{4,5},{5,4},{6,7},{7,6},{8,9},{9,8},{10,11... | collective-permute-start | bytes 786440 | tf_op jit(solution)/shard_map/ppermute | solution.py:353
  32.9 1.6 %copy-start.2 = (f32[4,2,256,256]{3,2,1,0:T(8,128)S(1)}, f32[4,2,256,256]{3,2,1,0:T(8,128)}, u32[]{:S(2)}) copy-start(f32[4,2,256,256]{3,2,1,0:T(8,128)} %copy-done.1) | copy-start | bytes 6291460
  39.3 5.5 %copy-start.5 = (f32[4,2,256,256]{3,2,1,0:T(8,128)S(1)}, f32[4,2,256,256]{3,2,1,0:T(8,128)}, u32[]{:S(2)}) copy-start(f32[4,2,256,256]{3,2,1,0:T(8,128)} %copy-done.3) | copy-start | bytes 6291460
  42.3 12.4 %collective-permute-start.8 = (f32[1,4,2,32,256]{4,3,2,1,0:T(8,128)S(1)}, f32[1,4,2,32,256]{4,3,2,1,0:T(8,128)S(1)}, u32[]{:S(2)}, u32[]{:S(2)}) collective-permute-start(f32[1,4,2,32,256]{4,3,2,1,0:T(8,128)S(1)} %get-tuple-element.51), channel_id=1, source_target_pairs={{0,2},{2,0},{4,6},{6,4},{8,10},{10,8},{12,14},{14,12},{1,3},{3,1},... | collective-permute-start | bytes 786440 | tf_op jit(solution)/shard_map/ppermute | solution.py:389
  46.8 11.8 %collective-permute-start.12 = (f32[1,4,2,32,256]{4,3,2,1,0:T(8,128)S(1)}, f32[1,4,2,32,256]{4,3,2,1,0:T(8,128)S(1)}, u32[]{:S(2)}, u32[]{:S(2)}) collective-permute-start(f32[1,4,2,32,256]{4,3,2,1,0:T(8,128)S(1)} %get-tuple-element.53), channel_id=1, source_target_pairs={{0,2},{2,0},{4,6},{6,4},{8,10},{10,8},{12,14},{14,12},{1,3},{3,1},... | collective-permute-start | bytes 786440 | tf_op jit(solution)/shard_map/ppermute | solution.py:389
  51.4 11.6 %collective-permute-start.20 = (f32[1,4,2,32,256]{4,3,2,1,0:T(8,128)S(1)}, f32[1,4,2,32,256]{4,3,2,1,0:T(8,128)S(1)}, u32[]{:S(2)}, u32[]{:S(2)}) collective-permute-start(f32[1,4,2,32,256]{4,3,2,1,0:T(8,128)S(1)} %get-tuple-element.57), channel_id=1, source_target_pairs={{0,2},{2,0},{4,6},{6,4},{8,10},{10,8},{12,14},{14,12},{1,3},{3,1},... | collective-permute-start | bytes 786440 | tf_op jit(solution)/shard_map/ppermute | solution.py:389
  53.4 14.6 %collective-permute-start.16 = (f32[1,4,2,32,256]{4,3,2,1,0:T(8,128)S(1)}, f32[1,4,2,32,256]{4,3,2,1,0:T(8,128)S(1)}, u32[]{:S(2)}, u32[]{:S(2)}) collective-permute-start(f32[1,4,2,32,256]{4,3,2,1,0:T(8,128)S(1)} %get-tuple-element.55), channel_id=1, source_target_pairs={{0,2},{2,0},{4,6},{6,4},{8,10},{10,8},{12,14},{14,12},{1,3},{3,1},... | collective-permute-start | bytes 786440 | tf_op jit(solution)/shard_map/ppermute | solution.py:389
  54.6 17.1 %collective-permute-start.5 = (f32[3,2,64,256]{3,2,1,0:T(8,128)S(1)}, f32[3,2,64,256]{3,2,1,0:T(8,128)S(1)}, u32[]{:S(2)}, u32[]{:S(2)}) collective-permute-start(f32[3,2,64,256]{3,2,1,0:T(8,128)S(1)} %get-tuple-element.49), channel_id=1, source_target_pairs={{0,1},{1,0},{2,3},{3,2},{4,5},{5,4},{6,7},{7,6},{8,9},{9,8},{10,11... | collective-permute-start | bytes 1179656 | tf_op jit(solution)/shard_map/ppermute | solution.py:409
  54.8 17.1 %collective-permute-start.11 = (f32[1,2,32,256]{3,2,1,0:T(8,128)S(1)}, f32[1,2,32,256]{3,2,1,0:T(8,128)S(1)}, u32[]{:S(2)}, u32[]{:S(2)}) collective-permute-start(f32[1,2,32,256]{3,2,1,0:T(8,128)S(1)} %get-tuple-element.77), channel_id=1, source_target_pairs={{0,12},{2,14},{4,0},{6,2},{8,4},{10,6},{12,8},{14,10},{1,13},{3,15... | collective-permute-start | bytes 196616 | tf_op jit(solution)/shard_map/ppermute | solution.py:393
  58.7 14.3 %collective-permute-start.10 = (f32[1,2,32,256]{3,2,1,0:T(8,128)S(1)}, f32[1,2,32,256]{3,2,1,0:T(8,128)S(1)}, u32[]{:S(2)}, u32[]{:S(2)}) collective-permute-start(f32[1,2,32,256]{3,2,1,0:T(8,128)S(1)} %get-tuple-element.78), channel_id=1, source_target_pairs={{0,8},{2,10},{4,12},{6,14},{8,0},{10,2},{12,4},{14,6},{1,9},{3,11}... | collective-permute-start | bytes 196616 | tf_op jit(solution)/shard_map/ppermute | solution.py:393
  63.0 12.9 %collective-permute-start.9 = (f32[1,2,32,256]{3,2,1,0:T(8,128)S(1)}, f32[1,2,32,256]{3,2,1,0:T(8,128)S(1)}, u32[]{:S(2)}, u32[]{:S(2)}) collective-permute-start(f32[1,2,32,256]{3,2,1,0:T(8,128)S(1)} %get-tuple-element.79), channel_id=1, source_target_pairs={{0,4},{2,6},{4,8},{6,10},{8,12},{10,14},{12,0},{14,2},{1,5},{3,7},... | collective-permute-start | bytes 196616 | tf_op jit(solution)/shard_map/ppermute | solution.py:393
  64.6 30.4 %copy-start.16 = (f32[2,256,128]{2,1,0:T(8,128)S(1)}, f32[2,256,128]{2,1,0:T(8,128)}, u32[]{:S(2)}) copy-start(f32[2,256,128]{2,1,0:T(8,128)} %copy-done.15) | copy-start | bytes 786436
  68.1 8.9 %collective-permute-start.15 = (f32[1,2,32,256]{3,2,1,0:T(8,128)S(1)}, f32[1,2,32,256]{3,2,1,0:T(8,128)S(1)}, u32[]{:S(2)}, u32[]{:S(2)}) collective-permute-start(f32[1,2,32,256]{3,2,1,0:T(8,128)S(1)} %get-tuple-element.73), channel_id=1, source_target_pairs={{0,12},{2,14},{4,0},{6,2},{8,4},{10,6},{12,8},{14,10},{1,13},{3,15... | collective-permute-start | bytes 196616 | tf_op jit(solution)/shard_map/ppermute | solution.py:393
  71.7 7.4 %collective-permute-start.14 = (f32[1,2,32,256]{3,2,1,0:T(8,128)S(1)}, f32[1,2,32,256]{3,2,1,0:T(8,128)S(1)}, u32[]{:S(2)}, u32[]{:S(2)}) collective-permute-start(f32[1,2,32,256]{3,2,1,0:T(8,128)S(1)} %get-tuple-element.74), channel_id=1, source_target_pairs={{0,8},{2,10},{4,12},{6,14},{8,0},{10,2},{12,4},{14,6},{1,9},{3,11}... | collective-permute-start | bytes 196616 | tf_op jit(solution)/shard_map/ppermute | solution.py:393
  71.9 12.0 %collective-permute-start.13 = (f32[1,2,32,256]{3,2,1,0:T(8,128)S(1)}, f32[1,2,32,256]{3,2,1,0:T(8,128)S(1)}, u32[]{:S(2)}, u32[]{:S(2)}) collective-permute-start(f32[1,2,32,256]{3,2,1,0:T(8,128)S(1)} %get-tuple-element.75), channel_id=1, source_target_pairs={{0,4},{2,6},{4,8},{6,10},{8,12},{10,14},{12,0},{14,2},{1,5},{3,7},... | collective-permute-start | bytes 196616 | tf_op jit(solution)/shard_map/ppermute | solution.py:393
  73.0 12.3 %collective-permute-start.23 = (f32[1,2,32,256]{3,2,1,0:T(8,128)S(1)}, f32[1,2,32,256]{3,2,1,0:T(8,128)S(1)}, u32[]{:S(2)}, u32[]{:S(2)}) collective-permute-start(f32[1,2,32,256]{3,2,1,0:T(8,128)S(1)} %get-tuple-element.65), channel_id=1, source_target_pairs={{0,12},{2,14},{4,0},{6,2},{8,4},{10,6},{12,8},{14,10},{1,13},{3,15... | collective-permute-start | bytes 196616 | tf_op jit(solution)/shard_map/ppermute | solution.py:393
  75.9 12.1 %collective-permute-start.22 = (f32[1,2,32,256]{3,2,1,0:T(8,128)S(1)}, f32[1,2,32,256]{3,2,1,0:T(8,128)S(1)}, u32[]{:S(2)}, u32[]{:S(2)}) collective-permute-start(f32[1,2,32,256]{3,2,1,0:T(8,128)S(1)} %get-tuple-element.66), channel_id=1, source_target_pairs={{0,8},{2,10},{4,12},{6,14},{8,0},{10,2},{12,4},{14,6},{1,9},{3,11}... | collective-permute-start | bytes 196616 | tf_op jit(solution)/shard_map/ppermute | solution.py:393
  77.0 11.9 %collective-permute-start.21 = (f32[1,2,32,256]{3,2,1,0:T(8,128)S(1)}, f32[1,2,32,256]{3,2,1,0:T(8,128)S(1)}, u32[]{:S(2)}, u32[]{:S(2)}) collective-permute-start(f32[1,2,32,256]{3,2,1,0:T(8,128)S(1)} %get-tuple-element.67), channel_id=1, source_target_pairs={{0,4},{2,6},{4,8},{6,10},{8,12},{10,14},{12,0},{14,2},{1,5},{3,7},... | collective-permute-start | bytes 196616 | tf_op jit(solution)/shard_map/ppermute | solution.py:393
  79.1 15.8 %collective-permute-start.7 = (f32[2,64,256]{2,1,0:T(8,128)S(1)}, f32[2,64,256]{2,1,0:T(8,128)S(1)}, u32[]{:S(2)}, u32[]{:S(2)}) collective-permute-start(f32[2,64,256]{2,1,0:T(8,128)S(1)} %get-tuple-element.62), channel_id=1, source_target_pairs={{0,2},{2,4},{4,6},{6,8},{8,10},{10,12},{12,14},{1,3},{3,5},{5,7},{... | collective-permute-start | bytes 393224 | tf_op jit(solution)/shard_map/ppermute | solution.py:411
  83.9 11.0 %collective-permute-start.6 = (f32[2,64,256]{2,1,0:T(8,128)S(1)}, f32[2,64,256]{2,1,0:T(8,128)S(1)}, u32[]{:S(2)}, u32[]{:S(2)}) collective-permute-start(f32[2,64,256]{2,1,0:T(8,128)S(1)} %get-tuple-element.63), channel_id=1, source_target_pairs={{2,0},{4,2},{6,4},{8,6},{10,8},{12,10},{14,12},{3,1},{5,3},{7,5},{... | collective-permute-start | bytes 393224 | tf_op jit(solution)/shard_map/ppermute | solution.py:410
  85.3 6.8 %collective-permute-start.19 = (f32[1,2,32,256]{3,2,1,0:T(8,128)S(1)}, f32[1,2,32,256]{3,2,1,0:T(8,128)S(1)}, u32[]{:S(2)}, u32[]{:S(2)}) collective-permute-start(f32[1,2,32,256]{3,2,1,0:T(8,128)S(1)} %get-tuple-element.69), channel_id=1, source_target_pairs={{0,12},{2,14},{4,0},{6,2},{8,4},{10,6},{12,8},{14,10},{1,13},{3,15... | collective-permute-start | bytes 196616 | tf_op jit(solution)/shard_map/ppermute | solution.py:393
  88.0 5.2 %collective-permute-start.18 = (f32[1,2,32,256]{3,2,1,0:T(8,128)S(1)}, f32[1,2,32,256]{3,2,1,0:T(8,128)S(1)}, u32[]{:S(2)}, u32[]{:S(2)}) collective-permute-start(f32[1,2,32,256]{3,2,1,0:T(8,128)S(1)} %get-tuple-element.70), channel_id=1, source_target_pairs={{0,8},{2,10},{4,12},{6,14},{8,0},{10,2},{12,4},{14,6},{1,9},{3,11}... | collective-permute-start | bytes 196616 | tf_op jit(solution)/shard_map/ppermute | solution.py:393
  88.9 6.1 %collective-permute-start.17 = (f32[1,2,32,256]{3,2,1,0:T(8,128)S(1)}, f32[1,2,32,256]{3,2,1,0:T(8,128)S(1)}, u32[]{:S(2)}, u32[]{:S(2)}) collective-permute-start(f32[1,2,32,256]{3,2,1,0:T(8,128)S(1)} %get-tuple-element.71), channel_id=1, source_target_pairs={{0,4},{2,6},{4,8},{6,10},{8,12},{10,14},{12,0},{14,2},{1,5},{3,7},... | collective-permute-start | bytes 196616 | tf_op jit(solution)/shard_map/ppermute | solution.py:393
  (11 other events, 11.7 us)

commit v3 on v2

v3 whole, which is shorter than its diff:
```python
import functools
import math

import jax
import jax.numpy as jnp
import ml_dtypes
import numpy as np
from jax import lax
from jax.experimental import pallas as pl
from jax.experimental.pallas import tpu as pltpu
from jax.sharding import PartitionSpec as P

damping_factor = 0.1
object_step = 0.5
probe_step = 0.05

F32 = jnp.float32
BF16 = jnp.bfloat16
VMEM_LIMIT = 16 * 1024 * 1024
COSTS = {'prepare': 2000000000, 'forward': 4000000000, 'inverse': 2400000000, 'strips': 1200000000, 'finish': 1000000000, 'order': 1000000000}
CHUNK = 64
TIE = None
GROUPS = ((1, (1, 0, 2)), (1, (0, 1, 2)), (1, (1, 0, 2)), (1, (0, 1, 2)))


def real_tables(size):
    half = size // 2
    counter = np.arange(half)
    phase = np.outer(counter, counter) % half
    even = np.exp(-2j * np.pi * phase / half) / math.sqrt(size)
    odd = even * np.exp(-2j * np.pi * counter / size)[:, None]
    right, left = [], []
    for matrix in (even, odd):
        real = np.block([[matrix.real, matrix.imag], [-matrix.imag, matrix.real]])
        for form in (real, real.T):
            high = form.astype(ml_dtypes.bfloat16)
            low = (form - high.astype(np.float64)).astype(ml_dtypes.bfloat16)
            right.append(np.concatenate([high, high, low], 0))
            left.append(np.concatenate([high, high, low], 1))
    return np.stack(right), np.stack(left)


def split(value):
    high = value.astype(BF16)
    return high, (value - high.astype(F32)).astype(BF16)


def product(left, right):
    return jnp.dot(left, right, preferred_element_type=F32)


def put_left(ref, parity, begin, value):
    size = value.shape[1]
    lines = slice(begin, begin + value.shape[0])
    high, low = split(value)
    ref[parity, lines, :size] = high
    ref[parity, lines, size : 2 * size] = low
    ref[parity, lines, 2 * size :] = high


def put_right(ref, parity, begin, value):
    size = value.shape[1]
    high, low = split(value)
    for index, piece in enumerate((high, low, high)):
        ref[parity, index * size + begin : index * size + begin + value.shape[0]] = piece


def spans(size, count):
    return [(begin, slice(begin, begin + count)) for begin in range(0, size, count)]


def pieces_of(value):
    high, middle = split(value)
    low = (value - high.astype(F32) - middle.astype(F32)).astype(BF16)
    return high, middle, low


def prepare_kernel(probe_ref, grid_ref, own_ref):
    parts, modes, size, columns = grid_ref.shape
    lines = columns // 128
    for part in range(parts):
        for mode in range(modes):
            for line in range(lines):
                grid_ref[part, mode, :, line * 128 : (line + 1) * 128] = probe_ref[
                    part, pl.ds(line * modes + mode, size, stride=lines * modes), :
                ]
    share = own_ref.shape[1]
    own_ref[...] = probe_ref[:, pl.ds(pl.multiple_of(lax.axis_index("pos") * share, share), share), :]


def order_kernel(measured_ref, order_ref, out_ref):
    half = order_ref.shape[1] // 2
    columns, rows = order_ref[0], order_ref[1]
    for slot in range(measured_ref.shape[0]):
        value = jnp.sqrt(measured_ref[slot] + damping_factor)
        value = sum(product(piece, columns) for piece in pieces_of(value))
        value = sum(product(rows, piece) for piece in pieces_of(value))
        out_ref[slot, 0] = value[:half]
        out_ref[slot, 1] = value[half:]


def load_rows(ref, index, begin, count):
    offset = lax.rem(begin, 8)
    span = count + 8
    value = ref[(*index, pl.ds(pl.multiple_of(begin - offset, 8), span))]
    return pltpu.roll(value, lax.rem(span - offset, span), 0)[:count]


def forward_kernel(
    slot, offset_ref, own_ref, pair_ref, next_ref, pair_other_ref, next_other_ref,
    probe_ref, row_ref, col_ref, far_ref, power_ref, patch_ref, extended, left_ref, right_ref,
    middle_ref,
):
    rows = own_ref.shape[1]
    size = patch_ref.shape[1]
    position, tile = lax.axis_index("pos"), lax.axis_index("tile")
    parity = lax.rem(position, 2)
    start = offset_ref[slot, 0] - (position - 1) * rows
    extended[:, rows : 2 * rows] = own_ref[...]
    for side, mine, other in (
        (1 - parity, pair_ref, pair_other_ref),
        (parity, next_ref, next_other_ref),
    ):
        lines = pl.ds(pl.multiple_of(side * (2 * rows), rows), rows)
        extended[tile, lines] = mine[...]
        extended[1 - tile, lines] = other[...]
    for part in (0, 1):
        patch_ref[part] = load_rows(extended, (part,), start, size)
    half = size // 2
    for mode in range(probe_ref.shape[1]):
        for begin, lines in spans(size, CHUNK):
            patch_real, patch_imag = patch_ref[0, lines], patch_ref[1, lines]
            probe_real, probe_imag = probe_ref[0, mode, lines], probe_ref[1, mode, lines]
            real = probe_real * patch_real - probe_imag * patch_imag
            imag = probe_real * patch_imag + probe_imag * patch_real
            a, b = real[:, :half], real[:, half:]
            c, d = imag[:, :half], imag[:, half:]
            put_left(left_ref, 0, begin, jnp.concatenate([a + b, c + d], 1))
            put_left(left_ref, 1, begin, jnp.concatenate([a - b, c - d], 1))
        for parity in (0, 1):
            middle_ref[parity] = product(left_ref[parity], row_ref[2 * parity])
        for begin, lines in spans(half, CHUNK // 2):
            under = slice(half + begin, half + begin + CHUNK // 2)
            for part in (0, 1):
                where = slice(part * half, (part + 1) * half)
                top = jnp.concatenate([middle_ref[0, lines, where], middle_ref[1, lines, where]], 1)
                low = jnp.concatenate([middle_ref[0, under, where], middle_ref[1, under, where]], 1)
                put_right(right_ref, 0, part * half + begin, top + low)
                put_right(right_ref, 1, part * half + begin, top - low)
        for parity in (0, 1):
            far_ref[mode, parity] = product(col_ref[2 * parity + 1], right_ref[parity])
            for begin, lines in spans(half, CHUNK):
                under = slice(half + begin, half + begin + CHUNK)
                real, imag = far_ref[mode, parity, lines], far_ref[mode, parity, under]
                power = real * real + imag * imag
                if mode == 0:
                    power_ref[parity, lines] = power
                else:
                    power_ref[parity, lines] += power


def block_index(block, position, bits):
    index = 0
    for bit in bits:
        differs = lax.rem(lax.div(position, 2**bit) + (block >> bit) % 2, 2)
        index = 2 * index + differs
    return index


def inverse_kernel(modes, bits, first, slots, *refs):
    if first:
        count_ref, *refs = refs
    row_ref, col_ref, probe_ref, *refs = refs
    *refs, left_ref, right_ref, middle_ref = refs
    far_refs, patch_refs = refs[:slots], refs[slots : 2 * slots]
    refs = refs[2 * slots :]
    if first:
        amplitude_ref, power_refs = refs[0], refs[1 : 1 + slots]
        other_refs = refs[1 + slots : 1 + 2 * slots]
        grad_ref, block_ref, ratio_ref = refs[1 + 2 * slots :]
        for slot in range(slots):
            model = jnp.sqrt(power_refs[slot][...] + other_refs[slot][...] + damping_factor)
            active = (slot < count_ref[0]).astype(F32)
            ratio_ref[slot] = (amplitude_ref[slot] / model - 1.0) * active
    else:
        _, ratio_ref, grad_ref, block_ref = refs
    size = probe_ref.shape[2]
    blocks, rows = block_ref.shape[0], block_ref.shape[3]
    half = size // 2
    position = lax.axis_index("pos")
    for index, mode in enumerate(modes):
        for slot in range(slots):
            for begin, lines in spans(half, CHUNK // 2):
                under = slice(half + begin, half + begin + CHUNK // 2)
                for parity in (0, 1):
                    ratio = ratio_ref[slot, parity, lines]
                    far = far_refs[slot].at[mode, parity]
                    put_right(right_ref, parity, begin, far[lines] * ratio)
                    put_right(right_ref, parity, half + begin, far[under] * ratio)
            for parity in (0, 1):
                middle_ref[parity] = product(col_ref[2 * parity], right_ref[parity])
            for begin, lines in spans(half, CHUNK // 2):
                under = slice(half + begin, half + begin + CHUNK // 2)
                for offset, sign in ((0, 1.0), (half, -1.0)):
                    real = middle_ref[0, lines] + sign * middle_ref[1, lines]
                    imag = middle_ref[0, under] + sign * middle_ref[1, under]
                    for parity in (0, 1):
                        where = slice(parity * half, (parity + 1) * half)
                        value = jnp.concatenate([real[:, where], imag[:, where]], 1)
                        put_left(left_ref, parity, offset + begin, value)
            for parity in (0, 1):
                middle_ref[parity] = product(left_ref[parity], row_ref[2 * parity + 1])
            for begin, lines in spans(size, rows):
                target = block_index(begin // rows, position, bits)
                a, b = middle_ref[0, lines], middle_ref[1, lines]
                plus, minus = a + b, a - b
                real = jnp.concatenate([plus[:, :half], minus[:, :half]], 1)
                imag = jnp.concatenate([plus[:, half:], minus[:, half:]], 1)
                probe_real, probe_imag = probe_ref[0, mode, lines], probe_ref[1, mode, lines]
                patch_real, patch_imag = patch_refs[slot][0, lines], patch_refs[slot][1, lines]
                grads = (
                    probe_real * real + probe_imag * imag,
                    probe_real * imag - probe_imag * real,
                )
                terms = (
                    patch_real * real + patch_imag * imag,
                    patch_real * imag - patch_imag * real,
                )
                for part in (0, 1):
                    if first and index == 0:
                        grad_ref[slot, part, lines] = grads[part]
                    else:
                        grad_ref[slot, part, lines] += grads[part]
                    if slot == 0:
                        block_ref[target, index, part] = terms[part]
                    else:
                        block_ref[target, index, part] += terms[part]


def strip_kernel(offset_ref, grad_ref, keep_ref, send_ref, spread):
    slots, _, size, _ = grad_ref.shape
    rows = size // 2
    position, tile = lax.axis_index("pos"), lax.axis_index("tile")
    parity = lax.rem(position, 2)
    half = rows // 2
    spread[:, :, :rows] = jnp.zeros(spread.shape[:2] + (rows, size), F32)
    spread[:, :, rows + size :] = jnp.zeros(spread.shape[:2] + (rows + 8, size), F32)
    spread[:, :, rows : rows + size] = grad_ref[...]
    for place, strip in enumerate((2 * (1 - parity), 2 * parity, 1)):
        for part in (0, 1):
            for ref, which in ((keep_ref, tile), (send_ref, 1 - tile)):
                total = None
                for slot in range(slots):
                    start = offset_ref[slot, 0] - (position - 1) * rows
                    begin = rows - start + strip * rows + which * half
                    value = load_rows(spread, (slot, part), begin, half)
                    total = value if total is None else total + value
                ref[place, part] = total


def finish_kernel(counts, probe_ref, strip_ref, mid_ref, pair_ref, next_ref, *refs):
    object_ref, out_ref = refs[-2:]
    half = object_ref.shape[1]
    begin = pl.multiple_of(lax.axis_index("tile") * half, half)
    object_ref[...] = strip_ref[:, pl.ds(begin, half), :] + object_step * (
        mid_ref[...] + pair_ref[...] + next_ref[...]
    )
    modes = sum(group for group, _ in counts)
    mode = 0
    for group, terms in counts:
        group_refs, refs = refs[:terms], refs[terms:]
        for index in range(group):
            for part in range(out_ref.shape[0]):
                value = sum(ref[index, part] for ref in group_refs)
                rows, columns = value.shape
                lines = columns // 128
                for line in range(lines):
                    where = pl.ds(line * modes + mode, rows, stride=lines * modes)
                    out_ref[part, where, :] = probe_ref[part, where, :] + probe_step * (
                        value[:, line * 128 : (line + 1) * 128]
                    )
            mode += 1


def call(kernel, out_shape, scalars, arrays, name, **options):
    smem = pl.BlockSpec(memory_space=pltpu.SMEM)
    vmem = pl.BlockSpec(memory_space=pltpu.VMEM)
    return pl.pallas_call(
        kernel,
        out_shape=out_shape,
        in_specs=[smem] * len(scalars) + [vmem] * len(arrays),
        out_specs=(vmem,) * len(out_shape),
        compiler_params=pltpu.CompilerParams(vmem_limit_bytes=VMEM_LIMIT),
        cost_estimate=pl.CostEstimate(flops=COSTS[name], bytes_accessed=0, transcendentals=0),
        name=name,
        **options,
    )(*scalars, *arrays)


def shape(*sizes):
    return jax.ShapeDtypeStruct(sizes, F32)


def on_device(object_field, probe, measured, offsets, counts):
    parts, strip_rows, columns = object_field.shape
    slots, size, _ = measured.shape
    modes = probe.shape[1]
    half = size // 2
    positions = lax.axis_size("pos")
    tiles = lax.axis_size("tile")
    position = lax.axis_index("pos")
    tile = lax.axis_index("tile")
    swap = [(0, 1), (1, 0)]
    pair = [(i, i ^ 1) for i in range(positions)]
    following = [(i, i + 1) for i in range(1, positions - 1, 2)]
    following += [(target, source) for source, target in following]
    tables = [jnp.asarray(table) for table in real_tables(size)]
    scratch = [
        pltpu.VMEM((2, size, 3 * size), BF16),
        pltpu.VMEM((2, 3 * size, size), BF16),
        pltpu.VMEM((2, size, size), F32),
    ]

    component = lax.dynamic_index_in_dim(object_field, tile, 0, keepdims=False)
    halo = [lax.ppermute(component, "pos", ring) for ring in (pair, following)]

    pixel_lines = size * size // 128
    share = pixel_lines // positions * modes
    order = np.zeros((size, size), ml_dtypes.bfloat16)
    for parity in (0, 1):
        for index in range(half):
            order[2 * index + parity, parity * half + index] = 1
    probe_lines = probe.reshape(parts, modes, pixel_lines, 128).transpose(0, 2, 1, 3)
    probe_grid, probe_own = call(
        prepare_kernel,
        (shape(parts, modes, size, size), shape(parts, share, 128)),
        [],
        [probe_lines.reshape(parts, pixel_lines * modes, 128)],
        "prepare",
    )
    (amplitude,) = call(
        order_kernel,
        (shape(slots, 2, half, size),),
        [],
        [measured, jnp.asarray(np.stack([order, order.T]))],
        "order",
    )
    from_pair, probe_grid = lax.optimization_barrier((halo[0], probe_grid))
    pair_other = lax.ppermute(from_pair, "tile", swap)
    from_next, pair_other = lax.optimization_barrier((halo[1], pair_other))
    halo = [from_pair, from_next, pair_other, lax.ppermute(from_next, "tile", swap)]

    far, power, patch = [], [], []
    for slot in range(slots):
        outs = call(
            functools.partial(forward_kernel, slot),
            (shape(modes, 2, size, size), shape(2, half, size), shape(parts, size, size)),
            [],
            [offsets, object_field, *halo, probe_grid, *tables],
            "forward",
            scratch_shapes=[pltpu.VMEM((parts, 3 * strip_rows + 8, columns), F32)] + scratch,
        )
        far.append(outs[0])
        power.append(outs[1])
        patch.append(outs[2])
    others = [lax.ppermute(value, "tile", swap) for value in power]

    block_rows = size // positions
    bit_count = positions.bit_length() - 1
    pending = []
    begin = 0
    for group, bits in GROUPS:
        bits = [*bits, *range(len(bits), bit_count)]
        first = begin == 0
        kernel = functools.partial(
            inverse_kernel, tuple(range(begin, begin + group)), bits, first, slots
        )
        outs = (shape(slots, 2, size, size), shape(positions, group, 2, block_rows, size))
        arrays = [*tables, probe_grid, *far, *patch]
        if first:
            outs += (shape(slots, 2, half, size),)
            arrays += [amplitude, *power, *others]
            grad, blocks, ratio = call(
                kernel, outs, [counts], arrays, "inverse", scratch_shapes=scratch
            )
        else:
            arrays += [grad, ratio]
            grad, blocks = call(
                kernel,
                outs,
                [],
                arrays,
                "inverse",
                input_output_aliases={len(arrays) - 2: 0},
                scratch_shapes=scratch,
            )
        begin += group
        pending.append((bits, blocks))

    half_rows = strip_rows // tiles
    strip_shape = shape(3, parts, half_rows, columns)
    kept, sent = call(
        strip_kernel,
        (strip_shape, strip_shape),
        [],
        [offsets, grad],
        "strips",
        scratch_shapes=[pltpu.VMEM((slots, parts, 2 * strip_rows + size + 8, columns), F32)],
    )
    strips = kept + lax.ppermute(sent, "tile", swap)
    from_pair = lax.ppermute(strips[0], "pos", pair)
    from_next = lax.ppermute(strips[1], "pos", following)

    sums = []
    for which, (bits, blocks) in enumerate(pending):
        for step, bit in enumerate(bits):
            if TIE and (which, step) == TIE:
                blocks, from_pair, from_next = lax.optimization_barrier(
                    (blocks, from_pair, from_next)
                )
            keep, send = jnp.split(blocks, 2)
            got = lax.ppermute(send, "pos", [(i, i ^ 2**bit) for i in range(positions)])
            blocks = keep + got
        sums.append([keep[0], got[0]])

    object_out, probe_out = call(
        functools.partial(finish_kernel, [(group, 2) for group, _ in GROUPS]),
        (shape(parts, half_rows, columns), shape(parts, share, 128)),
        [],
        [probe_own, object_field, strips[2], from_pair, from_next, *sum(sums, [])],
        "finish",
    )
    probe_out = probe_out.reshape(parts, share // modes, modes, 128).transpose(0, 2, 1, 3)
    return (object_out, probe_out.reshape(parts, modes, share // modes * 128))


def solution(mesh):
    in_specs = (
        P(None, ("group", "pos"), None),
        P(None, "tile", None),
        P(("group", "pos"), None, None),
        P(("group", "pos"), None),
        P(("group", "pos")),
    )
    out_specs = (P(None, ("group", "pos", "tile"), None), P(None, ("group", "tile"), "pos"))
    return jax.shard_map(
        on_device, mesh=mesh, in_specs=in_specs, out_specs=out_specs, check_vma=False
    )
```

time: 96.4 us -> 64.9 us (0.67)
  local copies, waits for them, and re-layouts: 16.6 us -> 2.73 us
  starting transfers between devices: 37.7 us -> 27.5 us
  Pallas kernels: 21 us -> 14.6 us
  other arithmetic: 3.06 us -> 0.27 us
  waiting for transfers between devices: 15.8 us -> 18 us
    unnamed x38 -> x14, local copies, waits for them, and re-layouts: 14.9 us -> 1.62 us
    ppermute x21 -> x18, starting transfers between devices: 37.1 us -> 26.9 us  [the longest x12 16.8 us: on_device(): lax.ppermute(send, 'pos', [(i, i ^ 2 ** bit) for i in range(positions)])]
    pallas_call x9 -> x10, Pallas kernels: 21 us -> 14.6 us  [call(): pl.pallas_call(kernel, out_shape=out_shape, in_specs=[smem] * len(scalars...]
    ppermute x21 -> x18, waiting for transfers between devices: 14.7 us -> 17.9 us  [the longest x12 12.6 us: on_device(): lax.ppermute(send, 'pos', [(i, i ^ 2 ** bit) for i in range(positions)])]
    another operation x5 -> x0, other arithmetic: 2.74 us -> none  [the longest x4 1.56 us: call(): jnp.stack(scalars).astype(jnp.int32)]
    ppermute x2, waiting for transfers between devices: 1.13 us -> 0.01 us  [on_device(): others = [lax.ppermute(value, 'tile', swap) for value in power]]
  transfers between devices with their start and end apart: 24 -> 21, of which waited for: 7 -> 9; matrix products, arithmetic and copies ran while one was open for 3% -> 1% of each run, Pallas kernels for 14% -> 14%
where the time goes in v3:
time: 64.9 us; the launch traced here: 64.7 us
  starting transfers between devices  27.5 us (42%)
  waiting for transfers between devices  18 us (28%)
  Pallas kernels  14.6 us (22%)
  local copies, waits for them, and re-layouts  2.73 us (4%)
  between operations  1.61 us (2%)
    ppermute x12, starting transfers between devices, on_device(): lax.ppermute(send, 'pos', [(i, i ^ 2 ** bit) for i in range(positions)])  16.8 us
    pallas_call x10, Pallas kernels, call(): pl.pallas_call(kernel, out_shape=out_shape, in_specs=[smem] * len(scalars...  14.6 us
    ppermute x12, waiting for transfers between devices, on_device(): lax.ppermute(send, 'pos', [(i, i ^ 2 ** bit) for i in range(positions)])  12.6 us
    ppermute x2, starting transfers between devices, on_device(): halo = [lax.ppermute(component, 'pos', ring) for ring in (pair, following)]  6.46 us
    ppermute x1, starting transfers between devices, on_device(): from_pair = lax.ppermute(strips[0], 'pos', pair)  2.85 us
    ppermute x2, waiting for transfers between devices, on_device(): halo = [lax.ppermute(component, 'pos', ring) for ring in (pair, following)]  2.82 us
    unnamed x14, local copies, waits for them, and re-layouts  1.62 us
    ppermute x1, waiting for transfers between devices, on_device(): pair_other = lax.ppermute(from_pair, 'tile', swap)  1.33 us
  transfers between devices with their start and end apart: 21, of which 9 were waited for; matrix products, arithmetic and copies ran while one was open for 1% of the time, Pallas kernels for 14%

profile of v3, /device:TPU:0, one launch (start us, length us, event | category | flops | bytes accessed | tf_op | source)
XLA Modules:
  0.0 64.7 jit_solution(13773026527798418708)
XLA Ops:
  0.6 0.9 %dynamic-slice_bitcast_fusion = f32[128,256]{1,0:T(8,128)S(1)} fusion(f32[2,128,256]{2,1,0:T(8,128)} %strip_ref.1, s32[]{:T(128)S(6)} %select_n.4), kind=kLoop, calls=%fused_computation.11 | loop fusion | bytes 262148 | tf_op jit(solution)/shard_map/jit(dynamic_index_in_dim)/squeeze | solution.py:324
  1.6 0.7 %collective-permute-start.1 = (f32[128,256]{1,0:T(8,128)S(1)}, f32[128,256]{1,0:T(8,128)S(1)}, u32[]{:S(2)}, u32[]{:S(2)}) collective-permute-start(f32[128,256]{1,0:T(8,128)S(1)} %dynamic-slice_bitcast_fusion), channel_id=1, source_target_pairs={{2,4},{6,8},{10,12},{4,2},{8,6},{12,10},{3,5},{7,9},{11,13},{5,3},... | collective-permute-start | bytes 393224 | tf_op jit(solution)/shard_map/ppermute | solution.py:325
  2.2 5.8 %collective-permute-start = (f32[128,256]{1,0:T(8,128)S(1)}, f32[128,256]{1,0:T(8,128)S(1)}, u32[]{:S(2)}, u32[]{:S(2)}) collective-permute-start(f32[128,256]{1,0:T(8,128)S(1)} %dynamic-slice_bitcast_fusion), channel_id=1, source_target_pairs={{0,2},{2,0},{4,6},{6,4},{8,10},{10,8},{12,14},{14,12},{1,3},{3,1},... | collective-permute-start | bytes 393224 | tf_op jit(solution)/shard_map/ppermute | solution.py:325
  8.0 1.6 %copy-done.3 = f32[2,4,65536]{2,1,0:T(4,128)S(1)} copy-done((f32[2,4,65536]{2,1,0:T(4,128)S(1)}, f32[2,4,65536]{2,1,0:T(4,128)}, u32[]{:S(2)}) %copy-start.3) | copy-done | bytes 2097176
  10.0 2.8 %collective-permute-done.pair_ref = f32[128,256]{1,0:T(8,128)S(1)} collective-permute-done((f32[128,256]{1,0:T(8,128)S(1)}, f32[128,256]{1,0:T(8,128)S(1)}, u32[]{:S(2)}, u32[]{:S(2)}) %collective-permute-start) | collective-permute-done | bytes 131104 | tf_op jit(solution)/shard_map/ppermute | solution.py:325
  12.9 1.3 %collective-permute-done.2.pair_other_ref = f32[128,256]{1,0:T(8,128)S(1)} collective-permute-done((f32[128,256]{1,0:T(8,128)S(1)}, f32[128,256]{1,0:T(8,128)S(1)}, u32[]{:S(2)}, u32[]{:S(2)}) %collective-permute-start.2) | collective-permute-done | bytes 131104 | tf_op jit(solution)/shard_map/ppermute | solution.py:349
  14.3 1.2 %collective-permute-done.3.next_other_ref = f32[128,256]{1,0:T(8,128)S(1)} collective-permute-done((f32[128,256]{1,0:T(8,128)S(1)}, f32[128,256]{1,0:T(8,128)S(1)}, u32[]{:S(2)}, u32[]{:S(2)}) %collective-permute-start.3) | collective-permute-done | bytes 131104 | tf_op jit(solution)/shard_map/ppermute | solution.py:351
  15.6 3.0 %forward.3 = (f32[4,2,256,256]{3,2,1,0:T(8,128)S(1)}, f32[2,128,256]{2,1,0:T(8,128)S(1)}, f32[2,256,256]{2,1,0:T(8,128)S(1)}) custom-call(s32[2,2]{1,0:T(2,128)S(1)} %copy-done.5, f32[2,128,256]{2,1,0:T(8,128)S(1)} %copy-done.2, f32[128,256]{1,0:T(8,128)S(1)} %collective-permute-done.pair_ref, f32[128,256]{1,0:T(8,128)S(1)} %collective-permute-done.1.next_ref, ...), custom_call_target="tpu_custom_call" | custom-call | flops 4000000000 | tf_op jit(solution)/shard_map/forward/pallas_call | solution.py:288
  18.8 3.0 %forward.2 = (f32[4,2,256,256]{3,2,1,0:T(8,128)S(1)}, f32[2,128,256]{2,1,0:T(8,128)S(1)}, f32[2,256,256]{2,1,0:T(8,128)S(1)}) custom-call(s32[2,2]{1,0:T(2,128)S(1)} %copy-done.5, f32[2,128,256]{2,1,0:T(8,128)S(1)} %copy-done.2, f32[128,256]{1,0:T(8,128)S(1)} %collective-permute-done.pair_ref, f32[128,256]{1,0:T(8,128)S(1)} %collective-permute-done.1.next_ref, ...), custom_call_target="tpu_custom_call" | custom-call | flops 4000000000 | tf_op jit(solution)/shard_map/forward/pallas_call | solution.py:288
  22.8 0.9 %order.1.refs_8_ = f32[2,2,128,256]{3,2,1,0:T(8,128)S(1)} custom-call(f32[2,256,256]{2,1,0:T(8,128)S(1)} %copy-done.4, bf16[2,256,256]{2,1,0:T(8,128)(2,1)S(1)} %copy-done.6), custom_call_target="tpu_custom_call" | custom-call | flops 1000000000 | tf_op jit(solution)/shard_map/order/pallas_call | solution.py:288
  23.8 1.6 %inverse.4 = (f32[2,2,256,256]{3,2,1,0:T(8,128)S(1)}, f32[8,1,2,32,256]{4,3,2,1,0:T(8,128)S(1)}, f32[2,2,128,256]{3,2,1,0:T(8,128)S(1)}) custom-call(s32[1]{0:T(128)S(6)} %copy.18.refs_0_, bf16[4,768,256]{2,1,0:T(8,128)(2,1)S(1)} %copy-done.1, bf16[4,256,768]{2,1,0:T(8,128)(2,1)S(1)} %copy-done, ...), custom_call_target="tpu_custom_call" | custom-call | flops 2400000000 | tf_op jit(solution)/shard_map/inverse/pallas_call | solution.py:288
  25.4 2.6 %collective-permute-start.9 = (f32[4,1,2,32,256]{4,3,2,1,0:T(8,128)S(1)}, f32[4,1,2,32,256]{4,3,2,1,0:T(8,128)S(1)}, u32[]{:S(2)}, u32[]{:S(2)}) collective-permute-start(f32[4,1,2,32,256]{4,3,2,1,0:T(8,128)S(1)} %split.73), channel_id=1, source_target_pairs={{0,4},{2,6},{4,0},{6,2},{8,12},{10,14},{12,8},{14,10},{1,5},{3,7},... | collective-permute-start | bytes 786440 | tf_op jit(solution)/shard_map/ppermute | solution.py:422
  28.0 1.4 %inverse.5 = (f32[2,2,256,256]{3,2,1,0:T(8,128)S(1)}, f32[8,1,2,32,256]{4,3,2,1,0:T(8,128)S(1)}) custom-call(bf16[4,768,256]{2,1,0:T(8,128)(2,1)S(1)} %copy-done.1, bf16[4,256,768]{2,1,0:T(8,128)(2,1)S(1)} %copy-done, f32[2,4,256,256]{3,2,1,0:T(8,128)S(1)} %get-tuple-element.29.probe_ref.refs_3_.refs_2_, ...), custom_call_target="tpu_custom_call", output_to_operand_aliasing={{0}: (7, {})} | custom-call | flops 2400000000 | tf_op jit(solution)/shard_map/inverse/pallas_call | solution.py:288
  29.5 1.6 %collective-permute-start.12 = (f32[4,1,2,32,256]{4,3,2,1,0:T(8,128)S(1)}, f32[4,1,2,32,256]{4,3,2,1,0:T(8,128)S(1)}, u32[]{:S(2)}, u32[]{:S(2)}) collective-permute-start(f32[4,1,2,32,256]{4,3,2,1,0:T(8,128)S(1)} %split.79), channel_id=1, source_target_pairs={{0,2},{2,0},{4,6},{6,4},{8,10},{10,8},{12,14},{14,12},{1,3},{3,1},... | collective-permute-start | bytes 786440 | tf_op jit(solution)/shard_map/ppermute | solution.py:422
  31.0 1.4 %inverse.6 = (f32[2,2,256,256]{3,2,1,0:T(8,128)S(1)}, f32[8,1,2,32,256]{4,3,2,1,0:T(8,128)S(1)}) custom-call(bf16[4,768,256]{2,1,0:T(8,128)(2,1)S(1)} %copy-done.1, bf16[4,256,768]{2,1,0:T(8,128)(2,1)S(1)} %copy-done, f32[2,4,256,256]{3,2,1,0:T(8,128)S(1)} %get-tuple-element.29.probe_ref.refs_3_.refs_2_, ...), custom_call_target="tpu_custom_call", output_to_operand_aliasing={{0}: (7, {})} | custom-call | flops 2400000000 | tf_op jit(solution)/shard_map/inverse/pallas_call | solution.py:288
  32.5 1.4 %inverse.7 = (f32[2,2,256,256]{3,2,1,0:T(8,128)S(1)}, f32[8,1,2,32,256]{4,3,2,1,0:T(8,128)S(1)}) custom-call(bf16[4,768,256]{2,1,0:T(8,128)(2,1)S(1)} %copy-done.1, bf16[4,256,768]{2,1,0:T(8,128)(2,1)S(1)} %copy-done, f32[2,4,256,256]{3,2,1,0:T(8,128)S(1)} %get-tuple-element.29.probe_ref.refs_3_.refs_2_, ...), custom_call_target="tpu_custom_call", output_to_operand_aliasing={{0}: (7, {})} | custom-call | flops 2400000000 | tf_op jit(solution)/shard_map/inverse/pallas_call | solution.py:288
  33.9 0.6 strips.1
  35.3 1.9 %collective-permute-start.10 = (f32[2,1,2,32,256]{4,3,2,1,0:T(8,128)S(1)}, f32[2,1,2,32,256]{4,3,2,1,0:T(8,128)S(1)}, u32[]{:S(2)}, u32[]{:S(2)}) collective-permute-start(f32[2,1,2,32,256]{4,3,2,1,0:T(8,128)S(1)} %split.97), channel_id=1, source_target_pairs={{0,2},{2,0},{4,6},{6,4},{8,10},{10,8},{12,14},{14,12},{1,3},{3,1},... | collective-permute-start | bytes 393224 | tf_op jit(solution)/shard_map/ppermute | solution.py:422
  37.2 1.0 %collective-permute-done.12 = f32[4,1,2,32,256]{4,3,2,1,0:T(8,128)S(1)} collective-permute-done((f32[4,1,2,32,256]{4,3,2,1,0:T(8,128)S(1)}, f32[4,1,2,32,256]{4,3,2,1,0:T(8,128)S(1)}, u32[]{:S(2)}, u32[]{:S(2)}) %collective-permute-start.12) | collective-permute-done | bytes 262176 | tf_op jit(solution)/shard_map/ppermute | solution.py:422
  38.3 0.6 collective-permute-start.13
  38.9 4.9 %collective-permute-done.15 = f32[4,1,2,32,256]{4,3,2,1,0:T(8,128)S(1)} collective-permute-done((f32[4,1,2,32,256]{4,3,2,1,0:T(8,128)S(1)}, f32[4,1,2,32,256]{4,3,2,1,0:T(8,128)S(1)}, u32[]{:S(2)}, u32[]{:S(2)}) %collective-permute-start.15) | collective-permute-done | bytes 262176 | tf_op jit(solution)/shard_map/ppermute | solution.py:422
  43.9 0.6 collective-permute-start.16
  44.6 1.5 %collective-permute-start.19 = (f32[2,1,2,32,256]{4,3,2,1,0:T(8,128)S(1)}, f32[2,1,2,32,256]{4,3,2,1,0:T(8,128)S(1)}, u32[]{:S(2)}, u32[]{:S(2)}) collective-permute-start(f32[2,1,2,32,256]{4,3,2,1,0:T(8,128)S(1)} %split.109), channel_id=1, source_target_pairs={{0,4},{2,6},{4,0},{6,2},{8,12},{10,14},{12,8},{14,10},{1,5},{3,7},... | collective-permute-start | bytes 393224 | tf_op jit(solution)/shard_map/ppermute | solution.py:422
  46.0 1.1 %collective-permute-done.10 = f32[2,1,2,32,256]{4,3,2,1,0:T(8,128)S(1)} collective-permute-done((f32[2,1,2,32,256]{4,3,2,1,0:T(8,128)S(1)}, f32[2,1,2,32,256]{4,3,2,1,0:T(8,128)S(1)}, u32[]{:S(2)}, u32[]{:S(2)}) %collective-permute-start.10) | collective-permute-done | bytes 131104 | tf_op jit(solution)/shard_map/ppermute | solution.py:422
  47.2 2.7 %collective-permute-start.11 = (f32[1,1,2,32,256]{4,3,2,1,0:T(8,128)S(1)}, f32[1,1,2,32,256]{4,3,2,1,0:T(8,128)S(1)}, u32[]{:S(2)}, u32[]{:S(2)}) collective-permute-start(f32[1,1,2,32,256]{4,3,2,1,0:T(8,128)S(1)} %get-tuple-element.61), channel_id=1, source_target_pairs={{0,8},{2,10},{4,12},{6,14},{8,0},{10,2},{12,4},{14,6},{1,9},{3,11}... | collective-permute-start | bytes 196616 | tf_op jit(solution)/shard_map/ppermute | solution.py:422
  50.3 2.6 %collective-permute-start.17 = (f32[1,1,2,32,256]{4,3,2,1,0:T(8,128)S(1)}, f32[1,1,2,32,256]{4,3,2,1,0:T(8,128)S(1)}, u32[]{:S(2)}, u32[]{:S(2)}) collective-permute-start(f32[1,1,2,32,256]{4,3,2,1,0:T(8,128)S(1)} %get-tuple-element.57), channel_id=1, source_target_pairs={{0,8},{2,10},{4,12},{6,14},{8,0},{10,2},{12,4},{14,6},{1,9},{3,11}... | collective-permute-start | bytes 196616 | tf_op jit(solution)/shard_map/ppermute | solution.py:422
  53.1 0.7 %collective-permute-start.8 = (f32[2,64,256]{2,1,0:T(8,128)S(1)}, f32[2,64,256]{2,1,0:T(8,128)S(1)}, u32[]{:S(2)}, u32[]{:S(2)}) collective-permute-start(f32[2,64,256]{2,1,0:T(8,128)S(1)} %get-tuple-element.52), channel_id=1, source_target_pairs={{2,4},{6,8},{10,12},{4,2},{8,6},{12,10},{3,5},{7,9},{11,13},{5,3},... | collective-permute-start | bytes 393224 | tf_op jit(solution)/shard_map/ppermute | solution.py:412
  53.7 2.8 %collective-permute-start.7 = (f32[2,64,256]{2,1,0:T(8,128)S(1)}, f32[2,64,256]{2,1,0:T(8,128)S(1)}, u32[]{:S(2)}, u32[]{:S(2)}) collective-permute-start(f32[2,64,256]{2,1,0:T(8,128)S(1)} %get-tuple-element.53), channel_id=1, source_target_pairs={{0,2},{2,0},{4,6},{6,4},{8,10},{10,8},{12,14},{14,12},{1,3},{3,1},... | collective-permute-start | bytes 393224 | tf_op jit(solution)/shard_map/ppermute | solution.py:411
  56.6 1.6 %collective-permute-start.20 = (f32[1,1,2,32,256]{4,3,2,1,0:T(8,128)S(1)}, f32[1,1,2,32,256]{4,3,2,1,0:T(8,128)S(1)}, u32[]{:S(2)}, u32[]{:S(2)}) collective-permute-start(f32[1,1,2,32,256]{4,3,2,1,0:T(8,128)S(1)} %get-tuple-element.55), channel_id=1, source_target_pairs={{0,8},{2,10},{4,12},{6,14},{8,0},{10,2},{12,4},{14,6},{1,9},{3,11}... | collective-permute-start | bytes 196616 | tf_op jit(solution)/shard_map/ppermute | solution.py:422
  58.5 1.4 %collective-permute-done.17 = f32[1,1,2,32,256]{4,3,2,1,0:T(8,128)S(1)} collective-permute-done((f32[1,1,2,32,256]{4,3,2,1,0:T(8,128)S(1)}, f32[1,1,2,32,256]{4,3,2,1,0:T(8,128)S(1)}, u32[]{:S(2)}, u32[]{:S(2)}) %collective-permute-start.17) | collective-permute-done | bytes 65568 | tf_op jit(solution)/shard_map/ppermute | solution.py:422
  59.9 3.9 %collective-permute-done.20 = f32[1,1,2,32,256]{4,3,2,1,0:T(8,128)S(1)} collective-permute-done((f32[1,1,2,32,256]{4,3,2,1,0:T(8,128)S(1)}, f32[1,1,2,32,256]{4,3,2,1,0:T(8,128)S(1)}, u32[]{:S(2)}, u32[]{:S(2)}) %collective-permute-start.20) | collective-permute-done | bytes 65568 | tf_op jit(solution)/shard_map/ppermute | solution.py:422
  63.8 0.9 %finish.1 = (f32[2,64,256]{2,1,0:T(8,128)}, f32[2,256,128]{2,1,0:T(8,128)}) custom-call(f32[2,256,128]{2,1,0:T(8,128)S(1)} %get-tuple-element.27.probe_ref, f32[2,128,256]{2,1,0:T(8,128)S(1)} %copy-done.2, f32[2,64,256]{2,1,0:T(8,128)S(1)} %get-tuple-element.54.mid_ref, f32[2,64,256]{2,1,0:T(8,128)S(1)} %collective-permute-done.7.pair_ref, ...), custom_call_target="tpu_custom_call" | custom-call | flops 1000000000 | tf_op jit(solution)/shard_map/finish/pallas_call | solution.py:288
  (57 shorter events, 3.1 us)
Async XLA Ops:
  1.6 11.3 %collective-permute-start.1 = (f32[128,256]{1,0:T(8,128)S(1)}, f32[128,256]{1,0:T(8,128)S(1)}, u32[]{:S(2)}, u32[]{:S(2)}) collective-permute-start(f32[128,256]{1,0:T(8,128)S(1)} %dynamic-slice_bitcast_fusion), channel_id=1, source_target_pairs={{2,4},{6,8},{10,12},{4,2},{8,6},{12,10},{3,5},{7,9},{11,13},{5,3},... | collective-permute-start | bytes 393224 | tf_op jit(solution)/shard_map/ppermute | solution.py:325
  2.2 10.6 %collective-permute-start = (f32[128,256]{1,0:T(8,128)S(1)}, f32[128,256]{1,0:T(8,128)S(1)}, u32[]{:S(2)}, u32[]{:S(2)}) collective-permute-start(f32[128,256]{1,0:T(8,128)S(1)} %dynamic-slice_bitcast_fusion), channel_id=1, source_target_pairs={{0,2},{2,0},{4,6},{6,4},{8,10},{10,8},{12,14},{14,12},{1,3},{3,1},... | collective-permute-start | bytes 393224 | tf_op jit(solution)/shard_map/ppermute | solution.py:325
  8.0 1.6 %copy-start.3 = (f32[2,4,65536]{2,1,0:T(4,128)S(1)}, f32[2,4,65536]{2,1,0:T(4,128)}, u32[]{:S(2)}) copy-start(f32[2,4,65536]{2,1,0:T(4,128)} %param.9) | copy-start | bytes 6291460
  9.6 5.9 %copy-start = (bf16[4,256,768]{2,1,0:T(8,128)(2,1)S(1)}, bf16[4,256,768]{2,1,0:T(8,128)(2,1)}, u32[]{:S(2)}) copy-start(bf16[4,256,768]{2,1,0:T(8,128)(2,1)} %constant.17.clone.col_ref.refs_2_.refs_1_) | copy-start | bytes 4718596
  9.6 5.9 %copy-start.1 = (bf16[4,768,256]{2,1,0:T(8,128)(2,1)S(1)}, bf16[4,768,256]{2,1,0:T(8,128)(2,1)}, u32[]{:S(2)}) copy-start(bf16[4,768,256]{2,1,0:T(8,128)(2,1)} %constant.16.clone.row_ref.refs_1_.refs_0_) | copy-start | bytes 4718596
  9.6 5.9 %copy-start.2 = (f32[2,128,256]{2,1,0:T(8,128)S(1)}, f32[2,128,256]{2,1,0:T(8,128)}, u32[]{:S(2)}) copy-start(f32[2,128,256]{2,1,0:T(8,128)} %strip_ref.1) | copy-start | bytes 786436
  9.6 5.9 %copy-start.5 = (s32[2,2]{1,0:T(2,128)S(1)}, s32[2,2]{1,0:T(2,128)}, u32[]{:S(2)}) copy-start(s32[2,2]{1,0:T(2,128)} %offset_ref.5) | copy-start | bytes 52
  12.8 1.3 %collective-permute-start.2 = (f32[128,256]{1,0:T(8,128)S(1)}, f32[128,256]{1,0:T(8,128)S(1)}, u32[]{:S(2)}, u32[]{:S(2)}) collective-permute-start(f32[128,256]{1,0:T(8,128)S(1)} %collective-permute-done.pair_ref), channel_id=1, source_target_pairs={{0,1},{1,0},{2,3},{3,2},{4,5},{5,4},{6,7},{7,6},{8,9},{9,8},{10,11... | collective-permute-start | bytes 393224 | tf_op jit(solution)/shard_map/ppermute | solution.py:349
  14.2 1.3 %collective-permute-start.3 = (f32[128,256]{1,0:T(8,128)S(1)}, f32[128,256]{1,0:T(8,128)S(1)}, u32[]{:S(2)}, u32[]{:S(2)}) collective-permute-start(f32[128,256]{1,0:T(8,128)S(1)} %collective-permute-done.1.next_ref), channel_id=1, source_target_pairs={{0,1},{1,0},{2,3},{3,2},{4,5},{5,4},{6,7},{7,6},{8,9},{9,8},{10,11... | collective-permute-start | bytes 393224 | tf_op jit(solution)/shard_map/ppermute | solution.py:351
  18.5 4.3 %copy-start.4 = (f32[2,256,256]{2,1,0:T(8,128)S(1)}, f32[2,256,256]{2,1,0:T(8,128)}, u32[]{:S(2)}) copy-start(f32[2,256,256]{2,1,0:T(8,128)} %measured_ref.1) | copy-start | bytes 1572868
  18.6 4.3 %copy-start.6 = (bf16[2,256,256]{2,1,0:T(8,128)(2,1)S(1)}, bf16[2,256,256]{2,1,0:T(8,128)(2,1)}, u32[]{:S(2)}) copy-start(bf16[2,256,256]{2,1,0:T(8,128)(2,1)} %constant.18.clone.order_ref) | copy-start | bytes 786436
  18.6 5.2 %collective-permute-start.5 = (f32[2,128,256]{2,1,0:T(8,128)S(1)}, f32[2,128,256]{2,1,0:T(8,128)S(1)}, u32[]{:S(2)}, u32[]{:S(2)}) collective-permute-start(f32[2,128,256]{2,1,0:T(8,128)S(1)} %get-tuple-element.38.refs_10_), channel_id=1, source_target_pairs={{0,1},{1,0},{2,3},{3,2},{4,5},{5,4},{6,7},{7,6},{8,9},{9,8},{10,11... | collective-permute-start | bytes 786440 | tf_op jit(solution)/shard_map/ppermute | solution.py:366
  21.7 2.1 %collective-permute-start.4 = (f32[2,128,256]{2,1,0:T(8,128)S(1)}, f32[2,128,256]{2,1,0:T(8,128)S(1)}, u32[]{:S(2)}, u32[]{:S(2)}) collective-permute-start(f32[2,128,256]{2,1,0:T(8,128)S(1)} %get-tuple-element.37.refs_9_), channel_id=1, source_target_pairs={{0,1},{1,0},{2,3},{3,2},{4,5},{5,4},{6,7},{7,6},{8,9},{9,8},{10,11... | collective-permute-start | bytes 786440 | tf_op jit(solution)/shard_map/ppermute | solution.py:366
  25.4 9.8 %collective-permute-start.9 = (f32[4,1,2,32,256]{4,3,2,1,0:T(8,128)S(1)}, f32[4,1,2,32,256]{4,3,2,1,0:T(8,128)S(1)}, u32[]{:S(2)}, u32[]{:S(2)}) collective-permute-start(f32[4,1,2,32,256]{4,3,2,1,0:T(8,128)S(1)} %split.73), channel_id=1, source_target_pairs={{0,4},{2,6},{4,0},{6,2},{8,12},{10,14},{12,8},{14,10},{1,5},{3,7},... | collective-permute-start | bytes 786440 | tf_op jit(solution)/shard_map/ppermute | solution.py:422
  29.5 8.7 %collective-permute-start.12 = (f32[4,1,2,32,256]{4,3,2,1,0:T(8,128)S(1)}, f32[4,1,2,32,256]{4,3,2,1,0:T(8,128)S(1)}, u32[]{:S(2)}, u32[]{:S(2)}) collective-permute-start(f32[4,1,2,32,256]{4,3,2,1,0:T(8,128)S(1)} %split.79), channel_id=1, source_target_pairs={{0,2},{2,0},{4,6},{6,4},{8,10},{10,8},{12,14},{14,12},{1,3},{3,1},... | collective-permute-start | bytes 786440 | tf_op jit(solution)/shard_map/ppermute | solution.py:422
  34.5 9.3 %collective-permute-start.15 = (f32[4,1,2,32,256]{4,3,2,1,0:T(8,128)S(1)}, f32[4,1,2,32,256]{4,3,2,1,0:T(8,128)S(1)}, u32[]{:S(2)}, u32[]{:S(2)}) collective-permute-start(f32[4,1,2,32,256]{4,3,2,1,0:T(8,128)S(1)} %split.85), channel_id=1, source_target_pairs={{0,4},{2,6},{4,0},{6,2},{8,12},{10,14},{12,8},{14,10},{1,5},{3,7},... | collective-permute-start | bytes 786440 | tf_op jit(solution)/shard_map/ppermute | solution.py:422
  35.1 9.4 %collective-permute-start.18 = (f32[4,1,2,32,256]{4,3,2,1,0:T(8,128)S(1)}, f32[4,1,2,32,256]{4,3,2,1,0:T(8,128)S(1)}, u32[]{:S(2)}, u32[]{:S(2)}) collective-permute-start(f32[4,1,2,32,256]{4,3,2,1,0:T(8,128)S(1)} %split.91), channel_id=1, source_target_pairs={{0,2},{2,0},{4,6},{6,4},{8,10},{10,8},{12,14},{14,12},{1,3},{3,1},... | collective-permute-start | bytes 786440 | tf_op jit(solution)/shard_map/ppermute | solution.py:422
  35.2 17.7 %collective-permute-start.6 = (f32[3,2,64,256]{3,2,1,0:T(8,128)S(1)}, f32[3,2,64,256]{3,2,1,0:T(8,128)S(1)}, u32[]{:S(2)}, u32[]{:S(2)}) collective-permute-start(f32[3,2,64,256]{3,2,1,0:T(8,128)S(1)} %get-tuple-element.45), channel_id=1, source_target_pairs={{0,1},{1,0},{2,3},{3,2},{4,5},{5,4},{6,7},{7,6},{8,9},{9,8},{10,11... | collective-permute-start | bytes 1179656 | tf_op jit(solution)/shard_map/ppermute | solution.py:410
  35.3 11.8 %collective-permute-start.10 = (f32[2,1,2,32,256]{4,3,2,1,0:T(8,128)S(1)}, f32[2,1,2,32,256]{4,3,2,1,0:T(8,128)S(1)}, u32[]{:S(2)}, u32[]{:S(2)}) collective-permute-start(f32[2,1,2,32,256]{4,3,2,1,0:T(8,128)S(1)} %split.97), channel_id=1, source_target_pairs={{0,2},{2,0},{4,6},{6,4},{8,10},{10,8},{12,14},{14,12},{1,3},{3,1},... | collective-permute-start | bytes 393224 | tf_op jit(solution)/shard_map/ppermute | solution.py:422
  38.3 11.5 %collective-permute-start.13 = (f32[2,1,2,32,256]{4,3,2,1,0:T(8,128)S(1)}, f32[2,1,2,32,256]{4,3,2,1,0:T(8,128)S(1)}, u32[]{:S(2)}, u32[]{:S(2)}) collective-permute-start(f32[2,1,2,32,256]{4,3,2,1,0:T(8,128)S(1)} %split.101), channel_id=1, source_target_pairs={{0,4},{2,6},{4,0},{6,2},{8,12},{10,14},{12,8},{14,10},{1,5},{3,7},... | collective-permute-start | bytes 393224 | tf_op jit(solution)/shard_map/ppermute | solution.py:422
  43.9 6.4 %collective-permute-start.16 = (f32[2,1,2,32,256]{4,3,2,1,0:T(8,128)S(1)}, f32[2,1,2,32,256]{4,3,2,1,0:T(8,128)S(1)}, u32[]{:S(2)}, u32[]{:S(2)}) collective-permute-start(f32[2,1,2,32,256]{4,3,2,1,0:T(8,128)S(1)} %split.105), channel_id=1, source_target_pairs={{0,2},{2,0},{4,6},{6,4},{8,10},{10,8},{12,14},{14,12},{1,3},{3,1},... | collective-permute-start | bytes 393224 | tf_op jit(solution)/shard_map/ppermute | solution.py:422
  44.6 9.2 %collective-permute-start.19 = (f32[2,1,2,32,256]{4,3,2,1,0:T(8,128)S(1)}, f32[2,1,2,32,256]{4,3,2,1,0:T(8,128)S(1)}, u32[]{:S(2)}, u32[]{:S(2)}) collective-permute-start(f32[2,1,2,32,256]{4,3,2,1,0:T(8,128)S(1)} %split.109), channel_id=1, source_target_pairs={{0,4},{2,6},{4,0},{6,2},{8,12},{10,14},{12,8},{14,10},{1,5},{3,7},... | collective-permute-start | bytes 393224 | tf_op jit(solution)/shard_map/ppermute | solution.py:422
  47.2 9.5 %collective-permute-start.11 = (f32[1,1,2,32,256]{4,3,2,1,0:T(8,128)S(1)}, f32[1,1,2,32,256]{4,3,2,1,0:T(8,128)S(1)}, u32[]{:S(2)}, u32[]{:S(2)}) collective-permute-start(f32[1,1,2,32,256]{4,3,2,1,0:T(8,128)S(1)} %get-tuple-element.61), channel_id=1, source_target_pairs={{0,8},{2,10},{4,12},{6,14},{8,0},{10,2},{12,4},{14,6},{1,9},{3,11}... | collective-permute-start | bytes 196616 | tf_op jit(solution)/shard_map/ppermute | solution.py:422
  49.9 8.7 %collective-permute-start.14 = (f32[1,1,2,32,256]{4,3,2,1,0:T(8,128)S(1)}, f32[1,1,2,32,256]{4,3,2,1,0:T(8,128)S(1)}, u32[]{:S(2)}, u32[]{:S(2)}) collective-permute-start(f32[1,1,2,32,256]{4,3,2,1,0:T(8,128)S(1)} %get-tuple-element.59), channel_id=1, source_target_pairs={{0,8},{2,10},{4,12},{6,14},{8,0},{10,2},{12,4},{14,6},{1,9},{3,11}... | collective-permute-start | bytes 196616 | tf_op jit(solution)/shard_map/ppermute | solution.py:422
  50.3 9.6 %collective-permute-start.17 = (f32[1,1,2,32,256]{4,3,2,1,0:T(8,128)S(1)}, f32[1,1,2,32,256]{4,3,2,1,0:T(8,128)S(1)}, u32[]{:S(2)}, u32[]{:S(2)}) collective-permute-start(f32[1,1,2,32,256]{4,3,2,1,0:T(8,128)S(1)} %get-tuple-element.57), channel_id=1, source_target_pairs={{0,8},{2,10},{4,12},{6,14},{8,0},{10,2},{12,4},{14,6},{1,9},{3,11}... | collective-permute-start | bytes 196616 | tf_op jit(solution)/shard_map/ppermute | solution.py:422
  53.1 10.7 %collective-permute-start.8 = (f32[2,64,256]{2,1,0:T(8,128)S(1)}, f32[2,64,256]{2,1,0:T(8,128)S(1)}, u32[]{:S(2)}, u32[]{:S(2)}) collective-permute-start(f32[2,64,256]{2,1,0:T(8,128)S(1)} %get-tuple-element.52), channel_id=1, source_target_pairs={{2,4},{6,8},{10,12},{4,2},{8,6},{12,10},{3,5},{7,9},{11,13},{5,3},... | collective-permute-start | bytes 393224 | tf_op jit(solution)/shard_map/ppermute | solution.py:412
  53.7 10.1 %collective-permute-start.7 = (f32[2,64,256]{2,1,0:T(8,128)S(1)}, f32[2,64,256]{2,1,0:T(8,128)S(1)}, u32[]{:S(2)}, u32[]{:S(2)}) collective-permute-start(f32[2,64,256]{2,1,0:T(8,128)S(1)} %get-tuple-element.53), channel_id=1, source_target_pairs={{0,2},{2,0},{4,6},{6,4},{8,10},{10,8},{12,14},{14,12},{1,3},{3,1},... | collective-permute-start | bytes 393224 | tf_op jit(solution)/shard_map/ppermute | solution.py:411
  56.6 7.2 %collective-permute-start.20 = (f32[1,1,2,32,256]{4,3,2,1,0:T(8,128)S(1)}, f32[1,1,2,32,256]{4,3,2,1,0:T(8,128)S(1)}, u32[]{:S(2)}, u32[]{:S(2)}) collective-permute-start(f32[1,1,2,32,256]{4,3,2,1,0:T(8,128)S(1)} %get-tuple-element.55), channel_id=1, source_target_pairs={{0,8},{2,10},{4,12},{6,14},{8,0},{10,2},{12,4},{14,6},{1,9},{3,11}... | collective-permute-start | bytes 196616 | tf_op jit(solution)/shard_map/ppermute | solution.py:422

commit v4 on v3

--- a/solution.py
+++ b/solution.py
@@ -17,7 +17,7 @@
 F32 = jnp.float32
 BF16 = jnp.bfloat16
 VMEM_LIMIT = 16 * 1024 * 1024
-COSTS = {'prepare': 2000000000, 'forward': 4000000000, 'inverse': 2400000000, 'strips': 1200000000, 'finish': 1000000000, 'order': 1000000000}
+COSTS = {'prepare': 2000000000, 'forward': 4000000000, 'inverse': 2400000000, 'strips': 1200000000, 'finish': 1000000000, 'order': 1000000000, 'pick': 1000000}
 CHUNK = 64
 TIE = None
 GROUPS = ((1, (1, 0, 2)), (1, (0, 1, 2)), (1, (1, 0, 2)), (1, (0, 1, 2)))
@@ -127,7 +127,9 @@
     for part in (0, 1):
         patch_ref[part] = load_rows(extended, (part,), start, size)
     half = size // 2
-    for mode in range(probe_ref.shape[1]):
+    modes = probe_ref.shape[1]
+
+    def spread_rows(mode):
         for begin, lines in spans(size, CHUNK):
             patch_real, patch_imag = patch_ref[0, lines], patch_ref[1, lines]
             probe_real, probe_imag = probe_ref[0, mode, lines], probe_ref[1, mode, lines]
@@ -135,20 +137,36 @@
             imag = probe_real * patch_imag + probe_imag * patch_real
             a, b = real[:, :half], real[:, half:]
             c, d = imag[:, :half], imag[:, half:]
-            put_left(left_ref, 0, begin, jnp.concatenate([a + b, c + d], 1))
-            put_left(left_ref, 1, begin, jnp.concatenate([a - b, c - d], 1))
+            put_left(left_ref, 2 * (mode % 2), begin, jnp.concatenate([a + b, c + d], 1))
+            put_left(left_ref, 2 * (mode % 2) + 1, begin, jnp.concatenate([a - b, c - d], 1))
+
+    def row_products(mode):
         for parity in (0, 1):
-            middle_ref[parity] = product(left_ref[parity], row_ref[2 * parity])
+            which = 2 * (mode % 2) + parity
+            middle_ref[which] = product(left_ref[which], row_ref[2 * parity])
+
+    def spread_columns(mode):
+        first = 2 * (mode % 2)
         for begin, lines in spans(half, CHUNK // 2):
             under = slice(half + begin, half + begin + CHUNK // 2)
             for part in (0, 1):
                 where = slice(part * half, (part + 1) * half)
-                top = jnp.concatenate([middle_ref[0, lines, where], middle_ref[1, lines, where]], 1)
-                low = jnp.concatenate([middle_ref[0, under, where], middle_ref[1, under, where]], 1)
-                put_right(right_ref, 0, part * half + begin, top + low)
-                put_right(right_ref, 1, part * half + begin, top - low)
+                top = jnp.concatenate(
+                    [middle_ref[first, lines, where], middle_ref[first + 1, lines, where]], 1
+                )
+                low = jnp.concatenate(
+                    [middle_ref[first, under, where], middle_ref[first + 1, under, where]], 1
+                )
+                put_right(right_ref, first, part * half + begin, top + low)
+                put_right(right_ref, first + 1, part * half + begin, top - low)
+
+    def column_products(mode):
         for parity in (0, 1):
-            far_ref[mode, parity] = product(col_ref[2 * parity + 1], right_ref[parity])
+            which = 2 * (mode % 2) + parity
+            far_ref[mode, parity] = product(col_ref[2 * parity + 1], right_ref[which])
+
+    def add_power(mode):
+        for parity in (0, 1):
             for begin, lines in spans(half, CHUNK):
                 under = slice(half + begin, half + begin + CHUNK)
                 real, imag = far_ref[mode, parity, lines], far_ref[mode, parity, under]
@@ -157,6 +175,19 @@
                     power_ref[parity, lines] = power
                 else:
                     power_ref[parity, lines] += power
+
+    spread_rows(0)
+    row_products(0)
+    for mode in range(modes):
+        if mode + 1 < modes:
+            spread_rows(mode + 1)
+        spread_columns(mode)
+        if mode + 1 < modes:
+            row_products(mode + 1)
+        column_products(mode)
+        if mode > 0:
+            add_power(mode - 1)
+    add_power(modes - 1)
 
 
 def block_index(block, position, bits):
@@ -188,54 +219,73 @@
     blocks, rows = block_ref.shape[0], block_ref.shape[3]
     half = size // 2
     position = lax.axis_index("pos")
+
+    def spread_columns(slot, mode, parity):
+        for begin, lines in spans(half, CHUNK):
+            under = slice(half + begin, half + begin + CHUNK)
+            ratio = ratio_ref[slot, parity, lines]
+            far = far_refs[slot].at[mode, parity]
+            put_right(right_ref, 2 * slot + parity, begin, far[lines] * ratio)
+            put_right(right_ref, 2 * slot + parity, half + begin, far[under] * ratio)
+
+    def column_products(slot, parity):
+        which = 2 * slot + parity
+        middle_ref[which] = product(col_ref[2 * parity], right_ref[which])
+
+    def spread_rows(slot):
+        for begin, lines in spans(half, CHUNK // 2):
+            under = slice(half + begin, half + begin + CHUNK // 2)
+            for offset, sign in ((0, 1.0), (half, -1.0)):
+                real = middle_ref[2 * slot, lines] + sign * middle_ref[2 * slot + 1, lines]
+                imag = middle_ref[2 * slot, under] + sign * middle_ref[2 * slot + 1, under]
+                for parity in (0, 1):
+                    where = slice(parity * half, (parity + 1) * half)
+                    value = jnp.concatenate([real[:, where], imag[:, where]], 1)
+                    put_left(left_ref, 2 * slot + parity, offset + begin, value)
+
+    def row_products(slot, parity):
+        which = 2 * slot + parity
+        middle_ref[which] = product(left_ref[which], row_ref[2 * parity + 1])
+
+    def add_terms(slot, index, mode):
+        for begin, lines in spans(size, rows):
+            target = block_index(begin // rows, position, bits)
+            a, b = middle_ref[2 * slot, lines], middle_ref[2 * slot + 1, lines]
+            plus, minus = a + b, a - b
+            real = jnp.concatenate([plus[:, :half], minus[:, :half]], 1)
+            imag = jnp.concatenate([plus[:, half:], minus[:, half:]], 1)
+            probe_real, probe_imag = probe_ref[0, mode, lines], probe_ref[1, mode, lines]
+            patch_real, patch_imag = patch_refs[slot][0, lines], patch_refs[slot][1, lines]
+            grads = (
+                probe_real * real + probe_imag * imag,
+                probe_real * imag - probe_imag * real,
+            )
+            terms = (
+                patch_real * real + patch_imag * imag,
+                patch_real * imag - patch_imag * real,
+            )
+            for part in (0, 1):
+                if first and index == 0:
+                    grad_ref[slot, part, lines] = grads[part]
+                else:
+                    grad_ref[slot, part, lines] += grads[part]
+                if slot == 0:
+                    block_ref[target, index, part] = terms[part]
+                else:
+                    block_ref[target, index, part] += terms[part]
+
     for index, mode in enumerate(modes):
         for slot in range(slots):
-            for begin, lines in spans(half, CHUNK // 2):
-                under = slice(half + begin, half + begin + CHUNK // 2)
-                for parity in (0, 1):
-                    ratio = ratio_ref[slot, parity, lines]
-                    far = far_refs[slot].at[mode, parity]
-                    put_right(right_ref, parity, begin, far[lines] * ratio)
-                    put_right(right_ref, parity, half + begin, far[under] * ratio)
             for parity in (0, 1):
-                middle_ref[parity] = product(col_ref[2 * parity], right_ref[parity])
-            for begin, lines in spans(half, CHUNK // 2):
-                under = slice(half + begin, half + begin + CHUNK // 2)
-                for offset, sign in ((0, 1.0), (half, -1.0)):
-                    real = middle_ref[0, lines] + sign * middle_ref[1, lines]
-                    imag = middle_ref[0, under] + sign * middle_ref[1, under]
-                    for parity in (0, 1):
-                        where = slice(parity * half, (parity + 1) * half)
-                        value = jnp.concatenate([real[:, where], imag[:, where]], 1)
-                        put_left(left_ref, parity, offset + begin, value)
+                spread_columns(slot, mode, parity)
+                column_products(slot, parity)
+        for slot in range(slots):
+            spread_rows(slot)
+            if slot > 0:
+                add_terms(slot - 1, index, mode)
             for parity in (0, 1):
-                middle_ref[parity] = product(left_ref[parity], row_ref[2 * parity + 1])
-            for begin, lines in spans(size, rows):
-                target = block_index(begin // rows, position, bits)
-                a, b = middle_ref[0, lines], middle_ref[1, lines]
-                plus, minus = a + b, a - b
-                real = jnp.concatenate([plus[:, :half], minus[:, :half]], 1)
-                imag = jnp.concatenate([plus[:, half:], minus[:, half:]], 1)
-                probe_real, probe_imag = probe_ref[0, mode, lines], probe_ref[1, mode, lines]
-                patch_real, patch_imag = patch_refs[slot][0, lines], patch_refs[slot][1, lines]
-                grads = (
-                    probe_real * real + probe_imag * imag,
-                    probe_real * imag - probe_imag * real,
-                )
-                terms = (
-                    patch_real * real + patch_imag * imag,
-                    patch_real * imag - patch_imag * real,
-                )
-                for part in (0, 1):
-                    if first and index == 0:
-                        grad_ref[slot, part, lines] = grads[part]
-                    else:
-                        grad_ref[slot, part, lines] += grads[part]
-                    if slot == 0:
-                        block_ref[target, index, part] = terms[part]
-                    else:
-                        block_ref[target, index, part] += terms[part]
-
+                row_products(slot, parity)
+        add_terms(slots - 1, index, mode)
 
 def strip_kernel(offset_ref, grad_ref, keep_ref, send_ref, spread):
     slots, _, size, _ = grad_ref.shape
@@ -282,6 +332,10 @@
             mode += 1
 
 
+def pick_kernel(part_ref, out_ref):
+    out_ref[...] = part_ref[...]
+
+
 def call(kernel, out_shape, scalars, arrays, name, **options):
     smem = pl.BlockSpec(memory_space=pltpu.SMEM)
     vmem = pl.BlockSpec(memory_space=pltpu.VMEM)
@@ -316,13 +370,13 @@
     following += [(target, source) for source, target in following]
     tables = [jnp.asarray(table) for table in real_tables(size)]
     scratch = [
-        pltpu.VMEM((2, size, 3 * size), BF16),
-        pltpu.VMEM((2, 3 * size, size), BF16),
-        pltpu.VMEM((2, size, size), F32),
+        pltpu.VMEM((4, size, 3 * size), BF16),
+        pltpu.VMEM((4, 3 * size, size), BF16),
+        pltpu.VMEM((4, size, size), F32),
     ]
 
     component = lax.dynamic_index_in_dim(object_field, tile, 0, keepdims=False)
-    halo = [lax.ppermute(component, "pos", ring) for ring in (pair, following)]
+    from_pair = lax.ppermute(component, "pos", pair)
 
     pixel_lines = size * size // 128
     share = pixel_lines // positions * modes
@@ -345,9 +399,11 @@
         [measured, jnp.asarray(np.stack([order, order.T]))],
         "order",
     )
-    from_pair, probe_grid = lax.optimization_barrier((halo[0], probe_grid))
+    (again,) = call(pick_kernel, (shape(strip_rows, columns),), [], [component], "pick")
+    from_next = lax.ppermute(again, "pos", following)
+    from_pair, probe_grid = lax.optimization_barrier((from_pair, probe_grid))
     pair_other = lax.ppermute(from_pair, "tile", swap)
-    from_next, pair_other = lax.optimization_barrier((halo[1], pair_other))
+    from_next, pair_other = lax.optimization_barrier((from_next, pair_other))
     halo = [from_pair, from_next, pair_other, lax.ppermute(from_next, "tile", swap)]
 
     far, power, patch = [], [], []

time: 64.9 us -> 60.2 us (0.928)
  starting transfers between devices: 27.5 us -> 24.2 us
  Pallas kernels: 14.6 us -> 12.5 us
  waiting for transfers between devices: 18 us -> 18.7 us
    ppermute x2, starting transfers between devices: 6.46 us -> 3.67 us  [the longest x1 3 us: on_device(): from_pair = lax.ppermute(component, 'pos', pair)]
    ppermute x12, waiting for transfers between devices: 12.6 us -> 15.3 us  [on_device(): lax.ppermute(send, 'pos', [(i, i ^ 2 ** bit) for i in range(positions)])]
    pallas_call x10 -> x11, Pallas kernels: 14.6 us -> 12.5 us  [call(): pl.pallas_call(kernel, out_shape=out_shape, in_specs=[smem] * len(scalars...]
    ppermute x2, waiting for transfers between devices: 2.82 us -> 0.79 us  [the longest x1 0.79 us: on_device(): from_pair = lax.ppermute(component, 'pos', pair)]
    ppermute x12, starting transfers between devices: 16.8 us -> 16 us  [on_device(): lax.ppermute(send, 'pos', [(i, i ^ 2 ** bit) for i in range(positions)])]
  transfers between devices with their start and end apart: 21 -> 21, of which waited for: 9 -> 10; matrix products, arithmetic and copies ran while one was open for 1% -> 1% of each run, Pallas kernels for 14% -> 13%
where the time goes in v4:
time: 60.2 us; the launch traced here: 60 us
  starting transfers between devices  24.2 us (40%)
  waiting for transfers between devices  18.7 us (31%)
  Pallas kernels  12.5 us (21%)
  local copies, waits for them, and re-layouts  2.72 us (5%)
  between operations  1.62 us (3%)
    ppermute x12, starting transfers between devices, on_device(): lax.ppermute(send, 'pos', [(i, i ^ 2 ** bit) for i in range(positions)])  16 us
    ppermute x12, waiting for transfers between devices, on_device(): lax.ppermute(send, 'pos', [(i, i ^ 2 ** bit) for i in range(positions)])  15.3 us
    pallas_call x11, Pallas kernels, call(): pl.pallas_call(kernel, out_shape=out_shape, in_specs=[smem] * len(scalars...  12.5 us
    ppermute x1, starting transfers between devices, on_device(): from_pair = lax.ppermute(strips[0], 'pos', pair)  3.13 us
    ppermute x1, starting transfers between devices, on_device(): from_pair = lax.ppermute(component, 'pos', pair)  3 us
    unnamed x14, local copies, waits for them, and re-layouts  1.61 us
    ppermute x1, waiting for transfers between devices, on_device(): pair_other = lax.ppermute(from_pair, 'tile', swap)  1.34 us
  transfers between devices with their start and end apart: 21, of which 10 were waited for; matrix products, arithmetic and copies ran while one was open for 1% of the time, Pallas kernels for 13%

profile of v4, /device:TPU:0, one launch (start us, length us, event | category | flops | bytes accessed | tf_op | source)
XLA Modules:
  0.0 60.0 jit_solution(7453651572082319767)
XLA Ops:
  0.6 0.9 %dynamic-slice_bitcast_fusion.part_ref = f32[128,256]{1,0:T(8,128)S(1)} fusion(f32[2,128,256]{2,1,0:T(8,128)} %strip_ref.1, s32[]{:T(128)S(6)} %select_n.4), kind=kLoop, calls=%fused_computation.11 | loop fusion | bytes 262148 | tf_op jit(solution)/shard_map/jit(dynamic_index_in_dim)/squeeze | solution.py:378
  1.6 3.0 %collective-permute-start = (f32[128,256]{1,0:T(8,128)S(1)}, f32[128,256]{1,0:T(8,128)S(1)}, u32[]{:S(2)}, u32[]{:S(2)}) collective-permute-start(f32[128,256]{1,0:T(8,128)S(1)} %dynamic-slice_bitcast_fusion.part_ref), channel_id=1, source_target_pairs={{0,2},{2,0},{4,6},{6,4},{8,10},{10,8},{12,14},{14,12},{1,3},{3,1},... | collective-permute-start | bytes 393224 | tf_op jit(solution)/shard_map/ppermute | solution.py:379
  4.6 0.7 %collective-permute-start.1 = (f32[128,256]{1,0:T(8,128)S(1)}, f32[128,256]{1,0:T(8,128)S(1)}, u32[]{:S(2)}, u32[]{:S(2)}) collective-permute-start(f32[128,256]{1,0:T(8,128)S(1)} %pick.1), channel_id=1, source_target_pairs={{2,4},{6,8},{10,12},{4,2},{8,6},{12,10},{3,5},{7,9},{11,13},{5,3},... | collective-permute-start | bytes 393224 | tf_op jit(solution)/shard_map/ppermute | solution.py:403
  5.3 1.6 %copy-done.3 = f32[2,4,65536]{2,1,0:T(4,128)S(1)} copy-done((f32[2,4,65536]{2,1,0:T(4,128)S(1)}, f32[2,4,65536]{2,1,0:T(4,128)}, u32[]{:S(2)}) %copy-start.3) | copy-done | bytes 2097176
  7.3 0.8 %collective-permute-done.pair_ref = f32[128,256]{1,0:T(8,128)S(1)} collective-permute-done((f32[128,256]{1,0:T(8,128)S(1)}, f32[128,256]{1,0:T(8,128)S(1)}, u32[]{:S(2)}, u32[]{:S(2)}) %collective-permute-start) | collective-permute-done | bytes 131104 | tf_op jit(solution)/shard_map/ppermute | solution.py:379
  8.1 1.3 %collective-permute-done.2.pair_other_ref = f32[128,256]{1,0:T(8,128)S(1)} collective-permute-done((f32[128,256]{1,0:T(8,128)S(1)}, f32[128,256]{1,0:T(8,128)S(1)}, u32[]{:S(2)}, u32[]{:S(2)}) %collective-permute-start.2) | collective-permute-done | bytes 131104 | tf_op jit(solution)/shard_map/ppermute | solution.py:405
  9.6 1.2 %collective-permute-done.3.next_other_ref = f32[128,256]{1,0:T(8,128)S(1)} collective-permute-done((f32[128,256]{1,0:T(8,128)S(1)}, f32[128,256]{1,0:T(8,128)S(1)}, u32[]{:S(2)}, u32[]{:S(2)}) %collective-permute-start.3) | collective-permute-done | bytes 131104 | tf_op jit(solution)/shard_map/ppermute | solution.py:407
  10.8 2.3 %forward.3 = (f32[4,2,256,256]{3,2,1,0:T(8,128)S(1)}, f32[2,128,256]{2,1,0:T(8,128)S(1)}, f32[2,256,256]{2,1,0:T(8,128)S(1)}) custom-call(s32[2,2]{1,0:T(2,128)S(1)} %copy-done.5, f32[2,128,256]{2,1,0:T(8,128)S(1)} %copy-done.2, f32[128,256]{1,0:T(8,128)S(1)} %collective-permute-done.pair_ref, f32[128,256]{1,0:T(8,128)S(1)} %collective-permute-done.1.next_ref, ...), custom_call_target="tpu_custom_call" | custom-call | flops 4000000000 | tf_op jit(solution)/shard_map/forward/pallas_call | solution.py:342
  13.3 2.3 %forward.2 = (f32[4,2,256,256]{3,2,1,0:T(8,128)S(1)}, f32[2,128,256]{2,1,0:T(8,128)S(1)}, f32[2,256,256]{2,1,0:T(8,128)S(1)}) custom-call(s32[2,2]{1,0:T(2,128)S(1)} %copy-done.5, f32[2,128,256]{2,1,0:T(8,128)S(1)} %copy-done.2, f32[128,256]{1,0:T(8,128)S(1)} %collective-permute-done.pair_ref, f32[128,256]{1,0:T(8,128)S(1)} %collective-permute-done.1.next_ref, ...), custom_call_target="tpu_custom_call" | custom-call | flops 4000000000 | tf_op jit(solution)/shard_map/forward/pallas_call | solution.py:342
  16.7 0.9 %order.1.refs_8_ = f32[2,2,128,256]{3,2,1,0:T(8,128)S(1)} custom-call(f32[2,256,256]{2,1,0:T(8,128)S(1)} %copy-done.4, bf16[2,256,256]{2,1,0:T(8,128)(2,1)S(1)} %copy-done.6), custom_call_target="tpu_custom_call" | custom-call | flops 1000000000 | tf_op jit(solution)/shard_map/order/pallas_call | solution.py:342
  17.7 1.4 %inverse.4 = (f32[2,2,256,256]{3,2,1,0:T(8,128)S(1)}, f32[8,1,2,32,256]{4,3,2,1,0:T(8,128)S(1)}, f32[2,2,128,256]{3,2,1,0:T(8,128)S(1)}) custom-call(s32[1]{0:T(128)S(6)} %copy.18.refs_0_, bf16[4,768,256]{2,1,0:T(8,128)(2,1)S(1)} %copy-done.1, bf16[4,256,768]{2,1,0:T(8,128)(2,1)S(1)} %copy-done, ...), custom_call_target="tpu_custom_call" | custom-call | flops 2400000000 | tf_op jit(solution)/shard_map/inverse/pallas_call | solution.py:342
  19.1 4.6 %collective-permute-start.9 = (f32[4,1,2,32,256]{4,3,2,1,0:T(8,128)S(1)}, f32[4,1,2,32,256]{4,3,2,1,0:T(8,128)S(1)}, u32[]{:S(2)}, u32[]{:S(2)}) collective-permute-start(f32[4,1,2,32,256]{4,3,2,1,0:T(8,128)S(1)} %split.73), channel_id=1, source_target_pairs={{0,4},{2,6},{4,0},{6,2},{8,12},{10,14},{12,8},{14,10},{1,5},{3,7},... | collective-permute-start | bytes 786440 | tf_op jit(solution)/shard_map/ppermute | solution.py:478
  23.7 1.2 %inverse.5 = (f32[2,2,256,256]{3,2,1,0:T(8,128)S(1)}, f32[8,1,2,32,256]{4,3,2,1,0:T(8,128)S(1)}) custom-call(bf16[4,768,256]{2,1,0:T(8,128)(2,1)S(1)} %copy-done.1, bf16[4,256,768]{2,1,0:T(8,128)(2,1)S(1)} %copy-done, f32[2,4,256,256]{3,2,1,0:T(8,128)S(1)} %get-tuple-element.29.probe_ref.refs_3_.refs_2_, ...), custom_call_target="tpu_custom_call", output_to_operand_aliasing={{0}: (7, {})} | custom-call | flops 2400000000 | tf_op jit(solution)/shard_map/inverse/pallas_call | solution.py:342
  25.0 0.7 %collective-permute-start.12 = (f32[4,1,2,32,256]{4,3,2,1,0:T(8,128)S(1)}, f32[4,1,2,32,256]{4,3,2,1,0:T(8,128)S(1)}, u32[]{:S(2)}, u32[]{:S(2)}) collective-permute-start(f32[4,1,2,32,256]{4,3,2,1,0:T(8,128)S(1)} %split.79), channel_id=1, source_target_pairs={{0,2},{2,0},{4,6},{6,4},{8,10},{10,8},{12,14},{14,12},{1,3},{3,1},... | collective-permute-start | bytes 786440 | tf_op jit(solution)/shard_map/ppermute | solution.py:478
  25.7 1.2 %inverse.6 = (f32[2,2,256,256]{3,2,1,0:T(8,128)S(1)}, f32[8,1,2,32,256]{4,3,2,1,0:T(8,128)S(1)}) custom-call(bf16[4,768,256]{2,1,0:T(8,128)(2,1)S(1)} %copy-done.1, bf16[4,256,768]{2,1,0:T(8,128)(2,1)S(1)} %copy-done, f32[2,4,256,256]{3,2,1,0:T(8,128)S(1)} %get-tuple-element.29.probe_ref.refs_3_.refs_2_, ...), custom_call_target="tpu_custom_call", output_to_operand_aliasing={{0}: (7, {})} | custom-call | flops 2400000000 | tf_op jit(solution)/shard_map/inverse/pallas_call | solution.py:342
  26.9 1.2 %inverse.7 = (f32[2,2,256,256]{3,2,1,0:T(8,128)S(1)}, f32[8,1,2,32,256]{4,3,2,1,0:T(8,128)S(1)}) custom-call(bf16[4,768,256]{2,1,0:T(8,128)(2,1)S(1)} %copy-done.1, bf16[4,256,768]{2,1,0:T(8,128)(2,1)S(1)} %copy-done, f32[2,4,256,256]{3,2,1,0:T(8,128)S(1)} %get-tuple-element.29.probe_ref.refs_3_.refs_2_, ...), custom_call_target="tpu_custom_call", output_to_operand_aliasing={{0}: (7, {})} | custom-call | flops 2400000000 | tf_op jit(solution)/shard_map/inverse/pallas_call | solution.py:342
  28.1 0.6 strips.1
  29.3 1.0 %collective-permute-start.18 = (f32[4,1,2,32,256]{4,3,2,1,0:T(8,128)S(1)}, f32[4,1,2,32,256]{4,3,2,1,0:T(8,128)S(1)}, u32[]{:S(2)}, u32[]{:S(2)}) collective-permute-start(f32[4,1,2,32,256]{4,3,2,1,0:T(8,128)S(1)} %split.91), channel_id=1, source_target_pairs={{0,2},{2,0},{4,6},{6,4},{8,10},{10,8},{12,14},{14,12},{1,3},{3,1},... | collective-permute-start | bytes 786440 | tf_op jit(solution)/shard_map/ppermute | solution.py:478
  30.4 1.1 %collective-permute-start.10 = (f32[2,1,2,32,256]{4,3,2,1,0:T(8,128)S(1)}, f32[2,1,2,32,256]{4,3,2,1,0:T(8,128)S(1)}, u32[]{:S(2)}, u32[]{:S(2)}) collective-permute-start(f32[2,1,2,32,256]{4,3,2,1,0:T(8,128)S(1)} %split.97), channel_id=1, source_target_pairs={{0,2},{2,0},{4,6},{6,4},{8,10},{10,8},{12,14},{14,12},{1,3},{3,1},... | collective-permute-start | bytes 393224 | tf_op jit(solution)/shard_map/ppermute | solution.py:478
  31.5 2.8 %collective-permute-done.12 = f32[4,1,2,32,256]{4,3,2,1,0:T(8,128)S(1)} collective-permute-done((f32[4,1,2,32,256]{4,3,2,1,0:T(8,128)S(1)}, f32[4,1,2,32,256]{4,3,2,1,0:T(8,128)S(1)}, u32[]{:S(2)}, u32[]{:S(2)}) %collective-permute-start.12) | collective-permute-done | bytes 262176 | tf_op jit(solution)/shard_map/ppermute | solution.py:478
  34.4 3.7 %collective-permute-done.15 = f32[4,1,2,32,256]{4,3,2,1,0:T(8,128)S(1)} collective-permute-done((f32[4,1,2,32,256]{4,3,2,1,0:T(8,128)S(1)}, f32[4,1,2,32,256]{4,3,2,1,0:T(8,128)S(1)}, u32[]{:S(2)}, u32[]{:S(2)}) %collective-permute-start.15) | collective-permute-done | bytes 262176 | tf_op jit(solution)/shard_map/ppermute | solution.py:478
  38.1 1.5 %collective-permute-start.16 = (f32[2,1,2,32,256]{4,3,2,1,0:T(8,128)S(1)}, f32[2,1,2,32,256]{4,3,2,1,0:T(8,128)S(1)}, u32[]{:S(2)}, u32[]{:S(2)}) collective-permute-start(f32[2,1,2,32,256]{4,3,2,1,0:T(8,128)S(1)} %split.105), channel_id=1, source_target_pairs={{0,2},{2,0},{4,6},{6,4},{8,10},{10,8},{12,14},{14,12},{1,3},{3,1},... | collective-permute-start | bytes 393224 | tf_op jit(solution)/shard_map/ppermute | solution.py:478
  40.2 2.4 %collective-permute-done.10 = f32[2,1,2,32,256]{4,3,2,1,0:T(8,128)S(1)} collective-permute-done((f32[2,1,2,32,256]{4,3,2,1,0:T(8,128)S(1)}, f32[2,1,2,32,256]{4,3,2,1,0:T(8,128)S(1)}, u32[]{:S(2)}, u32[]{:S(2)}) %collective-permute-start.10) | collective-permute-done | bytes 131104 | tf_op jit(solution)/shard_map/ppermute | solution.py:478
  42.7 2.7 %collective-permute-start.11 = (f32[1,1,2,32,256]{4,3,2,1,0:T(8,128)S(1)}, f32[1,1,2,32,256]{4,3,2,1,0:T(8,128)S(1)}, u32[]{:S(2)}, u32[]{:S(2)}) collective-permute-start(f32[1,1,2,32,256]{4,3,2,1,0:T(8,128)S(1)} %get-tuple-element.61), channel_id=1, source_target_pairs={{0,8},{2,10},{4,12},{6,14},{8,0},{10,2},{12,4},{14,6},{1,9},{3,11}... | collective-permute-start | bytes 196616 | tf_op jit(solution)/shard_map/ppermute | solution.py:478
  45.8 2.7 %collective-permute-start.17 = (f32[1,1,2,32,256]{4,3,2,1,0:T(8,128)S(1)}, f32[1,1,2,32,256]{4,3,2,1,0:T(8,128)S(1)}, u32[]{:S(2)}, u32[]{:S(2)}) collective-permute-start(f32[1,1,2,32,256]{4,3,2,1,0:T(8,128)S(1)} %get-tuple-element.57), channel_id=1, source_target_pairs={{0,8},{2,10},{4,12},{6,14},{8,0},{10,2},{12,4},{14,6},{1,9},{3,11}... | collective-permute-start | bytes 196616 | tf_op jit(solution)/shard_map/ppermute | solution.py:478
  48.6 0.7 %collective-permute-start.8 = (f32[2,64,256]{2,1,0:T(8,128)S(1)}, f32[2,64,256]{2,1,0:T(8,128)S(1)}, u32[]{:S(2)}, u32[]{:S(2)}) collective-permute-start(f32[2,64,256]{2,1,0:T(8,128)S(1)} %get-tuple-element.52), channel_id=1, source_target_pairs={{2,4},{6,8},{10,12},{4,2},{8,6},{12,10},{3,5},{7,9},{11,13},{5,3},... | collective-permute-start | bytes 393224 | tf_op jit(solution)/shard_map/ppermute | solution.py:468
  49.3 3.1 %collective-permute-start.7 = (f32[2,64,256]{2,1,0:T(8,128)S(1)}, f32[2,64,256]{2,1,0:T(8,128)S(1)}, u32[]{:S(2)}, u32[]{:S(2)}) collective-permute-start(f32[2,64,256]{2,1,0:T(8,128)S(1)} %get-tuple-element.53), channel_id=1, source_target_pairs={{0,2},{2,0},{4,6},{6,4},{8,10},{10,8},{12,14},{14,12},{1,3},{3,1},... | collective-permute-start | bytes 393224 | tf_op jit(solution)/shard_map/ppermute | solution.py:467
  52.5 0.5 collective-permute-start.20
  53.0 0.9 %collective-permute-done.14 = f32[1,1,2,32,256]{4,3,2,1,0:T(8,128)S(1)} collective-permute-done((f32[1,1,2,32,256]{4,3,2,1,0:T(8,128)S(1)}, f32[1,1,2,32,256]{4,3,2,1,0:T(8,128)S(1)}, u32[]{:S(2)}, u32[]{:S(2)}) %collective-permute-start.14) | collective-permute-done | bytes 65568 | tf_op jit(solution)/shard_map/ppermute | solution.py:478
  53.9 1.4 %collective-permute-done.17 = f32[1,1,2,32,256]{4,3,2,1,0:T(8,128)S(1)} collective-permute-done((f32[1,1,2,32,256]{4,3,2,1,0:T(8,128)S(1)}, f32[1,1,2,32,256]{4,3,2,1,0:T(8,128)S(1)}, u32[]{:S(2)}, u32[]{:S(2)}) %collective-permute-start.17) | collective-permute-done | bytes 65568 | tf_op jit(solution)/shard_map/ppermute | solution.py:478
  55.3 3.9 %collective-permute-done.20 = f32[1,1,2,32,256]{4,3,2,1,0:T(8,128)S(1)} collective-permute-done((f32[1,1,2,32,256]{4,3,2,1,0:T(8,128)S(1)}, f32[1,1,2,32,256]{4,3,2,1,0:T(8,128)S(1)}, u32[]{:S(2)}, u32[]{:S(2)}) %collective-permute-start.20) | collective-permute-done | bytes 65568 | tf_op jit(solution)/shard_map/ppermute | solution.py:478
  59.1 0.9 %finish.1 = (f32[2,64,256]{2,1,0:T(8,128)}, f32[2,256,128]{2,1,0:T(8,128)}) custom-call(f32[2,256,128]{2,1,0:T(8,128)S(1)} %get-tuple-element.27.probe_ref, f32[2,128,256]{2,1,0:T(8,128)S(1)} %copy-done.2, f32[2,64,256]{2,1,0:T(8,128)S(1)} %get-tuple-element.54.mid_ref, f32[2,64,256]{2,1,0:T(8,128)S(1)} %collective-permute-done.7.pair_ref, ...), custom_call_target="tpu_custom_call" | custom-call | flops 1000000000 | tf_op jit(solution)/shard_map/finish/pallas_call | solution.py:342
  (58 shorter events, 3.3 us)
Async XLA Ops:
  1.6 6.5 %collective-permute-start = (f32[128,256]{1,0:T(8,128)S(1)}, f32[128,256]{1,0:T(8,128)S(1)}, u32[]{:S(2)}, u32[]{:S(2)}) collective-permute-start(f32[128,256]{1,0:T(8,128)S(1)} %dynamic-slice_bitcast_fusion.part_ref), channel_id=1, source_target_pairs={{0,2},{2,0},{4,6},{6,4},{8,10},{10,8},{12,14},{14,12},{1,3},{3,1},... | collective-permute-start | bytes 393224 | tf_op jit(solution)/shard_map/ppermute | solution.py:379
  4.6 3.5 %collective-permute-start.1 = (f32[128,256]{1,0:T(8,128)S(1)}, f32[128,256]{1,0:T(8,128)S(1)}, u32[]{:S(2)}, u32[]{:S(2)}) collective-permute-start(f32[128,256]{1,0:T(8,128)S(1)} %pick.1), channel_id=1, source_target_pairs={{2,4},{6,8},{10,12},{4,2},{8,6},{12,10},{3,5},{7,9},{11,13},{5,3},... | collective-permute-start | bytes 393224 | tf_op jit(solution)/shard_map/ppermute | solution.py:403
  5.2 1.6 %copy-start.3 = (f32[2,4,65536]{2,1,0:T(4,128)S(1)}, f32[2,4,65536]{2,1,0:T(4,128)}, u32[]{:S(2)}) copy-start(f32[2,4,65536]{2,1,0:T(4,128)} %param.9) | copy-start | bytes 6291460
  6.8 3.9 %copy-start = (bf16[4,256,768]{2,1,0:T(8,128)(2,1)S(1)}, bf16[4,256,768]{2,1,0:T(8,128)(2,1)}, u32[]{:S(2)}) copy-start(bf16[4,256,768]{2,1,0:T(8,128)(2,1)} %constant.17.clone.col_ref.refs_2_.refs_1_) | copy-start | bytes 4718596
  6.8 3.9 %copy-start.1 = (bf16[4,768,256]{2,1,0:T(8,128)(2,1)S(1)}, bf16[4,768,256]{2,1,0:T(8,128)(2,1)}, u32[]{:S(2)}) copy-start(bf16[4,768,256]{2,1,0:T(8,128)(2,1)} %constant.16.clone.row_ref.refs_1_.refs_0_) | copy-start | bytes 4718596
  6.8 3.9 %copy-start.2 = (f32[2,128,256]{2,1,0:T(8,128)S(1)}, f32[2,128,256]{2,1,0:T(8,128)}, u32[]{:S(2)}) copy-start(f32[2,128,256]{2,1,0:T(8,128)} %strip_ref.1) | copy-start | bytes 786436
  6.8 3.9 %copy-start.5 = (s32[2,2]{1,0:T(2,128)S(1)}, s32[2,2]{1,0:T(2,128)}, u32[]{:S(2)}) copy-start(s32[2,2]{1,0:T(2,128)} %offset_ref.5) | copy-start | bytes 52
  8.1 1.3 %collective-permute-start.2 = (f32[128,256]{1,0:T(8,128)S(1)}, f32[128,256]{1,0:T(8,128)S(1)}, u32[]{:S(2)}, u32[]{:S(2)}) collective-permute-start(f32[128,256]{1,0:T(8,128)S(1)} %collective-permute-done.pair_ref), channel_id=1, source_target_pairs={{0,1},{1,0},{2,3},{3,2},{4,5},{5,4},{6,7},{7,6},{8,9},{9,8},{10,11... | collective-permute-start | bytes 393224 | tf_op jit(solution)/shard_map/ppermute | solution.py:405
  9.4 1.3 %collective-permute-start.3 = (f32[128,256]{1,0:T(8,128)S(1)}, f32[128,256]{1,0:T(8,128)S(1)}, u32[]{:S(2)}, u32[]{:S(2)}) collective-permute-start(f32[128,256]{1,0:T(8,128)S(1)} %collective-permute-done.1.next_ref), channel_id=1, source_target_pairs={{0,1},{1,0},{2,3},{3,2},{4,5},{5,4},{6,7},{7,6},{8,9},{9,8},{10,11... | collective-permute-start | bytes 393224 | tf_op jit(solution)/shard_map/ppermute | solution.py:407
  13.1 3.6 %copy-start.4 = (f32[2,256,256]{2,1,0:T(8,128)S(1)}, f32[2,256,256]{2,1,0:T(8,128)}, u32[]{:S(2)}) copy-start(f32[2,256,256]{2,1,0:T(8,128)} %measured_ref.1) | copy-start | bytes 1572868
  13.1 3.6 %copy-start.6 = (bf16[2,256,256]{2,1,0:T(8,128)(2,1)S(1)}, bf16[2,256,256]{2,1,0:T(8,128)(2,1)}, u32[]{:S(2)}) copy-start(bf16[2,256,256]{2,1,0:T(8,128)(2,1)} %constant.18.clone.order_ref) | copy-start | bytes 786436
  13.1 4.6 %collective-permute-start.5 = (f32[2,128,256]{2,1,0:T(8,128)S(1)}, f32[2,128,256]{2,1,0:T(8,128)S(1)}, u32[]{:S(2)}, u32[]{:S(2)}) collective-permute-start(f32[2,128,256]{2,1,0:T(8,128)S(1)} %get-tuple-element.38.refs_10_), channel_id=1, source_target_pairs={{0,1},{1,0},{2,3},{3,2},{4,5},{5,4},{6,7},{7,6},{8,9},{9,8},{10,11... | collective-permute-start | bytes 786440 | tf_op jit(solution)/shard_map/ppermute | solution.py:422
  15.6 2.1 %collective-permute-start.4 = (f32[2,128,256]{2,1,0:T(8,128)S(1)}, f32[2,128,256]{2,1,0:T(8,128)S(1)}, u32[]{:S(2)}, u32[]{:S(2)}) collective-permute-start(f32[2,128,256]{2,1,0:T(8,128)S(1)} %get-tuple-element.37.refs_9_), channel_id=1, source_target_pairs={{0,1},{1,0},{2,3},{3,2},{4,5},{5,4},{6,7},{7,6},{8,9},{9,8},{10,11... | collective-permute-start | bytes 786440 | tf_op jit(solution)/shard_map/ppermute | solution.py:422
  19.1 11.2 %collective-permute-start.9 = (f32[4,1,2,32,256]{4,3,2,1,0:T(8,128)S(1)}, f32[4,1,2,32,256]{4,3,2,1,0:T(8,128)S(1)}, u32[]{:S(2)}, u32[]{:S(2)}) collective-permute-start(f32[4,1,2,32,256]{4,3,2,1,0:T(8,128)S(1)} %split.73), channel_id=1, source_target_pairs={{0,4},{2,6},{4,0},{6,2},{8,12},{10,14},{12,8},{14,10},{1,5},{3,7},... | collective-permute-start | bytes 786440 | tf_op jit(solution)/shard_map/ppermute | solution.py:478
  25.0 9.3 %collective-permute-start.12 = (f32[4,1,2,32,256]{4,3,2,1,0:T(8,128)S(1)}, f32[4,1,2,32,256]{4,3,2,1,0:T(8,128)S(1)}, u32[]{:S(2)}, u32[]{:S(2)}) collective-permute-start(f32[4,1,2,32,256]{4,3,2,1,0:T(8,128)S(1)} %split.79), channel_id=1, source_target_pairs={{0,2},{2,0},{4,6},{6,4},{8,10},{10,8},{12,14},{14,12},{1,3},{3,1},... | collective-permute-start | bytes 786440 | tf_op jit(solution)/shard_map/ppermute | solution.py:478
  28.8 9.3 %collective-permute-start.15 = (f32[4,1,2,32,256]{4,3,2,1,0:T(8,128)S(1)}, f32[4,1,2,32,256]{4,3,2,1,0:T(8,128)S(1)}, u32[]{:S(2)}, u32[]{:S(2)}) collective-permute-start(f32[4,1,2,32,256]{4,3,2,1,0:T(8,128)S(1)} %split.85), channel_id=1, source_target_pairs={{0,4},{2,6},{4,0},{6,2},{8,12},{10,14},{12,8},{14,10},{1,5},{3,7},... | collective-permute-start | bytes 786440 | tf_op jit(solution)/shard_map/ppermute | solution.py:478
  29.3 10.5 %collective-permute-start.18 = (f32[4,1,2,32,256]{4,3,2,1,0:T(8,128)S(1)}, f32[4,1,2,32,256]{4,3,2,1,0:T(8,128)S(1)}, u32[]{:S(2)}, u32[]{:S(2)}) collective-permute-start(f32[4,1,2,32,256]{4,3,2,1,0:T(8,128)S(1)} %split.91), channel_id=1, source_target_pairs={{0,2},{2,0},{4,6},{6,4},{8,10},{10,8},{12,14},{14,12},{1,3},{3,1},... | collective-permute-start | bytes 786440 | tf_op jit(solution)/shard_map/ppermute | solution.py:478
  30.3 18.2 %collective-permute-start.6 = (f32[3,2,64,256]{3,2,1,0:T(8,128)S(1)}, f32[3,2,64,256]{3,2,1,0:T(8,128)S(1)}, u32[]{:S(2)}, u32[]{:S(2)}) collective-permute-start(f32[3,2,64,256]{3,2,1,0:T(8,128)S(1)} %get-tuple-element.45), channel_id=1, source_target_pairs={{0,1},{1,0},{2,3},{3,2},{4,5},{5,4},{6,7},{7,6},{8,9},{9,8},{10,11... | collective-permute-start | bytes 1179656 | tf_op jit(solution)/shard_map/ppermute | solution.py:466
  30.4 12.3 %collective-permute-start.10 = (f32[2,1,2,32,256]{4,3,2,1,0:T(8,128)S(1)}, f32[2,1,2,32,256]{4,3,2,1,0:T(8,128)S(1)}, u32[]{:S(2)}, u32[]{:S(2)}) collective-permute-start(f32[2,1,2,32,256]{4,3,2,1,0:T(8,128)S(1)} %split.97), channel_id=1, source_target_pairs={{0,2},{2,0},{4,6},{6,4},{8,10},{10,8},{12,14},{14,12},{1,3},{3,1},... | collective-permute-start | bytes 393224 | tf_op jit(solution)/shard_map/ppermute | solution.py:478
  34.3 11.1 %collective-permute-start.13 = (f32[2,1,2,32,256]{4,3,2,1,0:T(8,128)S(1)}, f32[2,1,2,32,256]{4,3,2,1,0:T(8,128)S(1)}, u32[]{:S(2)}, u32[]{:S(2)}) collective-permute-start(f32[2,1,2,32,256]{4,3,2,1,0:T(8,128)S(1)} %split.101), channel_id=1, source_target_pairs={{0,4},{2,6},{4,0},{6,2},{8,12},{10,14},{12,8},{14,10},{1,5},{3,7},... | collective-permute-start | bytes 393224 | tf_op jit(solution)/shard_map/ppermute | solution.py:478
  38.1 7.7 %collective-permute-start.16 = (f32[2,1,2,32,256]{4,3,2,1,0:T(8,128)S(1)}, f32[2,1,2,32,256]{4,3,2,1,0:T(8,128)S(1)}, u32[]{:S(2)}, u32[]{:S(2)}) collective-permute-start(f32[2,1,2,32,256]{4,3,2,1,0:T(8,128)S(1)} %split.105), channel_id=1, source_target_pairs={{0,2},{2,0},{4,6},{6,4},{8,10},{10,8},{12,14},{14,12},{1,3},{3,1},... | collective-permute-start | bytes 393224 | tf_op jit(solution)/shard_map/ppermute | solution.py:478
  39.9 9.4 %collective-permute-start.19 = (f32[2,1,2,32,256]{4,3,2,1,0:T(8,128)S(1)}, f32[2,1,2,32,256]{4,3,2,1,0:T(8,128)S(1)}, u32[]{:S(2)}, u32[]{:S(2)}) collective-permute-start(f32[2,1,2,32,256]{4,3,2,1,0:T(8,128)S(1)} %split.109), channel_id=1, source_target_pairs={{0,4},{2,6},{4,0},{6,2},{8,12},{10,14},{12,8},{14,10},{1,5},{3,7},... | collective-permute-start | bytes 393224 | tf_op jit(solution)/shard_map/ppermute | solution.py:478
  42.7 9.8 %collective-permute-start.11 = (f32[1,1,2,32,256]{4,3,2,1,0:T(8,128)S(1)}, f32[1,1,2,32,256]{4,3,2,1,0:T(8,128)S(1)}, u32[]{:S(2)}, u32[]{:S(2)}) collective-permute-start(f32[1,1,2,32,256]{4,3,2,1,0:T(8,128)S(1)} %get-tuple-element.61), channel_id=1, source_target_pairs={{0,8},{2,10},{4,12},{6,14},{8,0},{10,2},{12,4},{14,6},{1,9},{3,11}... | collective-permute-start | bytes 196616 | tf_op jit(solution)/shard_map/ppermute | solution.py:478
  45.4 8.5 %collective-permute-start.14 = (f32[1,1,2,32,256]{4,3,2,1,0:T(8,128)S(1)}, f32[1,1,2,32,256]{4,3,2,1,0:T(8,128)S(1)}, u32[]{:S(2)}, u32[]{:S(2)}) collective-permute-start(f32[1,1,2,32,256]{4,3,2,1,0:T(8,128)S(1)} %get-tuple-element.59), channel_id=1, source_target_pairs={{0,8},{2,10},{4,12},{6,14},{8,0},{10,2},{12,4},{14,6},{1,9},{3,11}... | collective-permute-start | bytes 196616 | tf_op jit(solution)/shard_map/ppermute | solution.py:478
  45.8 9.4 %collective-permute-start.17 = (f32[1,1,2,32,256]{4,3,2,1,0:T(8,128)S(1)}, f32[1,1,2,32,256]{4,3,2,1,0:T(8,128)S(1)}, u32[]{:S(2)}, u32[]{:S(2)}) collective-permute-start(f32[1,1,2,32,256]{4,3,2,1,0:T(8,128)S(1)} %get-tuple-element.57), channel_id=1, source_target_pairs={{0,8},{2,10},{4,12},{6,14},{8,0},{10,2},{12,4},{14,6},{1,9},{3,11}... | collective-permute-start | bytes 196616 | tf_op jit(solution)/shard_map/ppermute | solution.py:478
  48.6 10.5 %collective-permute-start.8 = (f32[2,64,256]{2,1,0:T(8,128)S(1)}, f32[2,64,256]{2,1,0:T(8,128)S(1)}, u32[]{:S(2)}, u32[]{:S(2)}) collective-permute-start(f32[2,64,256]{2,1,0:T(8,128)S(1)} %get-tuple-element.52), channel_id=1, source_target_pairs={{2,4},{6,8},{10,12},{4,2},{8,6},{12,10},{3,5},{7,9},{11,13},{5,3},... | collective-permute-start | bytes 393224 | tf_op jit(solution)/shard_map/ppermute | solution.py:468
  49.3 9.9 %collective-permute-start.7 = (f32[2,64,256]{2,1,0:T(8,128)S(1)}, f32[2,64,256]{2,1,0:T(8,128)S(1)}, u32[]{:S(2)}, u32[]{:S(2)}) collective-permute-start(f32[2,64,256]{2,1,0:T(8,128)S(1)} %get-tuple-element.53), channel_id=1, source_target_pairs={{0,2},{2,0},{4,6},{6,4},{8,10},{10,8},{12,14},{14,12},{1,3},{3,1},... | collective-permute-start | bytes 393224 | tf_op jit(solution)/shard_map/ppermute | solution.py:467
  52.5 6.7 %collective-permute-start.20 = (f32[1,1,2,32,256]{4,3,2,1,0:T(8,128)S(1)}, f32[1,1,2,32,256]{4,3,2,1,0:T(8,128)S(1)}, u32[]{:S(2)}, u32[]{:S(2)}) collective-permute-start(f32[1,1,2,32,256]{4,3,2,1,0:T(8,128)S(1)} %get-tuple-element.55), channel_id=1, source_target_pairs={{0,8},{2,10},{4,12},{6,14},{8,0},{10,2},{12,4},{14,6},{1,9},{3,11}... | collective-permute-start | bytes 196616 | tf_op jit(solution)/shard_map/ppermute | solution.py:478

commit v5 on v4

--- a/solution.py
+++ b/solution.py
@@ -19,8 +19,8 @@
 VMEM_LIMIT = 16 * 1024 * 1024
 COSTS = {'prepare': 2000000000, 'forward': 4000000000, 'inverse': 2400000000, 'strips': 1200000000, 'finish': 1000000000, 'order': 1000000000, 'pick': 1000000}
 CHUNK = 64
-TIE = None
-GROUPS = ((1, (1, 0, 2)), (1, (0, 1, 2)), (1, (1, 0, 2)), (1, (0, 1, 2)))
+PATTERN = (0, 1, 0, 1)
+STEPS = (((0,), 1), ((1,), 0), ((2,), 1), ((3,), 0), ((0,), 0), ((1,), 1), ((2,), 0), ((3,), 1), ((0, 1), 2), ((2, 3), 2))
 
 
 def real_tables(size):
@@ -423,25 +423,22 @@
 
     block_rows = size // positions
     bit_count = positions.bit_length() - 1
-    pending = []
-    begin = 0
-    for group, bits in GROUPS:
-        bits = [*bits, *range(len(bits), bit_count)]
-        first = begin == 0
-        kernel = functools.partial(
-            inverse_kernel, tuple(range(begin, begin + group)), bits, first, slots
-        )
-        outs = (shape(slots, 2, size, size), shape(positions, group, 2, block_rows, size))
+    later = list(range(2, bit_count))
+    grad, blocks = None, []
+    for mode in range(modes):
+        bits = [(1, 0), (0, 1)][PATTERN[mode % 4]]
+        kernel = functools.partial(inverse_kernel, (mode,), [*bits, *later], mode == 0, slots)
+        outs = (shape(slots, 2, size, size), shape(positions, 1, 2, block_rows, size))
         arrays = [*tables, probe_grid, *far, *patch]
-        if first:
+        if mode == 0:
             outs += (shape(slots, 2, half, size),)
             arrays += [amplitude, *power, *others]
-            grad, blocks, ratio = call(
+            grad, terms, ratio = call(
                 kernel, outs, [counts], arrays, "inverse", scratch_shapes=scratch
             )
         else:
             arrays += [grad, ratio]
-            grad, blocks = call(
+            grad, terms = call(
                 kernel,
                 outs,
                 [],
@@ -450,8 +447,7 @@
                 input_output_aliases={len(arrays) - 2: 0},
                 scratch_shapes=scratch,
             )
-        begin += group
-        pending.append((bits, blocks))
+        blocks.append(jnp.split(terms, 2))
 
     half_rows = strip_rows // tiles
     strip_shape = shape(3, parts, half_rows, columns)
@@ -464,23 +460,30 @@
         scratch_shapes=[pltpu.VMEM((slots, parts, 2 * strip_rows + size + 8, columns), F32)],
     )
     strips = kept + lax.ppermute(sent, "tile", swap)
+    def exchange(bit, *sends):
+        payload = sends[0] if len(sends) == 1 else jnp.concatenate(sends, 0)
+        got = lax.ppermute(payload, "pos", [(i, i ^ 2**bit) for i in range(positions)])
+        ends = np.cumsum([send.shape[0] for send in sends])
+        return [got[end - send.shape[0] : end] for send, end in zip(sends, ends)]
+
+    def advance(modes_at, bit):
+        gots = exchange(bit, *(blocks[mode][1] for mode in modes_at))
+        for mode, got in zip(modes_at, gots):
+            keep = blocks[mode][0]
+            blocks[mode] = jnp.split(keep + got, 2) if keep.shape[0] > 1 else [keep, got]
+
+    for modes_at, bit in STEPS:
+        if modes_at == "tie":
+            blocks[bit], strips = lax.optimization_barrier((blocks[bit], strips))
+            continue
+        for now in [bit] if bit < 2 else later:
+            advance(modes_at, now)
     from_pair = lax.ppermute(strips[0], "pos", pair)
     from_next = lax.ppermute(strips[1], "pos", following)
-
-    sums = []
-    for which, (bits, blocks) in enumerate(pending):
-        for step, bit in enumerate(bits):
-            if TIE and (which, step) == TIE:
-                blocks, from_pair, from_next = lax.optimization_barrier(
-                    (blocks, from_pair, from_next)
-                )
-            keep, send = jnp.split(blocks, 2)
-            got = lax.ppermute(send, "pos", [(i, i ^ 2**bit) for i in range(positions)])
-            blocks = keep + got
-        sums.append([keep[0], got[0]])
+    sums = [[keep[0], got[0]] for keep, got in blocks]
 
     object_out, probe_out = call(
-        functools.partial(finish_kernel, [(group, 2) for group, _ in GROUPS]),
+        functools.partial(finish_kernel, [(1, 2)] * modes),
         (shape(parts, half_rows, columns), shape(parts, share, 128)),
         [],
         [probe_own, object_field, strips[2], from_pair, from_next, *sum(sums, [])],

time: 60.2 us -> 57.9 us (0.962)
  waiting for transfers between devices: 18.7 us -> 16.6 us
    ppermute x12 -> x10, waiting for transfers between devices: 15.3 us -> 13.3 us  [exchange(): lax.ppermute(payload, 'pos', [(i, i ^ 2 ** bit) for i in range(positions)])]
    ppermute x12 -> x10, starting transfers between devices: 16 us -> 14.5 us  [exchange(): lax.ppermute(payload, 'pos', [(i, i ^ 2 ** bit) for i in range(positions)])]
    ppermute x1, starting transfers between devices: 3.13 us -> 4.18 us  [on_device(): from_pair = lax.ppermute(strips[0], 'pos', pair)]
  transfers between devices with their start and end apart: 21 -> 19, of which waited for: 10 -> 9; matrix products, arithmetic and copies ran while one was open for 1% -> 1% of each run, Pallas kernels for 13% -> 14%
where the time goes in v5:
time: 57.9 us; the launch traced here: 57.7 us
  starting transfers between devices  23.8 us (41%)
  waiting for transfers between devices  16.6 us (29%)
  Pallas kernels  12.5 us (22%)
  local copies, waits for them, and re-layouts  2.74 us (5%)
  between operations  1.67 us (3%)
    ppermute x10, starting transfers between devices, exchange(): lax.ppermute(payload, 'pos', [(i, i ^ 2 ** bit) for i in range(positions)])  14.5 us
    ppermute x10, waiting for transfers between devices, exchange(): lax.ppermute(payload, 'pos', [(i, i ^ 2 ** bit) for i in range(positions)])  13.3 us
    pallas_call x11, Pallas kernels, call(): pl.pallas_call(kernel, out_shape=out_shape, in_specs=[smem] * len(scalars...  12.5 us
    ppermute x1, starting transfers between devices, on_device(): from_pair = lax.ppermute(strips[0], 'pos', pair)  4.18 us
    ppermute x1, starting transfers between devices, on_device(): from_pair = lax.ppermute(component, 'pos', pair)  3 us
    unnamed x14, local copies, waits for them, and re-layouts  1.61 us
    ppermute x1, waiting for transfers between devices, on_device(): pair_other = lax.ppermute(from_pair, 'tile', swap)  1.34 us
    ppermute x1, waiting for transfers between devices, on_device(): lax.ppermute(from_next, 'tile', swap)  1.2 us
  transfers between devices with their start and end apart: 19, of which 9 were waited for; matrix products, arithmetic and copies ran while one was open for 1% of the time, Pallas kernels for 14%

profile of v5, /device:TPU:0, one launch (start us, length us, event | category | flops | bytes accessed | tf_op | source)
XLA Modules:
  0.0 57.7 jit_solution(14544443095070540904)
XLA Ops:
  0.6 0.9 %dynamic-slice_bitcast_fusion.part_ref = f32[128,256]{1,0:T(8,128)S(1)} fusion(f32[2,128,256]{2,1,0:T(8,128)} %strip_ref.1, s32[]{:T(128)S(6)} %select_n.4), kind=kLoop, calls=%fused_computation.13 | loop fusion | bytes 262148 | tf_op jit(solution)/shard_map/jit(dynamic_index_in_dim)/squeeze | solution.py:378
  1.6 3.0 %collective-permute-start = (f32[128,256]{1,0:T(8,128)S(1)}, f32[128,256]{1,0:T(8,128)S(1)}, u32[]{:S(2)}, u32[]{:S(2)}) collective-permute-start(f32[128,256]{1,0:T(8,128)S(1)} %dynamic-slice_bitcast_fusion.part_ref), channel_id=1, source_target_pairs={{0,2},{2,0},{4,6},{6,4},{8,10},{10,8},{12,14},{14,12},{1,3},{3,1},... | collective-permute-start | bytes 393224 | tf_op jit(solution)/shard_map/ppermute | solution.py:379
  4.6 0.7 %collective-permute-start.1 = (f32[128,256]{1,0:T(8,128)S(1)}, f32[128,256]{1,0:T(8,128)S(1)}, u32[]{:S(2)}, u32[]{:S(2)}) collective-permute-start(f32[128,256]{1,0:T(8,128)S(1)} %pick.1), channel_id=1, source_target_pairs={{2,4},{6,8},{10,12},{4,2},{8,6},{12,10},{3,5},{7,9},{11,13},{5,3},... | collective-permute-start | bytes 393224 | tf_op jit(solution)/shard_map/ppermute | solution.py:403
  5.3 1.6 %copy-done.3 = f32[2,4,65536]{2,1,0:T(4,128)S(1)} copy-done((f32[2,4,65536]{2,1,0:T(4,128)S(1)}, f32[2,4,65536]{2,1,0:T(4,128)}, u32[]{:S(2)}) %copy-start.3) | copy-done | bytes 2097176
  7.3 0.8 %collective-permute-done.pair_ref = f32[128,256]{1,0:T(8,128)S(1)} collective-permute-done((f32[128,256]{1,0:T(8,128)S(1)}, f32[128,256]{1,0:T(8,128)S(1)}, u32[]{:S(2)}, u32[]{:S(2)}) %collective-permute-start) | collective-permute-done | bytes 131104 | tf_op jit(solution)/shard_map/ppermute | solution.py:379
  8.1 1.3 %collective-permute-done.2.pair_other_ref = f32[128,256]{1,0:T(8,128)S(1)} collective-permute-done((f32[128,256]{1,0:T(8,128)S(1)}, f32[128,256]{1,0:T(8,128)S(1)}, u32[]{:S(2)}, u32[]{:S(2)}) %collective-permute-start.2) | collective-permute-done | bytes 131104 | tf_op jit(solution)/shard_map/ppermute | solution.py:405
  9.6 1.2 %collective-permute-done.3.next_other_ref = f32[128,256]{1,0:T(8,128)S(1)} collective-permute-done((f32[128,256]{1,0:T(8,128)S(1)}, f32[128,256]{1,0:T(8,128)S(1)}, u32[]{:S(2)}, u32[]{:S(2)}) %collective-permute-start.3) | collective-permute-done | bytes 131104 | tf_op jit(solution)/shard_map/ppermute | solution.py:407
  10.8 2.3 %forward.3 = (f32[4,2,256,256]{3,2,1,0:T(8,128)S(1)}, f32[2,128,256]{2,1,0:T(8,128)S(1)}, f32[2,256,256]{2,1,0:T(8,128)S(1)}) custom-call(s32[2,2]{1,0:T(2,128)S(1)} %copy-done.5, f32[2,128,256]{2,1,0:T(8,128)S(1)} %copy-done.2, f32[128,256]{1,0:T(8,128)S(1)} %collective-permute-done.pair_ref, f32[128,256]{1,0:T(8,128)S(1)} %collective-permute-done.1.next_ref, ...), custom_call_target="tpu_custom_call" | custom-call | flops 4000000000 | tf_op jit(solution)/shard_map/forward/pallas_call | solution.py:342
  13.3 2.3 %forward.2 = (f32[4,2,256,256]{3,2,1,0:T(8,128)S(1)}, f32[2,128,256]{2,1,0:T(8,128)S(1)}, f32[2,256,256]{2,1,0:T(8,128)S(1)}) custom-call(s32[2,2]{1,0:T(2,128)S(1)} %copy-done.5, f32[2,128,256]{2,1,0:T(8,128)S(1)} %copy-done.2, f32[128,256]{1,0:T(8,128)S(1)} %collective-permute-done.pair_ref, f32[128,256]{1,0:T(8,128)S(1)} %collective-permute-done.1.next_ref, ...), custom_call_target="tpu_custom_call" | custom-call | flops 4000000000 | tf_op jit(solution)/shard_map/forward/pallas_call | solution.py:342
  15.6 0.4 collective-permute-start.4
  16.7 0.9 %order.1.refs_8_ = f32[2,2,128,256]{3,2,1,0:T(8,128)S(1)} custom-call(f32[2,256,256]{2,1,0:T(8,128)S(1)} %copy-done.4, bf16[2,256,256]{2,1,0:T(8,128)(2,1)S(1)} %copy-done.6), custom_call_target="tpu_custom_call" | custom-call | flops 1000000000 | tf_op jit(solution)/shard_map/order/pallas_call | solution.py:342
  17.7 1.4 %inverse.4 = (f32[2,2,256,256]{3,2,1,0:T(8,128)S(1)}, f32[8,1,2,32,256]{4,3,2,1,0:T(8,128)S(1)}, f32[2,2,128,256]{3,2,1,0:T(8,128)S(1)}) custom-call(s32[1]{0:T(128)S(6)} %copy.18.refs_0_, bf16[4,768,256]{2,1,0:T(8,128)(2,1)S(1)} %copy-done.1, bf16[4,256,768]{2,1,0:T(8,128)(2,1)S(1)} %copy-done, ...), custom_call_target="tpu_custom_call" | custom-call | flops 2400000000 | tf_op jit(solution)/shard_map/inverse/pallas_call | solution.py:342
  19.1 4.6 %collective-permute-start.9 = (f32[4,1,2,32,256]{4,3,2,1,0:T(8,128)S(1)}, f32[4,1,2,32,256]{4,3,2,1,0:T(8,128)S(1)}, u32[]{:S(2)}, u32[]{:S(2)}) collective-permute-start(f32[4,1,2,32,256]{4,3,2,1,0:T(8,128)S(1)} %split.73), channel_id=1, source_target_pairs={{0,4},{2,6},{4,0},{6,2},{8,12},{10,14},{12,8},{14,10},{1,5},{3,7},... | collective-permute-start | bytes 786440 | tf_op jit(solution)/shard_map/ppermute | solution.py:465
  23.7 1.2 %inverse.5 = (f32[2,2,256,256]{3,2,1,0:T(8,128)S(1)}, f32[8,1,2,32,256]{4,3,2,1,0:T(8,128)S(1)}) custom-call(bf16[4,768,256]{2,1,0:T(8,128)(2,1)S(1)} %copy-done.1, bf16[4,256,768]{2,1,0:T(8,128)(2,1)S(1)} %copy-done, f32[2,4,256,256]{3,2,1,0:T(8,128)S(1)} %get-tuple-element.29.probe_ref.refs_3_.refs_2_, ...), custom_call_target="tpu_custom_call", output_to_operand_aliasing={{0}: (7, {})} | custom-call | flops 2400000000 | tf_op jit(solution)/shard_map/inverse/pallas_call | solution.py:342
  25.0 0.7 %collective-permute-start.11 = (f32[4,1,2,32,256]{4,3,2,1,0:T(8,128)S(1)}, f32[4,1,2,32,256]{4,3,2,1,0:T(8,128)S(1)}, u32[]{:S(2)}, u32[]{:S(2)}) collective-permute-start(f32[4,1,2,32,256]{4,3,2,1,0:T(8,128)S(1)} %split.79), channel_id=1, source_target_pairs={{0,2},{2,0},{4,6},{6,4},{8,10},{10,8},{12,14},{14,12},{1,3},{3,1},... | collective-permute-start | bytes 786440 | tf_op jit(solution)/shard_map/ppermute | solution.py:465
  25.7 1.2 %inverse.6 = (f32[2,2,256,256]{3,2,1,0:T(8,128)S(1)}, f32[8,1,2,32,256]{4,3,2,1,0:T(8,128)S(1)}) custom-call(bf16[4,768,256]{2,1,0:T(8,128)(2,1)S(1)} %copy-done.1, bf16[4,256,768]{2,1,0:T(8,128)(2,1)S(1)} %copy-done, f32[2,4,256,256]{3,2,1,0:T(8,128)S(1)} %get-tuple-element.29.probe_ref.refs_3_.refs_2_, ...), custom_call_target="tpu_custom_call", output_to_operand_aliasing={{0}: (7, {})} | custom-call | flops 2400000000 | tf_op jit(solution)/shard_map/inverse/pallas_call | solution.py:342
  26.9 1.2 %inverse.7 = (f32[2,2,256,256]{3,2,1,0:T(8,128)S(1)}, f32[8,1,2,32,256]{4,3,2,1,0:T(8,128)S(1)}) custom-call(bf16[4,768,256]{2,1,0:T(8,128)(2,1)S(1)} %copy-done.1, bf16[4,256,768]{2,1,0:T(8,128)(2,1)S(1)} %copy-done, f32[2,4,256,256]{3,2,1,0:T(8,128)S(1)} %get-tuple-element.29.probe_ref.refs_3_.refs_2_, ...), custom_call_target="tpu_custom_call", output_to_operand_aliasing={{0}: (7, {})} | custom-call | flops 2400000000 | tf_op jit(solution)/shard_map/inverse/pallas_call | solution.py:342
  28.1 0.6 %strips.1 = (f32[3,2,64,256]{3,2,1,0:T(8,128)S(1)}, f32[3,2,64,256]{3,2,1,0:T(8,128)S(1)}) custom-call(s32[2,2]{1,0:T(2,128)S(1)} %copy-done.5, f32[2,2,256,256]{3,2,1,0:T(8,128)S(1)} %get-tuple-element.43.grad_ref), custom_call_target="tpu_custom_call" | custom-call | flops 1200000000 | tf_op jit(solution)/shard_map/strips/pallas_call | solution.py:342
  28.8 0.5 collective-permute-start.14
  29.3 1.0 %collective-permute-start.16 = (f32[4,1,2,32,256]{4,3,2,1,0:T(8,128)S(1)}, f32[4,1,2,32,256]{4,3,2,1,0:T(8,128)S(1)}, u32[]{:S(2)}, u32[]{:S(2)}) collective-permute-start(f32[4,1,2,32,256]{4,3,2,1,0:T(8,128)S(1)} %split.91), channel_id=1, source_target_pairs={{0,2},{2,0},{4,6},{6,4},{8,10},{10,8},{12,14},{14,12},{1,3},{3,1},... | collective-permute-start | bytes 786440 | tf_op jit(solution)/shard_map/ppermute | solution.py:465
  30.4 1.1 %collective-permute-start.10 = (f32[2,1,2,32,256]{4,3,2,1,0:T(8,128)S(1)}, f32[2,1,2,32,256]{4,3,2,1,0:T(8,128)S(1)}, u32[]{:S(2)}, u32[]{:S(2)}) collective-permute-start(f32[2,1,2,32,256]{4,3,2,1,0:T(8,128)S(1)} %split.97), channel_id=1, source_target_pairs={{0,2},{2,0},{4,6},{6,4},{8,10},{10,8},{12,14},{14,12},{1,3},{3,1},... | collective-permute-start | bytes 393224 | tf_op jit(solution)/shard_map/ppermute | solution.py:465
  31.5 2.8 %collective-permute-done.11 = f32[4,1,2,32,256]{4,3,2,1,0:T(8,128)S(1)} collective-permute-done((f32[4,1,2,32,256]{4,3,2,1,0:T(8,128)S(1)}, f32[4,1,2,32,256]{4,3,2,1,0:T(8,128)S(1)}, u32[]{:S(2)}, u32[]{:S(2)}) %collective-permute-start.11) | collective-permute-done | bytes 262176 | tf_op jit(solution)/shard_map/ppermute | solution.py:465
  34.4 3.7 %collective-permute-done.14 = f32[4,1,2,32,256]{4,3,2,1,0:T(8,128)S(1)} collective-permute-done((f32[4,1,2,32,256]{4,3,2,1,0:T(8,128)S(1)}, f32[4,1,2,32,256]{4,3,2,1,0:T(8,128)S(1)}, u32[]{:S(2)}, u32[]{:S(2)}) %collective-permute-start.14) | collective-permute-done | bytes 262176 | tf_op jit(solution)/shard_map/ppermute | solution.py:465
  38.1 1.5 %collective-permute-start.15 = (f32[2,1,2,32,256]{4,3,2,1,0:T(8,128)S(1)}, f32[2,1,2,32,256]{4,3,2,1,0:T(8,128)S(1)}, u32[]{:S(2)}, u32[]{:S(2)}) collective-permute-start(f32[2,1,2,32,256]{4,3,2,1,0:T(8,128)S(1)} %split.105), channel_id=1, source_target_pairs={{0,2},{2,0},{4,6},{6,4},{8,10},{10,8},{12,14},{14,12},{1,3},{3,1},... | collective-permute-start | bytes 393224 | tf_op jit(solution)/shard_map/ppermute | solution.py:465
  40.2 2.4 %collective-permute-done.10 = f32[2,1,2,32,256]{4,3,2,1,0:T(8,128)S(1)} collective-permute-done((f32[2,1,2,32,256]{4,3,2,1,0:T(8,128)S(1)}, f32[2,1,2,32,256]{4,3,2,1,0:T(8,128)S(1)}, u32[]{:S(2)}, u32[]{:S(2)}) %collective-permute-start.10) | collective-permute-done | bytes 131104 | tf_op jit(solution)/shard_map/ppermute | solution.py:465
  42.8 2.7 %collective-permute-start.13 = (f32[2,1,2,32,256]{4,3,2,1,0:T(8,128)S(1)}, f32[2,1,2,32,256]{4,3,2,1,0:T(8,128)S(1)}, u32[]{:S(2)}, u32[]{:S(2)}) collective-permute-start(f32[2,1,2,32,256]{4,3,2,1,0:T(8,128)S(1)} %pad_maximum_fusion), channel_id=1, source_target_pairs={{0,8},{2,10},{4,12},{6,14},{8,0},{10,2},{12,4},{14,6},{1,9},{3,11}... | collective-permute-start | bytes 393224 | tf_op jit(solution)/shard_map/ppermute | solution.py:465
  45.5 2.1 %collective-permute-start.18 = (f32[2,1,2,32,256]{4,3,2,1,0:T(8,128)S(1)}, f32[2,1,2,32,256]{4,3,2,1,0:T(8,128)S(1)}, u32[]{:S(2)}, u32[]{:S(2)}) collective-permute-start(f32[2,1,2,32,256]{4,3,2,1,0:T(8,128)S(1)} %pad_maximum_fusion.1), channel_id=1, source_target_pairs={{0,8},{2,10},{4,12},{6,14},{8,0},{10,2},{12,4},{14,6},{1,9},{3,11}... | collective-permute-start | bytes 393224 | tf_op jit(solution)/shard_map/ppermute | solution.py:465
  47.8 0.7 %collective-permute-start.8 = (f32[2,64,256]{2,1,0:T(8,128)S(1)}, f32[2,64,256]{2,1,0:T(8,128)S(1)}, u32[]{:S(2)}, u32[]{:S(2)}) collective-permute-start(f32[2,64,256]{2,1,0:T(8,128)S(1)} %get-tuple-element.52), channel_id=1, source_target_pairs={{2,4},{6,8},{10,12},{4,2},{8,6},{12,10},{3,5},{7,9},{11,13},{5,3},... | collective-permute-start | bytes 393224 | tf_op jit(solution)/shard_map/ppermute | solution.py:482
  48.4 4.2 %collective-permute-start.7 = (f32[2,64,256]{2,1,0:T(8,128)S(1)}, f32[2,64,256]{2,1,0:T(8,128)S(1)}, u32[]{:S(2)}, u32[]{:S(2)}) collective-permute-start(f32[2,64,256]{2,1,0:T(8,128)S(1)} %get-tuple-element.53), channel_id=1, source_target_pairs={{0,2},{2,0},{4,6},{6,4},{8,10},{10,8},{12,14},{14,12},{1,3},{3,1},... | collective-permute-start | bytes 393224 | tf_op jit(solution)/shard_map/ppermute | solution.py:481
  52.6 1.4 %collective-permute-done.13 = f32[2,1,2,32,256]{4,3,2,1,0:T(8,128)S(1)} collective-permute-done((f32[2,1,2,32,256]{4,3,2,1,0:T(8,128)S(1)}, f32[2,1,2,32,256]{4,3,2,1,0:T(8,128)S(1)}, u32[]{:S(2)}, u32[]{:S(2)}) %collective-permute-start.13) | collective-permute-done | bytes 131104 | tf_op jit(solution)/shard_map/ppermute | solution.py:465
  54.0 2.8 %collective-permute-done.18 = f32[2,1,2,32,256]{4,3,2,1,0:T(8,128)S(1)} collective-permute-done((f32[2,1,2,32,256]{4,3,2,1,0:T(8,128)S(1)}, f32[2,1,2,32,256]{4,3,2,1,0:T(8,128)S(1)}, u32[]{:S(2)}, u32[]{:S(2)}) %collective-permute-start.18) | collective-permute-done | bytes 131104 | tf_op jit(solution)/shard_map/ppermute | solution.py:465
  56.8 0.9 %finish.1 = (f32[2,64,256]{2,1,0:T(8,128)}, f32[2,256,128]{2,1,0:T(8,128)}) custom-call(f32[2,256,128]{2,1,0:T(8,128)S(1)} %get-tuple-element.27.probe_ref, f32[2,128,256]{2,1,0:T(8,128)S(1)} %copy-done.2, f32[2,64,256]{2,1,0:T(8,128)S(1)} %get-tuple-element.54.mid_ref, f32[2,64,256]{2,1,0:T(8,128)S(1)} %collective-permute-done.7.pair_ref, ...), custom_call_target="tpu_custom_call" | custom-call | flops 1000000000 | tf_op jit(solution)/shard_map/finish/pallas_call | solution.py:342
  (58 shorter events, 2.0 us)
Async XLA Ops:
  1.6 6.5 %collective-permute-start = (f32[128,256]{1,0:T(8,128)S(1)}, f32[128,256]{1,0:T(8,128)S(1)}, u32[]{:S(2)}, u32[]{:S(2)}) collective-permute-start(f32[128,256]{1,0:T(8,128)S(1)} %dynamic-slice_bitcast_fusion.part_ref), channel_id=1, source_target_pairs={{0,2},{2,0},{4,6},{6,4},{8,10},{10,8},{12,14},{14,12},{1,3},{3,1},... | collective-permute-start | bytes 393224 | tf_op jit(solution)/shard_map/ppermute | solution.py:379
  4.6 3.5 %collective-permute-start.1 = (f32[128,256]{1,0:T(8,128)S(1)}, f32[128,256]{1,0:T(8,128)S(1)}, u32[]{:S(2)}, u32[]{:S(2)}) collective-permute-start(f32[128,256]{1,0:T(8,128)S(1)} %pick.1), channel_id=1, source_target_pairs={{2,4},{6,8},{10,12},{4,2},{8,6},{12,10},{3,5},{7,9},{11,13},{5,3},... | collective-permute-start | bytes 393224 | tf_op jit(solution)/shard_map/ppermute | solution.py:403
  5.2 1.6 %copy-start.3 = (f32[2,4,65536]{2,1,0:T(4,128)S(1)}, f32[2,4,65536]{2,1,0:T(4,128)}, u32[]{:S(2)}) copy-start(f32[2,4,65536]{2,1,0:T(4,128)} %param.9) | copy-start | bytes 6291460
  6.8 3.9 %copy-start = (bf16[4,256,768]{2,1,0:T(8,128)(2,1)S(1)}, bf16[4,256,768]{2,1,0:T(8,128)(2,1)}, u32[]{:S(2)}) copy-start(bf16[4,256,768]{2,1,0:T(8,128)(2,1)} %constant.17.clone.col_ref.refs_2_.refs_1_) | copy-start | bytes 4718596
  6.8 3.9 %copy-start.1 = (bf16[4,768,256]{2,1,0:T(8,128)(2,1)S(1)}, bf16[4,768,256]{2,1,0:T(8,128)(2,1)}, u32[]{:S(2)}) copy-start(bf16[4,768,256]{2,1,0:T(8,128)(2,1)} %constant.16.clone.row_ref.refs_1_.refs_0_) | copy-start | bytes 4718596
  6.8 3.9 %copy-start.2 = (f32[2,128,256]{2,1,0:T(8,128)S(1)}, f32[2,128,256]{2,1,0:T(8,128)}, u32[]{:S(2)}) copy-start(f32[2,128,256]{2,1,0:T(8,128)} %strip_ref.1) | copy-start | bytes 786436
  6.8 3.9 %copy-start.5 = (s32[2,2]{1,0:T(2,128)S(1)}, s32[2,2]{1,0:T(2,128)}, u32[]{:S(2)}) copy-start(s32[2,2]{1,0:T(2,128)} %offset_ref.5) | copy-start | bytes 52
  8.1 1.3 %collective-permute-start.2 = (f32[128,256]{1,0:T(8,128)S(1)}, f32[128,256]{1,0:T(8,128)S(1)}, u32[]{:S(2)}, u32[]{:S(2)}) collective-permute-start(f32[128,256]{1,0:T(8,128)S(1)} %collective-permute-done.pair_ref), channel_id=1, source_target_pairs={{0,1},{1,0},{2,3},{3,2},{4,5},{5,4},{6,7},{7,6},{8,9},{9,8},{10,11... | collective-permute-start | bytes 393224 | tf_op jit(solution)/shard_map/ppermute | solution.py:405
  9.4 1.3 %collective-permute-start.3 = (f32[128,256]{1,0:T(8,128)S(1)}, f32[128,256]{1,0:T(8,128)S(1)}, u32[]{:S(2)}, u32[]{:S(2)}) collective-permute-start(f32[128,256]{1,0:T(8,128)S(1)} %collective-permute-done.1.next_ref), channel_id=1, source_target_pairs={{0,1},{1,0},{2,3},{3,2},{4,5},{5,4},{6,7},{7,6},{8,9},{9,8},{10,11... | collective-permute-start | bytes 393224 | tf_op jit(solution)/shard_map/ppermute | solution.py:407
  13.1 3.6 %copy-start.4 = (f32[2,256,256]{2,1,0:T(8,128)S(1)}, f32[2,256,256]{2,1,0:T(8,128)}, u32[]{:S(2)}) copy-start(f32[2,256,256]{2,1,0:T(8,128)} %measured_ref.1) | copy-start | bytes 1572868
  13.1 3.6 %copy-start.6 = (bf16[2,256,256]{2,1,0:T(8,128)(2,1)S(1)}, bf16[2,256,256]{2,1,0:T(8,128)(2,1)}, u32[]{:S(2)}) copy-start(bf16[2,256,256]{2,1,0:T(8,128)(2,1)} %constant.18.clone.order_ref) | copy-start | bytes 786436
  13.1 4.6 %collective-permute-start.5 = (f32[2,128,256]{2,1,0:T(8,128)S(1)}, f32[2,128,256]{2,1,0:T(8,128)S(1)}, u32[]{:S(2)}, u32[]{:S(2)}) collective-permute-start(f32[2,128,256]{2,1,0:T(8,128)S(1)} %get-tuple-element.38.refs_10_), channel_id=1, source_target_pairs={{0,1},{1,0},{2,3},{3,2},{4,5},{5,4},{6,7},{7,6},{8,9},{9,8},{10,11... | collective-permute-start | bytes 786440 | tf_op jit(solution)/shard_map/ppermute | solution.py:422
  15.6 2.1 %collective-permute-start.4 = (f32[2,128,256]{2,1,0:T(8,128)S(1)}, f32[2,128,256]{2,1,0:T(8,128)S(1)}, u32[]{:S(2)}, u32[]{:S(2)}) collective-permute-start(f32[2,128,256]{2,1,0:T(8,128)S(1)} %get-tuple-element.37.refs_9_), channel_id=1, source_target_pairs={{0,1},{1,0},{2,3},{3,2},{4,5},{5,4},{6,7},{7,6},{8,9},{9,8},{10,11... | collective-permute-start | bytes 786440 | tf_op jit(solution)/shard_map/ppermute | solution.py:422
  19.1 11.2 %collective-permute-start.9 = (f32[4,1,2,32,256]{4,3,2,1,0:T(8,128)S(1)}, f32[4,1,2,32,256]{4,3,2,1,0:T(8,128)S(1)}, u32[]{:S(2)}, u32[]{:S(2)}) collective-permute-start(f32[4,1,2,32,256]{4,3,2,1,0:T(8,128)S(1)} %split.73), channel_id=1, source_target_pairs={{0,4},{2,6},{4,0},{6,2},{8,12},{10,14},{12,8},{14,10},{1,5},{3,7},... | collective-permute-start | bytes 786440 | tf_op jit(solution)/shard_map/ppermute | solution.py:465
  25.0 9.3 %collective-permute-start.11 = (f32[4,1,2,32,256]{4,3,2,1,0:T(8,128)S(1)}, f32[4,1,2,32,256]{4,3,2,1,0:T(8,128)S(1)}, u32[]{:S(2)}, u32[]{:S(2)}) collective-permute-start(f32[4,1,2,32,256]{4,3,2,1,0:T(8,128)S(1)} %split.79), channel_id=1, source_target_pairs={{0,2},{2,0},{4,6},{6,4},{8,10},{10,8},{12,14},{14,12},{1,3},{3,1},... | collective-permute-start | bytes 786440 | tf_op jit(solution)/shard_map/ppermute | solution.py:465
  28.8 9.3 %collective-permute-start.14 = (f32[4,1,2,32,256]{4,3,2,1,0:T(8,128)S(1)}, f32[4,1,2,32,256]{4,3,2,1,0:T(8,128)S(1)}, u32[]{:S(2)}, u32[]{:S(2)}) collective-permute-start(f32[4,1,2,32,256]{4,3,2,1,0:T(8,128)S(1)} %split.85), channel_id=1, source_target_pairs={{0,4},{2,6},{4,0},{6,2},{8,12},{10,14},{12,8},{14,10},{1,5},{3,7},... | collective-permute-start | bytes 786440 | tf_op jit(solution)/shard_map/ppermute | solution.py:465
  29.3 10.5 %collective-permute-start.16 = (f32[4,1,2,32,256]{4,3,2,1,0:T(8,128)S(1)}, f32[4,1,2,32,256]{4,3,2,1,0:T(8,128)S(1)}, u32[]{:S(2)}, u32[]{:S(2)}) collective-permute-start(f32[4,1,2,32,256]{4,3,2,1,0:T(8,128)S(1)} %split.91), channel_id=1, source_target_pairs={{0,2},{2,0},{4,6},{6,4},{8,10},{10,8},{12,14},{14,12},{1,3},{3,1},... | collective-permute-start | bytes 786440 | tf_op jit(solution)/shard_map/ppermute | solution.py:465
  30.3 17.4 %collective-permute-start.6 = (f32[3,2,64,256]{3,2,1,0:T(8,128)S(1)}, f32[3,2,64,256]{3,2,1,0:T(8,128)S(1)}, u32[]{:S(2)}, u32[]{:S(2)}) collective-permute-start(f32[3,2,64,256]{3,2,1,0:T(8,128)S(1)} %get-tuple-element.45), channel_id=1, source_target_pairs={{0,1},{1,0},{2,3},{3,2},{4,5},{5,4},{6,7},{7,6},{8,9},{9,8},{10,11... | collective-permute-start | bytes 1179656 | tf_op jit(solution)/shard_map/ppermute | solution.py:462
  30.4 12.3 %collective-permute-start.10 = (f32[2,1,2,32,256]{4,3,2,1,0:T(8,128)S(1)}, f32[2,1,2,32,256]{4,3,2,1,0:T(8,128)S(1)}, u32[]{:S(2)}, u32[]{:S(2)}) collective-permute-start(f32[2,1,2,32,256]{4,3,2,1,0:T(8,128)S(1)} %split.97), channel_id=1, source_target_pairs={{0,2},{2,0},{4,6},{6,4},{8,10},{10,8},{12,14},{14,12},{1,3},{3,1},... | collective-permute-start | bytes 393224 | tf_op jit(solution)/shard_map/ppermute | solution.py:465
  34.3 8.4 %collective-permute-start.12 = (f32[2,1,2,32,256]{4,3,2,1,0:T(8,128)S(1)}, f32[2,1,2,32,256]{4,3,2,1,0:T(8,128)S(1)}, u32[]{:S(2)}, u32[]{:S(2)}) collective-permute-start(f32[2,1,2,32,256]{4,3,2,1,0:T(8,128)S(1)} %split.101), channel_id=1, source_target_pairs={{0,4},{2,6},{4,0},{6,2},{8,12},{10,14},{12,8},{14,10},{1,5},{3,7},... | collective-permute-start | bytes 393224 | tf_op jit(solution)/shard_map/ppermute | solution.py:465
  38.1 7.3 %collective-permute-start.15 = (f32[2,1,2,32,256]{4,3,2,1,0:T(8,128)S(1)}, f32[2,1,2,32,256]{4,3,2,1,0:T(8,128)S(1)}, u32[]{:S(2)}, u32[]{:S(2)}) collective-permute-start(f32[2,1,2,32,256]{4,3,2,1,0:T(8,128)S(1)} %split.105), channel_id=1, source_target_pairs={{0,2},{2,0},{4,6},{6,4},{8,10},{10,8},{12,14},{14,12},{1,3},{3,1},... | collective-permute-start | bytes 393224 | tf_op jit(solution)/shard_map/ppermute | solution.py:465
  39.9 5.6 %collective-permute-start.17 = (f32[2,1,2,32,256]{4,3,2,1,0:T(8,128)S(1)}, f32[2,1,2,32,256]{4,3,2,1,0:T(8,128)S(1)}, u32[]{:S(2)}, u32[]{:S(2)}) collective-permute-start(f32[2,1,2,32,256]{4,3,2,1,0:T(8,128)S(1)} %split.109), channel_id=1, source_target_pairs={{0,4},{2,6},{4,0},{6,2},{8,12},{10,14},{12,8},{14,10},{1,5},{3,7},... | collective-permute-start | bytes 393224 | tf_op jit(solution)/shard_map/ppermute | solution.py:465
  42.8 11.2 %collective-permute-start.13 = (f32[2,1,2,32,256]{4,3,2,1,0:T(8,128)S(1)}, f32[2,1,2,32,256]{4,3,2,1,0:T(8,128)S(1)}, u32[]{:S(2)}, u32[]{:S(2)}) collective-permute-start(f32[2,1,2,32,256]{4,3,2,1,0:T(8,128)S(1)} %pad_maximum_fusion), channel_id=1, source_target_pairs={{0,8},{2,10},{4,12},{6,14},{8,0},{10,2},{12,4},{14,6},{1,9},{3,11}... | collective-permute-start | bytes 393224 | tf_op jit(solution)/shard_map/ppermute | solution.py:465
  45.5 11.3 %collective-permute-start.18 = (f32[2,1,2,32,256]{4,3,2,1,0:T(8,128)S(1)}, f32[2,1,2,32,256]{4,3,2,1,0:T(8,128)S(1)}, u32[]{:S(2)}, u32[]{:S(2)}) collective-permute-start(f32[2,1,2,32,256]{4,3,2,1,0:T(8,128)S(1)} %pad_maximum_fusion.1), channel_id=1, source_target_pairs={{0,8},{2,10},{4,12},{6,14},{8,0},{10,2},{12,4},{14,6},{1,9},{3,11}... | collective-permute-start | bytes 393224 | tf_op jit(solution)/shard_map/ppermute | solution.py:465
  47.8 9.0 %collective-permute-start.8 = (f32[2,64,256]{2,1,0:T(8,128)S(1)}, f32[2,64,256]{2,1,0:T(8,128)S(1)}, u32[]{:S(2)}, u32[]{:S(2)}) collective-permute-start(f32[2,64,256]{2,1,0:T(8,128)S(1)} %get-tuple-element.52), channel_id=1, source_target_pairs={{2,4},{6,8},{10,12},{4,2},{8,6},{12,10},{3,5},{7,9},{11,13},{5,3},... | collective-permute-start | bytes 393224 | tf_op jit(solution)/shard_map/ppermute | solution.py:482
  48.4 8.4 %collective-permute-start.7 = (f32[2,64,256]{2,1,0:T(8,128)S(1)}, f32[2,64,256]{2,1,0:T(8,128)S(1)}, u32[]{:S(2)}, u32[]{:S(2)}) collective-permute-start(f32[2,64,256]{2,1,0:T(8,128)S(1)} %get-tuple-element.53), channel_id=1, source_target_pairs={{0,2},{2,0},{4,6},{6,4},{8,10},{10,8},{12,14},{14,12},{1,3},{3,1},... | collective-permute-start | bytes 393224 | tf_op jit(solution)/shard_map/ppermute | solution.py:481

commit v6 on v5

--- a/solution.py
+++ b/solution.py
@@ -17,10 +17,10 @@
 F32 = jnp.float32
 BF16 = jnp.bfloat16
 VMEM_LIMIT = 16 * 1024 * 1024
-COSTS = {'prepare': 2000000000, 'forward': 4000000000, 'inverse': 2400000000, 'strips': 1200000000, 'finish': 1000000000, 'order': 1000000000, 'pick': 1000000}
+COSTS = {'prepare': 2000000000, 'forward': 4000000000, 'inverse': 2400000000, 'strips': 1200000000, 'finish': 1000000000, 'order': 1000000000, 'pick': 3000000000}
 CHUNK = 64
-PATTERN = (0, 1, 0, 1)
-STEPS = (((0,), 1), ((1,), 0), ((2,), 1), ((3,), 0), ((0,), 0), ((1,), 1), ((2,), 0), ((3,), 1), ((0, 1), 2), ((2, 3), 2))
+PATTERN = (0, 1, 1, 0)
+STEPS = (((0,), 1), ((1,), 0), ((2,), 0), ((3,), 1), ((0,), 0), ((1,), 1), ((2,), 1), ((3,), 0), ((0, 1), 2), ((2, 3), 2))
 
 
 def real_tables(size):
@@ -198,32 +198,44 @@
     return index
 
 
-def inverse_kernel(modes, bits, first, slots, *refs):
-    if first:
-        count_ref, *refs = refs
-    row_ref, col_ref, probe_ref, *refs = refs
-    *refs, left_ref, right_ref, middle_ref = refs
-    far_refs, patch_refs = refs[:slots], refs[slots : 2 * slots]
-    refs = refs[2 * slots :]
-    if first:
-        amplitude_ref, power_refs = refs[0], refs[1 : 1 + slots]
-        other_refs = refs[1 + slots : 1 + 2 * slots]
-        grad_ref, block_ref, ratio_ref = refs[1 + 2 * slots :]
-        for slot in range(slots):
-            model = jnp.sqrt(power_refs[slot][...] + other_refs[slot][...] + damping_factor)
+def inverse_kernel(mode, bits, slots, fresh, start, *refs):
+    count = len(slots)
+
+    def take(number):
+        nonlocal refs
+        taken, refs = refs[:number], refs[number:]
+        return taken
+
+    if fresh:
+        (count_ref,) = take(1)
+    row_ref, col_ref, probe_ref = take(3)
+    far_refs, patch_refs = take(count), take(count)
+    if fresh:
+        amplitude_ref, *power_refs = take(1 + 2 * count)
+    else:
+        ratio_refs = take(count)
+        take(count)
+    if not start:
+        take(1)
+    grad_refs, (block_ref,) = take(count), take(1)
+    if fresh:
+        ratio_refs = take(count)
+        for index, slot in enumerate(slots):
+            model = jnp.sqrt(
+                power_refs[index][...] + power_refs[count + index][...] + damping_factor
+            )
             active = (slot < count_ref[0]).astype(F32)
-            ratio_ref[slot] = (amplitude_ref[slot] / model - 1.0) * active
-    else:
-        _, ratio_ref, grad_ref, block_ref = refs
+            ratio_refs[index][...] = (amplitude_ref[slot] / model - 1.0) * active
+    left_ref, right_ref, middle_ref = refs
     size = probe_ref.shape[2]
-    blocks, rows = block_ref.shape[0], block_ref.shape[3]
+    rows = block_ref.shape[3]
     half = size // 2
     position = lax.axis_index("pos")
 
-    def spread_columns(slot, mode, parity):
+    def spread_columns(slot, parity):
         for begin, lines in spans(half, CHUNK):
             under = slice(half + begin, half + begin + CHUNK)
-            ratio = ratio_ref[slot, parity, lines]
+            ratio = ratio_refs[slot][parity, lines]
             far = far_refs[slot].at[mode, parity]
             put_right(right_ref, 2 * slot + parity, begin, far[lines] * ratio)
             put_right(right_ref, 2 * slot + parity, half + begin, far[under] * ratio)
@@ -247,7 +259,7 @@
         which = 2 * slot + parity
         middle_ref[which] = product(left_ref[which], row_ref[2 * parity + 1])
 
-    def add_terms(slot, index, mode):
+    def add_terms(slot):
         for begin, lines in spans(size, rows):
             target = block_index(begin // rows, position, bits)
             a, b = middle_ref[2 * slot, lines], middle_ref[2 * slot + 1, lines]
@@ -265,37 +277,39 @@
                 patch_real * imag - patch_imag * real,
             )
             for part in (0, 1):
-                if first and index == 0:
-                    grad_ref[slot, part, lines] = grads[part]
+                if fresh:
+                    grad_refs[slot][part, lines] = grads[part]
                 else:
-                    grad_ref[slot, part, lines] += grads[part]
-                if slot == 0:
-                    block_ref[target, index, part] = terms[part]
+                    grad_refs[slot][part, lines] += grads[part]
+                if start and slot == 0:
+                    block_ref[target, 0, part] = terms[part]
                 else:
-                    block_ref[target, index, part] += terms[part]
-
-    for index, mode in enumerate(modes):
-        for slot in range(slots):
-            for parity in (0, 1):
-                spread_columns(slot, mode, parity)
-                column_products(slot, parity)
-        for slot in range(slots):
-            spread_rows(slot)
-            if slot > 0:
-                add_terms(slot - 1, index, mode)
-            for parity in (0, 1):
-                row_products(slot, parity)
-        add_terms(slots - 1, index, mode)
-
-def strip_kernel(offset_ref, grad_ref, keep_ref, send_ref, spread):
-    slots, _, size, _ = grad_ref.shape
+                    block_ref[target, 0, part] += terms[part]
+
+    for slot in range(count):
+        for parity in (0, 1):
+            spread_columns(slot, parity)
+            column_products(slot, parity)
+    for slot in range(count):
+        spread_rows(slot)
+        if slot > 0:
+            add_terms(slot - 1)
+        for parity in (0, 1):
+            row_products(slot, parity)
+    add_terms(count - 1)
+
+
+def strip_kernel(offset_ref, *refs):
+    *grad_refs, keep_ref, send_ref, spread = refs
+    slots, size = len(grad_refs), grad_refs[0].shape[1]
     rows = size // 2
     position, tile = lax.axis_index("pos"), lax.axis_index("tile")
     parity = lax.rem(position, 2)
     half = rows // 2
     spread[:, :, :rows] = jnp.zeros(spread.shape[:2] + (rows, size), F32)
     spread[:, :, rows + size :] = jnp.zeros(spread.shape[:2] + (rows + 8, size), F32)
-    spread[:, :, rows : rows + size] = grad_ref[...]
+    for slot in range(slots):
+        spread[slot, :, rows : rows + size] = grad_refs[slot][...]
     for place, strip in enumerate((2 * (1 - parity), 2 * parity, 1)):
         for part in (0, 1):
             for ref, which in ((keep_ref, tile), (send_ref, 1 - tile)):
@@ -403,7 +417,9 @@
     from_next = lax.ppermute(again, "pos", following)
     from_pair, probe_grid = lax.optimization_barrier((from_pair, probe_grid))
     pair_other = lax.ppermute(from_pair, "tile", swap)
-    from_next, pair_other = lax.optimization_barrier((from_next, pair_other))
+    from_next, pair_other, amplitude = lax.optimization_barrier(
+        (from_next, pair_other, amplitude)
+    )
     halo = [from_pair, from_next, pair_other, lax.ppermute(from_next, "tile", swap)]
 
     far, power, patch = [], [], []
@@ -424,27 +440,38 @@
     block_rows = size // positions
     bit_count = positions.bit_length() - 1
     later = list(range(2, bit_count))
-    grad, blocks = None, []
+    every = tuple(range(slots))
+    grad_shape = shape(2, size, size)
+    term_shape = shape(positions, 1, 2, block_rows, size)
+    grads, ratios, blocks = [], [], []
     for mode in range(modes):
-        bits = [(1, 0), (0, 1)][PATTERN[mode % 4]]
-        kernel = functools.partial(inverse_kernel, (mode,), [*bits, *later], mode == 0, slots)
-        outs = (shape(slots, 2, size, size), shape(positions, 1, 2, block_rows, size))
-        arrays = [*tables, probe_grid, *far, *patch]
+        bits = [*[(1, 0), (0, 1)][PATTERN[mode % 4]], *later]
         if mode == 0:
-            outs += (shape(slots, 2, half, size),)
-            arrays += [amplitude, *power, *others]
-            grad, terms, ratio = call(
-                kernel, outs, [counts], arrays, "inverse", scratch_shapes=scratch
-            )
+            for slot in every:
+                arrays = [*tables, probe_grid, far[slot], patch[slot]]
+                arrays += [amplitude, power[slot], others[slot]]
+                if slot > 0:
+                    arrays.append(terms)
+                grad, terms, ratio = call(
+                    functools.partial(inverse_kernel, mode, bits, (slot,), True, slot == 0),
+                    (grad_shape, term_shape, shape(2, half, size)),
+                    [counts],
+                    arrays,
+                    "inverse",
+                    input_output_aliases={} if slot == 0 else {len(arrays): 1},
+                    scratch_shapes=scratch,
+                )
+                grads.append(grad)
+                ratios.append(ratio)
         else:
-            arrays += [grad, ratio]
-            grad, terms = call(
-                kernel,
-                outs,
+            arrays = [*tables, probe_grid, *far, *patch, *ratios, *grads]
+            *grads, terms = call(
+                functools.partial(inverse_kernel, mode, bits, every, False, True),
+                (grad_shape,) * slots + (term_shape,),
                 [],
                 arrays,
                 "inverse",
-                input_output_aliases={len(arrays) - 2: 0},
+                input_output_aliases={len(arrays) - slots + slot: slot for slot in every},
                 scratch_shapes=scratch,
             )
         blocks.append(jnp.split(terms, 2))
@@ -455,7 +482,7 @@
         strip_kernel,
         (strip_shape, strip_shape),
         [],
-        [offsets, grad],
+        [offsets, *grads],
         "strips",
         scratch_shapes=[pltpu.VMEM((slots, parts, 2 * strip_rows + size + 8, columns), F32)],
     )
@@ -473,9 +500,6 @@
             blocks[mode] = jnp.split(keep + got, 2) if keep.shape[0] > 1 else [keep, got]
 
     for modes_at, bit in STEPS:
-        if modes_at == "tie":
-            blocks[bit], strips = lax.optimization_barrier((blocks[bit], strips))
-            continue
         for now in [bit] if bit < 2 else later:
             advance(modes_at, now)
     from_pair = lax.ppermute(strips[0], "pos", pair)

time: 57.9 us -> 57.1 us (0.986)
  local copies, waits for them, and re-layouts: 2.74 us -> 1.17 us
    unnamed x14, local copies, waits for them, and re-layouts: 1.61 us -> 0.05 us
    ppermute x1, waiting for transfers between devices: 0.79 us -> 2.31 us  [on_device(): from_pair = lax.ppermute(component, 'pos', pair)]
    ppermute x1, waiting for transfers between devices: 1.34 us -> 0.37 us  [on_device(): pair_other = lax.ppermute(from_pair, 'tile', swap)]
    pallas_call x11 -> x12, Pallas kernels: 12.5 us -> 12.8 us  [call(): pl.pallas_call(kernel, out_shape=out_shape, in_specs=[smem] * len(scalars...]
  transfers between devices with their start and end apart: 19 -> 19, of which waited for: 9 -> 8; matrix products, arithmetic and copies ran while one was open for 1% -> 1% of each run, Pallas kernels for 14% -> 15%
where the time goes in v6:
time: 57.1 us; the launch traced here: 57 us
  starting transfers between devices  24.2 us (42%)
  waiting for transfers between devices  16.8 us (29%)
  Pallas kernels  12.8 us (22%)
  between operations  1.73 us (3%)
  local copies, waits for them, and re-layouts  1.17 us (2%)
    ppermute x10, starting transfers between devices, exchange(): lax.ppermute(payload, 'pos', [(i, i ^ 2 ** bit) for i in range(positions)])  14.6 us
    ppermute x10, waiting for transfers between devices, exchange(): lax.ppermute(payload, 'pos', [(i, i ^ 2 ** bit) for i in range(positions)])  12.9 us
    pallas_call x12, Pallas kernels, call(): pl.pallas_call(kernel, out_shape=out_shape, in_specs=[smem] * len(scalars...  12.8 us
    ppermute x1, starting transfers between devices, on_device(): from_pair = lax.ppermute(strips[0], 'pos', pair)  4.32 us
    ppermute x1, starting transfers between devices, on_device(): from_pair = lax.ppermute(component, 'pos', pair)  3 us
    ppermute x1, waiting for transfers between devices, on_device(): from_pair = lax.ppermute(component, 'pos', pair)  2.31 us
    ppermute x1, waiting for transfers between devices, on_device(): lax.ppermute(from_next, 'tile', swap)  1.14 us
  transfers between devices with their start and end apart: 19, of which 8 were waited for; matrix products, arithmetic and copies ran while one was open for 1% of the time, Pallas kernels for 15%

profile of v6, /device:TPU:0, one launch (start us, length us, event | category | flops | bytes accessed | tf_op | source)
XLA Modules:
  0.0 57.0 jit_solution(3691856853513135609)
XLA Ops:
  0.6 0.9 %dynamic-slice_bitcast_fusion.part_ref = f32[128,256]{1,0:T(8,128)S(1)} fusion(f32[2,128,256]{2,1,0:T(8,128)} %strip_ref.1, s32[]{:T(128)S(6)} %select_n.4), kind=kLoop, calls=%fused_computation.13 | loop fusion | bytes 262148 | tf_op jit(solution)/shard_map/jit(dynamic_index_in_dim)/squeeze | solution.py:392
  1.6 3.0 %collective-permute-start = (f32[128,256]{1,0:T(8,128)S(1)}, f32[128,256]{1,0:T(8,128)S(1)}, u32[]{:S(2)}, u32[]{:S(2)}) collective-permute-start(f32[128,256]{1,0:T(8,128)S(1)} %dynamic-slice_bitcast_fusion.part_ref), channel_id=1, source_target_pairs={{0,2},{2,0},{4,6},{6,4},{8,10},{10,8},{12,14},{14,12},{1,3},{3,1},... | collective-permute-start | bytes 393224 | tf_op jit(solution)/shard_map/ppermute | solution.py:393
  4.6 0.7 %collective-permute-start.1 = (f32[128,256]{1,0:T(8,128)S(1)}, f32[128,256]{1,0:T(8,128)S(1)}, u32[]{:S(2)}, u32[]{:S(2)}) collective-permute-start(f32[128,256]{1,0:T(8,128)S(1)} %pick.1), channel_id=1, source_target_pairs={{2,4},{6,8},{10,12},{4,2},{8,6},{12,10},{3,5},{7,9},{11,13},{5,3},... | collective-permute-start | bytes 393224 | tf_op jit(solution)/shard_map/ppermute | solution.py:417
  5.3 0.4 prepare.1
  5.8 2.3 %collective-permute-done.pair_ref = f32[128,256]{1,0:T(8,128)S(1)} collective-permute-done((f32[128,256]{1,0:T(8,128)S(1)}, f32[128,256]{1,0:T(8,128)S(1)}, u32[]{:S(2)}, u32[]{:S(2)}) %collective-permute-start) | collective-permute-done | bytes 131104 | tf_op jit(solution)/shard_map/ppermute | solution.py:393
  8.1 0.9 %order.1.refs_6_ = f32[2,2,128,256]{3,2,1,0:T(8,128)S(1)} custom-call(f32[2,256,256]{2,1,0:T(8,128)S(1)} %copy-done.4, bf16[2,256,256]{2,1,0:T(8,128)(2,1)S(1)} %copy-done.6), custom_call_target="tpu_custom_call" | custom-call | flops 1000000000 | tf_op jit(solution)/shard_map/order/pallas_call | solution.py:356
  9.0 0.4 collective-permute-done.2.pair_other_ref
  9.6 1.1 %collective-permute-done.3.next_other_ref = f32[128,256]{1,0:T(8,128)S(1)} collective-permute-done((f32[128,256]{1,0:T(8,128)S(1)}, f32[128,256]{1,0:T(8,128)S(1)}, u32[]{:S(2)}, u32[]{:S(2)}) %collective-permute-start.3) | collective-permute-done | bytes 131104 | tf_op jit(solution)/shard_map/ppermute | solution.py:423
  10.8 2.3 %forward.2 = (f32[4,2,256,256]{3,2,1,0:T(8,128)S(1)}, f32[2,128,256]{2,1,0:T(8,128)S(1)}, f32[2,256,256]{2,1,0:T(8,128)S(1)}) custom-call(s32[2,2]{1,0:T(2,128)S(1)} %copy-done.5, f32[2,128,256]{2,1,0:T(8,128)S(1)} %copy-done.2, f32[128,256]{1,0:T(8,128)S(1)} %collective-permute-done.pair_ref, f32[128,256]{1,0:T(8,128)S(1)} %collective-permute-done.1.next_ref, ...), custom_call_target="tpu_custom_call" | custom-call | flops 4000000000 | tf_op jit(solution)/shard_map/forward/pallas_call | solution.py:356
  13.4 2.2 %forward.3 = (f32[4,2,256,256]{3,2,1,0:T(8,128)S(1)}, f32[2,128,256]{2,1,0:T(8,128)S(1)}, f32[2,256,256]{2,1,0:T(8,128)S(1)}) custom-call(s32[2,2]{1,0:T(2,128)S(1)} %copy-done.5, f32[2,128,256]{2,1,0:T(8,128)S(1)} %copy-done.2, f32[128,256]{1,0:T(8,128)S(1)} %collective-permute-done.pair_ref, f32[128,256]{1,0:T(8,128)S(1)} %collective-permute-done.1.next_ref, ...), custom_call_target="tpu_custom_call" | custom-call | flops 4000000000 | tf_op jit(solution)/shard_map/forward/pallas_call | solution.py:356
  15.6 0.4 collective-permute-start.5
  16.6 0.9 %inverse.5 = (f32[2,256,256]{2,1,0:T(8,128)S(1)}, f32[8,1,2,32,256]{4,3,2,1,0:T(8,128)S(1)}, f32[2,128,256]{2,1,0:T(8,128)S(1)}) custom-call(s32[1]{0:T(128)S(6)} %copy.26.refs_0_, bf16[4,768,256]{2,1,0:T(8,128)(2,1)S(1)} %copy-done.1, bf16[4,256,768]{2,1,0:T(8,128)(2,1)S(1)} %copy-done, f32[2,4,256,256]{3,2,1,0:T(8,128)S(1)} %get-tuple-element.36.probe_ref.refs_3_.refs_2_, ...), custom_call_target="tpu_custom_call" | custom-call | flops 2400000000 | tf_op jit(solution)/shard_map/inverse/pallas_call | solution.py:356
  17.6 0.9 %inverse.6 = (f32[2,256,256]{2,1,0:T(8,128)S(1)}, f32[8,1,2,32,256]{4,3,2,1,0:T(8,128)S(1)}, f32[2,128,256]{2,1,0:T(8,128)S(1)}) custom-call(s32[1]{0:T(128)S(6)} %copy.26.refs_0_, bf16[4,768,256]{2,1,0:T(8,128)(2,1)S(1)} %copy-done.1, bf16[4,256,768]{2,1,0:T(8,128)(2,1)S(1)} %copy-done, ...), custom_call_target="tpu_custom_call", output_to_operand_aliasing={{1}: (9, {})} | custom-call | flops 2400000000 | tf_op jit(solution)/shard_map/inverse/pallas_call | solution.py:356
  18.5 4.6 %collective-permute-start.9 = (f32[4,1,2,32,256]{4,3,2,1,0:T(8,128)S(1)}, f32[4,1,2,32,256]{4,3,2,1,0:T(8,128)S(1)}, u32[]{:S(2)}, u32[]{:S(2)}) collective-permute-start(f32[4,1,2,32,256]{4,3,2,1,0:T(8,128)S(1)} %split.73), channel_id=1, source_target_pairs={{0,4},{2,6},{4,0},{6,2},{8,12},{10,14},{12,8},{14,10},{1,5},{3,7},... | collective-permute-start | bytes 786440 | tf_op jit(solution)/shard_map/ppermute | solution.py:492
  23.1 1.2 %inverse.7 = (f32[2,256,256]{2,1,0:T(8,128)S(1)}, f32[2,256,256]{2,1,0:T(8,128)S(1)}, f32[8,1,2,32,256]{4,3,2,1,0:T(8,128)S(1)}) custom-call(bf16[4,768,256]{2,1,0:T(8,128)(2,1)S(1)} %copy-done.1, bf16[4,256,768]{2,1,0:T(8,128)(2,1)S(1)} %copy-done, ...), custom_call_target="tpu_custom_call", output_to_operand_aliasing={{0}: (9, {}), {1}: (10, {})} | custom-call | flops 2400000000 | tf_op jit(solution)/shard_map/inverse/pallas_call | solution.py:356
  24.4 0.7 %collective-permute-start.11 = (f32[4,1,2,32,256]{4,3,2,1,0:T(8,128)S(1)}, f32[4,1,2,32,256]{4,3,2,1,0:T(8,128)S(1)}, u32[]{:S(2)}, u32[]{:S(2)}) collective-permute-start(f32[4,1,2,32,256]{4,3,2,1,0:T(8,128)S(1)} %split.79), channel_id=1, source_target_pairs={{0,2},{2,0},{4,6},{6,4},{8,10},{10,8},{12,14},{14,12},{1,3},{3,1},... | collective-permute-start | bytes 786440 | tf_op jit(solution)/shard_map/ppermute | solution.py:492
  25.1 1.2 %inverse.8 = (f32[2,256,256]{2,1,0:T(8,128)S(1)}, f32[2,256,256]{2,1,0:T(8,128)S(1)}, f32[8,1,2,32,256]{4,3,2,1,0:T(8,128)S(1)}) custom-call(bf16[4,768,256]{2,1,0:T(8,128)(2,1)S(1)} %copy-done.1, bf16[4,256,768]{2,1,0:T(8,128)(2,1)S(1)} %copy-done, ...), custom_call_target="tpu_custom_call", output_to_operand_aliasing={{0}: (9, {}), {1}: (10, {})} | custom-call | flops 2400000000 | tf_op jit(solution)/shard_map/inverse/pallas_call | solution.py:356
  26.3 1.2 %inverse.9 = (f32[2,256,256]{2,1,0:T(8,128)S(1)}, f32[2,256,256]{2,1,0:T(8,128)S(1)}, f32[8,1,2,32,256]{4,3,2,1,0:T(8,128)S(1)}) custom-call(bf16[4,768,256]{2,1,0:T(8,128)(2,1)S(1)} %copy-done.1, bf16[4,256,768]{2,1,0:T(8,128)(2,1)S(1)} %copy-done, ...), custom_call_target="tpu_custom_call", output_to_operand_aliasing={{0}: (9, {}), {1}: (10, {})} | custom-call | flops 2400000000 | tf_op jit(solution)/shard_map/inverse/pallas_call | solution.py:356
  27.5 1.5 %collective-permute-start.14 = (f32[4,1,2,32,256]{4,3,2,1,0:T(8,128)S(1)}, f32[4,1,2,32,256]{4,3,2,1,0:T(8,128)S(1)}, u32[]{:S(2)}, u32[]{:S(2)}) collective-permute-start(f32[4,1,2,32,256]{4,3,2,1,0:T(8,128)S(1)} %split.85), channel_id=1, source_target_pairs={{0,2},{2,0},{4,6},{6,4},{8,10},{10,8},{12,14},{14,12},{1,3},{3,1},... | collective-permute-start | bytes 786440 | tf_op jit(solution)/shard_map/ppermute | solution.py:492
  29.0 0.6 %strips.1 = (f32[3,2,64,256]{3,2,1,0:T(8,128)S(1)}, f32[3,2,64,256]{3,2,1,0:T(8,128)S(1)}) custom-call(s32[2,2]{1,0:T(2,128)S(1)} %copy-done.5, f32[2,256,256]{2,1,0:T(8,128)S(1)} %get-tuple-element.56.refs_0_, f32[2,256,256]{2,1,0:T(8,128)S(1)} %get-tuple-element.57.refs_1_), custom_call_target="tpu_custom_call" | custom-call | flops 1200000000 | tf_op jit(solution)/shard_map/strips/pallas_call | solution.py:356
  29.8 0.9 %collective-permute-start.10 = (f32[2,1,2,32,256]{4,3,2,1,0:T(8,128)S(1)}, f32[2,1,2,32,256]{4,3,2,1,0:T(8,128)S(1)}, u32[]{:S(2)}, u32[]{:S(2)}) collective-permute-start(f32[2,1,2,32,256]{4,3,2,1,0:T(8,128)S(1)} %split.97), channel_id=1, source_target_pairs={{0,2},{2,0},{4,6},{6,4},{8,10},{10,8},{12,14},{14,12},{1,3},{3,1},... | collective-permute-start | bytes 393224 | tf_op jit(solution)/shard_map/ppermute | solution.py:492
  30.7 2.9 %collective-permute-done.11 = f32[4,1,2,32,256]{4,3,2,1,0:T(8,128)S(1)} collective-permute-done((f32[4,1,2,32,256]{4,3,2,1,0:T(8,128)S(1)}, f32[4,1,2,32,256]{4,3,2,1,0:T(8,128)S(1)}, u32[]{:S(2)}, u32[]{:S(2)}) %collective-permute-start.11) | collective-permute-done | bytes 262176 | tf_op jit(solution)/shard_map/ppermute | solution.py:492
  33.8 5.5 %collective-permute-done.14 = f32[4,1,2,32,256]{4,3,2,1,0:T(8,128)S(1)} collective-permute-done((f32[4,1,2,32,256]{4,3,2,1,0:T(8,128)S(1)}, f32[4,1,2,32,256]{4,3,2,1,0:T(8,128)S(1)}, u32[]{:S(2)}, u32[]{:S(2)}) %collective-permute-start.14) | collective-permute-done | bytes 262176 | tf_op jit(solution)/shard_map/ppermute | solution.py:492
  39.4 0.9 %collective-permute-start.17 = (f32[2,1,2,32,256]{4,3,2,1,0:T(8,128)S(1)}, f32[2,1,2,32,256]{4,3,2,1,0:T(8,128)S(1)}, u32[]{:S(2)}, u32[]{:S(2)}) collective-permute-start(f32[2,1,2,32,256]{4,3,2,1,0:T(8,128)S(1)} %split.109), channel_id=1, source_target_pairs={{0,2},{2,0},{4,6},{6,4},{8,10},{10,8},{12,14},{14,12},{1,3},{3,1},... | collective-permute-start | bytes 393224 | tf_op jit(solution)/shard_map/ppermute | solution.py:492
  40.3 1.1 %collective-permute-done.10 = f32[2,1,2,32,256]{4,3,2,1,0:T(8,128)S(1)} collective-permute-done((f32[2,1,2,32,256]{4,3,2,1,0:T(8,128)S(1)}, f32[2,1,2,32,256]{4,3,2,1,0:T(8,128)S(1)}, u32[]{:S(2)}, u32[]{:S(2)}) %collective-permute-start.10) | collective-permute-done | bytes 131104 | tf_op jit(solution)/shard_map/ppermute | solution.py:492
  41.6 2.9 %collective-permute-start.13 = (f32[2,1,2,32,256]{4,3,2,1,0:T(8,128)S(1)}, f32[2,1,2,32,256]{4,3,2,1,0:T(8,128)S(1)}, u32[]{:S(2)}, u32[]{:S(2)}) collective-permute-start(f32[2,1,2,32,256]{4,3,2,1,0:T(8,128)S(1)} %pad_maximum_fusion), channel_id=1, source_target_pairs={{0,8},{2,10},{4,12},{6,14},{8,0},{10,2},{12,4},{14,6},{1,9},{3,11}... | collective-permute-start | bytes 393224 | tf_op jit(solution)/shard_map/ppermute | solution.py:492
  44.6 3.0 %collective-permute-start.18 = (f32[2,1,2,32,256]{4,3,2,1,0:T(8,128)S(1)}, f32[2,1,2,32,256]{4,3,2,1,0:T(8,128)S(1)}, u32[]{:S(2)}, u32[]{:S(2)}) collective-permute-start(f32[2,1,2,32,256]{4,3,2,1,0:T(8,128)S(1)} %pad_maximum_fusion.1), channel_id=1, source_target_pairs={{0,8},{2,10},{4,12},{6,14},{8,0},{10,2},{12,4},{14,6},{1,9},{3,11}... | collective-permute-start | bytes 393224 | tf_op jit(solution)/shard_map/ppermute | solution.py:492
  47.7 0.7 %collective-permute-start.8 = (f32[2,64,256]{2,1,0:T(8,128)S(1)}, f32[2,64,256]{2,1,0:T(8,128)S(1)}, u32[]{:S(2)}, u32[]{:S(2)}) collective-permute-start(f32[2,64,256]{2,1,0:T(8,128)S(1)} %get-tuple-element.66), channel_id=1, source_target_pairs={{2,4},{6,8},{10,12},{4,2},{8,6},{12,10},{3,5},{7,9},{11,13},{5,3},... | collective-permute-start | bytes 393224 | tf_op jit(solution)/shard_map/ppermute | solution.py:506
  48.4 4.3 %collective-permute-start.7 = (f32[2,64,256]{2,1,0:T(8,128)S(1)}, f32[2,64,256]{2,1,0:T(8,128)S(1)}, u32[]{:S(2)}, u32[]{:S(2)}) collective-permute-start(f32[2,64,256]{2,1,0:T(8,128)S(1)} %get-tuple-element.67), channel_id=1, source_target_pairs={{0,2},{2,0},{4,6},{6,4},{8,10},{10,8},{12,14},{14,12},{1,3},{3,1},... | collective-permute-start | bytes 393224 | tf_op jit(solution)/shard_map/ppermute | solution.py:505
  52.7 0.5 collective-permute-done.13
  53.3 2.8 %collective-permute-done.18 = f32[2,1,2,32,256]{4,3,2,1,0:T(8,128)S(1)} collective-permute-done((f32[2,1,2,32,256]{4,3,2,1,0:T(8,128)S(1)}, f32[2,1,2,32,256]{4,3,2,1,0:T(8,128)S(1)}, u32[]{:S(2)}, u32[]{:S(2)}) %collective-permute-start.18) | collective-permute-done | bytes 131104 | tf_op jit(solution)/shard_map/ppermute | solution.py:492
  56.1 0.9 %finish.1 = (f32[2,64,256]{2,1,0:T(8,128)}, f32[2,256,128]{2,1,0:T(8,128)}) custom-call(f32[2,256,128]{2,1,0:T(8,128)S(1)} %get-tuple-element.34.probe_ref, f32[2,128,256]{2,1,0:T(8,128)S(1)} %copy-done.2, f32[2,64,256]{2,1,0:T(8,128)S(1)} %get-tuple-element.68.mid_ref, f32[2,64,256]{2,1,0:T(8,128)S(1)} %collective-permute-done.7.pair_ref, ...), custom_call_target="tpu_custom_call" | custom-call | flops 1000000000 | tf_op jit(solution)/shard_map/finish/pallas_call | solution.py:356
  (59 shorter events, 1.4 us)
Async XLA Ops:
  1.6 3.7 %copy-start.3 = (f32[2,4,65536]{2,1,0:T(4,128)S(1)}, f32[2,4,65536]{2,1,0:T(4,128)}, u32[]{:S(2)}) copy-start(f32[2,4,65536]{2,1,0:T(4,128)} %param.9) | copy-start | bytes 6291460
  1.6 6.5 %collective-permute-start = (f32[128,256]{1,0:T(8,128)S(1)}, f32[128,256]{1,0:T(8,128)S(1)}, u32[]{:S(2)}, u32[]{:S(2)}) collective-permute-start(f32[128,256]{1,0:T(8,128)S(1)} %dynamic-slice_bitcast_fusion.part_ref), channel_id=1, source_target_pairs={{0,2},{2,0},{4,6},{6,4},{8,10},{10,8},{12,14},{14,12},{1,3},{3,1},... | collective-permute-start | bytes 393224 | tf_op jit(solution)/shard_map/ppermute | solution.py:393
  4.6 4.5 %collective-permute-start.1 = (f32[128,256]{1,0:T(8,128)S(1)}, f32[128,256]{1,0:T(8,128)S(1)}, u32[]{:S(2)}, u32[]{:S(2)}) collective-permute-start(f32[128,256]{1,0:T(8,128)S(1)} %pick.1), channel_id=1, source_target_pairs={{2,4},{6,8},{10,12},{4,2},{8,6},{12,10},{3,5},{7,9},{11,13},{5,3},... | collective-permute-start | bytes 393224 | tf_op jit(solution)/shard_map/ppermute | solution.py:417
  5.3 2.8 %copy-start.4 = (f32[2,256,256]{2,1,0:T(8,128)S(1)}, f32[2,256,256]{2,1,0:T(8,128)}, u32[]{:S(2)}) copy-start(f32[2,256,256]{2,1,0:T(8,128)} %measured_ref.1) | copy-start | bytes 1572868
  5.3 2.8 %copy-start.6 = (bf16[2,256,256]{2,1,0:T(8,128)(2,1)S(1)}, bf16[2,256,256]{2,1,0:T(8,128)(2,1)}, u32[]{:S(2)}) copy-start(bf16[2,256,256]{2,1,0:T(8,128)(2,1)} %constant.18.clone.order_ref) | copy-start | bytes 786436
  5.7 5.1 %copy-start = (bf16[4,256,768]{2,1,0:T(8,128)(2,1)S(1)}, bf16[4,256,768]{2,1,0:T(8,128)(2,1)}, u32[]{:S(2)}) copy-start(bf16[4,256,768]{2,1,0:T(8,128)(2,1)} %constant.17.clone.col_ref.refs_2_.refs_1_) | copy-start | bytes 4718596
  5.7 5.1 %copy-start.1 = (bf16[4,768,256]{2,1,0:T(8,128)(2,1)S(1)}, bf16[4,768,256]{2,1,0:T(8,128)(2,1)}, u32[]{:S(2)}) copy-start(bf16[4,768,256]{2,1,0:T(8,128)(2,1)} %constant.16.clone.row_ref.refs_1_.refs_0_) | copy-start | bytes 4718596
  5.7 5.0 %copy-start.2 = (f32[2,128,256]{2,1,0:T(8,128)S(1)}, f32[2,128,256]{2,1,0:T(8,128)}, u32[]{:S(2)}) copy-start(f32[2,128,256]{2,1,0:T(8,128)} %strip_ref.1) | copy-start | bytes 786436
  5.7 5.0 %copy-start.5 = (s32[2,2]{1,0:T(2,128)S(1)}, s32[2,2]{1,0:T(2,128)}, u32[]{:S(2)}) copy-start(s32[2,2]{1,0:T(2,128)} %offset_ref.5) | copy-start | bytes 52
  8.1 1.3 %collective-permute-start.2 = (f32[128,256]{1,0:T(8,128)S(1)}, f32[128,256]{1,0:T(8,128)S(1)}, u32[]{:S(2)}, u32[]{:S(2)}) collective-permute-start(f32[128,256]{1,0:T(8,128)S(1)} %collective-permute-done.pair_ref), channel_id=1, source_target_pairs={{0,1},{1,0},{2,3},{3,2},{4,5},{5,4},{6,7},{7,6},{8,9},{9,8},{10,11... | collective-permute-start | bytes 393224 | tf_op jit(solution)/shard_map/ppermute | solution.py:419
  9.4 1.3 %collective-permute-start.3 = (f32[128,256]{1,0:T(8,128)S(1)}, f32[128,256]{1,0:T(8,128)S(1)}, u32[]{:S(2)}, u32[]{:S(2)}) collective-permute-start(f32[128,256]{1,0:T(8,128)S(1)} %collective-permute-done.1.next_ref), channel_id=1, source_target_pairs={{0,1},{1,0},{2,3},{3,2},{4,5},{5,4},{6,7},{7,6},{8,9},{9,8},{10,11... | collective-permute-start | bytes 393224 | tf_op jit(solution)/shard_map/ppermute | solution.py:423
  13.1 3.5 %collective-permute-start.4 = (f32[2,128,256]{2,1,0:T(8,128)S(1)}, f32[2,128,256]{2,1,0:T(8,128)S(1)}, u32[]{:S(2)}, u32[]{:S(2)}) collective-permute-start(f32[2,128,256]{2,1,0:T(8,128)S(1)} %get-tuple-element.45.refs_7_), channel_id=1, source_target_pairs={{0,1},{1,0},{2,3},{3,2},{4,5},{5,4},{6,7},{7,6},{8,9},{9,8},{10,11... | collective-permute-start | bytes 786440 | tf_op jit(solution)/shard_map/ppermute | solution.py:438
  15.6 2.0 %collective-permute-start.5 = (f32[2,128,256]{2,1,0:T(8,128)S(1)}, f32[2,128,256]{2,1,0:T(8,128)S(1)}, u32[]{:S(2)}, u32[]{:S(2)}) collective-permute-start(f32[2,128,256]{2,1,0:T(8,128)S(1)} %get-tuple-element.47.refs_7_), channel_id=1, source_target_pairs={{0,1},{1,0},{2,3},{3,2},{4,5},{5,4},{6,7},{7,6},{8,9},{9,8},{10,11... | collective-permute-start | bytes 786440 | tf_op jit(solution)/shard_map/ppermute | solution.py:438
  18.5 11.2 %collective-permute-start.9 = (f32[4,1,2,32,256]{4,3,2,1,0:T(8,128)S(1)}, f32[4,1,2,32,256]{4,3,2,1,0:T(8,128)S(1)}, u32[]{:S(2)}, u32[]{:S(2)}) collective-permute-start(f32[4,1,2,32,256]{4,3,2,1,0:T(8,128)S(1)} %split.73), channel_id=1, source_target_pairs={{0,4},{2,6},{4,0},{6,2},{8,12},{10,14},{12,8},{14,10},{1,5},{3,7},... | collective-permute-start | bytes 786440 | tf_op jit(solution)/shard_map/ppermute | solution.py:492
  24.4 9.3 %collective-permute-start.11 = (f32[4,1,2,32,256]{4,3,2,1,0:T(8,128)S(1)}, f32[4,1,2,32,256]{4,3,2,1,0:T(8,128)S(1)}, u32[]{:S(2)}, u32[]{:S(2)}) collective-permute-start(f32[4,1,2,32,256]{4,3,2,1,0:T(8,128)S(1)} %split.79), channel_id=1, source_target_pairs={{0,2},{2,0},{4,6},{6,4},{8,10},{10,8},{12,14},{14,12},{1,3},{3,1},... | collective-permute-start | bytes 786440 | tf_op jit(solution)/shard_map/ppermute | solution.py:492
  27.5 11.7 %collective-permute-start.14 = (f32[4,1,2,32,256]{4,3,2,1,0:T(8,128)S(1)}, f32[4,1,2,32,256]{4,3,2,1,0:T(8,128)S(1)}, u32[]{:S(2)}, u32[]{:S(2)}) collective-permute-start(f32[4,1,2,32,256]{4,3,2,1,0:T(8,128)S(1)} %split.85), channel_id=1, source_target_pairs={{0,2},{2,0},{4,6},{6,4},{8,10},{10,8},{12,14},{14,12},{1,3},{3,1},... | collective-permute-start | bytes 786440 | tf_op jit(solution)/shard_map/ppermute | solution.py:492
  29.0 10.4 %collective-permute-start.16 = (f32[4,1,2,32,256]{4,3,2,1,0:T(8,128)S(1)}, f32[4,1,2,32,256]{4,3,2,1,0:T(8,128)S(1)}, u32[]{:S(2)}, u32[]{:S(2)}) collective-permute-start(f32[4,1,2,32,256]{4,3,2,1,0:T(8,128)S(1)} %split.91), channel_id=1, source_target_pairs={{0,4},{2,6},{4,0},{6,2},{8,12},{10,14},{12,8},{14,10},{1,5},{3,7},... | collective-permute-start | bytes 786440 | tf_op jit(solution)/shard_map/ppermute | solution.py:492
  29.6 18.0 %collective-permute-start.6 = (f32[3,2,64,256]{3,2,1,0:T(8,128)S(1)}, f32[3,2,64,256]{3,2,1,0:T(8,128)S(1)}, u32[]{:S(2)}, u32[]{:S(2)}) collective-permute-start(f32[3,2,64,256]{3,2,1,0:T(8,128)S(1)} %get-tuple-element.59), channel_id=1, source_target_pairs={{0,1},{1,0},{2,3},{3,2},{4,5},{5,4},{6,7},{7,6},{8,9},{9,8},{10,11... | collective-permute-start | bytes 1179656 | tf_op jit(solution)/shard_map/ppermute | solution.py:489
  29.8 11.7 %collective-permute-start.10 = (f32[2,1,2,32,256]{4,3,2,1,0:T(8,128)S(1)}, f32[2,1,2,32,256]{4,3,2,1,0:T(8,128)S(1)}, u32[]{:S(2)}, u32[]{:S(2)}) collective-permute-start(f32[2,1,2,32,256]{4,3,2,1,0:T(8,128)S(1)} %split.97), channel_id=1, source_target_pairs={{0,2},{2,0},{4,6},{6,4},{8,10},{10,8},{12,14},{14,12},{1,3},{3,1},... | collective-permute-start | bytes 393224 | tf_op jit(solution)/shard_map/ppermute | solution.py:492
  33.7 7.8 %collective-permute-start.12 = (f32[2,1,2,32,256]{4,3,2,1,0:T(8,128)S(1)}, f32[2,1,2,32,256]{4,3,2,1,0:T(8,128)S(1)}, u32[]{:S(2)}, u32[]{:S(2)}) collective-permute-start(f32[2,1,2,32,256]{4,3,2,1,0:T(8,128)S(1)} %split.101), channel_id=1, source_target_pairs={{0,4},{2,6},{4,0},{6,2},{8,12},{10,14},{12,8},{14,10},{1,5},{3,7},... | collective-permute-start | bytes 393224 | tf_op jit(solution)/shard_map/ppermute | solution.py:492
  39.3 5.2 %collective-permute-start.15 = (f32[2,1,2,32,256]{4,3,2,1,0:T(8,128)S(1)}, f32[2,1,2,32,256]{4,3,2,1,0:T(8,128)S(1)}, u32[]{:S(2)}, u32[]{:S(2)}) collective-permute-start(f32[2,1,2,32,256]{4,3,2,1,0:T(8,128)S(1)} %split.105), channel_id=1, source_target_pairs={{0,4},{2,6},{4,0},{6,2},{8,12},{10,14},{12,8},{14,10},{1,5},{3,7},... | collective-permute-start | bytes 393224 | tf_op jit(solution)/shard_map/ppermute | solution.py:492
  39.4 5.1 %collective-permute-start.17 = (f32[2,1,2,32,256]{4,3,2,1,0:T(8,128)S(1)}, f32[2,1,2,32,256]{4,3,2,1,0:T(8,128)S(1)}, u32[]{:S(2)}, u32[]{:S(2)}) collective-permute-start(f32[2,1,2,32,256]{4,3,2,1,0:T(8,128)S(1)} %split.109), channel_id=1, source_target_pairs={{0,2},{2,0},{4,6},{6,4},{8,10},{10,8},{12,14},{14,12},{1,3},{3,1},... | collective-permute-start | bytes 393224 | tf_op jit(solution)/shard_map/ppermute | solution.py:492
  41.6 11.7 %collective-permute-start.13 = (f32[2,1,2,32,256]{4,3,2,1,0:T(8,128)S(1)}, f32[2,1,2,32,256]{4,3,2,1,0:T(8,128)S(1)}, u32[]{:S(2)}, u32[]{:S(2)}) collective-permute-start(f32[2,1,2,32,256]{4,3,2,1,0:T(8,128)S(1)} %pad_maximum_fusion), channel_id=1, source_target_pairs={{0,8},{2,10},{4,12},{6,14},{8,0},{10,2},{12,4},{14,6},{1,9},{3,11}... | collective-permute-start | bytes 393224 | tf_op jit(solution)/shard_map/ppermute | solution.py:492
  44.6 11.4 %collective-permute-start.18 = (f32[2,1,2,32,256]{4,3,2,1,0:T(8,128)S(1)}, f32[2,1,2,32,256]{4,3,2,1,0:T(8,128)S(1)}, u32[]{:S(2)}, u32[]{:S(2)}) collective-permute-start(f32[2,1,2,32,256]{4,3,2,1,0:T(8,128)S(1)} %pad_maximum_fusion.1), channel_id=1, source_target_pairs={{0,8},{2,10},{4,12},{6,14},{8,0},{10,2},{12,4},{14,6},{1,9},{3,11}... | collective-permute-start | bytes 393224 | tf_op jit(solution)/shard_map/ppermute | solution.py:492
  47.7 8.3 %collective-permute-start.8 = (f32[2,64,256]{2,1,0:T(8,128)S(1)}, f32[2,64,256]{2,1,0:T(8,128)S(1)}, u32[]{:S(2)}, u32[]{:S(2)}) collective-permute-start(f32[2,64,256]{2,1,0:T(8,128)S(1)} %get-tuple-element.66), channel_id=1, source_target_pairs={{2,4},{6,8},{10,12},{4,2},{8,6},{12,10},{3,5},{7,9},{11,13},{5,3},... | collective-permute-start | bytes 393224 | tf_op jit(solution)/shard_map/ppermute | solution.py:506
  48.4 7.7 %collective-permute-start.7 = (f32[2,64,256]{2,1,0:T(8,128)S(1)}, f32[2,64,256]{2,1,0:T(8,128)S(1)}, u32[]{:S(2)}, u32[]{:S(2)}) collective-permute-start(f32[2,64,256]{2,1,0:T(8,128)S(1)} %get-tuple-element.67), channel_id=1, source_target_pairs={{0,2},{2,0},{4,6},{6,4},{8,10},{10,8},{12,14},{14,12},{1,3},{3,1},... | collective-permute-start | bytes 393224 | tf_op jit(solution)/shard_map/ppermute | solution.py:505

commit v7 on v6

--- a/solution.py
+++ b/solution.py
@@ -19,8 +19,8 @@
 VMEM_LIMIT = 16 * 1024 * 1024
 COSTS = {'prepare': 2000000000, 'forward': 4000000000, 'inverse': 2400000000, 'strips': 1200000000, 'finish': 1000000000, 'order': 1000000000, 'pick': 3000000000}
 CHUNK = 64
-PATTERN = (0, 1, 1, 0)
-STEPS = (((0,), 1), ((1,), 0), ((2,), 0), ((3,), 1), ((0,), 0), ((1,), 1), ((2,), 1), ((3,), 0), ((0, 1), 2), ((2, 3), 2))
+PATTERN = (0, 1, 1, 2)
+STEPS = (((0,), 1), ((1,), 0), ((2,), 0), ((3,), 1), ((0,), 2), ((1,), 1), ((3,), 0), ((2,), 1), ((0,), 0), ((1,), 2), ((2, 3), 2))
 
 
 def real_tables(size):
@@ -445,7 +445,7 @@
     term_shape = shape(positions, 1, 2, block_rows, size)
     grads, ratios, blocks = [], [], []
     for mode in range(modes):
-        bits = [*[(1, 0), (0, 1)][PATTERN[mode % 4]], *later]
+        bits = [(1, *later, 0), (0, 1, *later), (1, 0, *later)][PATTERN[mode % 4]]
         if mode == 0:
             for slot in every:
                 arrays = [*tables, probe_grid, far[slot], patch[slot]]

time: 57.1 us -> 56.9 us (level)
  waiting for transfers between devices: 16.8 us -> 14.4 us
  starting transfers between devices: 24.2 us -> 26.4 us
    ppermute x10 -> x11, starting transfers between devices: 14.6 us -> 18 us  [exchange(): lax.ppermute(payload, 'pos', [(i, i ^ 2 ** bit) for i in range(positions)])]
    ppermute x10 -> x11, waiting for transfers between devices: 12.9 us -> 10.3 us  [exchange(): lax.ppermute(payload, 'pos', [(i, i ^ 2 ** bit) for i in range(positions)])]
    ppermute x1, starting transfers between devices: 4.32 us -> 3.17 us  [on_device(): from_pair = lax.ppermute(strips[0], 'pos', pair)]
  transfers between devices with their start and end apart: 19 -> 20, of which waited for: 8 -> 9; matrix products, arithmetic and copies ran while one was open for 1% -> 1% of each run, Pallas kernels for 15% -> 15%
where the time goes in v7:
time: 56.9 us; the launch traced here: 56.8 us
  starting transfers between devices  26.4 us (46%)
  waiting for transfers between devices  14.4 us (25%)
  Pallas kernels  12.8 us (22%)
  between operations  1.69 us (3%)
  local copies, waits for them, and re-layouts  1.16 us (2%)
    ppermute x11, starting transfers between devices, exchange(): lax.ppermute(payload, 'pos', [(i, i ^ 2 ** bit) for i in range(positions)])  18 us
    pallas_call x12, Pallas kernels, call(): pl.pallas_call(kernel, out_shape=out_shape, in_specs=[smem] * len(scalars...  12.8 us
    ppermute x11, waiting for transfers between devices, exchange(): lax.ppermute(payload, 'pos', [(i, i ^ 2 ** bit) for i in range(positions)])  10.3 us
    ppermute x1, starting transfers between devices, on_device(): from_pair = lax.ppermute(strips[0], 'pos', pair)  3.17 us
    ppermute x1, starting transfers between devices, on_device(): from_pair = lax.ppermute(component, 'pos', pair)  3 us
    ppermute x1, waiting for transfers between devices, on_device(): from_pair = lax.ppermute(component, 'pos', pair)  2.31 us
    ppermute x1, waiting for transfers between devices, on_device(): lax.ppermute(from_next, 'tile', swap)  1.14 us
  transfers between devices with their start and end apart: 20, of which 9 were waited for; matrix products, arithmetic and copies ran while one was open for 1% of the time, Pallas kernels for 15%

profile of v7, /device:TPU:0, one launch (start us, length us, event | category | flops | bytes accessed | tf_op | source)
XLA Modules:
  0.0 56.8 jit_solution(9890066208669311694)
XLA Ops:
  0.6 0.9 %dynamic-slice_bitcast_fusion.part_ref = f32[128,256]{1,0:T(8,128)S(1)} fusion(f32[2,128,256]{2,1,0:T(8,128)} %strip_ref.1, s32[]{:T(128)S(6)} %select_n.4), kind=kLoop, calls=%fused_computation.12 | loop fusion | bytes 262148 | tf_op jit(solution)/shard_map/jit(dynamic_index_in_dim)/squeeze | solution.py:392
  1.6 3.0 %collective-permute-start = (f32[128,256]{1,0:T(8,128)S(1)}, f32[128,256]{1,0:T(8,128)S(1)}, u32[]{:S(2)}, u32[]{:S(2)}) collective-permute-start(f32[128,256]{1,0:T(8,128)S(1)} %dynamic-slice_bitcast_fusion.part_ref), channel_id=1, source_target_pairs={{0,2},{2,0},{4,6},{6,4},{8,10},{10,8},{12,14},{14,12},{1,3},{3,1},... | collective-permute-start | bytes 393224 | tf_op jit(solution)/shard_map/ppermute | solution.py:393
  4.6 0.7 %collective-permute-start.1 = (f32[128,256]{1,0:T(8,128)S(1)}, f32[128,256]{1,0:T(8,128)S(1)}, u32[]{:S(2)}, u32[]{:S(2)}) collective-permute-start(f32[128,256]{1,0:T(8,128)S(1)} %pick.1), channel_id=1, source_target_pairs={{2,4},{6,8},{10,12},{4,2},{8,6},{12,10},{3,5},{7,9},{11,13},{5,3},... | collective-permute-start | bytes 393224 | tf_op jit(solution)/shard_map/ppermute | solution.py:417
  5.3 0.4 prepare.1
  5.8 2.3 %collective-permute-done.pair_ref = f32[128,256]{1,0:T(8,128)S(1)} collective-permute-done((f32[128,256]{1,0:T(8,128)S(1)}, f32[128,256]{1,0:T(8,128)S(1)}, u32[]{:S(2)}, u32[]{:S(2)}) %collective-permute-start) | collective-permute-done | bytes 131104 | tf_op jit(solution)/shard_map/ppermute | solution.py:393
  8.1 0.9 %order.1.refs_6_ = f32[2,2,128,256]{3,2,1,0:T(8,128)S(1)} custom-call(f32[2,256,256]{2,1,0:T(8,128)S(1)} %copy-done.4, bf16[2,256,256]{2,1,0:T(8,128)(2,1)S(1)} %copy-done.6), custom_call_target="tpu_custom_call" | custom-call | flops 1000000000 | tf_op jit(solution)/shard_map/order/pallas_call | solution.py:356
  9.0 0.4 collective-permute-done.2.pair_other_ref
  9.6 1.1 %collective-permute-done.3.next_other_ref = f32[128,256]{1,0:T(8,128)S(1)} collective-permute-done((f32[128,256]{1,0:T(8,128)S(1)}, f32[128,256]{1,0:T(8,128)S(1)}, u32[]{:S(2)}, u32[]{:S(2)}) %collective-permute-start.3) | collective-permute-done | bytes 131104 | tf_op jit(solution)/shard_map/ppermute | solution.py:423
  10.8 2.3 %forward.2 = (f32[4,2,256,256]{3,2,1,0:T(8,128)S(1)}, f32[2,128,256]{2,1,0:T(8,128)S(1)}, f32[2,256,256]{2,1,0:T(8,128)S(1)}) custom-call(s32[2,2]{1,0:T(2,128)S(1)} %copy-done.5, f32[2,128,256]{2,1,0:T(8,128)S(1)} %copy-done.2, f32[128,256]{1,0:T(8,128)S(1)} %collective-permute-done.pair_ref, f32[128,256]{1,0:T(8,128)S(1)} %collective-permute-done.1.next_ref, ...), custom_call_target="tpu_custom_call" | custom-call | flops 4000000000 | tf_op jit(solution)/shard_map/forward/pallas_call | solution.py:356
  13.4 2.2 %forward.3 = (f32[4,2,256,256]{3,2,1,0:T(8,128)S(1)}, f32[2,128,256]{2,1,0:T(8,128)S(1)}, f32[2,256,256]{2,1,0:T(8,128)S(1)}) custom-call(s32[2,2]{1,0:T(2,128)S(1)} %copy-done.5, f32[2,128,256]{2,1,0:T(8,128)S(1)} %copy-done.2, f32[128,256]{1,0:T(8,128)S(1)} %collective-permute-done.pair_ref, f32[128,256]{1,0:T(8,128)S(1)} %collective-permute-done.1.next_ref, ...), custom_call_target="tpu_custom_call" | custom-call | flops 4000000000 | tf_op jit(solution)/shard_map/forward/pallas_call | solution.py:356
  16.6 0.9 %inverse.5 = (f32[2,256,256]{2,1,0:T(8,128)S(1)}, f32[8,1,2,32,256]{4,3,2,1,0:T(8,128)S(1)}, f32[2,128,256]{2,1,0:T(8,128)S(1)}) custom-call(s32[1]{0:T(128)S(6)} %copy.26.refs_0_, bf16[4,768,256]{2,1,0:T(8,128)(2,1)S(1)} %copy-done.1, bf16[4,256,768]{2,1,0:T(8,128)(2,1)S(1)} %copy-done, f32[2,4,256,256]{3,2,1,0:T(8,128)S(1)} %get-tuple-element.36.probe_ref.refs_3_.refs_2_, ...), custom_call_target="tpu_custom_call" | custom-call | flops 2400000000 | tf_op jit(solution)/shard_map/inverse/pallas_call | solution.py:356
  17.6 0.9 %inverse.6 = (f32[2,256,256]{2,1,0:T(8,128)S(1)}, f32[8,1,2,32,256]{4,3,2,1,0:T(8,128)S(1)}, f32[2,128,256]{2,1,0:T(8,128)S(1)}) custom-call(s32[1]{0:T(128)S(6)} %copy.26.refs_0_, bf16[4,768,256]{2,1,0:T(8,128)(2,1)S(1)} %copy-done.1, bf16[4,256,768]{2,1,0:T(8,128)(2,1)S(1)} %copy-done, ...), custom_call_target="tpu_custom_call", output_to_operand_aliasing={{1}: (9, {})} | custom-call | flops 2400000000 | tf_op jit(solution)/shard_map/inverse/pallas_call | solution.py:356
  18.5 4.6 %collective-permute-start.9 = (f32[4,1,2,32,256]{4,3,2,1,0:T(8,128)S(1)}, f32[4,1,2,32,256]{4,3,2,1,0:T(8,128)S(1)}, u32[]{:S(2)}, u32[]{:S(2)}) collective-permute-start(f32[4,1,2,32,256]{4,3,2,1,0:T(8,128)S(1)} %split.73), channel_id=1, source_target_pairs={{0,4},{2,6},{4,0},{6,2},{8,12},{10,14},{12,8},{14,10},{1,5},{3,7},... | collective-permute-start | bytes 786440 | tf_op jit(solution)/shard_map/ppermute | solution.py:492
  23.1 1.2 %inverse.7 = (f32[2,256,256]{2,1,0:T(8,128)S(1)}, f32[2,256,256]{2,1,0:T(8,128)S(1)}, f32[8,1,2,32,256]{4,3,2,1,0:T(8,128)S(1)}) custom-call(bf16[4,768,256]{2,1,0:T(8,128)(2,1)S(1)} %copy-done.1, bf16[4,256,768]{2,1,0:T(8,128)(2,1)S(1)} %copy-done, ...), custom_call_target="tpu_custom_call", output_to_operand_aliasing={{0}: (9, {}), {1}: (10, {})} | custom-call | flops 2400000000 | tf_op jit(solution)/shard_map/inverse/pallas_call | solution.py:356
  24.3 0.7 %collective-permute-start.12 = (f32[4,1,2,32,256]{4,3,2,1,0:T(8,128)S(1)}, f32[4,1,2,32,256]{4,3,2,1,0:T(8,128)S(1)}, u32[]{:S(2)}, u32[]{:S(2)}) collective-permute-start(f32[4,1,2,32,256]{4,3,2,1,0:T(8,128)S(1)} %split.79), channel_id=1, source_target_pairs={{0,2},{2,0},{4,6},{6,4},{8,10},{10,8},{12,14},{14,12},{1,3},{3,1},... | collective-permute-start | bytes 786440 | tf_op jit(solution)/shard_map/ppermute | solution.py:492
  25.1 1.2 %inverse.8 = (f32[2,256,256]{2,1,0:T(8,128)S(1)}, f32[2,256,256]{2,1,0:T(8,128)S(1)}, f32[8,1,2,32,256]{4,3,2,1,0:T(8,128)S(1)}) custom-call(bf16[4,768,256]{2,1,0:T(8,128)(2,1)S(1)} %copy-done.1, bf16[4,256,768]{2,1,0:T(8,128)(2,1)S(1)} %copy-done, ...), custom_call_target="tpu_custom_call", output_to_operand_aliasing={{0}: (9, {}), {1}: (10, {})} | custom-call | flops 2400000000 | tf_op jit(solution)/shard_map/inverse/pallas_call | solution.py:356
  26.3 1.2 %inverse.9 = (f32[2,256,256]{2,1,0:T(8,128)S(1)}, f32[2,256,256]{2,1,0:T(8,128)S(1)}, f32[8,1,2,32,256]{4,3,2,1,0:T(8,128)S(1)}) custom-call(bf16[4,768,256]{2,1,0:T(8,128)(2,1)S(1)} %copy-done.1, bf16[4,256,768]{2,1,0:T(8,128)(2,1)S(1)} %copy-done, ...), custom_call_target="tpu_custom_call", output_to_operand_aliasing={{0}: (9, {}), {1}: (10, {})} | custom-call | flops 2400000000 | tf_op jit(solution)/shard_map/inverse/pallas_call | solution.py:356
  27.6 1.4 %collective-permute-start.15 = (f32[4,1,2,32,256]{4,3,2,1,0:T(8,128)S(1)}, f32[4,1,2,32,256]{4,3,2,1,0:T(8,128)S(1)}, u32[]{:S(2)}, u32[]{:S(2)}) collective-permute-start(f32[4,1,2,32,256]{4,3,2,1,0:T(8,128)S(1)} %split.85), channel_id=1, source_target_pairs={{0,2},{2,0},{4,6},{6,4},{8,10},{10,8},{12,14},{14,12},{1,3},{3,1},... | collective-permute-start | bytes 786440 | tf_op jit(solution)/shard_map/ppermute | solution.py:492
  29.0 0.6 %strips.1 = (f32[3,2,64,256]{3,2,1,0:T(8,128)S(1)}, f32[3,2,64,256]{3,2,1,0:T(8,128)S(1)}) custom-call(s32[2,2]{1,0:T(2,128)S(1)} %copy-done.5, f32[2,256,256]{2,1,0:T(8,128)S(1)} %get-tuple-element.56.refs_0_, f32[2,256,256]{2,1,0:T(8,128)S(1)} %get-tuple-element.57.refs_1_), custom_call_target="tpu_custom_call" | custom-call | flops 1200000000 | tf_op jit(solution)/shard_map/strips/pallas_call | solution.py:356
  29.8 3.1 %collective-permute-start.10 = (f32[2,1,2,32,256]{4,3,2,1,0:T(8,128)S(1)}, f32[2,1,2,32,256]{4,3,2,1,0:T(8,128)S(1)}, u32[]{:S(2)}, u32[]{:S(2)}) collective-permute-start(f32[2,1,2,32,256]{4,3,2,1,0:T(8,128)S(1)} %split.97), channel_id=1, source_target_pairs={{0,8},{2,10},{4,12},{6,14},{8,0},{10,2},{12,4},{14,6},{1,9},{3,11}... | collective-permute-start | bytes 393224 | tf_op jit(solution)/shard_map/ppermute | solution.py:492
  32.8 0.8 %collective-permute-done.12 = f32[4,1,2,32,256]{4,3,2,1,0:T(8,128)S(1)} collective-permute-done((f32[4,1,2,32,256]{4,3,2,1,0:T(8,128)S(1)}, f32[4,1,2,32,256]{4,3,2,1,0:T(8,128)S(1)}, u32[]{:S(2)}, u32[]{:S(2)}) %collective-permute-start.12) | collective-permute-done | bytes 262176 | tf_op jit(solution)/shard_map/ppermute | solution.py:492
  33.7 0.9 %collective-permute-start.13 = (f32[2,1,2,32,256]{4,3,2,1,0:T(8,128)S(1)}, f32[2,1,2,32,256]{4,3,2,1,0:T(8,128)S(1)}, u32[]{:S(2)}, u32[]{:S(2)}) collective-permute-start(f32[2,1,2,32,256]{4,3,2,1,0:T(8,128)S(1)} %split.101), channel_id=1, source_target_pairs={{0,4},{2,6},{4,0},{6,2},{8,12},{10,14},{12,8},{14,10},{1,5},{3,7},... | collective-permute-start | bytes 393224 | tf_op jit(solution)/shard_map/ppermute | solution.py:492
  34.6 3.5 %collective-permute-done.15 = f32[4,1,2,32,256]{4,3,2,1,0:T(8,128)S(1)} collective-permute-done((f32[4,1,2,32,256]{4,3,2,1,0:T(8,128)S(1)}, f32[4,1,2,32,256]{4,3,2,1,0:T(8,128)S(1)}, u32[]{:S(2)}, u32[]{:S(2)}) %collective-permute-start.15) | collective-permute-done | bytes 262176 | tf_op jit(solution)/shard_map/ppermute | solution.py:492
  38.5 2.5 %collective-permute-done.17 = f32[4,1,2,32,256]{4,3,2,1,0:T(8,128)S(1)} collective-permute-done((f32[4,1,2,32,256]{4,3,2,1,0:T(8,128)S(1)}, f32[4,1,2,32,256]{4,3,2,1,0:T(8,128)S(1)}, u32[]{:S(2)}, u32[]{:S(2)}) %collective-permute-start.17) | collective-permute-done | bytes 262176 | tf_op jit(solution)/shard_map/ppermute | solution.py:492
  41.1 0.7 %collective-permute-start.18 = (f32[2,1,2,32,256]{4,3,2,1,0:T(8,128)S(1)}, f32[2,1,2,32,256]{4,3,2,1,0:T(8,128)S(1)}, u32[]{:S(2)}, u32[]{:S(2)}) collective-permute-start(f32[2,1,2,32,256]{4,3,2,1,0:T(8,128)S(1)} %split.109), channel_id=1, source_target_pairs={{0,2},{2,0},{4,6},{6,4},{8,10},{10,8},{12,14},{14,12},{1,3},{3,1},... | collective-permute-start | bytes 393224 | tf_op jit(solution)/shard_map/ppermute | solution.py:492
  41.9 1.4 %collective-permute-start.11 = (f32[1,1,2,32,256]{4,3,2,1,0:T(8,128)S(1)}, f32[1,1,2,32,256]{4,3,2,1,0:T(8,128)S(1)}, u32[]{:S(2)}, u32[]{:S(2)}) collective-permute-start(f32[1,1,2,32,256]{4,3,2,1,0:T(8,128)S(1)} %get-tuple-element.77), channel_id=1, source_target_pairs={{0,2},{2,0},{4,6},{6,4},{8,10},{10,8},{12,14},{14,12},{1,3},{3,1},... | collective-permute-start | bytes 196616 | tf_op jit(solution)/shard_map/ppermute | solution.py:492
  43.6 3.0 %collective-permute-start.14 = (f32[1,1,2,32,256]{4,3,2,1,0:T(8,128)S(1)}, f32[1,1,2,32,256]{4,3,2,1,0:T(8,128)S(1)}, u32[]{:S(2)}, u32[]{:S(2)}) collective-permute-start(f32[1,1,2,32,256]{4,3,2,1,0:T(8,128)S(1)} %get-tuple-element.75), channel_id=1, source_target_pairs={{0,8},{2,10},{4,12},{6,14},{8,0},{10,2},{12,4},{14,6},{1,9},{3,11}... | collective-permute-start | bytes 196616 | tf_op jit(solution)/shard_map/ppermute | solution.py:492
  46.7 1.7 %collective-permute-start.19 = (f32[2,1,2,32,256]{4,3,2,1,0:T(8,128)S(1)}, f32[2,1,2,32,256]{4,3,2,1,0:T(8,128)S(1)}, u32[]{:S(2)}, u32[]{:S(2)}) collective-permute-start(f32[2,1,2,32,256]{4,3,2,1,0:T(8,128)S(1)} %pad_maximum_fusion), channel_id=1, source_target_pairs={{0,8},{2,10},{4,12},{6,14},{8,0},{10,2},{12,4},{14,6},{1,9},{3,11}... | collective-permute-start | bytes 393224 | tf_op jit(solution)/shard_map/ppermute | solution.py:492
  48.5 0.7 %collective-permute-start.8 = (f32[2,64,256]{2,1,0:T(8,128)S(1)}, f32[2,64,256]{2,1,0:T(8,128)S(1)}, u32[]{:S(2)}, u32[]{:S(2)}) collective-permute-start(f32[2,64,256]{2,1,0:T(8,128)S(1)} %get-tuple-element.66), channel_id=1, source_target_pairs={{2,4},{6,8},{10,12},{4,2},{8,6},{12,10},{3,5},{7,9},{11,13},{5,3},... | collective-permute-start | bytes 393224 | tf_op jit(solution)/shard_map/ppermute | solution.py:506
  49.2 3.2 %collective-permute-start.7 = (f32[2,64,256]{2,1,0:T(8,128)S(1)}, f32[2,64,256]{2,1,0:T(8,128)S(1)}, u32[]{:S(2)}, u32[]{:S(2)}) collective-permute-start(f32[2,64,256]{2,1,0:T(8,128)S(1)} %get-tuple-element.67), channel_id=1, source_target_pairs={{0,2},{2,0},{4,6},{6,4},{8,10},{10,8},{12,14},{14,12},{1,3},{3,1},... | collective-permute-start | bytes 393224 | tf_op jit(solution)/shard_map/ppermute | solution.py:505
  52.4 3.2 %collective-permute-done.19 = f32[2,1,2,32,256]{4,3,2,1,0:T(8,128)S(1)} collective-permute-done((f32[2,1,2,32,256]{4,3,2,1,0:T(8,128)S(1)}, f32[2,1,2,32,256]{4,3,2,1,0:T(8,128)S(1)}, u32[]{:S(2)}, u32[]{:S(2)}) %collective-permute-start.19) | collective-permute-done | bytes 131104 | tf_op jit(solution)/shard_map/ppermute | solution.py:492
  55.9 0.9 %finish.1 = (f32[2,64,256]{2,1,0:T(8,128)}, f32[2,256,128]{2,1,0:T(8,128)}) custom-call(f32[2,256,128]{2,1,0:T(8,128)S(1)} %get-tuple-element.34.probe_ref, f32[2,128,256]{2,1,0:T(8,128)S(1)} %copy-done.2, f32[2,64,256]{2,1,0:T(8,128)S(1)} %get-tuple-element.68.mid_ref, f32[2,64,256]{2,1,0:T(8,128)S(1)} %collective-permute-done.7.pair_ref, ...), custom_call_target="tpu_custom_call" | custom-call | flops 1000000000 | tf_op jit(solution)/shard_map/finish/pallas_call | solution.py:356
  (59 shorter events, 2.5 us)
Async XLA Ops:
  1.6 3.7 %copy-start.3 = (f32[2,4,65536]{2,1,0:T(4,128)S(1)}, f32[2,4,65536]{2,1,0:T(4,128)}, u32[]{:S(2)}) copy-start(f32[2,4,65536]{2,1,0:T(4,128)} %param.9) | copy-start | bytes 6291460
  1.6 6.5 %collective-permute-start = (f32[128,256]{1,0:T(8,128)S(1)}, f32[128,256]{1,0:T(8,128)S(1)}, u32[]{:S(2)}, u32[]{:S(2)}) collective-permute-start(f32[128,256]{1,0:T(8,128)S(1)} %dynamic-slice_bitcast_fusion.part_ref), channel_id=1, source_target_pairs={{0,2},{2,0},{4,6},{6,4},{8,10},{10,8},{12,14},{14,12},{1,3},{3,1},... | collective-permute-start | bytes 393224 | tf_op jit(solution)/shard_map/ppermute | solution.py:393
  4.6 4.5 %collective-permute-start.1 = (f32[128,256]{1,0:T(8,128)S(1)}, f32[128,256]{1,0:T(8,128)S(1)}, u32[]{:S(2)}, u32[]{:S(2)}) collective-permute-start(f32[128,256]{1,0:T(8,128)S(1)} %pick.1), channel_id=1, source_target_pairs={{2,4},{6,8},{10,12},{4,2},{8,6},{12,10},{3,5},{7,9},{11,13},{5,3},... | collective-permute-start | bytes 393224 | tf_op jit(solution)/shard_map/ppermute | solution.py:417
  5.3 2.8 %copy-start.4 = (f32[2,256,256]{2,1,0:T(8,128)S(1)}, f32[2,256,256]{2,1,0:T(8,128)}, u32[]{:S(2)}) copy-start(f32[2,256,256]{2,1,0:T(8,128)} %measured_ref.1) | copy-start | bytes 1572868
  5.3 2.8 %copy-start.6 = (bf16[2,256,256]{2,1,0:T(8,128)(2,1)S(1)}, bf16[2,256,256]{2,1,0:T(8,128)(2,1)}, u32[]{:S(2)}) copy-start(bf16[2,256,256]{2,1,0:T(8,128)(2,1)} %constant.18.clone.order_ref) | copy-start | bytes 786436
  5.7 5.1 %copy-start = (bf16[4,256,768]{2,1,0:T(8,128)(2,1)S(1)}, bf16[4,256,768]{2,1,0:T(8,128)(2,1)}, u32[]{:S(2)}) copy-start(bf16[4,256,768]{2,1,0:T(8,128)(2,1)} %constant.17.clone.col_ref.refs_2_.refs_1_) | copy-start | bytes 4718596
  5.7 5.1 %copy-start.1 = (bf16[4,768,256]{2,1,0:T(8,128)(2,1)S(1)}, bf16[4,768,256]{2,1,0:T(8,128)(2,1)}, u32[]{:S(2)}) copy-start(bf16[4,768,256]{2,1,0:T(8,128)(2,1)} %constant.16.clone.row_ref.refs_1_.refs_0_) | copy-start | bytes 4718596
  5.7 5.0 %copy-start.2 = (f32[2,128,256]{2,1,0:T(8,128)S(1)}, f32[2,128,256]{2,1,0:T(8,128)}, u32[]{:S(2)}) copy-start(f32[2,128,256]{2,1,0:T(8,128)} %strip_ref.1) | copy-start | bytes 786436
  5.7 5.0 %copy-start.5 = (s32[2,2]{1,0:T(2,128)S(1)}, s32[2,2]{1,0:T(2,128)}, u32[]{:S(2)}) copy-start(s32[2,2]{1,0:T(2,128)} %offset_ref.5) | copy-start | bytes 52
  8.1 1.3 %collective-permute-start.2 = (f32[128,256]{1,0:T(8,128)S(1)}, f32[128,256]{1,0:T(8,128)S(1)}, u32[]{:S(2)}, u32[]{:S(2)}) collective-permute-start(f32[128,256]{1,0:T(8,128)S(1)} %collective-permute-done.pair_ref), channel_id=1, source_target_pairs={{0,1},{1,0},{2,3},{3,2},{4,5},{5,4},{6,7},{7,6},{8,9},{9,8},{10,11... | collective-permute-start | bytes 393224 | tf_op jit(solution)/shard_map/ppermute | solution.py:419
  9.4 1.3 %collective-permute-start.3 = (f32[128,256]{1,0:T(8,128)S(1)}, f32[128,256]{1,0:T(8,128)S(1)}, u32[]{:S(2)}, u32[]{:S(2)}) collective-permute-start(f32[128,256]{1,0:T(8,128)S(1)} %collective-permute-done.1.next_ref), channel_id=1, source_target_pairs={{0,1},{1,0},{2,3},{3,2},{4,5},{5,4},{6,7},{7,6},{8,9},{9,8},{10,11... | collective-permute-start | bytes 393224 | tf_op jit(solution)/shard_map/ppermute | solution.py:423
  13.1 3.5 %collective-permute-start.4 = (f32[2,128,256]{2,1,0:T(8,128)S(1)}, f32[2,128,256]{2,1,0:T(8,128)S(1)}, u32[]{:S(2)}, u32[]{:S(2)}) collective-permute-start(f32[2,128,256]{2,1,0:T(8,128)S(1)} %get-tuple-element.45.refs_7_), channel_id=1, source_target_pairs={{0,1},{1,0},{2,3},{3,2},{4,5},{5,4},{6,7},{7,6},{8,9},{9,8},{10,11... | collective-permute-start | bytes 786440 | tf_op jit(solution)/shard_map/ppermute | solution.py:438
  15.6 2.0 %collective-permute-start.5 = (f32[2,128,256]{2,1,0:T(8,128)S(1)}, f32[2,128,256]{2,1,0:T(8,128)S(1)}, u32[]{:S(2)}, u32[]{:S(2)}) collective-permute-start(f32[2,128,256]{2,1,0:T(8,128)S(1)} %get-tuple-element.47.refs_7_), channel_id=1, source_target_pairs={{0,1},{1,0},{2,3},{3,2},{4,5},{5,4},{6,7},{7,6},{8,9},{9,8},{10,11... | collective-permute-start | bytes 786440 | tf_op jit(solution)/shard_map/ppermute | solution.py:438
  18.5 11.2 %collective-permute-start.9 = (f32[4,1,2,32,256]{4,3,2,1,0:T(8,128)S(1)}, f32[4,1,2,32,256]{4,3,2,1,0:T(8,128)S(1)}, u32[]{:S(2)}, u32[]{:S(2)}) collective-permute-start(f32[4,1,2,32,256]{4,3,2,1,0:T(8,128)S(1)} %split.73), channel_id=1, source_target_pairs={{0,4},{2,6},{4,0},{6,2},{8,12},{10,14},{12,8},{14,10},{1,5},{3,7},... | collective-permute-start | bytes 786440 | tf_op jit(solution)/shard_map/ppermute | solution.py:492
  24.3 9.3 %collective-permute-start.12 = (f32[4,1,2,32,256]{4,3,2,1,0:T(8,128)S(1)}, f32[4,1,2,32,256]{4,3,2,1,0:T(8,128)S(1)}, u32[]{:S(2)}, u32[]{:S(2)}) collective-permute-start(f32[4,1,2,32,256]{4,3,2,1,0:T(8,128)S(1)} %split.79), channel_id=1, source_target_pairs={{0,2},{2,0},{4,6},{6,4},{8,10},{10,8},{12,14},{14,12},{1,3},{3,1},... | collective-permute-start | bytes 786440 | tf_op jit(solution)/shard_map/ppermute | solution.py:492
  27.6 10.5 %collective-permute-start.15 = (f32[4,1,2,32,256]{4,3,2,1,0:T(8,128)S(1)}, f32[4,1,2,32,256]{4,3,2,1,0:T(8,128)S(1)}, u32[]{:S(2)}, u32[]{:S(2)}) collective-permute-start(f32[4,1,2,32,256]{4,3,2,1,0:T(8,128)S(1)} %split.85), channel_id=1, source_target_pairs={{0,2},{2,0},{4,6},{6,4},{8,10},{10,8},{12,14},{14,12},{1,3},{3,1},... | collective-permute-start | bytes 786440 | tf_op jit(solution)/shard_map/ppermute | solution.py:492
  29.0 12.1 %collective-permute-start.17 = (f32[4,1,2,32,256]{4,3,2,1,0:T(8,128)S(1)}, f32[4,1,2,32,256]{4,3,2,1,0:T(8,128)S(1)}, u32[]{:S(2)}, u32[]{:S(2)}) collective-permute-start(f32[4,1,2,32,256]{4,3,2,1,0:T(8,128)S(1)} %split.91), channel_id=1, source_target_pairs={{0,4},{2,6},{4,0},{6,2},{8,12},{10,14},{12,8},{14,10},{1,5},{3,7},... | collective-permute-start | bytes 786440 | tf_op jit(solution)/shard_map/ppermute | solution.py:492
  29.6 18.8 %collective-permute-start.6 = (f32[3,2,64,256]{3,2,1,0:T(8,128)S(1)}, f32[3,2,64,256]{3,2,1,0:T(8,128)S(1)}, u32[]{:S(2)}, u32[]{:S(2)}) collective-permute-start(f32[3,2,64,256]{3,2,1,0:T(8,128)S(1)} %get-tuple-element.59), channel_id=1, source_target_pairs={{0,1},{1,0},{2,3},{3,2},{4,5},{5,4},{6,7},{7,6},{8,9},{9,8},{10,11... | collective-permute-start | bytes 1179656 | tf_op jit(solution)/shard_map/ppermute | solution.py:489
  29.8 12.1 %collective-permute-start.10 = (f32[2,1,2,32,256]{4,3,2,1,0:T(8,128)S(1)}, f32[2,1,2,32,256]{4,3,2,1,0:T(8,128)S(1)}, u32[]{:S(2)}, u32[]{:S(2)}) collective-permute-start(f32[2,1,2,32,256]{4,3,2,1,0:T(8,128)S(1)} %split.97), channel_id=1, source_target_pairs={{0,8},{2,10},{4,12},{6,14},{8,0},{10,2},{12,4},{14,6},{1,9},{3,11}... | collective-permute-start | bytes 393224 | tf_op jit(solution)/shard_map/ppermute | solution.py:492
  33.7 9.9 %collective-permute-start.13 = (f32[2,1,2,32,256]{4,3,2,1,0:T(8,128)S(1)}, f32[2,1,2,32,256]{4,3,2,1,0:T(8,128)S(1)}, u32[]{:S(2)}, u32[]{:S(2)}) collective-permute-start(f32[2,1,2,32,256]{4,3,2,1,0:T(8,128)S(1)} %split.101), channel_id=1, source_target_pairs={{0,4},{2,6},{4,0},{6,2},{8,12},{10,14},{12,8},{14,10},{1,5},{3,7},... | collective-permute-start | bytes 393224 | tf_op jit(solution)/shard_map/ppermute | solution.py:492
  38.2 8.4 %collective-permute-start.16 = (f32[2,1,2,32,256]{4,3,2,1,0:T(8,128)S(1)}, f32[2,1,2,32,256]{4,3,2,1,0:T(8,128)S(1)}, u32[]{:S(2)}, u32[]{:S(2)}) collective-permute-start(f32[2,1,2,32,256]{4,3,2,1,0:T(8,128)S(1)} %split.105), channel_id=1, source_target_pairs={{0,4},{2,6},{4,0},{6,2},{8,12},{10,14},{12,8},{14,10},{1,5},{3,7},... | collective-permute-start | bytes 393224 | tf_op jit(solution)/shard_map/ppermute | solution.py:492
  41.1 5.5 %collective-permute-start.18 = (f32[2,1,2,32,256]{4,3,2,1,0:T(8,128)S(1)}, f32[2,1,2,32,256]{4,3,2,1,0:T(8,128)S(1)}, u32[]{:S(2)}, u32[]{:S(2)}) collective-permute-start(f32[2,1,2,32,256]{4,3,2,1,0:T(8,128)S(1)} %split.109), channel_id=1, source_target_pairs={{0,2},{2,0},{4,6},{6,4},{8,10},{10,8},{12,14},{14,12},{1,3},{3,1},... | collective-permute-start | bytes 393224 | tf_op jit(solution)/shard_map/ppermute | solution.py:492
  41.9 13.7 %collective-permute-start.11 = (f32[1,1,2,32,256]{4,3,2,1,0:T(8,128)S(1)}, f32[1,1,2,32,256]{4,3,2,1,0:T(8,128)S(1)}, u32[]{:S(2)}, u32[]{:S(2)}) collective-permute-start(f32[1,1,2,32,256]{4,3,2,1,0:T(8,128)S(1)} %get-tuple-element.77), channel_id=1, source_target_pairs={{0,2},{2,0},{4,6},{6,4},{8,10},{10,8},{12,14},{14,12},{1,3},{3,1},... | collective-permute-start | bytes 196616 | tf_op jit(solution)/shard_map/ppermute | solution.py:492
  43.6 12.0 %collective-permute-start.14 = (f32[1,1,2,32,256]{4,3,2,1,0:T(8,128)S(1)}, f32[1,1,2,32,256]{4,3,2,1,0:T(8,128)S(1)}, u32[]{:S(2)}, u32[]{:S(2)}) collective-permute-start(f32[1,1,2,32,256]{4,3,2,1,0:T(8,128)S(1)} %get-tuple-element.75), channel_id=1, source_target_pairs={{0,8},{2,10},{4,12},{6,14},{8,0},{10,2},{12,4},{14,6},{1,9},{3,11}... | collective-permute-start | bytes 196616 | tf_op jit(solution)/shard_map/ppermute | solution.py:492
  46.7 8.9 %collective-permute-start.19 = (f32[2,1,2,32,256]{4,3,2,1,0:T(8,128)S(1)}, f32[2,1,2,32,256]{4,3,2,1,0:T(8,128)S(1)}, u32[]{:S(2)}, u32[]{:S(2)}) collective-permute-start(f32[2,1,2,32,256]{4,3,2,1,0:T(8,128)S(1)} %pad_maximum_fusion), channel_id=1, source_target_pairs={{0,8},{2,10},{4,12},{6,14},{8,0},{10,2},{12,4},{14,6},{1,9},{3,11}... | collective-permute-start | bytes 393224 | tf_op jit(solution)/shard_map/ppermute | solution.py:492
  48.5 7.1 %collective-permute-start.8 = (f32[2,64,256]{2,1,0:T(8,128)S(1)}, f32[2,64,256]{2,1,0:T(8,128)S(1)}, u32[]{:S(2)}, u32[]{:S(2)}) collective-permute-start(f32[2,64,256]{2,1,0:T(8,128)S(1)} %get-tuple-element.66), channel_id=1, source_target_pairs={{2,4},{6,8},{10,12},{4,2},{8,6},{12,10},{3,5},{7,9},{11,13},{5,3},... | collective-permute-start | bytes 393224 | tf_op jit(solution)/shard_map/ppermute | solution.py:506
  49.2 6.7 %collective-permute-start.7 = (f32[2,64,256]{2,1,0:T(8,128)S(1)}, f32[2,64,256]{2,1,0:T(8,128)S(1)}, u32[]{:S(2)}, u32[]{:S(2)}) collective-permute-start(f32[2,64,256]{2,1,0:T(8,128)S(1)} %get-tuple-element.67), channel_id=1, source_target_pairs={{0,2},{2,0},{4,6},{6,4},{8,10},{10,8},{12,14},{14,12},{1,3},{3,1},... | collective-permute-start | bytes 393224 | tf_op jit(solution)/shard_map/ppermute | solution.py:505

commit v8 on v7

--- a/solution.py
+++ b/solution.py
@@ -18,7 +18,7 @@
 BF16 = jnp.bfloat16
 VMEM_LIMIT = 16 * 1024 * 1024
 COSTS = {'prepare': 2000000000, 'forward': 4000000000, 'inverse': 2400000000, 'strips': 1200000000, 'finish': 1000000000, 'order': 1000000000, 'pick': 3000000000}
-CHUNK = 64
+CHUNK = 128
 PATTERN = (0, 1, 1, 2)
 STEPS = (((0,), 1), ((1,), 0), ((2,), 0), ((3,), 1), ((0,), 2), ((1,), 1), ((3,), 0), ((2,), 1), ((0,), 0), ((1,), 2), ((2, 3), 2))
 

time: 56.9 us -> 56.9 us (level)
  no operation moved by 1% of the time
where the time goes in v8:
time: 56.9 us; the launch traced here: 56.8 us
  starting transfers between devices  26.4 us (46%)
  waiting for transfers between devices  14.4 us (25%)
  Pallas kernels  12.8 us (22%)
  between operations  1.69 us (3%)
  local copies, waits for them, and re-layouts  1.16 us (2%)
    ppermute x11, starting transfers between devices, exchange(): lax.ppermute(payload, 'pos', [(i, i ^ 2 ** bit) for i in range(positions)])  18 us
    pallas_call x12, Pallas kernels, call(): pl.pallas_call(kernel, out_shape=out_shape, in_specs=[smem] * len(scalars...  12.8 us
    ppermute x11, waiting for transfers between devices, exchange(): lax.ppermute(payload, 'pos', [(i, i ^ 2 ** bit) for i in range(positions)])  10.2 us
    ppermute x1, starting transfers between devices, on_device(): from_pair = lax.ppermute(strips[0], 'pos', pair)  3.18 us
    ppermute x1, starting transfers between devices, on_device(): from_pair = lax.ppermute(component, 'pos', pair)  3 us
    ppermute x1, waiting for transfers between devices, on_device(): from_pair = lax.ppermute(component, 'pos', pair)  2.31 us
    ppermute x1, waiting for transfers between devices, on_device(): lax.ppermute(from_next, 'tile', swap)  1.14 us
  transfers between devices with their start and end apart: 20, of which 9 were waited for; matrix products, arithmetic and copies ran while one was open for 1% of the time, Pallas kernels for 15%

profile of v8, /device:TPU:0, one launch (start us, length us, event | category | flops | bytes accessed | tf_op | source)
XLA Modules:
  0.0 56.8 jit_solution(9890066208669311694)
XLA Ops:
  0.6 0.9 %dynamic-slice_bitcast_fusion.part_ref = f32[128,256]{1,0:T(8,128)S(1)} fusion(f32[2,128,256]{2,1,0:T(8,128)} %strip_ref.1, s32[]{:T(128)S(6)} %select_n.4), kind=kLoop, calls=%fused_computation.12 | loop fusion | bytes 262148 | tf_op jit(solution)/shard_map/jit(dynamic_index_in_dim)/squeeze | solution.py:392
  1.6 3.0 %collective-permute-start = (f32[128,256]{1,0:T(8,128)S(1)}, f32[128,256]{1,0:T(8,128)S(1)}, u32[]{:S(2)}, u32[]{:S(2)}) collective-permute-start(f32[128,256]{1,0:T(8,128)S(1)} %dynamic-slice_bitcast_fusion.part_ref), channel_id=1, source_target_pairs={{0,2},{2,0},{4,6},{6,4},{8,10},{10,8},{12,14},{14,12},{1,3},{3,1},... | collective-permute-start | bytes 393224 | tf_op jit(solution)/shard_map/ppermute | solution.py:393
  4.6 0.7 %collective-permute-start.1 = (f32[128,256]{1,0:T(8,128)S(1)}, f32[128,256]{1,0:T(8,128)S(1)}, u32[]{:S(2)}, u32[]{:S(2)}) collective-permute-start(f32[128,256]{1,0:T(8,128)S(1)} %pick.1), channel_id=1, source_target_pairs={{2,4},{6,8},{10,12},{4,2},{8,6},{12,10},{3,5},{7,9},{11,13},{5,3},... | collective-permute-start | bytes 393224 | tf_op jit(solution)/shard_map/ppermute | solution.py:417
  5.3 0.4 prepare.1
  5.8 2.3 %collective-permute-done.pair_ref = f32[128,256]{1,0:T(8,128)S(1)} collective-permute-done((f32[128,256]{1,0:T(8,128)S(1)}, f32[128,256]{1,0:T(8,128)S(1)}, u32[]{:S(2)}, u32[]{:S(2)}) %collective-permute-start) | collective-permute-done | bytes 131104 | tf_op jit(solution)/shard_map/ppermute | solution.py:393
  8.1 0.9 %order.1.refs_6_ = f32[2,2,128,256]{3,2,1,0:T(8,128)S(1)} custom-call(f32[2,256,256]{2,1,0:T(8,128)S(1)} %copy-done.4, bf16[2,256,256]{2,1,0:T(8,128)(2,1)S(1)} %copy-done.6), custom_call_target="tpu_custom_call" | custom-call | flops 1000000000 | tf_op jit(solution)/shard_map/order/pallas_call | solution.py:356
  9.0 0.4 collective-permute-done.2.pair_other_ref
  9.6 1.1 %collective-permute-done.3.next_other_ref = f32[128,256]{1,0:T(8,128)S(1)} collective-permute-done((f32[128,256]{1,0:T(8,128)S(1)}, f32[128,256]{1,0:T(8,128)S(1)}, u32[]{:S(2)}, u32[]{:S(2)}) %collective-permute-start.3) | collective-permute-done | bytes 131104 | tf_op jit(solution)/shard_map/ppermute | solution.py:423
  10.8 2.3 %forward.2 = (f32[4,2,256,256]{3,2,1,0:T(8,128)S(1)}, f32[2,128,256]{2,1,0:T(8,128)S(1)}, f32[2,256,256]{2,1,0:T(8,128)S(1)}) custom-call(s32[2,2]{1,0:T(2,128)S(1)} %copy-done.5, f32[2,128,256]{2,1,0:T(8,128)S(1)} %copy-done.2, f32[128,256]{1,0:T(8,128)S(1)} %collective-permute-done.pair_ref, f32[128,256]{1,0:T(8,128)S(1)} %collective-permute-done.1.next_ref, ...), custom_call_target="tpu_custom_call" | custom-call | flops 4000000000 | tf_op jit(solution)/shard_map/forward/pallas_call | solution.py:356
  13.4 2.2 %forward.3 = (f32[4,2,256,256]{3,2,1,0:T(8,128)S(1)}, f32[2,128,256]{2,1,0:T(8,128)S(1)}, f32[2,256,256]{2,1,0:T(8,128)S(1)}) custom-call(s32[2,2]{1,0:T(2,128)S(1)} %copy-done.5, f32[2,128,256]{2,1,0:T(8,128)S(1)} %copy-done.2, f32[128,256]{1,0:T(8,128)S(1)} %collective-permute-done.pair_ref, f32[128,256]{1,0:T(8,128)S(1)} %collective-permute-done.1.next_ref, ...), custom_call_target="tpu_custom_call" | custom-call | flops 4000000000 | tf_op jit(solution)/shard_map/forward/pallas_call | solution.py:356
  16.6 0.9 %inverse.5 = (f32[2,256,256]{2,1,0:T(8,128)S(1)}, f32[8,1,2,32,256]{4,3,2,1,0:T(8,128)S(1)}, f32[2,128,256]{2,1,0:T(8,128)S(1)}) custom-call(s32[1]{0:T(128)S(6)} %copy.26.refs_0_, bf16[4,768,256]{2,1,0:T(8,128)(2,1)S(1)} %copy-done.1, bf16[4,256,768]{2,1,0:T(8,128)(2,1)S(1)} %copy-done, f32[2,4,256,256]{3,2,1,0:T(8,128)S(1)} %get-tuple-element.36.probe_ref.refs_3_.refs_2_, ...), custom_call_target="tpu_custom_call" | custom-call | flops 2400000000 | tf_op jit(solution)/shard_map/inverse/pallas_call | solution.py:356
  17.6 0.9 %inverse.6 = (f32[2,256,256]{2,1,0:T(8,128)S(1)}, f32[8,1,2,32,256]{4,3,2,1,0:T(8,128)S(1)}, f32[2,128,256]{2,1,0:T(8,128)S(1)}) custom-call(s32[1]{0:T(128)S(6)} %copy.26.refs_0_, bf16[4,768,256]{2,1,0:T(8,128)(2,1)S(1)} %copy-done.1, bf16[4,256,768]{2,1,0:T(8,128)(2,1)S(1)} %copy-done, ...), custom_call_target="tpu_custom_call", output_to_operand_aliasing={{1}: (9, {})} | custom-call | flops 2400000000 | tf_op jit(solution)/shard_map/inverse/pallas_call | solution.py:356
  18.5 4.6 %collective-permute-start.9 = (f32[4,1,2,32,256]{4,3,2,1,0:T(8,128)S(1)}, f32[4,1,2,32,256]{4,3,2,1,0:T(8,128)S(1)}, u32[]{:S(2)}, u32[]{:S(2)}) collective-permute-start(f32[4,1,2,32,256]{4,3,2,1,0:T(8,128)S(1)} %split.73), channel_id=1, source_target_pairs={{0,4},{2,6},{4,0},{6,2},{8,12},{10,14},{12,8},{14,10},{1,5},{3,7},... | collective-permute-start | bytes 786440 | tf_op jit(solution)/shard_map/ppermute | solution.py:492
  23.1 1.2 %inverse.7 = (f32[2,256,256]{2,1,0:T(8,128)S(1)}, f32[2,256,256]{2,1,0:T(8,128)S(1)}, f32[8,1,2,32,256]{4,3,2,1,0:T(8,128)S(1)}) custom-call(bf16[4,768,256]{2,1,0:T(8,128)(2,1)S(1)} %copy-done.1, bf16[4,256,768]{2,1,0:T(8,128)(2,1)S(1)} %copy-done, ...), custom_call_target="tpu_custom_call", output_to_operand_aliasing={{0}: (9, {}), {1}: (10, {})} | custom-call | flops 2400000000 | tf_op jit(solution)/shard_map/inverse/pallas_call | solution.py:356
  24.3 0.7 %collective-permute-start.12 = (f32[4,1,2,32,256]{4,3,2,1,0:T(8,128)S(1)}, f32[4,1,2,32,256]{4,3,2,1,0:T(8,128)S(1)}, u32[]{:S(2)}, u32[]{:S(2)}) collective-permute-start(f32[4,1,2,32,256]{4,3,2,1,0:T(8,128)S(1)} %split.79), channel_id=1, source_target_pairs={{0,2},{2,0},{4,6},{6,4},{8,10},{10,8},{12,14},{14,12},{1,3},{3,1},... | collective-permute-start | bytes 786440 | tf_op jit(solution)/shard_map/ppermute | solution.py:492
  25.1 1.2 %inverse.8 = (f32[2,256,256]{2,1,0:T(8,128)S(1)}, f32[2,256,256]{2,1,0:T(8,128)S(1)}, f32[8,1,2,32,256]{4,3,2,1,0:T(8,128)S(1)}) custom-call(bf16[4,768,256]{2,1,0:T(8,128)(2,1)S(1)} %copy-done.1, bf16[4,256,768]{2,1,0:T(8,128)(2,1)S(1)} %copy-done, ...), custom_call_target="tpu_custom_call", output_to_operand_aliasing={{0}: (9, {}), {1}: (10, {})} | custom-call | flops 2400000000 | tf_op jit(solution)/shard_map/inverse/pallas_call | solution.py:356
  26.3 1.2 %inverse.9 = (f32[2,256,256]{2,1,0:T(8,128)S(1)}, f32[2,256,256]{2,1,0:T(8,128)S(1)}, f32[8,1,2,32,256]{4,3,2,1,0:T(8,128)S(1)}) custom-call(bf16[4,768,256]{2,1,0:T(8,128)(2,1)S(1)} %copy-done.1, bf16[4,256,768]{2,1,0:T(8,128)(2,1)S(1)} %copy-done, ...), custom_call_target="tpu_custom_call", output_to_operand_aliasing={{0}: (9, {}), {1}: (10, {})} | custom-call | flops 2400000000 | tf_op jit(solution)/shard_map/inverse/pallas_call | solution.py:356
  27.6 1.4 %collective-permute-start.15 = (f32[4,1,2,32,256]{4,3,2,1,0:T(8,128)S(1)}, f32[4,1,2,32,256]{4,3,2,1,0:T(8,128)S(1)}, u32[]{:S(2)}, u32[]{:S(2)}) collective-permute-start(f32[4,1,2,32,256]{4,3,2,1,0:T(8,128)S(1)} %split.85), channel_id=1, source_target_pairs={{0,2},{2,0},{4,6},{6,4},{8,10},{10,8},{12,14},{14,12},{1,3},{3,1},... | collective-permute-start | bytes 786440 | tf_op jit(solution)/shard_map/ppermute | solution.py:492
  29.0 0.6 %strips.1 = (f32[3,2,64,256]{3,2,1,0:T(8,128)S(1)}, f32[3,2,64,256]{3,2,1,0:T(8,128)S(1)}) custom-call(s32[2,2]{1,0:T(2,128)S(1)} %copy-done.5, f32[2,256,256]{2,1,0:T(8,128)S(1)} %get-tuple-element.56.refs_0_, f32[2,256,256]{2,1,0:T(8,128)S(1)} %get-tuple-element.57.refs_1_), custom_call_target="tpu_custom_call" | custom-call | flops 1200000000 | tf_op jit(solution)/shard_map/strips/pallas_call | solution.py:356
  29.8 3.1 %collective-permute-start.10 = (f32[2,1,2,32,256]{4,3,2,1,0:T(8,128)S(1)}, f32[2,1,2,32,256]{4,3,2,1,0:T(8,128)S(1)}, u32[]{:S(2)}, u32[]{:S(2)}) collective-permute-start(f32[2,1,2,32,256]{4,3,2,1,0:T(8,128)S(1)} %split.97), channel_id=1, source_target_pairs={{0,8},{2,10},{4,12},{6,14},{8,0},{10,2},{12,4},{14,6},{1,9},{3,11}... | collective-permute-start | bytes 393224 | tf_op jit(solution)/shard_map/ppermute | solution.py:492
  32.9 0.7 %collective-permute-done.12 = f32[4,1,2,32,256]{4,3,2,1,0:T(8,128)S(1)} collective-permute-done((f32[4,1,2,32,256]{4,3,2,1,0:T(8,128)S(1)}, f32[4,1,2,32,256]{4,3,2,1,0:T(8,128)S(1)}, u32[]{:S(2)}, u32[]{:S(2)}) %collective-permute-start.12) | collective-permute-done | bytes 262176 | tf_op jit(solution)/shard_map/ppermute | solution.py:492
  33.7 0.9 %collective-permute-start.13 = (f32[2,1,2,32,256]{4,3,2,1,0:T(8,128)S(1)}, f32[2,1,2,32,256]{4,3,2,1,0:T(8,128)S(1)}, u32[]{:S(2)}, u32[]{:S(2)}) collective-permute-start(f32[2,1,2,32,256]{4,3,2,1,0:T(8,128)S(1)} %split.101), channel_id=1, source_target_pairs={{0,4},{2,6},{4,0},{6,2},{8,12},{10,14},{12,8},{14,10},{1,5},{3,7},... | collective-permute-start | bytes 393224 | tf_op jit(solution)/shard_map/ppermute | solution.py:492
  34.6 3.6 %collective-permute-done.15 = f32[4,1,2,32,256]{4,3,2,1,0:T(8,128)S(1)} collective-permute-done((f32[4,1,2,32,256]{4,3,2,1,0:T(8,128)S(1)}, f32[4,1,2,32,256]{4,3,2,1,0:T(8,128)S(1)}, u32[]{:S(2)}, u32[]{:S(2)}) %collective-permute-start.15) | collective-permute-done | bytes 262176 | tf_op jit(solution)/shard_map/ppermute | solution.py:492
  38.5 2.5 %collective-permute-done.17 = f32[4,1,2,32,256]{4,3,2,1,0:T(8,128)S(1)} collective-permute-done((f32[4,1,2,32,256]{4,3,2,1,0:T(8,128)S(1)}, f32[4,1,2,32,256]{4,3,2,1,0:T(8,128)S(1)}, u32[]{:S(2)}, u32[]{:S(2)}) %collective-permute-start.17) | collective-permute-done | bytes 262176 | tf_op jit(solution)/shard_map/ppermute | solution.py:492
  41.1 0.7 %collective-permute-start.18 = (f32[2,1,2,32,256]{4,3,2,1,0:T(8,128)S(1)}, f32[2,1,2,32,256]{4,3,2,1,0:T(8,128)S(1)}, u32[]{:S(2)}, u32[]{:S(2)}) collective-permute-start(f32[2,1,2,32,256]{4,3,2,1,0:T(8,128)S(1)} %split.109), channel_id=1, source_target_pairs={{0,2},{2,0},{4,6},{6,4},{8,10},{10,8},{12,14},{14,12},{1,3},{3,1},... | collective-permute-start | bytes 393224 | tf_op jit(solution)/shard_map/ppermute | solution.py:492
  41.9 1.4 %collective-permute-start.11 = (f32[1,1,2,32,256]{4,3,2,1,0:T(8,128)S(1)}, f32[1,1,2,32,256]{4,3,2,1,0:T(8,128)S(1)}, u32[]{:S(2)}, u32[]{:S(2)}) collective-permute-start(f32[1,1,2,32,256]{4,3,2,1,0:T(8,128)S(1)} %get-tuple-element.77), channel_id=1, source_target_pairs={{0,2},{2,0},{4,6},{6,4},{8,10},{10,8},{12,14},{14,12},{1,3},{3,1},... | collective-permute-start | bytes 196616 | tf_op jit(solution)/shard_map/ppermute | solution.py:492
  43.6 3.0 %collective-permute-start.14 = (f32[1,1,2,32,256]{4,3,2,1,0:T(8,128)S(1)}, f32[1,1,2,32,256]{4,3,2,1,0:T(8,128)S(1)}, u32[]{:S(2)}, u32[]{:S(2)}) collective-permute-start(f32[1,1,2,32,256]{4,3,2,1,0:T(8,128)S(1)} %get-tuple-element.75), channel_id=1, source_target_pairs={{0,8},{2,10},{4,12},{6,14},{8,0},{10,2},{12,4},{14,6},{1,9},{3,11}... | collective-permute-start | bytes 196616 | tf_op jit(solution)/shard_map/ppermute | solution.py:492
  46.7 1.7 %collective-permute-start.19 = (f32[2,1,2,32,256]{4,3,2,1,0:T(8,128)S(1)}, f32[2,1,2,32,256]{4,3,2,1,0:T(8,128)S(1)}, u32[]{:S(2)}, u32[]{:S(2)}) collective-permute-start(f32[2,1,2,32,256]{4,3,2,1,0:T(8,128)S(1)} %pad_maximum_fusion), channel_id=1, source_target_pairs={{0,8},{2,10},{4,12},{6,14},{8,0},{10,2},{12,4},{14,6},{1,9},{3,11}... | collective-permute-start | bytes 393224 | tf_op jit(solution)/shard_map/ppermute | solution.py:492
  48.5 0.7 %collective-permute-start.8 = (f32[2,64,256]{2,1,0:T(8,128)S(1)}, f32[2,64,256]{2,1,0:T(8,128)S(1)}, u32[]{:S(2)}, u32[]{:S(2)}) collective-permute-start(f32[2,64,256]{2,1,0:T(8,128)S(1)} %get-tuple-element.66), channel_id=1, source_target_pairs={{2,4},{6,8},{10,12},{4,2},{8,6},{12,10},{3,5},{7,9},{11,13},{5,3},... | collective-permute-start | bytes 393224 | tf_op jit(solution)/shard_map/ppermute | solution.py:506
  49.2 3.2 %collective-permute-start.7 = (f32[2,64,256]{2,1,0:T(8,128)S(1)}, f32[2,64,256]{2,1,0:T(8,128)S(1)}, u32[]{:S(2)}, u32[]{:S(2)}) collective-permute-start(f32[2,64,256]{2,1,0:T(8,128)S(1)} %get-tuple-element.67), channel_id=1, source_target_pairs={{0,2},{2,0},{4,6},{6,4},{8,10},{10,8},{12,14},{14,12},{1,3},{3,1},... | collective-permute-start | bytes 393224 | tf_op jit(solution)/shard_map/ppermute | solution.py:505
  52.4 3.2 %collective-permute-done.19 = f32[2,1,2,32,256]{4,3,2,1,0:T(8,128)S(1)} collective-permute-done((f32[2,1,2,32,256]{4,3,2,1,0:T(8,128)S(1)}, f32[2,1,2,32,256]{4,3,2,1,0:T(8,128)S(1)}, u32[]{:S(2)}, u32[]{:S(2)}) %collective-permute-start.19) | collective-permute-done | bytes 131104 | tf_op jit(solution)/shard_map/ppermute | solution.py:492
  55.9 0.9 %finish.1 = (f32[2,64,256]{2,1,0:T(8,128)}, f32[2,256,128]{2,1,0:T(8,128)}) custom-call(f32[2,256,128]{2,1,0:T(8,128)S(1)} %get-tuple-element.34.probe_ref, f32[2,128,256]{2,1,0:T(8,128)S(1)} %copy-done.2, f32[2,64,256]{2,1,0:T(8,128)S(1)} %get-tuple-element.68.mid_ref, f32[2,64,256]{2,1,0:T(8,128)S(1)} %collective-permute-done.7.pair_ref, ...), custom_call_target="tpu_custom_call" | custom-call | flops 1000000000 | tf_op jit(solution)/shard_map/finish/pallas_call | solution.py:356
  (59 shorter events, 2.5 us)
Async XLA Ops:
  1.6 3.7 %copy-start.3 = (f32[2,4,65536]{2,1,0:T(4,128)S(1)}, f32[2,4,65536]{2,1,0:T(4,128)}, u32[]{:S(2)}) copy-start(f32[2,4,65536]{2,1,0:T(4,128)} %param.9) | copy-start | bytes 6291460
  1.6 6.5 %collective-permute-start = (f32[128,256]{1,0:T(8,128)S(1)}, f32[128,256]{1,0:T(8,128)S(1)}, u32[]{:S(2)}, u32[]{:S(2)}) collective-permute-start(f32[128,256]{1,0:T(8,128)S(1)} %dynamic-slice_bitcast_fusion.part_ref), channel_id=1, source_target_pairs={{0,2},{2,0},{4,6},{6,4},{8,10},{10,8},{12,14},{14,12},{1,3},{3,1},... | collective-permute-start | bytes 393224 | tf_op jit(solution)/shard_map/ppermute | solution.py:393
  4.6 4.5 %collective-permute-start.1 = (f32[128,256]{1,0:T(8,128)S(1)}, f32[128,256]{1,0:T(8,128)S(1)}, u32[]{:S(2)}, u32[]{:S(2)}) collective-permute-start(f32[128,256]{1,0:T(8,128)S(1)} %pick.1), channel_id=1, source_target_pairs={{2,4},{6,8},{10,12},{4,2},{8,6},{12,10},{3,5},{7,9},{11,13},{5,3},... | collective-permute-start | bytes 393224 | tf_op jit(solution)/shard_map/ppermute | solution.py:417
  5.3 2.8 %copy-start.4 = (f32[2,256,256]{2,1,0:T(8,128)S(1)}, f32[2,256,256]{2,1,0:T(8,128)}, u32[]{:S(2)}) copy-start(f32[2,256,256]{2,1,0:T(8,128)} %measured_ref.1) | copy-start | bytes 1572868
  5.3 2.8 %copy-start.6 = (bf16[2,256,256]{2,1,0:T(8,128)(2,1)S(1)}, bf16[2,256,256]{2,1,0:T(8,128)(2,1)}, u32[]{:S(2)}) copy-start(bf16[2,256,256]{2,1,0:T(8,128)(2,1)} %constant.18.clone.order_ref) | copy-start | bytes 786436
  5.7 5.1 %copy-start = (bf16[4,256,768]{2,1,0:T(8,128)(2,1)S(1)}, bf16[4,256,768]{2,1,0:T(8,128)(2,1)}, u32[]{:S(2)}) copy-start(bf16[4,256,768]{2,1,0:T(8,128)(2,1)} %constant.17.clone.col_ref.refs_2_.refs_1_) | copy-start | bytes 4718596
  5.7 5.1 %copy-start.1 = (bf16[4,768,256]{2,1,0:T(8,128)(2,1)S(1)}, bf16[4,768,256]{2,1,0:T(8,128)(2,1)}, u32[]{:S(2)}) copy-start(bf16[4,768,256]{2,1,0:T(8,128)(2,1)} %constant.16.clone.row_ref.refs_1_.refs_0_) | copy-start | bytes 4718596
  5.7 5.0 %copy-start.2 = (f32[2,128,256]{2,1,0:T(8,128)S(1)}, f32[2,128,256]{2,1,0:T(8,128)}, u32[]{:S(2)}) copy-start(f32[2,128,256]{2,1,0:T(8,128)} %strip_ref.1) | copy-start | bytes 786436
  5.7 5.0 %copy-start.5 = (s32[2,2]{1,0:T(2,128)S(1)}, s32[2,2]{1,0:T(2,128)}, u32[]{:S(2)}) copy-start(s32[2,2]{1,0:T(2,128)} %offset_ref.5) | copy-start | bytes 52
  8.1 1.3 %collective-permute-start.2 = (f32[128,256]{1,0:T(8,128)S(1)}, f32[128,256]{1,0:T(8,128)S(1)}, u32[]{:S(2)}, u32[]{:S(2)}) collective-permute-start(f32[128,256]{1,0:T(8,128)S(1)} %collective-permute-done.pair_ref), channel_id=1, source_target_pairs={{0,1},{1,0},{2,3},{3,2},{4,5},{5,4},{6,7},{7,6},{8,9},{9,8},{10,11... | collective-permute-start | bytes 393224 | tf_op jit(solution)/shard_map/ppermute | solution.py:419
  9.4 1.3 %collective-permute-start.3 = (f32[128,256]{1,0:T(8,128)S(1)}, f32[128,256]{1,0:T(8,128)S(1)}, u32[]{:S(2)}, u32[]{:S(2)}) collective-permute-start(f32[128,256]{1,0:T(8,128)S(1)} %collective-permute-done.1.next_ref), channel_id=1, source_target_pairs={{0,1},{1,0},{2,3},{3,2},{4,5},{5,4},{6,7},{7,6},{8,9},{9,8},{10,11... | collective-permute-start | bytes 393224 | tf_op jit(solution)/shard_map/ppermute | solution.py:423
  13.1 3.5 %collective-permute-start.4 = (f32[2,128,256]{2,1,0:T(8,128)S(1)}, f32[2,128,256]{2,1,0:T(8,128)S(1)}, u32[]{:S(2)}, u32[]{:S(2)}) collective-permute-start(f32[2,128,256]{2,1,0:T(8,128)S(1)} %get-tuple-element.45.refs_7_), channel_id=1, source_target_pairs={{0,1},{1,0},{2,3},{3,2},{4,5},{5,4},{6,7},{7,6},{8,9},{9,8},{10,11... | collective-permute-start | bytes 786440 | tf_op jit(solution)/shard_map/ppermute | solution.py:438
  15.6 2.0 %collective-permute-start.5 = (f32[2,128,256]{2,1,0:T(8,128)S(1)}, f32[2,128,256]{2,1,0:T(8,128)S(1)}, u32[]{:S(2)}, u32[]{:S(2)}) collective-permute-start(f32[2,128,256]{2,1,0:T(8,128)S(1)} %get-tuple-element.47.refs_7_), channel_id=1, source_target_pairs={{0,1},{1,0},{2,3},{3,2},{4,5},{5,4},{6,7},{7,6},{8,9},{9,8},{10,11... | collective-permute-start | bytes 786440 | tf_op jit(solution)/shard_map/ppermute | solution.py:438
  18.5 11.2 %collective-permute-start.9 = (f32[4,1,2,32,256]{4,3,2,1,0:T(8,128)S(1)}, f32[4,1,2,32,256]{4,3,2,1,0:T(8,128)S(1)}, u32[]{:S(2)}, u32[]{:S(2)}) collective-permute-start(f32[4,1,2,32,256]{4,3,2,1,0:T(8,128)S(1)} %split.73), channel_id=1, source_target_pairs={{0,4},{2,6},{4,0},{6,2},{8,12},{10,14},{12,8},{14,10},{1,5},{3,7},... | collective-permute-start | bytes 786440 | tf_op jit(solution)/shard_map/ppermute | solution.py:492
  24.3 9.3 %collective-permute-start.12 = (f32[4,1,2,32,256]{4,3,2,1,0:T(8,128)S(1)}, f32[4,1,2,32,256]{4,3,2,1,0:T(8,128)S(1)}, u32[]{:S(2)}, u32[]{:S(2)}) collective-permute-start(f32[4,1,2,32,256]{4,3,2,1,0:T(8,128)S(1)} %split.79), channel_id=1, source_target_pairs={{0,2},{2,0},{4,6},{6,4},{8,10},{10,8},{12,14},{14,12},{1,3},{3,1},... | collective-permute-start | bytes 786440 | tf_op jit(solution)/shard_map/ppermute | solution.py:492
  27.6 10.5 %collective-permute-start.15 = (f32[4,1,2,32,256]{4,3,2,1,0:T(8,128)S(1)}, f32[4,1,2,32,256]{4,3,2,1,0:T(8,128)S(1)}, u32[]{:S(2)}, u32[]{:S(2)}) collective-permute-start(f32[4,1,2,32,256]{4,3,2,1,0:T(8,128)S(1)} %split.85), channel_id=1, source_target_pairs={{0,2},{2,0},{4,6},{6,4},{8,10},{10,8},{12,14},{14,12},{1,3},{3,1},... | collective-permute-start | bytes 786440 | tf_op jit(solution)/shard_map/ppermute | solution.py:492
  29.0 12.1 %collective-permute-start.17 = (f32[4,1,2,32,256]{4,3,2,1,0:T(8,128)S(1)}, f32[4,1,2,32,256]{4,3,2,1,0:T(8,128)S(1)}, u32[]{:S(2)}, u32[]{:S(2)}) collective-permute-start(f32[4,1,2,32,256]{4,3,2,1,0:T(8,128)S(1)} %split.91), channel_id=1, source_target_pairs={{0,4},{2,6},{4,0},{6,2},{8,12},{10,14},{12,8},{14,10},{1,5},{3,7},... | collective-permute-start | bytes 786440 | tf_op jit(solution)/shard_map/ppermute | solution.py:492
  29.6 18.8 %collective-permute-start.6 = (f32[3,2,64,256]{3,2,1,0:T(8,128)S(1)}, f32[3,2,64,256]{3,2,1,0:T(8,128)S(1)}, u32[]{:S(2)}, u32[]{:S(2)}) collective-permute-start(f32[3,2,64,256]{3,2,1,0:T(8,128)S(1)} %get-tuple-element.59), channel_id=1, source_target_pairs={{0,1},{1,0},{2,3},{3,2},{4,5},{5,4},{6,7},{7,6},{8,9},{9,8},{10,11... | collective-permute-start | bytes 1179656 | tf_op jit(solution)/shard_map/ppermute | solution.py:489
  29.8 12.1 %collective-permute-start.10 = (f32[2,1,2,32,256]{4,3,2,1,0:T(8,128)S(1)}, f32[2,1,2,32,256]{4,3,2,1,0:T(8,128)S(1)}, u32[]{:S(2)}, u32[]{:S(2)}) collective-permute-start(f32[2,1,2,32,256]{4,3,2,1,0:T(8,128)S(1)} %split.97), channel_id=1, source_target_pairs={{0,8},{2,10},{4,12},{6,14},{8,0},{10,2},{12,4},{14,6},{1,9},{3,11}... | collective-permute-start | bytes 393224 | tf_op jit(solution)/shard_map/ppermute | solution.py:492
  33.7 9.9 %collective-permute-start.13 = (f32[2,1,2,32,256]{4,3,2,1,0:T(8,128)S(1)}, f32[2,1,2,32,256]{4,3,2,1,0:T(8,128)S(1)}, u32[]{:S(2)}, u32[]{:S(2)}) collective-permute-start(f32[2,1,2,32,256]{4,3,2,1,0:T(8,128)S(1)} %split.101), channel_id=1, source_target_pairs={{0,4},{2,6},{4,0},{6,2},{8,12},{10,14},{12,8},{14,10},{1,5},{3,7},... | collective-permute-start | bytes 393224 | tf_op jit(solution)/shard_map/ppermute | solution.py:492
  38.2 8.4 %collective-permute-start.16 = (f32[2,1,2,32,256]{4,3,2,1,0:T(8,128)S(1)}, f32[2,1,2,32,256]{4,3,2,1,0:T(8,128)S(1)}, u32[]{:S(2)}, u32[]{:S(2)}) collective-permute-start(f32[2,1,2,32,256]{4,3,2,1,0:T(8,128)S(1)} %split.105), channel_id=1, source_target_pairs={{0,4},{2,6},{4,0},{6,2},{8,12},{10,14},{12,8},{14,10},{1,5},{3,7},... | collective-permute-start | bytes 393224 | tf_op jit(solution)/shard_map/ppermute | solution.py:492
  41.1 5.5 %collective-permute-start.18 = (f32[2,1,2,32,256]{4,3,2,1,0:T(8,128)S(1)}, f32[2,1,2,32,256]{4,3,2,1,0:T(8,128)S(1)}, u32[]{:S(2)}, u32[]{:S(2)}) collective-permute-start(f32[2,1,2,32,256]{4,3,2,1,0:T(8,128)S(1)} %split.109), channel_id=1, source_target_pairs={{0,2},{2,0},{4,6},{6,4},{8,10},{10,8},{12,14},{14,12},{1,3},{3,1},... | collective-permute-start | bytes 393224 | tf_op jit(solution)/shard_map/ppermute | solution.py:492
  41.9 13.7 %collective-permute-start.11 = (f32[1,1,2,32,256]{4,3,2,1,0:T(8,128)S(1)}, f32[1,1,2,32,256]{4,3,2,1,0:T(8,128)S(1)}, u32[]{:S(2)}, u32[]{:S(2)}) collective-permute-start(f32[1,1,2,32,256]{4,3,2,1,0:T(8,128)S(1)} %get-tuple-element.77), channel_id=1, source_target_pairs={{0,2},{2,0},{4,6},{6,4},{8,10},{10,8},{12,14},{14,12},{1,3},{3,1},... | collective-permute-start | bytes 196616 | tf_op jit(solution)/shard_map/ppermute | solution.py:492
  43.6 12.0 %collective-permute-start.14 = (f32[1,1,2,32,256]{4,3,2,1,0:T(8,128)S(1)}, f32[1,1,2,32,256]{4,3,2,1,0:T(8,128)S(1)}, u32[]{:S(2)}, u32[]{:S(2)}) collective-permute-start(f32[1,1,2,32,256]{4,3,2,1,0:T(8,128)S(1)} %get-tuple-element.75), channel_id=1, source_target_pairs={{0,8},{2,10},{4,12},{6,14},{8,0},{10,2},{12,4},{14,6},{1,9},{3,11}... | collective-permute-start | bytes 196616 | tf_op jit(solution)/shard_map/ppermute | solution.py:492
  46.7 8.9 %collective-permute-start.19 = (f32[2,1,2,32,256]{4,3,2,1,0:T(8,128)S(1)}, f32[2,1,2,32,256]{4,3,2,1,0:T(8,128)S(1)}, u32[]{:S(2)}, u32[]{:S(2)}) collective-permute-start(f32[2,1,2,32,256]{4,3,2,1,0:T(8,128)S(1)} %pad_maximum_fusion), channel_id=1, source_target_pairs={{0,8},{2,10},{4,12},{6,14},{8,0},{10,2},{12,4},{14,6},{1,9},{3,11}... | collective-permute-start | bytes 393224 | tf_op jit(solution)/shard_map/ppermute | solution.py:492
  48.5 7.1 %collective-permute-start.8 = (f32[2,64,256]{2,1,0:T(8,128)S(1)}, f32[2,64,256]{2,1,0:T(8,128)S(1)}, u32[]{:S(2)}, u32[]{:S(2)}) collective-permute-start(f32[2,64,256]{2,1,0:T(8,128)S(1)} %get-tuple-element.66), channel_id=1, source_target_pairs={{2,4},{6,8},{10,12},{4,2},{8,6},{12,10},{3,5},{7,9},{11,13},{5,3},... | collective-permute-start | bytes 393224 | tf_op jit(solution)/shard_map/ppermute | solution.py:506
  49.2 6.7 %collective-permute-start.7 = (f32[2,64,256]{2,1,0:T(8,128)S(1)}, f32[2,64,256]{2,1,0:T(8,128)S(1)}, u32[]{:S(2)}, u32[]{:S(2)}) collective-permute-start(f32[2,64,256]{2,1,0:T(8,128)S(1)} %get-tuple-element.67), channel_id=1, source_target_pairs={{0,2},{2,0},{4,6},{6,4},{8,10},{10,8},{12,14},{14,12},{1,3},{3,1},... | collective-permute-start | bytes 393224 | tf_op jit(solution)/shard_map/ppermute | solution.py:505
